TPU v7x, 32 devices: a whole 2x2x4 slice. The times are simulated.
32 devices in a mesh: dp: 8 (over z, y), mp: 4 (over x, core).
Axes of the slice: x: 2, y: 2, z: 4, core: 2. Of those that a mesh axis runs over, the one named last changes fastest.
Arguments:
- block_input: bfloat16 [96, 256, 768], P('dp'), may hold values from -6 to 6
- cotangent: bfloat16 [96, 256, 768], P('dp')
- crop_boxes: int32 [96, 4], P('dp'), may hold values from 0 to 16, as said below
- front_weights: float32 [7, 768, 768], P(None, 'dp', 'mp'), may hold values from -0.21875 to 0.21875
- back_weights: float32 [5, 768, 768], P(None, 'mp', 'dp')
- split_biases: float32 [6, 768], P(None, ('mp', 'dp')), may hold values from -4 to 4
- norm_params: float32 [6, 768], P(None, 'dp')
- pos_table: float32 [256, 768], P('dp'), may hold values from -6 to 6
- front_first: float32 [7, 768, 768], P(None, 'dp', 'mp'), may hold values from -5.722046e-06 to 5.722046e-06
- back_weight_first_moment: float32 [5, 768, 768], P(None, 'mp', 'dp'), may hold values from -5.722046e-06 to 5.722046e-06
- split_first: float32 [6, 768], P(None, ('mp', 'dp')), may hold values from -5.722046e-06 to 5.722046e-06
- norm_first: float32 [6, 768], P(None, 'dp'), may hold values from -5.722046e-06 to 5.722046e-06
- table_first: float32 [256, 768], P('dp'), may hold values from -7.1525574e-07 to 7.1525574e-07
- front_second: float32 [7, 768, 768], P(None, 'dp', 'mp'), may hold values from 7.436057e-13 to 2.9744228e-12
- back_second: float32 [5, 768, 768], P(None, 'mp', 'dp'), may hold values from 7.436057e-13 to 2.9744228e-12
- split_second: float32 [6, 768], P(None, ('mp', 'dp')), may hold values from 7.436057e-13 to 2.9744228e-12
- norm_second: float32 [6, 768], P(None, 'dp'), may hold values from 7.436057e-13 to 2.9744228e-12
- table_second: float32 [256, 768], P('dp'), may hold values from 1.1612473e-14 to 4.644989e-14
Outputs:
- block_output: bfloat16 [96, 256, 768], P('dp')
- input_grad: bfloat16 [96, 256, 768], P('dp')
- clip_norm: float32 [], replicated
- new_front: float32 [7, 768, 768], P(None, 'dp', 'mp')
- new_back: float32 [5, 768, 768], P(None, 'mp', 'dp')
- new_split: float32 [6, 768], P(None, ('mp', 'dp'))
- new_norm: float32 [6, 768], P(None, 'dp')
- new_table: float32 [256, 768], P('dp')
- front_first_new: float32 [7, 768, 768], P(None, 'dp', 'mp')
- back_first_new: float32 [5, 768, 768], P(None, 'mp', 'dp')
- split_first_new: float32 [6, 768], P(None, ('mp', 'dp'))
- norm_first_new: float32 [6, 768], P(None, 'dp')
- table_first_new: float32 [256, 768], P('dp')
- front_second_new: float32 [7, 768, 768], P(None, 'dp', 'mp')
- back_second_new: float32 [5, 768, 768], P(None, 'mp', 'dp')
- split_second_new: float32 [6, 768], P(None, ('mp', 'dp'))
- norm_second_new: float32 [6, 768], P(None, 'dp')
- table_second_new: float32 [256, 768], P('dp')
- norm_grad: float32 [6, 768], P(None, 'dp')
Inputs may be any that keep to these rules, and one draw needn't show every extreme that they name: `crop_boxes`: each row holds one grid's crop height and breadth, each 12 to 16, then its top row and left column, each at most 16 minus the height or breadth; the first grid is the whole 16 x 16 table.
All inputs are finite; a program needn't handle non-finite values.
Results may differ from a plain program's by a relative error of at most 0.019.
Values may be sent and summed in bfloat16 or wider, within the bound.
No kernel may reach another device: no remote copies, remote signals or barrier semaphores. Data moves between devices by JAX's collectives and lax.ppermute only.
A program may use at most 256 MiB of HBM per device.

v0:
```python
import jax
import jax.numpy as jnp
from jax import lax
from jax.sharding import PartitionSpec as P

D = 768
HEADS = 16
SIDE = 16
STEP = 5


NORM_EPS = 1e-05
BETA_FIRST = 0.9
BETA_SECOND = 0.95
ADAM_EPS = 1e-08
RATE_MATRIX = 0.05
RATE_TABLE = 0.2
RATE_VECTOR = 0.5
DECAY_RATE = 0.1
CLIP_LIMIT = 0.01
MASK_FILL = -1e30


def layer_norm(inputs, norm_gain, norm_shift):
    average = jnp.mean(inputs, axis=-1, keepdims=True)
    centred = inputs - average
    spread = jnp.mean(centred * centred, axis=-1, keepdims=True)
    return centred * lax.rsqrt(spread + NORM_EPS) * norm_gain + norm_shift


def position_codes(crop_boxes, cell_count, grid_side):
    height = crop_boxes[:, 0:1]
    breadth = crop_boxes[:, 1:2]
    top_row = crop_boxes[:, 2:3]
    left_col = crop_boxes[:, 3:4]
    position = jnp.arange(cell_count, dtype=jnp.int32)[None, :]
    is_valid = position < height * breadth
    target = (top_row + position // breadth) * grid_side + left_col + position % breadth
    target = jnp.where(is_valid, target, -1)
    onehot_tokens = target[:, :, None] == jnp.arange(cell_count, dtype=jnp.int32)[None, None, :]
    return (onehot_tokens, is_valid)


def exact_gelu(inputs):
    return jax.nn.gelu(inputs, approximate=False)


def adam_step(weight, gradient, first, second, rate, decay):
    first_new = BETA_FIRST * first + (1.0 - BETA_FIRST) * gradient
    second_new = BETA_SECOND * second + (1.0 - BETA_SECOND) * gradient * gradient
    first_hat = first_new / (1.0 - BETA_FIRST**STEP)
    second_hat = second_new / (1.0 - BETA_SECOND**STEP)
    weight_new = weight - rate * (first_hat / (jnp.sqrt(second_hat) + ADAM_EPS) + decay * weight)
    return (weight_new, first_new, second_new)


def body(
    block_input,
    cotangent,
    crop_boxes,
    front_weights,
    back_weights,
    split_biases,
    norm_params,
    pos_table,
    front_first,
    back_weight_first_moment,
    split_first,
    norm_first,
    table_first,
    front_second,
    back_second,
    split_second,
    norm_second,
    table_second,
):
    gathered_front, gathered_back, gathered_split, gathered_norm, gathered_table = (
        lax.all_gather(front_weights.astype(jnp.bfloat16), "dp", axis=1, tiled=True),
        lax.all_gather(back_weights.astype(jnp.bfloat16), "dp", axis=2, tiled=True),
        lax.all_gather(split_biases.astype(jnp.bfloat16), "dp", axis=1, tiled=True),
        lax.all_gather(norm_params.astype(jnp.bfloat16), "dp", axis=1, tiled=True),
        lax.all_gather(pos_table.astype(jnp.bfloat16), "dp", axis=0, tiled=True),
    )
    grid_count, cell_count, model_width = block_input.shape
    local_width = gathered_front.shape[2]
    head_size = D // HEADS
    heads_here = local_width // head_size
    tokens = grid_count * cell_count
    score_scale = head_size ** (-0.5)
    norm_vectors = gathered_norm.astype(jnp.float32)
    split_vectors = gathered_split.astype(jnp.float32)
    onehot_tokens, is_valid = position_codes(crop_boxes, cell_count, SIDE)
    token_embeddings = block_input.astype(jnp.float32) + jnp.einsum(
        "vfu,uk->vfk",
        onehot_tokens.astype(jnp.bfloat16),
        gathered_table,
        preferred_element_type=jnp.float32,
    )
    token_embeddings = token_embeddings.reshape(tokens, model_width)
    first_full, first_back = jax.vjp(layer_norm, token_embeddings, norm_vectors[0], norm_vectors[1])
    normed_first = first_full.astype(jnp.bfloat16)
    projected = jnp.einsum(
        "rd,jde->jre", normed_first, gathered_front[:3], preferred_element_type=jnp.float32
    )
    head_shape = (grid_count, cell_count, heads_here, head_size)
    queries = (projected[0] + split_vectors[0]).astype(jnp.bfloat16).reshape(head_shape)
    key_rows = projected[1].astype(jnp.bfloat16).reshape(head_shape)
    value_rows = (projected[2] + split_vectors[1]).astype(jnp.bfloat16).reshape(head_shape)
    key_mask = is_valid[:, None, None, :]

    def attention_scores():
        raw = (
            jnp.einsum("gqhs,gkhs->ghqk", queries, key_rows, preferred_element_type=jnp.float32)
            * score_scale
        )
        return jnp.where(key_mask, raw, MASK_FILL)

    scores = attention_scores()
    top_score = jnp.max(scores, axis=-1, keepdims=True)
    log_total = top_score + jnp.log(jnp.sum(jnp.exp(scores - top_score), axis=-1, keepdims=True))
    soft_low = jnp.exp(scores - log_total).astype(jnp.bfloat16)
    mixed = jnp.einsum("ghqk,gkhs->gqhs", soft_low, value_rows, preferred_element_type=jnp.float32)
    mixed_low = mixed.reshape(tokens, local_width).astype(jnp.bfloat16)
    attention_out = lax.psum(
        jnp.dot(mixed_low, gathered_back[0], preferred_element_type=jnp.float32).astype(
            jnp.bfloat16
        ),
        "mp",
    ).astype(jnp.float32)
    after_attention = token_embeddings + attention_out + norm_vectors[2]
    second_full, second_back = jax.vjp(
        layer_norm, after_attention, norm_vectors[3], norm_vectors[4]
    )
    normed_second = second_full.astype(jnp.bfloat16)
    hidden_pre = (
        jnp.einsum(
            "rd,jde->jre", normed_second, gathered_front[3:], preferred_element_type=jnp.float32
        )
        + split_vectors[2:, None, :]
    )
    hidden_act, gelu_back = jax.vjp(exact_gelu, hidden_pre)
    hidden_low = hidden_act.astype(jnp.bfloat16)
    mlp_out = lax.psum(
        jnp.einsum(
            "jre,jed->rd", hidden_low, gathered_back[1:], preferred_element_type=jnp.float32
        ).astype(jnp.bfloat16),
        "mp",
    ).astype(jnp.float32)
    block_output = (
        (after_attention + mlp_out + norm_vectors[5])
        .astype(jnp.bfloat16)
        .reshape(grid_count, cell_count, model_width)
    )
    grad_low = cotangent.reshape(tokens, model_width)
    grad_out = grad_low.astype(jnp.float32)
    grad_back_mlp = jnp.einsum(
        "jre,rd->jed", hidden_low, grad_low, preferred_element_type=jnp.float32
    )
    grad_hidden = jnp.einsum(
        "rd,jed->jre", grad_low, gathered_back[1:], preferred_element_type=jnp.float32
    )
    grad_pre = gelu_back(grad_hidden)[0].astype(jnp.bfloat16)
    grad_front_mlp = jnp.einsum(
        "rd,jre->jde", normed_second, grad_pre, preferred_element_type=jnp.float32
    )
    grad_split_mlp = jnp.sum(grad_pre, axis=1, dtype=jnp.float32)
    grad_normed_second = lax.psum(
        jnp.einsum(
            "jre,jde->rd", grad_pre, gathered_front[3:], preferred_element_type=jnp.float32
        ).astype(jnp.bfloat16),
        "mp",
    ).astype(jnp.float32)
    grad_after, grad_gain_second, grad_shift_second = second_back(grad_normed_second)
    grad_after = grad_after + grad_out
    grad_attn_low = grad_after.astype(jnp.bfloat16)
    grad_back_attn = jnp.einsum(
        "re,rd->ed", mixed_low, grad_attn_low, preferred_element_type=jnp.float32
    )
    grad_mixed = jnp.einsum(
        "rd,ed->re", grad_attn_low, gathered_back[0], preferred_element_type=jnp.float32
    )
    grad_mixed = grad_mixed.astype(jnp.bfloat16).reshape(head_shape)
    back_grad = jnp.concatenate([grad_back_attn[None], grad_back_mlp], axis=0)
    softmax_complete = jnp.exp(attention_scores() - log_total)
    soft_again = softmax_complete.astype(jnp.bfloat16)
    grad_value = jnp.einsum(
        "ghqk,gqhs->gkhs", soft_again, grad_mixed, preferred_element_type=jnp.float32
    ).astype(jnp.bfloat16)
    grad_soft = jnp.einsum(
        "gqhs,gkhs->ghqk", grad_mixed, value_rows, preferred_element_type=jnp.float32
    )
    grad_scores = (
        softmax_complete
        * (grad_soft - jnp.sum(grad_soft * softmax_complete, axis=-1, keepdims=True))
    ).astype(jnp.bfloat16)
    grad_query = (
        jnp.einsum("ghqk,gkhs->gqhs", grad_scores, key_rows, preferred_element_type=jnp.float32)
        * score_scale
    ).astype(jnp.bfloat16)
    grad_key = (
        jnp.einsum("ghqk,gqhs->gkhs", grad_scores, queries, preferred_element_type=jnp.float32)
        * score_scale
    ).astype(jnp.bfloat16)
    grad_projected = jnp.stack(
        [
            grad_query.reshape(tokens, local_width),
            grad_key.reshape(tokens, local_width),
            grad_value.reshape(tokens, local_width),
        ]
    )
    grad_front_attn = jnp.einsum(
        "rd,jre->jde", normed_first, grad_projected, preferred_element_type=jnp.float32
    )
    grad_split_attn = jnp.stack(
        [
            jnp.sum(grad_projected[0], axis=0, dtype=jnp.float32),
            jnp.sum(grad_projected[2], axis=0, dtype=jnp.float32),
        ]
    )
    grad_normed_first = lax.psum(
        jnp.einsum(
            "jre,jde->rd", grad_projected, gathered_front[:3], preferred_element_type=jnp.float32
        ).astype(jnp.bfloat16),
        "mp",
    ).astype(jnp.float32)
    grad_embedded, grad_gain_first, grad_shift_first = first_back(grad_normed_first)
    grad_embedded = grad_embedded + grad_after
    input_grad = grad_embedded.astype(jnp.bfloat16).reshape(grid_count, cell_count, model_width)
    grad_table = jnp.einsum(
        "ari,are->ie",
        onehot_tokens.astype(jnp.float32),
        grad_embedded.reshape(grid_count, cell_count, model_width),
        precision=lax.Precision.HIGHEST,
    )
    front_grad = jnp.concatenate([grad_front_attn, grad_front_mlp], axis=0)
    split_grad = jnp.concatenate([grad_split_attn, grad_split_mlp], axis=0)
    norm_grad = jnp.stack(
        [
            grad_gain_first,
            grad_shift_first,
            jnp.sum(grad_after, axis=0),
            grad_gain_second,
            grad_shift_second,
            jnp.sum(grad_out, axis=0),
        ]
    )
    front_share, back_share, split_share, norm_share, table_share = (
        lax.psum_scatter(front_grad, "dp", scatter_dimension=1, tiled=True),
        lax.psum_scatter(back_grad, "dp", scatter_dimension=2, tiled=True),
        lax.psum_scatter(split_grad, "dp", scatter_dimension=1, tiled=True),
        lax.psum_scatter(norm_grad, "dp", scatter_dimension=1, tiled=True),
        lax.psum_scatter(grad_table, "dp", scatter_dimension=0, tiled=True),
    )
    owner = (lax.axis_index("mp") == 0).astype(jnp.float32)
    local_square = (
        jnp.sum(front_share * front_share)
        + jnp.sum(back_share * back_share)
        + jnp.sum(split_share * split_share)
        + owner * (jnp.sum(norm_share * norm_share) + jnp.sum(table_share * table_share))
    )
    clip_norm = jnp.sqrt(lax.psum(local_square, ("dp", "mp")))
    factor = jnp.minimum(1.0, CLIP_LIMIT / (clip_norm + 1e-06))
    norm_clipped = norm_share * factor
    new_front, front_first_new, front_second_new = adam_step(
        front_weights, front_share * factor, front_first, front_second, RATE_MATRIX, DECAY_RATE
    )
    new_back, back_first_new, back_second_new = adam_step(
        back_weights,
        back_share * factor,
        back_weight_first_moment,
        back_second,
        RATE_MATRIX,
        DECAY_RATE,
    )
    new_split, split_first_new, split_second_new = adam_step(
        split_biases, split_share * factor, split_first, split_second, RATE_VECTOR, 0.0
    )
    new_norm, norm_first_new, norm_second_new = adam_step(
        norm_params, norm_clipped, norm_first, norm_second, RATE_VECTOR, 0.0
    )
    new_table, table_first_new, table_second_new = adam_step(
        pos_table, table_share * factor, table_first, table_second, RATE_TABLE, DECAY_RATE
    )
    return (
        block_output,
        input_grad,
        clip_norm,
        new_front,
        new_back,
        new_split,
        new_norm,
        new_table,
        front_first_new,
        back_first_new,
        split_first_new,
        norm_first_new,
        table_first_new,
        front_second_new,
        back_second_new,
        split_second_new,
        norm_second_new,
        table_second_new,
        norm_clipped,
    )


def solution(mesh):
    placed = (
        P("dp", None, None),
        P("dp", None, None),
        P("dp", None),
        P(None, "dp", "mp"),
        P(None, "mp", "dp"),
        P(None, ("mp", "dp")),
        P(None, "dp"),
        P("dp", None),
        P(None, "dp", "mp"),
        P(None, "mp", "dp"),
        P(None, ("mp", "dp")),
        P(None, "dp"),
        P("dp", None),
        P(None, "dp", "mp"),
        P(None, "mp", "dp"),
        P(None, ("mp", "dp")),
        P(None, "dp"),
        P("dp", None),
    )
    return jax.shard_map(
        body,
        mesh=mesh,
        in_specs=placed,
        out_specs=(
            P("dp", None, None),
            P("dp", None, None),
            P(),
            P(None, "dp", "mp"),
            P(None, "mp", "dp"),
            P(None, ("mp", "dp")),
            P(None, "dp"),
            P("dp", None),
            P(None, "dp", "mp"),
            P(None, "mp", "dp"),
            P(None, ("mp", "dp")),
            P(None, "dp"),
            P("dp", None),
            P(None, "dp", "mp"),
            P(None, "mp", "dp"),
            P(None, ("mp", "dp")),
            P(None, "dp"),
            P("dp", None),
            P(None, "dp"),
        ),
        check_vma=False,
    )
```

profile of v0, /device:TPU:0, one launch (start us, length us, event | category | flops | bytes accessed | tf_op | source)
XLA Modules:
  0.0 1084.0 jit_solution(15758157224161486688)
XLA Ops:
  13.0 28.0 %all-gather = bf16[8,96,6]{1,2,0:T(8,128)(2,1)S(1)} all-gather(bf16[1,96,6]{1,2,0:T(8,128)(2,1)S(1)} %convert_bitcast_fusion.1), channel_id=1, replica_groups=mesh['dp'=8,'mp'=4] {'dp'}, dimensions={0}, use_global_device_ids=true | all-gather | bytes 10368 | tf_op jit(solution)/shard_map/all_gather | solution.py:81
  41.0 26.5 %all-gather.1 = bf16[8,24,6]{1,2,0:T(8,128)(2,1)S(1)} all-gather(bf16[1,24,6]{1,2,0:T(8,128)(2,1)S(1)} %convert_bitcast_fusion), channel_id=1, replica_groups=mesh['dp'=8,'mp'=4] {'dp'}, dimensions={0}, use_global_device_ids=true | all-gather | bytes 2592 | tf_op jit(solution)/shard_map/all_gather | solution.py:80
  68.5 31.7 %all_gather.15 = bf16[256,768]{1,0:T(8,128)(2,1)S(1)} all-gather(bf16[32,768]{1,0:T(8,128)(2,1)S(1)} %convert_element_type.142), channel_id=1, replica_groups=mesh['dp'=8,'mp'=4] {'dp'}, dimensions={0}, use_global_device_ids=true | all-gather | bytes 442368 | tf_op jit(solution)/shard_map/all_gather | solution.py:82
  102.4 7.7 fusion.106
  115.7 7.5 add_convert_fusion.2
  126.2 12.1 %all-gather.5.cloned.1.call-done = bf16[7,768,192]{2,0,1:T(8,128)(2,1)} async-done(((bf16[7,96,192]{2,0,1:T(8,128)(2,1)}), bf16[7,768,192]{2,0,1:T(8,128)(2,1)}) %all-gather.5.cloned.1.call-update) | async-done | bytes 2064400 | tf_op jit(solution)/shard_map/all_gather | solution.py:78
  194.6 77.2 %all-reduce.6.cloned.1.call-done = bf16[3072,768]{1,0:T(8,128)(2,1)} async-done(((bf16[3072,768]{1,0:T(8,128)(2,1)}), bf16[3072,768]{1,0:T(8,128)(2,1)}) %all-reduce.6.cloned.1.call-update) | async-done | bytes 4718608 | tf_op jit(solution)/shard_map/psum | solution.py:124
  271.9 10.0 fusion.103
  293.9 22.5 %fusion.18 = (bf16[4,3072,192]{1,2,0:T(8,128)(2,1)}, f32[4,3072,192]{1,2,0:T(8,128)}) fusion(f32[3072,4,192]{0,2,1:T(8,128)S(1)} %bitcast.259, f32[4,192]{1,0:T(4,128)S(1)} %slice.107), kind=kLoop, calls=%fused_computation.42 | loop fusion | flops 155713536 | bytes 23596032 | tf_op jit(solution)/shard_map/convert_element_type | solution.py:142
  316.4 12.1 %convert_reduce_fusion.3 = (f32[4,192]{1,0:T(4,128)}, bf16[4,3072,192]{1,2,0:T(8,128)(2,1)}) fusion(f32[4,3072,192]{1,2,0:T(8,128)} %get-tuple-element.153, bf16[4,192,768]{2,1,0:T(8,128)(2,1)S(1)} %copy-done.14, bf16[3072,768,1]{1,0,2:T(8,128)(2,1)S(1)} %bitcast.256, f32[3072,4,192]{0,2,1:T(8,128)} %bitcast.260, f32[4,192]{1,0:T(4,128)S(1)} %slice.107), kind=kOutput, calls=%fused_computation.47 | convolution fusion | flops 3663985920 | bytes 29497344 | tf_op jit(solution)/shard_map/rd,jed->jre/dot_general | solution.py:159
  328.5 8.2 bitcast_convert_fusion.1
  336.7 8.7 bitcast_convert_fusion.2
  345.5 85.5 %all-reduce.8.cloned.1.call-done = bf16[3072,768]{1,0:T(8,128)(2,1)} async-done(((bf16[3072,768]{1,0:T(8,128)(2,1)}), bf16[3072,768]{1,0:T(8,128)(2,1)}) %all-reduce.8.cloned.1.call-update) | async-done | bytes 4718608 | tf_op jit(solution)/shard_map/psum | solution.py:167
  431.0 8.4 convert_reduce_fusion.1
  439.5 7.7 fusion.8
  462.1 8.6 convert_reduce_fusion.4
  470.7 12.9 %multiply_reduce_fusion = (f32[12,4,256]{2,1,0:T(4,128)S(1)}, f32[12,4,256,256]{2,3,1,0:T(8,128)}) fusion(f32[12,4,256,256]{2,3,1,0:T(8,128)} %copy-done.2, f32[12,4,256]{2,1,0:T(4,128)S(1)} %bitcast.274, pred[12,256]{1,0:T(8,128)(4,1)S(1)} %iota_compare_fusion.5, bf16[12,256,4,48]{1,0,3,2:T(8,128)(2,1)S(1)} %copy-done.9, ...), kind=kOutput, calls=%fused_computation.10 | convolution fusion | flops 317706240 | bytes 27626496 | tf_op jit(solution)/shard_map/gqhs,gkhs->ghqk/dot_general | solution.py:189
  483.7 7.4 multiply_convert_fusion
  515.8 6.8 bitcast_convert_fusion
  526.2 10.0 fusion.109
  537.4 155.6 %all-reduce.10.cloned.1.call-done = (bf16[3072,768]{1,0:T(8,128)(2,1)}, bf16[3072,768]{1,0:T(8,128)(2,1)}) async-done(((bf16[3072,768]{1,0:T(8,128)(2,1)}, bf16[3072,768]{1,0:T(8,128)(2,1)}), (bf16[3072,768]{1,0:T(8,128)(2,1)}, bf16[3072,768]{1,0:T(8,128)(2,1)})) %all-reduce.10.cloned.1.call-update) | async-done | bytes 9437200 | tf_op jit(solution)/shard_map/psum | solution.py:143
  693.0 7.6 convert_reduce_fusion
  700.8 7.6 fusion.9
  722.1 11.5 %fusion.101 = (bf16[3072,768]{1,0:T(8,128)(2,1)}, f32[3072,768]{1,0:T(8,128)S(1)}) fusion(f32[3072,768]{1,0:T(8,128)} %copy-done.1, f32[3072]{0:T(1024)S(1)} %negate_multiply_fusion.1, f32[3072]{0:T(1024)S(1)} %copy-done.33, f32[3072]{0:T(1024)S(1)} %copy-done.24, f32[12,256,768]{2,1,0:T(8,128)} %get-tuple-element.165, f32[3072]{0:T(1024)S(1)} %copy-done.29, ...), kind=kLoop, calls=%fused_computation.198 | loop fusion | flops 23592960 | bytes 37800960 | tf_op jit(solution)/shard_map/convert_element_type | solution.py:228
  740.0 7.2 fusion.41
  761.2 7.2 reshape.425
  772.7 22.1 %all-reduce = f32[6,192]{1,0:T(8,128)S(1)} all-reduce(f32[6,192]{1,0:T(8,128)S(1)} %pad_maximum_fusion.2), channel_id=4, replica_groups=mesh['dp'=8,'mp'=4] {'dp'}, use_global_device_ids=true, to_apply=%region_22.23.clone | all-reduce | flops 1152 | bytes 9216
  796.9 51.5 %reduce-scatter.16.cloned.1.call-done = f32[96,960]{1,0:T(8,128)} async-done(((f32[768,960]{1,0:T(8,128)}), f32[96,960]{1,0:T(8,128)}) %reduce-scatter.16.cloned.1.call-update) | async-done | bytes 368656
  850.6 62.7 %reduce-scatter.12.cloned.1.call-done = f32[32,768]{1,0:T(8,128)} async-done(((f32[256,768]{1,0:T(8,128)}), f32[32,768]{1,0:T(8,128)}) %reduce-scatter.12.cloned.1.call-update) | async-done | bytes 98320 | tf_op jit(solution)/shard_map/reduce_scatter | solution.py:252
  916.2 90.6 %reduce-scatter.14.cloned.1.call-done = f32[96,1344]{1,0:T(8,128)} async-done(((f32[768,1344]{1,0:T(8,128)}), f32[96,1344]{1,0:T(8,128)}) %reduce-scatter.14.cloned.1.call-update) | async-done | bytes 516112
  1011.2 8.5 add_convert_fusion
  1019.7 40.3 %psum.39 = f32[]{:T(128)} all-reduce(f32[]{:T(128)S(6)} %add.315), channel_id=1, replica_groups=mesh['dp'=8,'mp'=4] {'dp','mp'}, use_global_device_ids=true, to_apply=%region_34.35 | all-reduce | flops 1 | bytes 8 | tf_op jit(solution)/shard_map/psum | solution.py:261
  (265 shorter events, 191.2 us)
Async XLA Ops:
  7.2 116.1 %all-gather.7.cloned.1.call-start = ((), (), s32[]{:S(2)}) async-start(), calls=%async_computation.5 | async-start | bytes 3538944 | tf_op jit(solution)/shard_map/all_gather | solution.py:79
  9.4 128.9 %all-gather.5.cloned.1.call-start = ((), (), s32[]{:S(2)}) async-start(), calls=%async_computation.4 | async-start | bytes 3538944 | tf_op jit(solution)/shard_map/all_gather | solution.py:78
  11.6 260.3 %all-reduce.6.cloned.1.call-start = ((), (), s32[]{:S(2)}) async-start(), calls=%async_computation.6 | async-start | bytes 9437184 | tf_op jit(solution)/shard_map/psum | solution.py:124
  110.1 13.1 %copy-start.23 = (f32[3072]{0:T(1024)}, f32[3072]{0:T(1024)S(1)}, u32[]{:S(2)}) copy-start(f32[3072]{0:T(1024)S(1)} %div.138) | copy-start | bytes 36868
  179.1 251.9 %all-reduce.8.cloned.1.call-start = ((), (), s32[]{:S(2)}) async-start(), calls=%async_computation.7 | async-start | bytes 9437184 | tf_op jit(solution)/shard_map/psum | solution.py:167
  288.2 28.1 %slice-start.11 = ((s8[4718592]{0:T(1024)(128)(4,1)}), s8[4194304]{0:T(1024)(128)(4,1)S(1)}, s32[]{:S(2)}) async-start(s8[4718592]{0:T(1024)(128)(4,1)} %bitcast.254), calls=%async_computation.24 | async-start | bytes 8388608
  290.0 26.4 %slice-start.12 = ((s8[4718592]{0:T(1024)(128)(4,1)}), s8[524288]{0:T(1024)(128)(4,1)S(1)}, s32[]{:S(2)}) async-start(s8[4718592]{0:T(1024)(128)(4,1)} %bitcast.254), calls=%async_computation.25 | async-start | bytes 1048576
  293.8 22.5 %copy-start.6 = (f32[3072,768]{0,1}, f32[3072,768]{0,1:S(1)}, u32[]{:S(2)}) copy-start(f32[3072,768]{0,1:S(1)} %fusion.108) | copy-start | bytes 28311556
  293.8 22.5 %copy-start.14 = (bf16[4,192,768]{2,1,0:T(8,128)(2,1)S(1)}, bf16[4,192,768]{2,1,0:T(8,128)(2,1)}, u32[]{:S(2)}) copy-start(bf16[4,192,768]{2,1,0:T(8,128)(2,1)} %copy.194) | copy-start | bytes 3538948
  316.4 12.1 %copy-start.16 = (bf16[4,768,192]{1,2,0:T(8,128)(2,1)S(1)}, bf16[4,768,192]{1,2,0:T(8,128)(2,1)}, u32[]{:S(2)}) copy-start(bf16[4,768,192]{1,2,0:T(8,128)(2,1)} %copy.193) | copy-start | bytes 3538948
  336.7 356.4 %all-reduce.10.cloned.1.call-start = ((), (), s32[]{:S(2)}) async-start(), calls=%async_computation.12 | async-start | bytes 18874368 | tf_op jit(solution)/shard_map/psum | solution.py:143
  431.0 16.2 %slice-start = ((s8[9437184]{0:T(1024)(128)(4,1)}), s8[4194304]{0:T(1024)(128)(4,1)S(1)}, s32[]{:S(2)}) async-start(s8[9437184]{0:T(1024)(128)(4,1)} %bitcast.240), calls=%async_computation.13 | async-start | bytes 8388608
  431.0 16.2 %slice-start.1 = ((s8[9437184]{0:T(1024)(128)(4,1)}), s8[4194304]{0:T(1024)(128)(4,1)S(1)}, s32[]{:S(2)}) async-start(s8[9437184]{0:T(1024)(128)(4,1)} %bitcast.240), calls=%async_computation.14 | async-start | bytes 8388608
  462.1 21.6 %slice-start.6 = ((s8[12582912]{0:T(1024)(128)(4,1)}), s8[4194304]{0:T(1024)(128)(4,1)S(1)}, s32[]{:S(2)}) async-start(s8[12582912]{0:T(1024)(128)(4,1)} %bitcast.244), calls=%async_computation.19 | async-start | bytes 8388608
  462.1 21.6 %slice-start.7 = ((s8[12582912]{0:T(1024)(128)(4,1)}), s8[4194304]{0:T(1024)(128)(4,1)S(1)}, s32[]{:S(2)}) async-start(s8[12582912]{0:T(1024)(128)(4,1)} %bitcast.244), calls=%async_computation.20 | async-start | bytes 8388608
  470.7 12.9 %slice-start.8 = ((s8[12582912]{0:T(1024)(128)(4,1)}), s8[4194304]{0:T(1024)(128)(4,1)S(1)}, s32[]{:S(2)}) async-start(s8[12582912]{0:T(1024)(128)(4,1)} %bitcast.244), calls=%async_computation.21 | async-start | bytes 8388608
  522.5 272.9 %reduce-scatter.18.cloned.1.call-start = ((), (), s32[]{:S(2)}) async-start(), calls=%async_computation.11 | async-start | bytes 442368
  523.0 13.3 %slice-start.3 = ((s8[9437184]{0:T(1024)(128)(4,1)}), s8[1048576]{0:T(1024)(128)(4,1)S(1)}, s32[]{:S(2)}) async-start(s8[9437184]{0:T(1024)(128)(4,1)} %bitcast.242), calls=%async_computation.16 | async-start | bytes 2097152
  536.2 156.8 %copy-start.24 = (f32[3072]{0:T(1024)S(1)}, f32[3072]{0:T(1024)}, u32[]{:S(2)}) copy-start(f32[3072]{0:T(1024)} %copy-done.23) | copy-start | bytes 36868
  536.2 156.8 %copy-start.35 = (f32[768]{0:T(1024)S(1)}, f32[768]{0:T(1024)}, u32[]{:S(2)}) copy-start(f32[768]{0:T(1024)} %copy-done.34) | copy-start | bytes 9220
  537.4 163.3 %copy-start.31 = (f32[3072]{0:T(1024)S(1)}, f32[3072]{0:T(1024)}, u32[]{:S(2)}) copy-start(f32[3072]{0:T(1024)} %copy-done.30) | copy-start | bytes 36868
  537.4 163.3 %copy-start.28 = (f32[3072]{0:T(1024)S(1)}, f32[3072]{0:T(1024)}, u32[]{:S(2)}) copy-start(f32[3072]{0:T(1024)} %copy-done.27) | copy-start | bytes 36868
  709.4 139.0 %reduce-scatter.16.cloned.1.call-start = ((), (), s32[]{:S(2)}) async-start(), calls=%async_computation.10 | async-start | bytes 3538944
  721.8 191.5 %reduce-scatter.12.cloned.1.call-start = ((), (), s32[]{:S(2)}) async-start(), calls=%async_computation.8 | async-start | bytes 884736 | tf_op jit(solution)/shard_map/reduce_scatter | solution.py:252
  722.1 11.5 %copy-start.26 = (s32[12,256]{1,0:T(8,128)S(1)}, s32[12,256]{1,0:T(8,128)}, u32[]{:S(2)}) copy-start(s32[12,256]{1,0:T(8,128)} %copy-done.25) | copy-start | bytes 36868
  739.7 267.1 %reduce-scatter.14.cloned.1.call-start = ((), (), s32[]{:S(2)}) async-start(), calls=%async_computation.9 | async-start | bytes 4866048
  768.4 242.8 %copy-start.40 = (f32[768]{0:T(1024)S(1)}, f32[768]{0:T(1024)}, u32[]{:S(2)}) copy-start(f32[768]{0:T(1024)} %get-tuple-element.122) | copy-start | bytes 9220
  1011.2 49.5 %copy-start.12 = (f32[7,96,192]{1,2,0:T(8,128)S(1)}, f32[7,96,192]{1,2,0:T(8,128)}, u32[]{:S(2)}) copy-start(f32[7,96,192]{1,2,0:T(8,128)} %copy.172) | copy-start | bytes 1548292
  1011.2 57.9 %copy-start.41 = (f32[6,24]{1,0:T(8,128)S(1)}, f32[6,24]{1,0:T(8,128)}, u32[]{:S(2)}) copy-start(f32[6,24]{1,0:T(8,128)} %param.23) | copy-start | bytes 1732
  1019.7 54.8 %copy-start.19 = (f32[32,768]{1,0:T(8,128)S(1)}, f32[32,768]{1,0:T(8,128)}, u32[]{:S(2)}) copy-start(f32[32,768]{1,0:T(8,128)} %param.25) | copy-start | bytes 294916
  1019.7 54.8 %copy-start.20 = (f32[32,768]{1,0:T(8,128)S(1)}, f32[32,768]{1,0:T(8,128)}, u32[]{:S(2)}) copy-start(f32[32,768]{1,0:T(8,128)} %reduce-scatter.12.cloned.1.call-done) | copy-start | bytes 294916
  1019.7 54.8 %copy-start.36 = (f32[32,768]{1,0:T(8,128)S(1)}, f32[32,768]{1,0:T(8,128)}, u32[]{:S(2)}) copy-start(f32[32,768]{1,0:T(8,128)} %param.30) | copy-start | bytes 294916
  (39 other events, 310.4 us)
Sparse Core Ops, SparseCore 0:
  10.8 64.8 all-gather.6
  78.5 59.8 all-gather.4
  179.2 92.6 all-reduce.5
  336.8 94.1 all-reduce.7
  522.7 170.3 all-reduce.9
  709.5 61.5 reduce-scatter.17
  774.7 73.6 reduce-scatter.15
  851.7 61.5 reduce-scatter.11
  917.9 88.7 reduce-scatter.13
where the time goes:
time: 1090 us; the launch traced here: 1080 us
  waiting for transfers between devices  535 us (49%)
  other arithmetic  150 us (14%)
  blocking collectives  149 us (14%)
  matrix products  124 us (11%)
  local copies, waits for them, and re-layouts  104 us (10%)
  between operations  20.9 us (2%)
    psum x1, waiting for transfers between devices, body(): lax.psum(jnp.einsum('jre,jed->rd', hidden_low, gathered_back[1:], preferr...  156 us
    unnamed x12, waiting for transfers between devices  142 us
    psum x1, waiting for transfers between devices, body(): lax.psum(jnp.einsum('jre,jde->rd', grad_pre, gathered_front[3:], preferre...  85.5 us
    psum x1, waiting for transfers between devices, body(): lax.psum(jnp.dot(mixed_low, gathered_back[0], preferred_element_type=jnp....  77.2 us
    reduce_scatter x1, waiting for transfers between devices, body(): lax.psum_scatter(grad_table, 'dp', scatter_dimension=0, tiled=True)  62.7 us
    unnamed x148, local copies, waits for them, and re-layouts  57.3 us
    psum x1, blocking collectives, body(): clip_norm = jnp.sqrt(lax.psum(local_square, ('dp', 'mp')))  40.3 us
    all_gather x1, blocking collectives, body(): lax.all_gather(pos_table.astype(jnp.bfloat16), 'dp', axis=0, tiled=True)  31.7 us
  transfers between devices with their start and end apart: 9, of which 7 were waited for; matrix products, arithmetic and copies ran while one was open for 13% of the time, Pallas kernels for 0%

commit v1 on v0

v1 whole, which is shorter than its diff:
```python
import functools

import jax
import jax.numpy as jnp
from jax import lax
from jax.experimental import pallas as pl
from jax.experimental.pallas import tpu as pltpu
from jax.sharding import PartitionSpec as P

D = 768
HEADS = 16
HEAD = D // HEADS
SIDE = 16
CELLS = 256
STEP = 5
CORES = 2

NORM_EPS = 1e-05
BETA_FIRST = 0.9
BETA_SECOND = 0.95
ADAM_EPS = 1e-08
RATE_MATRIX = 0.05
RATE_TABLE = 0.2
RATE_VECTOR = 0.5
DECAY_RATE = 0.1
CLIP_LIMIT = 0.01
MASK_FILL = -1e30
SCALE = HEAD ** (-0.5)
LOG2E = 1.4426950408889634
INV_SQRT_2PI = 0.3989422804014327

BF = jnp.bfloat16
F32 = jnp.float32
VMEM_LIMIT = 60 * 1024 * 1024
NN = (((1,), (0,)), ((), ()))
NT = (((1,), (1,)), ((), ()))
TN = (((0,), (0,)), ((), ()))


def dot(a, b, dims=NN):
    return lax.dot_general(a, b, dims, preferred_element_type=F32)


def params(limit=VMEM_LIMIT):
    return pltpu.CompilerParams(vmem_limit_bytes=limit)


def norm_stats(v):
    mean = jnp.mean(v, axis=-1, keepdims=True)
    centred = v - mean
    spread = jnp.mean(centred * centred, axis=-1, keepdims=True)
    rstd = lax.rsqrt(spread + NORM_EPS)
    return centred * rstd, rstd


def norm_back(c, gain, u, rstd):
    cg = c * gain
    mean_cg = jnp.mean(cg, axis=-1, keepdims=True)
    mean_cgu = jnp.mean(cg * u, axis=-1, keepdims=True)
    return rstd * (cg - mean_cg - u * mean_cgu)


def head_window(h):
    low = h * HEAD
    first = low // 128
    last = (low + HEAD - 1) // 128
    return first, last + 1 - first


def head_mask(h):
    first, tiles = head_window(h)
    lane = lax.broadcasted_iota(jnp.int32, (1, tiles * 128), 1) + first * 128
    return (lane >= h * HEAD) & (lane < (h + 1) * HEAD)


def crop_target(position, height, breadth, top, left):
    row = (position >> 4) - top
    col = (position & (SIDE - 1)) - left
    inside = (row >= 0) & (row < height) & (col >= 0) & (col < breadth)
    return jnp.where(inside, row * breadth + col, -1)


def attention_forward_kernel(
    scal, crop, x_ref, table_ref, w_ref, vec_ref,
    emb_ref, n1_ref, q_ref, k_ref, v_ref, p_ref, mixed_ref, after_ref, n2_ref,
):
    grid = scal[0] + pl.program_id(0)
    height, breadth, top, left = crop[grid, 0], crop[grid, 1], crop[grid, 2], crop[grid, 3]
    target = crop_target(
        lax.broadcasted_iota(jnp.int32, (1, CELLS), 1), height, breadth, top, left
    )
    cell = lax.broadcasted_iota(jnp.int32, (CELLS, CELLS), 0)
    onehot = jnp.where(cell == target, 1.0, 0.0).astype(BF)
    emb = x_ref[0].astype(F32) + dot(onehot, table_ref[...])
    emb_ref[...] = emb
    u, _ = norm_stats(emb)
    n1 = (u * vec_ref[0:1, :] + vec_ref[1:2, :]).astype(BF)
    n1_ref[...] = n1
    q_ref[...] = (dot(n1, w_ref[0]) + vec_ref[8:9, :]).astype(BF)
    k_ref[...] = dot(n1, w_ref[1]).astype(BF)
    v_ref[...] = (dot(n1, w_ref[2]) + vec_ref[9:10, :]).astype(BF)
    valid = lax.broadcasted_iota(jnp.int32, (1, CELLS), 1) < height * breadth
    tiles_out = [None] * (D // 128)
    for h in range(HEADS):
        first, tiles = head_window(h)
        lanes = slice(first * 128, (first + tiles) * 128)
        mask = head_mask(h)
        qh = jnp.where(mask, q_ref[:, lanes], 0).astype(BF)
        vh = jnp.where(mask, v_ref[:, lanes], 0).astype(BF)
        s = jnp.where(valid, dot(qh, k_ref[:, lanes], NT), MASK_FILL)
        top_score = jnp.max(s, axis=-1, keepdims=True)
        e = jnp.exp2((s - top_score) * (SCALE * LOG2E))
        p = (e * (1.0 / jnp.sum(e, axis=-1, keepdims=True))).astype(BF)
        p_ref[0, h] = p
        o = dot(p, vh)
        for t in range(tiles):
            part = o[:, t * 128 : (t + 1) * 128]
            at = first + t
            tiles_out[at] = part if tiles_out[at] is None else tiles_out[at] + part
    for t in range(D // 128):
        mixed_ref[:, t * 128 : (t + 1) * 128] = tiles_out[t].astype(BF)
    attention = dot(mixed_ref[...], w_ref[3], NT)
    after = emb_ref[...] + attention + vec_ref[2:3, :]
    after_ref[...] = after
    u2, _ = norm_stats(after)
    n2_ref[...] = (u2 * vec_ref[3:4, :] + vec_ref[4:5, :]).astype(BF)


def up_kernel(scal, n2_ref, w_ref, vec_ref, g_ref, hidden_ref, gp_ref, mine_ref, other_ref, gt_ref):
    j = pl.program_id(0)
    grids = g_ref.shape[0]

    @pl.when(j == 0)
    def _():
        for n in range(grids):
            gt_ref[:, n * CELLS : (n + 1) * CELLS] = g_ref[n].T

    bias = vec_ref[pl.ds(10 + j, 1), :]
    for n in range(grids):
        rows = slice(n * CELLS, (n + 1) * CELLS)
        pre = dot(n2_ref[rows, :], w_ref[0]) + bias
        phi = 0.5 + 0.5 * lax.erf(pre * (0.5**0.5))
        density = jnp.exp2(pre * pre * (-0.5 * LOG2E)) * INV_SQRT_2PI
        hidden_ref[0, rows, :] = (pre * phi).astype(BF)
        gp_ref[0, rows, :] = (phi + pre * density).astype(BF)
    grad = dot(gt_ref[...], hidden_ref[0]).astype(BF)
    keep(scal[1], j, grad, mine_ref, other_ref)


def keep(core, j, grad, mine_ref, other_ref):
    @pl.when(core == j // 2)
    def _():
        mine_ref[j % 2] = grad

    @pl.when(core != j // 2)
    def _():
        other_ref[j % 2] = grad


def mlp_kernel(
    scal, hidden_ref, gp_ref, down_ref, up_ref, n2_ref, g_ref, after_ref, vec_ref,
    out_ref, ga_ref, galow_ref, mine_ref, other_ref, gb_ref, gn_ref,
    mlp_acc, dn2_acc, n2t_ref,
):
    j = pl.program_id(0)
    grids = g_ref.shape[0]

    @pl.when(j == 0)
    def _():
        for n in range(grids):
            rows = slice(n * CELLS, (n + 1) * CELLS)
            n2t_ref[:, rows] = n2_ref[rows, :].T
        mlp_acc[...] = jnp.zeros_like(mlp_acc)
        dn2_acc[...] = jnp.zeros_like(dn2_acc)
        gb_ref[...] = jnp.zeros_like(gb_ref)
        gn_ref[...] = jnp.zeros_like(gn_ref)

    colsum = jnp.zeros((1, D), F32)
    for n in range(grids):
        rows = slice(n * CELLS, (n + 1) * CELLS)
        gh = dot(g_ref[n], down_ref[0])
        gpre = (gh * gp_ref[0, rows, :].astype(F32)).astype(BF)
        gp_ref[0, rows, :] = gpre
        colsum = colsum + jnp.sum(gpre.astype(F32), axis=0, keepdims=True)
        mlp_acc[rows, :] += dot(hidden_ref[0, rows, :], down_ref[0], NT)
        dn2_acc[rows, :] += dot(gpre, up_ref[0], NT)
    gb_ref[pl.ds(j, 1), :] = colsum
    keep(scal[1], j, dot(n2t_ref[...], gp_ref[0]).astype(BF), mine_ref, other_ref)

    @pl.when(j == pl.num_programs(0) - 1)
    def _():
        sums = [jnp.zeros((1, D), F32)] * 4
        for n in range(grids):
            rows = slice(n * CELLS, (n + 1) * CELLS)
            after = after_ref[rows, :]
            out_ref[n] = (after + mlp_acc[rows, :] + vec_ref[5:6, :]).astype(BF)
            u, rstd = norm_stats(after)
            c = dn2_acc[rows, :]
            g = g_ref[n].astype(F32)
            ga = g + norm_back(c, vec_ref[3:4, :], u, rstd)
            ga_ref[rows, :] = ga
            galow_ref[rows, :] = ga.astype(BF)
            parts = (ga, c * u, c, g)
            sums = [s + jnp.sum(v, axis=0, keepdims=True) for s, v in zip(sums, parts)]
        for i in range(4):
            gn_ref[2 + i : 3 + i, :] = sums[i]


def attention_backward_kernel(
    scal, crop, ga_ref, galow_ref, mixed_ref, p_ref, q_ref, k_ref, v_ref, emb_ref, w_ref, vec_ref,
    dq_ref, dk_ref, dv_ref, ig_ref, table_ref, gs_ref, dm_ref,
):
    i = pl.program_id(0)
    grid = scal[0] + i
    height, breadth, top, left = crop[grid, 0], crop[grid, 1], crop[grid, 2], crop[grid, 3]

    @pl.when(i == 0)
    def _():
        table_ref[...] = jnp.zeros_like(table_ref)
        gs_ref[...] = jnp.zeros_like(gs_ref)

    dm_ref[...] = dot(galow_ref[...], w_ref[3]).astype(BF)
    outs = [[None] * (D // 128) for _ in range(3)]
    for h in range(HEADS):
        first, tiles = head_window(h)
        lanes = slice(first * 128, (first + tiles) * 128)
        mask = head_mask(h)
        qh = jnp.where(mask, q_ref[:, lanes], 0).astype(BF)
        kh = jnp.where(mask, k_ref[:, lanes], 0).astype(BF)
        dmh = jnp.where(mask, dm_ref[:, lanes], 0).astype(BF)
        p = p_ref[0, h]
        dp = dot(dmh, v_ref[:, lanes], NT)
        delta = jnp.sum(
            dmh.astype(F32) * mixed_ref[:, lanes].astype(F32), axis=-1, keepdims=True
        )
        ds = (p.astype(F32) * (dp - delta)).astype(BF)
        got = (dot(ds, kh), dot(ds, qh, TN), dot(p, dmh, TN))
        for o in range(3):
            for t in range(tiles):
                part = got[o][:, t * 128 : (t + 1) * 128]
                at = first + t
                outs[o][at] = part if outs[o][at] is None else outs[o][at] + part
    for t in range(D // 128):
        lanes = slice(t * 128, (t + 1) * 128)
        dq_ref[:, lanes] = (outs[0][t] * SCALE).astype(BF)
        dk_ref[:, lanes] = (outs[1][t] * SCALE).astype(BF)
        dv_ref[:, lanes] = outs[2][t].astype(BF)
    dq, dk, dv = dq_ref[...], dk_ref[...], dv_ref[...]
    c = dot(dq, w_ref[0], NT) + dot(dk, w_ref[1], NT) + dot(dv, w_ref[2], NT)
    u, rstd = norm_stats(emb_ref[...])
    ge = ga_ref[...] + norm_back(c, vec_ref[0:1, :], u, rstd)
    high = ge.astype(BF)
    ig_ref[0] = high
    low = (ge - high.astype(F32)).astype(BF)
    target = crop_target(
        lax.broadcasted_iota(jnp.int32, (CELLS, 1), 0), height, breadth, top, left
    )
    cell = lax.broadcasted_iota(jnp.int32, (CELLS, CELLS), 1)
    onehot = jnp.where(cell == target, 1.0, 0.0).astype(BF)
    table_ref[...] += dot(onehot, high) + dot(onehot, low)
    for row, v in enumerate((dq.astype(F32), dv.astype(F32), c * u, c)):
        gs_ref[row : row + 1, :] += jnp.sum(v, axis=0, keepdims=True)


def projection_grad_kernel(
    scal, n1_ref, galow_ref, dq_ref, dk_ref, dv_ref, mixed_ref, mine_ref, other_ref, t_ref
):
    core = scal[1]
    tokens = n1_ref.shape[0]
    for n in range(tokens // CELLS):
        rows = slice(n * CELLS, (n + 1) * CELLS)
        t_ref[:, rows] = n1_ref[rows, :].T
    keep(core, 0, dot(t_ref[...], dq_ref[...]).astype(BF), mine_ref, other_ref)
    keep(core, 1, dot(t_ref[...], dk_ref[...]).astype(BF), mine_ref, other_ref)
    keep(core, 2, dot(t_ref[...], dv_ref[...]).astype(BF), mine_ref, other_ref)
    for n in range(tokens // CELLS):
        rows = slice(n * CELLS, (n + 1) * CELLS)
        t_ref[:, rows] = galow_ref[rows, :].T
    keep(core, 3, dot(t_ref[...], mixed_ref[...]).astype(BF), mine_ref, other_ref)


def sds(shape, dtype):
    return jax.ShapeDtypeStruct(shape, dtype)


def whole_block(shape):
    zeros = (0,) * len(shape)
    return pl.BlockSpec(shape, lambda i, *_: zeros)


def attention_forward(scal, crop, x, table, w, vec, grids):
    tokens = grids * CELLS
    rows = pl.BlockSpec((CELLS, D), lambda i, *_: (i, 0))
    spec = pltpu.PrefetchScalarGridSpec(
        num_scalar_prefetch=2,
        grid=(grids,),
        in_specs=[
            pl.BlockSpec((1, CELLS, D), lambda i, s, c: (s[0] + i, 0, 0)),
            whole_block((CELLS, D)),
            whole_block((4, D, D)),
            whole_block((16, D)),
        ],
        out_specs=[
            rows, rows, rows, rows, rows,
            pl.BlockSpec((1, HEADS, CELLS, CELLS), lambda i, *_: (i, 0, 0, 0)),
            rows, rows, rows,
        ],
    )
    low, full = sds((tokens, D), BF), sds((tokens, D), F32)
    return pl.pallas_call(
        attention_forward_kernel,
        grid_spec=spec,
        out_shape=[
            full, low, low, low, low, sds((grids, HEADS, CELLS, CELLS), BF), low, full, low,
        ],
        compiler_params=params(),
        cost_estimate=pl.CostEstimate(
            flops=8 * tokens * D * D + 64 * tokens * CELLS * 256,
            bytes_accessed=24 * tokens * D,
            transcendentals=tokens * CELLS * HEADS,
        ),
        name="attention_forward",
    )(scal, crop, x, table, w, vec)


def up_forward(scal, n2, w, vec, cotangent, grids):
    tokens = grids * CELLS
    block = pl.BlockSpec((1, tokens, D), lambda j, *_: (j, 0, 0))
    half = whole_block((2, D, D))
    spec = pltpu.PrefetchScalarGridSpec(
        num_scalar_prefetch=1,
        grid=(4,),
        in_specs=[
            whole_block((tokens, D)),
            pl.BlockSpec((1, D, D), lambda j, *_: (j, 0, 0)),
            whole_block((16, D)),
            pl.BlockSpec((grids, CELLS, D), lambda j, s: (s[2], 0, 0)),
        ],
        out_specs=[block, block, half, half],
        scratch_shapes=[pltpu.VMEM((D, tokens), BF)],
    )
    return pl.pallas_call(
        up_kernel,
        grid_spec=spec,
        out_shape=[
            sds((4, tokens, D), BF), sds((4, tokens, D), BF), sds((2, D, D), BF), sds((2, D, D), BF),
        ],
        compiler_params=params(),
        cost_estimate=pl.CostEstimate(
            flops=16 * tokens * D * D, bytes_accessed=40 * tokens * D, transcendentals=8 * tokens * D
        ),
        name="up_forward",
    )(scal, n2, w, vec, cotangent)


def mlp_backward(scal, hidden, gp, down, up, n2, cotangent, after, vec, grids):
    tokens = grids * CELLS
    block = pl.BlockSpec((1, tokens, D), lambda j, *_: (j, 0, 0))
    weight = pl.BlockSpec((1, D, D), lambda j, *_: (j, 0, 0))
    half = whole_block((2, D, D))
    rows = whole_block((tokens, D))
    spec = pltpu.PrefetchScalarGridSpec(
        num_scalar_prefetch=1,
        grid=(4,),
        in_specs=[
            block, block, weight, weight, rows,
            pl.BlockSpec((grids, CELLS, D), lambda j, s: (s[2], 0, 0)),
            rows, whole_block((16, D)),
        ],
        out_specs=[
            whole_block((grids, CELLS, D)), rows, rows, half, half,
            whole_block((8, D)), whole_block((8, D)),
        ],
        scratch_shapes=[
            pltpu.VMEM((tokens, D), F32), pltpu.VMEM((tokens, D), F32), pltpu.VMEM((D, tokens), BF),
        ],
    )
    return pl.pallas_call(
        mlp_kernel,
        grid_spec=spec,
        out_shape=[
            sds((grids, CELLS, D), BF), sds((tokens, D), F32), sds((tokens, D), BF),
            sds((2, D, D), BF), sds((2, D, D), BF), sds((8, D), F32), sds((8, D), F32),
        ],
        compiler_params=params(),
        cost_estimate=pl.CostEstimate(
            flops=32 * tokens * D * D, bytes_accessed=40 * tokens * D, transcendentals=0
        ),
        name="mlp_backward",
    )(scal, hidden, gp, down, up, n2, cotangent, after, vec)


def attention_backward(scal, crop, ga, galow, mixed, p, q, k, v, emb, w, vec, grids):
    tokens = grids * CELLS
    rows = pl.BlockSpec((CELLS, D), lambda i, *_: (i, 0))
    spec = pltpu.PrefetchScalarGridSpec(
        num_scalar_prefetch=2,
        grid=(grids,),
        in_specs=[
            rows, rows, rows,
            pl.BlockSpec((1, HEADS, CELLS, CELLS), lambda i, *_: (i, 0, 0, 0)),
            rows, rows, rows, rows,
            whole_block((4, D, D)),
            whole_block((16, D)),
        ],
        out_specs=[
            rows, rows, rows,
            pl.BlockSpec((1, CELLS, D), lambda i, *_: (i, 0, 0)),
            whole_block((CELLS, D)),
            whole_block((8, D)),
        ],
        scratch_shapes=[pltpu.VMEM((CELLS, D), BF)],
    )
    low = sds((tokens, D), BF)
    return pl.pallas_call(
        attention_backward_kernel,
        grid_spec=spec,
        out_shape=[low, low, low, sds((grids, CELLS, D), BF), sds((CELLS, D), F32), sds((8, D), F32)],
        compiler_params=params(),
        cost_estimate=pl.CostEstimate(
            flops=8 * tokens * D * D + 128 * tokens * CELLS * 256,
            bytes_accessed=32 * tokens * D,
            transcendentals=0,
        ),
        name="attention_backward",
    )(scal, crop, ga, galow, mixed, p, q, k, v, emb, w, vec)


def projection_grad(scal, n1, galow, dq, dk, dv, mixed):
    tokens = n1.shape[0]
    spec = pltpu.PrefetchScalarGridSpec(
        num_scalar_prefetch=1,
        grid=(1,),
        in_specs=[whole_block((tokens, D))] * 6,
        out_specs=[whole_block((2, D, D))] * 2,
        scratch_shapes=[pltpu.VMEM((D, tokens), BF)],
    )
    return pl.pallas_call(
        projection_grad_kernel,
        grid_spec=spec,
        out_shape=[sds((2, D, D), BF), sds((2, D, D), BF)],
        compiler_params=params(),
        cost_estimate=pl.CostEstimate(
            flops=8 * tokens * D * D, bytes_accessed=20 * tokens * D, transcendentals=0
        ),
        name="projection_grad",
    )(scal, n1, galow, dq, dk, dv, mixed)


class Place:
    def __init__(self, dp_size, mp_size):
        self.z_size = dp_size // 2
        dp, mp = lax.axis_index("dp"), lax.axis_index("mp")
        self.dp, self.mp = dp, mp
        self.z, self.y = dp // 2, dp % 2
        self.x, self.c = mp // 2, mp % 2
        self.core_pairs = [(i, i ^ 1) for i in range(mp_size)]
        self.x_pairs = [(i, i ^ 2) for i in range(mp_size)]
        self.y_pairs = [(i, i ^ 1) for i in range(dp_size)]
        self.z_shift = [
            [(i, ((i // 2 + s) % self.z_size) * 2 + i % 2) for i in range(dp_size)]
            for s in range(self.z_size)
        ]

    def core(self, v):
        return lax.ppermute(v, "mp", self.core_pairs)

    def over_x(self, v):
        return lax.ppermute(v, "mp", self.x_pairs)

    def over_y(self, v):
        return lax.ppermute(v, "dp", self.y_pairs)

    def over_z(self, v, shift):
        return lax.ppermute(v, "dp", self.z_shift[shift])


def after_op(value, *earlier):
    return lax.optimization_barrier((value,) + earlier)[0]


def assemble_kernel(rows, extra, where_ref, *refs):
    pieces, outs, sem = refs[:10], refs[10:-1], refs[-1]
    z, y, x, c = where_ref[0], where_ref[1], where_ref[2], where_ref[3]
    depth = pieces[0].shape[1]
    copies = []

    def add(src, dst):
        copies.append(pltpu.make_async_copy(src, dst, sem.at[len(copies)]))

    for core_rel in range(2):
        own, by_x, by_y, diag0, diag1 = pieces[core_rel * 5 : core_rel * 5 + 5]
        core = c if core_rel == 0 else 1 - c
        for s in range(depth):
            zs = lax.rem(z - s + depth, depth)
            for xr in range(2):
                for yr in range(2):
                    xs = x if xr == 0 else 1 - x
                    ys = y if yr == 0 else 1 - y
                    dp = zs * 2 + ys
                    row = pl.ds(pl.multiple_of(dp * rows, rows), rows)
                    lane = pl.ds(pl.multiple_of(xs * (D // 2), D // 2), D // 2)
                    if xr and yr:
                        for b, diag in enumerate((diag0, diag1)):
                            add(diag.at[s, 0:rows], outs[0].at[core * 2 + b, row, lane])
                        first, second = diag0.at[s], diag1.at[s]
                    else:
                        src = (own, by_x, by_y)[xr + 2 * yr]
                        add(
                            src.at[:, s, 0:rows],
                            outs[0].at[pl.ds(core * 2, 2), row, lane],
                        )
                        first, second = src.at[0, s], src.at[1, s]
                    if extra:
                        share = pl.ds(pl.multiple_of((dp * 2 + core) * extra, extra), extra)
                        tail = slice(rows, rows + extra)
                        add(first.at[tail], outs[1].at[share, lane])
                        add(second.at[tail], outs[2].at[dp, xs, core])
    for copy in copies:
        copy.start()
    for copy in copies:
        copy.wait()


def assemble(where, pieces, extra, dp_size):
    rows = D // dp_size
    outs = [sds((4, D, D), BF)]
    if extra:
        outs += [sds((dp_size * 2 * extra, D), BF), sds((dp_size, 2, 2, extra, D // 2), BF)]
    count = (dp_size // 2) * 2 * (3 + 2 + (8 if extra else 0))
    hbm = pl.BlockSpec(memory_space=pl.ANY)
    return pl.pallas_call(
        functools.partial(assemble_kernel, rows, extra),
        in_specs=[pl.BlockSpec(memory_space=pltpu.SMEM)] + [hbm] * 10,
        out_specs=[pl.BlockSpec(memory_space=pltpu.VMEM)] * len(outs),
        out_shape=outs,
        scratch_shapes=[pltpu.SemaphoreType.DMA((count,))],
        compiler_params=params(),
        cost_estimate=pl.CostEstimate(flops=0, bytes_accessed=16 * D * D, transcendentals=0),
        name="assemble",
    )(where, *pieces)


def gather_chunk(place, where, u, extra, dp_size):
    parts = [u] + [place.over_z(u, s) for s in range(1, place.z_size)]
    own = jnp.stack(parts, axis=1)
    by_x, by_y = place.over_x(own), place.over_y(own)
    diag0, diag1 = place.over_y(by_x[0]), place.over_x(by_y[1])
    mine = (own, by_x, by_y, diag0, diag1)
    pieces = mine + tuple(place.core(v) for v in mine)
    return assemble(where, pieces, extra, dp_size), own, (diag0, diag1)


def reduce_group(place, mine, other):
    zs = place.z_size
    rows, lanes = D // (2 * zs), D // 2
    x, y, z, c = place.x, place.y, place.z, place.c
    h = (mine.astype(F32) + place.core(other).astype(F32)).astype(BF)
    h = h.reshape(2, zs, 2, rows, D)

    def y_part(v, at):
        return lax.dynamic_index_in_dim(v, at, axis=1, keepdims=False)

    def x_part(v, at):
        return jnp.where(at == 0, v[..., :lanes], v[..., lanes:])

    def join(a, b):
        return (a.astype(F32) + b.astype(F32)).astype(BF)

    a0 = join(y_part(h[0], y), place.over_y(y_part(h[0], 1 - y)))
    a1 = join(x_part(h[1], x), place.over_x(x_part(h[1], 1 - x)))
    b0 = join(x_part(a0, x), place.over_x(x_part(a0, 1 - x)))
    b1 = join(y_part(a1, y), place.over_y(y_part(a1, 1 - y)))
    b = jnp.stack([b0, b1])

    def z_part(at):
        return lax.dynamic_index_in_dim(b, at, axis=1, keepdims=False)

    total = z_part(z).astype(F32)
    for s in range(1, zs):
        total = total + place.over_z(z_part((z + s) % zs), s).astype(F32)
    left, right = total[..., : lanes // 2], total[..., lanes // 2 :]
    kept = jnp.where(c == 0, left, right)
    got = place.core(jnp.where(c == 0, right, left))
    return jnp.where(c == 0, jnp.concatenate([kept, got]), jnp.concatenate([got, kept]))


def collect_kernel(where_ref, own, by_core, by_x, by_both, out, sem):
    x, c = where_ref[2], where_ref[3]
    grids = own.shape[0]
    copies = []
    for n, (piece, mp) in enumerate(
        ((own, 2 * x + c), (by_core, 2 * x + 1 - c), (by_x, 2 - 2 * x + c), (by_both, 3 - 2 * x - c))
    ):
        copies.append(pltpu.make_async_copy(piece, out.at[pl.ds(mp * grids, grids)], sem.at[n]))
    for copy in copies:
        copy.start()
    for copy in copies:
        copy.wait()


def gather_grids(place, where, own):
    by_core, by_x = place.core(own), place.over_x(own)
    by_both = place.core(by_x)
    hbm = pl.BlockSpec(memory_space=pl.ANY)
    return pl.pallas_call(
        collect_kernel,
        in_specs=[pl.BlockSpec(memory_space=pltpu.SMEM)] + [hbm] * 4,
        out_specs=pl.BlockSpec(memory_space=pltpu.VMEM),
        out_shape=sds((4 * own.shape[0],) + own.shape[1:], own.dtype),
        scratch_shapes=[pltpu.SemaphoreType.DMA((4,))],
        compiler_params=params(),
        cost_estimate=pl.CostEstimate(flops=0, bytes_accessed=8 * own.size, transcendentals=0),
        name="collect",
    )(where, own, by_core, by_x, by_both)


def sum_everywhere(place, value):
    value = value + place.core(value)
    value = value + place.over_x(value)
    value = value + place.over_y(value)
    total = value
    for s in range(1, place.z_size):
        total = total + place.over_z(value, s)
    return total


def adam_step(weight, gradient, first, second, rate, decay):
    first_new = BETA_FIRST * first + (1.0 - BETA_FIRST) * gradient
    second_new = BETA_SECOND * second + (1.0 - BETA_SECOND) * gradient * gradient
    first_hat = first_new / (1.0 - BETA_FIRST**STEP)
    second_hat = second_new / (1.0 - BETA_SECOND**STEP)
    weight_new = weight - rate * (first_hat / (jnp.sqrt(second_hat) + ADAM_EPS) + decay * weight)
    return (weight_new, first_new, second_new)


def body(
    dp_size, mp_size,
    block_input, cotangent, crop_boxes, front_weights, back_weights, split_biases, norm_params,
    pos_table, front_first, back_weight_first_moment, split_first, norm_first, table_first,
    front_second, back_second, split_second, norm_second, table_second,
):
    place = Place(dp_size, mp_size)
    direct = dp_size == 8 and mp_size == 4
    x, y, z, c = place.x, place.y, place.z, place.c
    grids = block_input.shape[0] // mp_size
    scal = jnp.stack([place.mp * grids, c, place.mp, place.dp]).astype(jnp.int32)
    where = jnp.stack([z, y, x, c]).astype(jnp.int32)
    turned = jnp.swapaxes(back_weights, 1, 2).astype(BF)
    low_front = front_weights.astype(BF)
    rows, lanes = low_front.shape[1], low_front.shape[2]

    if direct:
        shards = jnp.concatenate([low_front[:3], turned[:1], low_front[3:], turned[1:]])
        shards = shards.reshape(3, 2, 2, rows, lanes)
        mine = lax.dynamic_index_in_dim(shards, c, axis=1, keepdims=False)
        sent = lax.dynamic_index_in_dim(shards, 1 - c, axis=1, keepdims=False)
        got = place.core(sent)
        units = jnp.where(
            c == 0, jnp.concatenate([mine, got], -1), jnp.concatenate([got, mine], -1)
        )
        extra = pos_table.shape[0] // 2
        half = jnp.where(c == 0, pos_table[:extra], pos_table[extra:]).astype(BF)
        half = jnp.where(x == 0, half[:, : D // 2], half[:, D // 2 :])
        packed = jnp.zeros((extra, D // 2), BF)
        packed = lax.dynamic_update_slice(packed, norm_params.astype(BF), (0, 0))
        packed = lax.dynamic_update_slice(packed, split_biases.astype(BF), (0, 128))
        first_unit = jnp.concatenate([units[0], jnp.stack([half, packed])], axis=1)
        (w_attn, table, codes), gate1, _ = gather_chunk(place, where, first_unit, extra, dp_size)
        second_unit = after_op(units[1], gate1)
        (w_up,), gate2, last2 = gather_chunk(place, where, second_unit, 0, dp_size)
        third_unit = after_op(units[2], gate2)
        (w_down,), _, _ = gather_chunk(place, where, third_unit, 0, dp_size)
        norms = jnp.swapaxes(codes[:, 0, 0, 0:6, : norm_params.shape[1]], 0, 1).reshape(6, D)
        splits = codes[:, :, :, 0:6, 128 : 128 + split_biases.shape[1]]
        splits = jnp.transpose(splits, (3, 1, 2, 0, 4)).reshape(6, D)
    else:

        def whole(v):
            v = lax.all_gather(v, "dp", axis=1, tiled=True)
            return lax.all_gather(v, "mp", axis=2, tiled=True)

        w_attn = whole(jnp.concatenate([low_front[:3], turned[:1]]))
        w_up, w_down = whole(low_front[3:]), whole(turned[1:])
        table = lax.all_gather(pos_table.astype(BF), "dp", axis=0, tiled=True)
        norms = lax.all_gather(norm_params.astype(BF), "dp", axis=1, tiled=True)
        splits = lax.all_gather(split_biases.astype(BF), ("mp", "dp"), axis=1, tiled=True)
    gap = jnp.zeros((2, D), F32)
    vec = jnp.concatenate([norms.astype(F32), gap, splits.astype(F32), gap])

    emb, n1, q, k, v, p, mixed, after, n2 = attention_forward(
        scal, crop_boxes, block_input, table, w_attn, vec, grids
    )
    hidden, gp, down_mine, down_other = up_forward(scal, n2, w_up, vec, cotangent, grids)
    out, ga, galow, up_mine, up_other, gb, gn = mlp_backward(
        scal, hidden, gp, w_down, w_up, n2, cotangent, after, vec, grids
    )
    dq, dk, dv, ig, dtable, gs = attention_backward(
        scal, crop_boxes, ga, galow, mixed, p, q, k, v, emb, w_attn, vec, grids
    )
    attn_mine, attn_other = projection_grad(scal, n1, galow, dq, dk, dv, mixed)

    norm_grad = jnp.concatenate([gs[2:4], gn[2:6]])
    split_grad = jnp.concatenate([gs[0:2], gb[0:4]])
    if direct:
        down_share = reduce_group(place, down_mine, down_other)
        up_share = reduce_group(place, up_mine, up_other)
        attn_share = reduce_group(place, attn_mine, attn_other)
        block_output = gather_grids(place, where, out)
        input_grad = gather_grids(place, where, ig)
        small = lax.psum(jnp.concatenate([dtable, norm_grad, split_grad]), ("dp", "mp"))
        dtable, norm_grad, split_grad = small[:CELLS], small[CELLS : CELLS + 6], small[CELLS + 6 :]
    else:

        def share(mine, other):
            full = jnp.where(
                c == 0, jnp.concatenate([mine, other]), jnp.concatenate([other, mine])
            ).astype(F32)
            full = lax.psum_scatter(full, "dp", scatter_dimension=1, tiled=True)
            return lax.psum_scatter(full, "mp", scatter_dimension=2, tiled=True)

        down_share = share(down_mine, down_other)
        up_share = share(up_mine, up_other)
        attn_share = share(attn_mine, attn_other)
        block_output = lax.all_gather(out, "mp", axis=0, tiled=True)
        input_grad = lax.all_gather(ig, "mp", axis=0, tiled=True)
        dtable = lax.psum(dtable, ("dp", "mp"))
        norm_grad = lax.psum(norm_grad, ("dp", "mp"))
        split_grad = lax.psum(split_grad, ("dp", "mp"))
    cells_here, norm_here = pos_table.shape[0], norm_params.shape[1]
    split_here = split_biases.shape[1]
    table_share = lax.dynamic_slice(dtable, (place.dp * cells_here, 0), (cells_here, D))
    norm_share = lax.dynamic_slice(norm_grad, (0, place.dp * norm_here), (6, norm_here))
    split_share = lax.dynamic_slice(
        split_grad, (0, (place.mp * dp_size + place.dp) * split_here), (6, split_here)
    )
    front_share = jnp.concatenate([attn_share[:3], up_share])
    back_share = jnp.concatenate([attn_share[3:], down_share])
    owner = (place.mp == 0).astype(F32)
    square = (
        jnp.sum(attn_share * attn_share)
        + jnp.sum(up_share * up_share)
        + jnp.sum(down_share * down_share)
        + jnp.sum(split_share * split_share)
        + owner * (jnp.sum(norm_share * norm_share) + jnp.sum(table_share * table_share))
    )
    if direct:
        clip_norm = jnp.sqrt(sum_everywhere(place, square.reshape(1, 1)))[0, 0]
    else:
        clip_norm = jnp.sqrt(lax.psum(square, ("dp", "mp")))
    factor = jnp.minimum(1.0, CLIP_LIMIT / (clip_norm + 1e-06))
    norm_clipped = norm_share * factor
    new_front, front_first_new, front_second_new = adam_step(
        front_weights, front_share * factor, front_first, front_second, RATE_MATRIX, DECAY_RATE
    )
    new_back, back_first_new, back_second_new = adam_step(
        back_weights,
        jnp.swapaxes(back_share, 1, 2) * factor,
        back_weight_first_moment,
        back_second,
        RATE_MATRIX,
        DECAY_RATE,
    )
    new_split, split_first_new, split_second_new = adam_step(
        split_biases, split_share * factor, split_first, split_second, RATE_VECTOR, 0.0
    )
    new_norm, norm_first_new, norm_second_new = adam_step(
        norm_params, norm_clipped, norm_first, norm_second, RATE_VECTOR, 0.0
    )
    new_table, table_first_new, table_second_new = adam_step(
        pos_table, table_share * factor, table_first, table_second, RATE_TABLE, DECAY_RATE
    )
    return (
        block_output, input_grad, clip_norm,
        new_front, new_back, new_split, new_norm, new_table,
        front_first_new, back_first_new, split_first_new, norm_first_new, table_first_new,
        front_second_new, back_second_new, split_second_new, norm_second_new, table_second_new,
        norm_clipped,
    )


def solution(mesh):
    front, back = P(None, "dp", "mp"), P(None, "mp", "dp")
    split, norm, table = P(None, ("mp", "dp")), P(None, "dp"), P("dp", None)
    state = (front, back, split, norm, table)
    rows = P("dp", None, None)
    return jax.shard_map(
        functools.partial(body, mesh.shape["dp"], mesh.shape["mp"]),
        mesh=mesh,
        in_specs=(rows, rows, P("dp", None)) + state * 3,
        out_specs=(rows, rows, P()) + state * 3 + (norm,),
        check_vma=False,
    )
```

time: 1090 us -> 563 us (0.52)
  waiting for transfers between devices: 535 us -> 243 us
  blocking collectives: 149 us -> 0 us
  Pallas kernels: 0 us -> 132 us
  matrix products: 124 us -> 0 us
  other arithmetic: 150 us -> 33.4 us
  starting transfers between devices: 1.16 us -> 84.1 us
  local copies, waits for them, and re-layouts: 104 us -> 38.4 us
    psum x3 -> x1, waiting for transfers between devices: 318 us -> 115 us  [body(): lax.psum(jnp.concatenate([dtable, norm_grad, split_grad]), ('dp', 'mp'))]
    unnamed x12 -> x1, waiting for transfers between devices: 142 us -> 0.02 us
    pallas_call x0 -> x10, Pallas kernels: none -> 132 us  [the longest x1 27.8 us: attention_backward(): pl.pallas_call(attention_backward_kernel, grid_spec=spec, out_shape=[low,...]
    ppermute x0 -> x76, waiting for transfers between devices: none -> 128 us  [the longest x21 46.9 us: over_z(): return lax.ppermute(v, 'dp', self.z_shift[shift])]
    dot_general x18 -> x0, matrix products: 115 us -> none  [the longest x1 12.9 us: body(): jnp.einsum('gqhs,gkhs->ghqk', grad_mixed, value_rows, preferred_element_t...]
    all_gather x3 -> x0, blocking collectives: 86.2 us -> none  [the longest x1 31.7 us: body(): lax.all_gather(pos_table.astype(jnp.bfloat16), 'dp', axis=0, tiled=True)]
    ppermute x0 -> x76, starting transfers between devices: none -> 84.1 us  [the longest x21 40.4 us: over_z(): return lax.ppermute(v, 'dp', self.z_shift[shift])]
    reduce_scatter x1 -> x0, waiting for transfers between devices: 62.7 us -> none  [body(): lax.psum_scatter(grad_table, 'dp', scatter_dimension=0, tiled=True)]
  transfers between devices with their start and end apart: 9 -> 77, of which waited for: 7 -> 30; matrix products, arithmetic and copies ran while one was open for 13% -> 10% of each run, Pallas kernels for 0% -> 24%
where the time goes in v1:
time: 563 us; the launch traced here: 555 us
  waiting for transfers between devices  243 us (43%)
  Pallas kernels  132 us (23%)
  starting transfers between devices  84.1 us (15%)
  local copies, waits for them, and re-layouts  38.4 us (7%)
  other arithmetic  33.4 us (6%)
  between operations  24.2 us (4%)
    psum x1, waiting for transfers between devices, body(): lax.psum(jnp.concatenate([dtable, norm_grad, split_grad]), ('dp', 'mp'))  115 us
    ppermute x21, waiting for transfers between devices, over_z(): return lax.ppermute(v, 'dp', self.z_shift[shift])  46.9 us
    ppermute x13, waiting for transfers between devices, over_y(): return lax.ppermute(v, 'dp', self.y_pairs)  46.9 us
    ppermute x21, starting transfers between devices, over_z(): return lax.ppermute(v, 'dp', self.z_shift[shift])  40.4 us
    ppermute x15, waiting for transfers between devices, over_x(): return lax.ppermute(v, 'mp', self.x_pairs)  33.5 us
    pallas_call x1, Pallas kernels, attention_backward(): pl.pallas_call(attention_backward_kernel, grid_spec=spec, out_shape=[low,...  27.8 us
    pallas_call x1, Pallas kernels, mlp_backward(): pl.pallas_call(mlp_kernel, grid_spec=spec, out_shape=[sds((grids, CELLS,...  27.4 us
    pallas_call x1, Pallas kernels, attention_forward(): pl.pallas_call(attention_forward_kernel, grid_spec=spec, out_shape=[full,...  19.8 us
  transfers between devices with their start and end apart: 77, of which 30 were waited for; matrix products, arithmetic and copies ran while one was open for 10% of the time, Pallas kernels for 24%

profile of v1, /device:TPU:0, one launch (start us, length us, event | category | flops | bytes accessed | tf_op | source)
XLA Modules:
  0.0 555.2 jit_solution(8914950716166773192)
XLA Ops:
  18.4 3.3 collective-permute-done.1
  21.7 6.9 %collective-permute-done.2 = bf16[2,112,384]{2,1,0:T(8,128)(2,1)S(1)} collective-permute-done((bf16[2,112,384]{2,1,0:T(8,128)(2,1)S(1)}, bf16[2,112,384]{2,1,0:T(8,128)(2,1)S(1)}, u32[]{:S(2)}, u32[]{:S(2)}) %collective-permute-start.2) | collective-permute-done | bytes 172064 | tf_op jit(solution)/shard_map/ppermute | solution.py:475
  28.7 4.2 collective-permute-start.13
  38.8 5.0 collective-permute-done.14
  45.4 3.6 collective-permute-start.25
  51.0 4.3 collective-permute-done.25
  56.4 3.7 collective-permute-done.26
  67.0 10.8 %collective-permute-done.17 = bf16[2,4,96,384]{3,2,0,1:T(8,128)(2,1)S(1)} collective-permute-done((bf16[2,4,96,384]{3,2,0,1:T(8,128)(2,1)S(1)}, bf16[2,4,96,384]{3,2,0,1:T(8,128)(2,1)S(1)}, u32[]{:S(2)}, u32[]{:S(2)}) %collective-permute-start.17) | collective-permute-done | bytes 589856 | tf_op jit(solution)/shard_map/ppermute | solution.py:472
  80.0 10.5 %collective-permute-done.29.refs_2_ = bf16[2,4,96,384]{3,2,1,0:T(8,128)(2,1)S(1)} collective-permute-done((bf16[2,4,96,384]{3,2,1,0:T(8,128)(2,1)S(1)}, bf16[2,4,96,384]{3,2,1,0:T(8,128)(2,1)S(1)}, u32[]{:S(2)}, u32[]{:S(2)}) %collective-permute-start.29) | collective-permute-done | bytes 589856 | tf_op jit(solution)/shard_map/ppermute | solution.py:472
  90.5 6.3 %collective-permute-done.18.refs_3_ = bf16[4,96,384]{2,1,0:T(8,128)(2,1)S(1)} collective-permute-done((bf16[4,96,384]{2,1,0:T(8,128)(2,1)S(1)}, bf16[4,96,384]{2,1,0:T(8,128)(2,1)S(1)}, u32[]{:S(2)}, u32[]{:S(2)}) %collective-permute-start.18) | collective-permute-done | bytes 294944 | tf_op jit(solution)/shard_map/ppermute | solution.py:472
  97.4 4.9 collective-permute-done.6.refs_3_
  120.7 5.8 %assemble.4.w_ref.up_ref = bf16[4,768,768]{2,1,0:T(8,128)(2,1)} custom-call(s32[4]{0:T(128)} %pad_add_fusion.where_ref, bf16[2,4,96,384]{3,2,1,0:T(8,128)(2,1)} %copy.91.refs_0_, bf16[2,4,96,384]{3,2,1,0:T(8,128)(2,1)} %copy.92.refs_1_, bf16[2,4,96,384]{3,2,1,0:T(8,128)(2,1)} %copy.93.refs_2_, bf16[4,96,384]{2,1,0:T(8,128)(2,1)} %copy-done.41, ...), custom_call_target="tpu_custom_call" | custom-call | bytes 9437184 | tf_op jit(solution)/shard_map/assemble/pallas_call | solution.py:532
  130.7 6.8 %assemble.3 = (bf16[4,768,768]{2,1,0:T(8,128)(2,1)}, bf16[256,768]{1,0:T(8,128)(2,1)}, bf16[8,2,2,16,384]{4,3,2,1,0:T(8,128)(2,1)}) custom-call(s32[4]{0:T(128)} %pad_add_fusion.where_ref, bf16[2,4,112,384]{3,2,1,0:T(8,128)(2,1)} %copy.82.refs_0_, bf16[2,4,112,384]{3,2,1,0:T(8,128)(2,1)} %copy.83.refs_1_, bf16[2,4,112,384]{3,2,1,0:T(8,128)(2,1)} %copy.84.refs_2_, ...), custom_call_target="tpu_custom_call" | custom-call | bytes 9437184 | tf_op jit(solution)/shard_map/assemble/pallas_call | solution.py:532
  140.0 19.8 %attention_forward.1 = (f32[768,768]{1,0:T(8,128)}, bf16[768,768]{1,0:T(8,128)(2,1)}, bf16[768,768]{1,0:T(8,128)(2,1)}, bf16[768,768]{1,0:T(8,128)(2,1)}, bf16[7...) custom-call(s32[4]{0:T(128)} %pad_add_fusion.1.scal, ...), custom_call_target="tpu_custom_call" | custom-call | flops 6845104128 | bytes 14155776 | tf_op jit(solution)/shard_map/attention_forward/pallas_call | solution.py:310
  159.8 16.3 %up_forward.1 = (bf16[4,768,768]{2,1,0:T(8,128)(2,1)}, bf16[4,768,768]{2,1,0:T(8,128)(2,1)}, bf16[2,768,768]{2,1,0:T(8,128)(2,1)}, bf16[2,768,768]{2,1,0:T(8,128)(2,1)}) custom-call(s32[4]{0:T(128)} %pad_add_fusion.1.scal, bf16[768,768]{1,0:T(8,128)(2,1)} %get-tuple-element.55.n2_ref, bf16[4,768,768]{2,1,0:T(8,128)(2,1)} %assemble.4.w_ref.up_ref, ...), custom_call_target="tpu_custom_call" | custom-call | flops 7247757312 | bytes 23592960 | tf_op jit(solution)/shard_map/up_forward/pallas_call | solution.py:342
  177.4 5.7 %assemble.5.down_ref = bf16[4,768,768]{2,1,0:T(8,128)(2,1)} custom-call(s32[4]{0:T(128)} %pad_add_fusion.where_ref, bf16[2,4,96,384]{3,2,1,0:T(8,128)(2,1)} %copy-done.6, bf16[2,4,96,384]{3,2,1,0:T(8,128)(2,1)} %copy-done.15, bf16[2,4,96,384]{3,2,1,0:T(8,128)(2,1)} %copy-done.17, bf16[4,96,384]{2,1,0:T(8,128)(2,1)} %copy-done.40, ...), custom_call_target="tpu_custom_call" | custom-call | bytes 9437184 | tf_op jit(solution)/shard_map/assemble/pallas_call | solution.py:532
  183.0 27.4 %mlp_backward.1 = (bf16[3,256,768]{2,1,0:T(8,128)(2,1)}, f32[768,768]{1,0:T(8,128)}, bf16[768,768]{1,0:T(8,128)(2,1)}, bf16[2,768,768]{2,1,0:T(8,128)(2,1)}, bf1...) custom-call(s32[4]{0:T(128)} %pad_add_fusion.1.scal, ...), custom_call_target="tpu_custom_call" | custom-call | flops 14495514624 | bytes 23592960 | tf_op jit(solution)/shard_map/mlp_backward/pallas_call | solution.py:378
  210.6 27.8 %attention_backward.1 = (bf16[768,768]{1,0:T(8,128)(2,1)}, bf16[768,768]{1,0:T(8,128)(2,1)}, bf16[768,768]{1,0:T(8,128)(2,1)}, bf16[3,256,768]{2,1,0:T(8,128)(2,...) custom-call(s32[4]{0:T(128)} %pad_add_fusion.1.scal, s32[12,4]{1,0:T(8,128)} %copy.90.crop, ...), custom_call_target="tpu_custom_call" | custom-call | flops 10066329600 | bytes 18874368 | tf_op jit(solution)/shard_map/attention_backward/pallas_call | solution.py:415
  239.3 4.1 concatenate.53
  243.5 12.2 %projection_grad.1 = (bf16[2,768,768]{2,1,0:T(8,128)(2,1)}, bf16[2,768,768]{2,1,0:T(8,128)(2,1)}) custom-call(s32[4]{0:T(128)} %pad_add_fusion.1.scal, bf16[768,768]{1,0:T(8,128)(2,1)} %get-tuple-element.71.n1_ref, bf16[768,768]{1,0:T(8,128)(2,1)} %get-tuple-element.63.galow_ref, bf16[768,768]{1,0:T(8,128)(2,1)} %get-tuple-element.72.dq_ref, ...), custom_call_target="tpu_custom_call" | custom-call | flops 3623878656 | bytes 11796480 | tf_op jit(solution)/shard_map/projection_grad/pallas_call | solution.py:438
  260.3 114.7 %all-reduce.3.cloned.1.call-done = f32[268,768]{1,0:T(8,128)} async-done(((f32[268,768]{1,0:T(8,128)}), f32[268,768]{1,0:T(8,128)}) %all-reduce.3.cloned.1.call-update) | async-done | bytes 823312 | tf_op jit(solution)/shard_map/psum | solution.py:711
  388.2 22.3 %collective-permute-done.38.by_x = bf16[3,256,768]{2,1,0:T(8,128)(2,1)} collective-permute-done((bf16[3,256,768]{2,1,0:T(8,128)(2,1)}, bf16[3,256,768]{2,1,0:T(8,128)(2,1)}, u32[]{:S(2)}, u32[]{:S(2)}) %collective-permute-start.38) | collective-permute-done | bytes 1179680 | tf_op jit(solution)/shard_map/ppermute | solution.py:469
  423.9 5.2 collect.3
  431.2 5.2 collect.2
  450.2 5.2 collective-permute-done.46
  463.2 3.1 collective-permute-done.65
  468.9 3.8 collective-permute-done.56
  480.3 11.1 %collective-permute-done.67 = bf16[2,96,384]{2,1,0:T(8,128)(2,1)S(1)} collective-permute-done((bf16[2,96,384]{2,1,0:T(8,128)(2,1)S(1)}, bf16[2,96,384]{2,1,0:T(8,128)(2,1)S(1)}, u32[]{:S(2)}, u32[]{:S(2)}) %collective-permute-start.67) | collective-permute-done | bytes 147488 | tf_op jit(solution)/shard_map/ppermute | solution.py:475
  491.6 4.4 collective-permute-start.59
  496.0 4.9 collective-permute-done.49
  524.2 3.2 collective-permute-start.73
  530.1 4.2 collective-permute-start.75
  (371 shorter events, 154.3 us)
Async XLA Ops:
  7.2 367.9 %all-reduce.3.cloned.1.call-start = ((), (), s32[]{:S(2)}) async-start(), calls=%async_computation | async-start | bytes 1671168 | tf_op jit(solution)/shard_map/psum | solution.py:711
  35.4 27.8 %collective-permute-start.4 = (bf16[2,4,112,384]{3,2,0,1:T(8,128)(2,1)S(1)}, bf16[2,4,112,384]{3,2,0,1:T(8,128)(2,1)S(1)}, u32[]{:S(2)}, u32[]{:S(2)}) collective-permute-start(bf16[2,4,112,384]{3,2,0,1:T(8,128)(2,1)S(1)} %pad_maximum_fusion), channel_id=1, source_target_pairs={{0,2},{1,3},{2,0},{3,1},{4,6},{5,7},{6,4},{7,5},{8,10},{9,11},{10,... | collective-permute-start | bytes 2064392 | tf_op jit(solution)/shard_map/ppermute | solution.py:469
  36.9 26.4 %collective-permute-start.5 = (bf16[2,4,112,384]{3,2,0,1:T(8,128)(2,1)S(1)}, bf16[2,4,112,384]{3,2,0,1:T(8,128)(2,1)S(1)}, u32[]{:S(2)}, u32[]{:S(2)}) collective-permute-start(bf16[2,4,112,384]{3,2,0,1:T(8,128)(2,1)S(1)} %pad_maximum_fusion), channel_id=1, source_target_pairs={{0,4},{4,0},{8,12},{12,8},{16,20},{20,16},{24,28},{28,24},{1,5},{5... | collective-permute-start | bytes 2064392 | tf_op jit(solution)/shard_map/ppermute | solution.py:472
  64.8 25.7 %collective-permute-start.29 = (bf16[2,4,96,384]{3,2,1,0:T(8,128)(2,1)S(1)}, bf16[2,4,96,384]{3,2,1,0:T(8,128)(2,1)S(1)}, u32[]{:S(2)}, u32[]{:S(2)}) collective-permute-start(bf16[2,4,96,384]{3,2,1,0:T(8,128)(2,1)S(1)} %pad_maximum_fusion.3.refs_0_), channel_id=1, source_target_pairs={{0,4},{4,0},{8,12},{12,8},{16,20},{20,16},{24,28},{28,24},{1,5},{5... | collective-permute-start | bytes 1769480 | tf_op jit(solution)/shard_map/ppermute | solution.py:472
  66.4 30.4 %collective-permute-start.18 = (bf16[4,96,384]{2,1,0:T(8,128)(2,1)S(1)}, bf16[4,96,384]{2,1,0:T(8,128)(2,1)S(1)}, u32[]{:S(2)}, u32[]{:S(2)}) collective-permute-start(bf16[4,96,384]{2,1,0:T(8,128)(2,1)S(1)} %slice_bitcast_fusion.5), channel_id=1, source_target_pairs={{0,4},{4,0},{8,12},{12,8},{16,20},{20,16},{24,28},{28,24},{1,5},{5... | collective-permute-start | bytes 884744 | tf_op jit(solution)/shard_map/ppermute | solution.py:472
  77.9 26.3 %collective-permute-start.21 = (bf16[2,4,96,384]{3,2,0,1:T(8,128)(2,1)S(1)}, bf16[2,4,96,384]{3,2,0,1:T(8,128)(2,1)S(1)}, u32[]{:S(2)}, u32[]{:S(2)}) collective-permute-start(bf16[2,4,96,384]{3,2,0,1:T(8,128)(2,1)S(1)} %collective-permute-done.16), channel_id=1, source_target_pairs={{0,1},{1,0},{2,3},{3,2},{4,5},{5,4},{6,7},{7,6},{8,9},{9,8},{10,11... | collective-permute-start | bytes 1769480 | tf_op jit(solution)/shard_map/ppermute | solution.py:466
  77.9 24.4 %collective-permute-start.6 = (bf16[4,112,384]{2,1,0:T(8,128)(2,1)S(1)}, bf16[4,112,384]{2,1,0:T(8,128)(2,1)}, u32[]{:S(2)}, u32[]{:S(2)}) collective-permute-start(bf16[4,112,384]{2,1,0:T(8,128)(2,1)S(1)} %slice_bitcast_fusion.1), channel_id=1, source_target_pairs={{0,4},{4,0},{8,12},{12,8},{16,20},{20,16},{24,28},{28,24},{1,5},{5... | collective-permute-start | bytes 1032200 | tf_op jit(solution)/shard_map/ppermute | solution.py:472
  104.2 23.3 %collective-permute-start.10 = (bf16[2,4,112,384]{3,2,0,1:T(8,128)(2,1)S(1)}, bf16[2,4,112,384]{3,2,0,1:T(8,128)(2,1)}, u32[]{:S(2)}, u32[]{:S(2)}) collective-permute-start(bf16[2,4,112,384]{3,2,0,1:T(8,128)(2,1)S(1)} %collective-permute-done.5), channel_id=1, source_target_pairs={{0,1},{1,0},{2,3},{3,2},{4,5},{5,4},{6,7},{7,6},{8,9},{9,8},{10,11... | collective-permute-start | bytes 2064392 | tf_op jit(solution)/shard_map/ppermute | solution.py:466
  105.4 24.7 %collective-permute-start.11 = (bf16[4,112,384]{2,1,0:T(8,128)(2,1)}, bf16[4,112,384]{2,1,0:T(8,128)(2,1)}, u32[]{:S(2)}, u32[]{:S(2)}) collective-permute-start(bf16[4,112,384]{2,1,0:T(8,128)(2,1)} %collective-permute-done.6.refs_3_), channel_id=1, source_target_pairs={{0,1},{1,0},{2,3},{3,2},{4,5},{5,4},{6,7},{7,6},{8,9},{9,8},{10,11... | collective-permute-start | bytes 1032200 | tf_op jit(solution)/shard_map/ppermute | solution.py:466
  105.6 25.0 %collective-permute-start.12 = (bf16[4,112,384]{2,1,0:T(8,128)(2,1)}, bf16[4,112,384]{2,1,0:T(8,128)(2,1)}, u32[]{:S(2)}, u32[]{:S(2)}) collective-permute-start(bf16[4,112,384]{2,1,0:T(8,128)(2,1)} %collective-permute-done.7.refs_4_), channel_id=1, source_target_pairs={{0,1},{1,0},{2,3},{3,2},{4,5},{5,4},{6,7},{7,6},{8,9},{9,8},{10,11... | collective-permute-start | bytes 1032200 | tf_op jit(solution)/shard_map/ppermute | solution.py:466
  106.7 22.7 %collective-permute-start.30 = (bf16[4,96,384]{2,1,0:T(8,128)(2,1)}, bf16[4,96,384]{2,1,0:T(8,128)(2,1)S(1)}, u32[]{:S(2)}, u32[]{:S(2)}) collective-permute-start(bf16[4,96,384]{2,1,0:T(8,128)(2,1)} %slice_bitcast_fusion.3), channel_id=1, source_target_pairs={{0,4},{4,0},{8,12},{12,8},{16,20},{20,16},{24,28},{28,24},{1,5},{5... | collective-permute-start | bytes 884744 | tf_op jit(solution)/shard_map/ppermute | solution.py:472
  127.4 48.6 %collective-permute-start.32 = (bf16[2,4,96,384]{3,2,1,0:T(8,128)(2,1)S(1)}, bf16[2,4,96,384]{3,2,1,0:T(8,128)(2,1)S(1)}, u32[]{:S(2)}, u32[]{:S(2)}) collective-permute-start(bf16[2,4,96,384]{3,2,1,0:T(8,128)(2,1)S(1)} %pad_maximum_fusion.3.refs_0_), channel_id=1, source_target_pairs={{0,1},{1,0},{2,3},{3,2},{4,5},{5,4},{6,7},{7,6},{8,9},{9,8},{10,11... | collective-permute-start | bytes 1769480 | tf_op jit(solution)/shard_map/ppermute | solution.py:466
  129.5 47.1 %collective-permute-start.33 = (bf16[2,4,96,384]{3,2,1,0:T(8,128)(2,1)S(1)}, bf16[2,4,96,384]{3,2,1,0:T(8,128)(2,1)S(1)}, u32[]{:S(2)}, u32[]{:S(2)}) collective-permute-start(bf16[2,4,96,384]{3,2,1,0:T(8,128)(2,1)S(1)} %copy-done.16), channel_id=1, source_target_pairs={{0,1},{1,0},{2,3},{3,2},{4,5},{5,4},{6,7},{7,6},{8,9},{9,8},{10,11... | collective-permute-start | bytes 1769480 | tf_op jit(solution)/shard_map/ppermute | solution.py:466
  130.1 46.5 %collective-permute-start.34 = (bf16[2,4,96,384]{3,2,1,0:T(8,128)(2,1)S(1)}, bf16[2,4,96,384]{3,2,1,0:T(8,128)(2,1)}, u32[]{:S(2)}, u32[]{:S(2)}) collective-permute-start(bf16[2,4,96,384]{3,2,1,0:T(8,128)(2,1)S(1)} %copy-done.18), channel_id=1, source_target_pairs={{0,1},{1,0},{2,3},{3,2},{4,5},{5,4},{6,7},{7,6},{8,9},{9,8},{10,11... | collective-permute-start | bytes 1769480 | tf_op jit(solution)/shard_map/ppermute | solution.py:466
  130.2 46.4 %collective-permute-start.35 = (bf16[4,96,384]{2,1,0:T(8,128)(2,1)S(1)}, bf16[4,96,384]{2,1,0:T(8,128)(2,1)}, u32[]{:S(2)}, u32[]{:S(2)}) collective-permute-start(bf16[4,96,384]{2,1,0:T(8,128)(2,1)S(1)} %collective-permute-done.30.refs_3_), channel_id=1, source_target_pairs={{0,1},{1,0},{2,3},{3,2},{4,5},{5,4},{6,7},{7,6},{8,9},{9,8},{10,11... | collective-permute-start | bytes 884744 | tf_op jit(solution)/shard_map/ppermute | solution.py:466
  130.6 46.0 %collective-permute-start.36 = (bf16[4,96,384]{2,1,0:T(8,128)(2,1)}, bf16[4,96,384]{2,1,0:T(8,128)(2,1)}, u32[]{:S(2)}, u32[]{:S(2)}) collective-permute-start(bf16[4,96,384]{2,1,0:T(8,128)(2,1)} %collective-permute-done.31.refs_4_), channel_id=1, source_target_pairs={{0,1},{1,0},{2,3},{3,2},{4,5},{5,4},{6,7},{7,6},{8,9},{9,8},{10,11... | collective-permute-start | bytes 884744 | tf_op jit(solution)/shard_map/ppermute | solution.py:466
  176.1 206.1 %collective-permute-start.61 = (bf16[2,768,768]{2,1,0:T(8,128)(2,1)}, bf16[2,768,768]{2,1,0:T(8,128)(2,1)}, u32[]{:S(2)}, u32[]{:S(2)}) collective-permute-start(bf16[2,768,768]{2,1,0:T(8,128)(2,1)} %get-tuple-element.80), channel_id=1, source_target_pairs={{0,1},{1,0},{2,3},{3,2},{4,5},{5,4},{6,7},{7,6},{8,9},{9,8},{10,11... | collective-permute-start | bytes 7077896 | tf_op jit(solution)/shard_map/ppermute | solution.py:466
  210.5 200.1 %collective-permute-start.52 = (bf16[2,768,768]{2,1,0:T(8,128)(2,1)}, bf16[2,768,768]{2,1,0:T(8,128)(2,1)}, u32[]{:S(2)}, u32[]{:S(2)}) collective-permute-start(bf16[2,768,768]{2,1,0:T(8,128)(2,1)} %get-tuple-element.78), channel_id=1, source_target_pairs={{0,1},{1,0},{2,3},{3,2},{4,5},{5,4},{6,7},{7,6},{8,9},{9,8},{10,11... | collective-permute-start | bytes 7077896 | tf_op jit(solution)/shard_map/ppermute | solution.py:466
  255.6 157.8 %collective-permute-start.43 = (bf16[2,768,768]{2,1,0:T(8,128)(2,1)}, bf16[2,768,768]{2,1,0:T(8,128)(2,1)}, u32[]{:S(2)}, u32[]{:S(2)}) collective-permute-start(bf16[2,768,768]{2,1,0:T(8,128)(2,1)} %get-tuple-element.76), channel_id=1, source_target_pairs={{0,1},{1,0},{2,3},{3,2},{4,5},{5,4},{6,7},{7,6},{8,9},{9,8},{10,11... | collective-permute-start | bytes 7077896 | tf_op jit(solution)/shard_map/ppermute | solution.py:466
  258.7 129.5 %collective-permute-start.41 = (bf16[3,256,768]{2,1,0:T(8,128)(2,1)}, bf16[3,256,768]{2,1,0:T(8,128)(2,1)}, u32[]{:S(2)}, u32[]{:S(2)}) collective-permute-start(bf16[3,256,768]{2,1,0:T(8,128)(2,1)} %get-tuple-element.70.own), channel_id=1, source_target_pairs={{0,2},{1,3},{2,0},{3,1},{4,6},{5,7},{6,4},{7,5},{8,10},{9,11},{10,... | collective-permute-start | bytes 3538952 | tf_op jit(solution)/shard_map/ppermute | solution.py:469
  260.2 158.1 %collective-permute-start.40 = (bf16[3,256,768]{2,1,0:T(8,128)(2,1)}, bf16[3,256,768]{2,1,0:T(8,128)(2,1)}, u32[]{:S(2)}, u32[]{:S(2)}) collective-permute-start(bf16[3,256,768]{2,1,0:T(8,128)(2,1)} %get-tuple-element.70.own), channel_id=1, source_target_pairs={{0,1},{1,0},{2,3},{3,2},{4,5},{5,4},{6,7},{7,6},{8,9},{9,8},{10,11... | collective-permute-start | bytes 3538952 | tf_op jit(solution)/shard_map/ppermute | solution.py:466
  382.2 28.3 %collective-permute-start.38 = (bf16[3,256,768]{2,1,0:T(8,128)(2,1)}, bf16[3,256,768]{2,1,0:T(8,128)(2,1)}, u32[]{:S(2)}, u32[]{:S(2)}) collective-permute-start(bf16[3,256,768]{2,1,0:T(8,128)(2,1)} %get-tuple-element.61.own), channel_id=1, source_target_pairs={{0,2},{1,3},{2,0},{3,1},{4,6},{5,7},{6,4},{7,5},{8,10},{9,11},{10,... | collective-permute-start | bytes 3538952 | tf_op jit(solution)/shard_map/ppermute | solution.py:469
  388.2 41.0 %collective-permute-start.37 = (bf16[3,256,768]{2,1,0:T(8,128)(2,1)}, bf16[3,256,768]{2,1,0:T(8,128)(2,1)}, u32[]{:S(2)}, u32[]{:S(2)}) collective-permute-start(bf16[3,256,768]{2,1,0:T(8,128)(2,1)} %get-tuple-element.61.own), channel_id=1, source_target_pairs={{0,1},{1,0},{2,3},{3,2},{4,5},{5,4},{6,7},{7,6},{8,9},{9,8},{10,11... | collective-permute-start | bytes 3538952 | tf_op jit(solution)/shard_map/ppermute | solution.py:466
  413.5 22.9 %collective-permute-start.64 = (bf16[4,2,96,384]{3,2,1,0:T(8,128)(2,1)}, bf16[4,2,96,384]{3,2,1,0:T(8,128)(2,1)}, u32[]{:S(2)}, u32[]{:S(2)}) collective-permute-start(bf16[4,2,96,384]{3,2,1,0:T(8,128)(2,1)} %copy.114), channel_id=1, source_target_pairs={{0,2},{1,3},{2,0},{3,1},{4,6},{5,7},{6,4},{7,5},{8,10},{9,11},{10,... | collective-permute-start | bytes 1769480 | tf_op jit(solution)/shard_map/ppermute | solution.py:469
  418.3 21.0 %collective-permute-start.62 = (bf16[4,96,768]{2,1,0:T(8,128)(2,1)}, bf16[4,96,768]{2,1,0:T(8,128)(2,1)}, u32[]{:S(2)}, u32[]{:S(2)}) collective-permute-start(bf16[4,96,768]{2,1,0:T(8,128)(2,1)} %dynamic-slice_bitcast_fusion), channel_id=1, source_target_pairs={{0,4},{4,0},{8,12},{12,8},{16,20},{20,16},{24,28},{28,24},{1,5},{5... | collective-permute-start | bytes 1769480 | tf_op jit(solution)/shard_map/ppermute | solution.py:472
  430.7 24.7 %collective-permute-start.46 = (bf16[4,2,96,384]{3,2,1,0:T(8,128)(2,1)}, bf16[4,2,96,384]{3,2,1,0:T(8,128)(2,1)}, u32[]{:S(2)}, u32[]{:S(2)}) collective-permute-start(bf16[4,2,96,384]{3,2,1,0:T(8,128)(2,1)} %copy.104), channel_id=1, source_target_pairs={{0,2},{1,3},{2,0},{3,1},{4,6},{5,7},{6,4},{7,5},{8,10},{9,11},{10,... | collective-permute-start | bytes 1769480 | tf_op jit(solution)/shard_map/ppermute | solution.py:469
  436.4 23.6 %collective-permute-start.44 = (bf16[4,96,768]{2,1,0:T(8,128)(2,1)}, bf16[4,96,768]{2,1,0:T(8,128)(2,1)S(1)}, u32[]{:S(2)}, u32[]{:S(2)}) collective-permute-start(bf16[4,96,768]{2,1,0:T(8,128)(2,1)} %dynamic-slice_bitcast_fusion.2), channel_id=1, source_target_pairs={{0,4},{4,0},{8,12},{12,8},{16,20},{20,16},{24,28},{28,24},{1,5},{5... | collective-permute-start | bytes 1769480 | tf_op jit(solution)/shard_map/ppermute | solution.py:472
  439.2 27.1 %collective-permute-start.65 = (bf16[4,96,384]{2,1,0:T(8,128)(2,1)S(1)}, bf16[4,96,384]{2,1,0:T(8,128)(2,1)S(1)}, u32[]{:S(2)}, u32[]{:S(2)}) collective-permute-start(bf16[4,96,384]{2,1,0:T(8,128)(2,1)S(1)} %dynamic-slice_bitcast_fusion.3), channel_id=1, source_target_pairs={{0,4},{4,0},{8,12},{12,8},{16,20},{20,16},{24,28},{28,24},{1,5},{5... | collective-permute-start | bytes 884744 | tf_op jit(solution)/shard_map/ppermute | solution.py:472
  447.5 25.2 %collective-permute-start.56 = (bf16[4,96,384]{2,1,0:T(8,128)(2,1)S(1)}, bf16[4,96,384]{2,1,0:T(8,128)(2,1)S(1)}, u32[]{:S(2)}, u32[]{:S(2)}) collective-permute-start(bf16[4,96,384]{2,1,0:T(8,128)(2,1)S(1)} %dynamic-slice_bitcast_fusion.4), channel_id=1, source_target_pairs={{0,4},{4,0},{8,12},{12,8},{16,20},{20,16},{24,28},{28,24},{1,5},{5... | collective-permute-start | bytes 884744 | tf_op jit(solution)/shard_map/ppermute | solution.py:472
  467.9 23.5 %collective-permute-start.67 = (bf16[2,96,384]{2,1,0:T(8,128)(2,1)S(1)}, bf16[2,96,384]{2,1,0:T(8,128)(2,1)S(1)}, u32[]{:S(2)}, u32[]{:S(2)}) collective-permute-start(bf16[2,96,384]{2,1,0:T(8,128)(2,1)S(1)} %get-tuple-element.160), channel_id=1, source_target_pairs={{0,16},{4,20},{8,24},{12,28},{16,0},{20,4},{24,8},{28,12},{1,17},{... | collective-permute-start | bytes 442376 | tf_op jit(solution)/shard_map/ppermute | solution.py:475
  474.3 30.0 %collective-permute-start.57 = (bf16[2,96,384]{2,1,0:T(8,128)(2,1)S(1)}, bf16[2,96,384]{2,1,0:T(8,128)(2,1)S(1)}, u32[]{:S(2)}, u32[]{:S(2)}) collective-permute-start(bf16[2,96,384]{2,1,0:T(8,128)(2,1)S(1)} %get-tuple-element.162), channel_id=1, source_target_pairs={{0,8},{4,12},{8,16},{12,20},{16,24},{20,28},{24,0},{28,4},{1,9},{5... | collective-permute-start | bytes 442376 | tf_op jit(solution)/shard_map/ppermute | solution.py:475
  478.0 26.2 %collective-permute-start.58 = (bf16[2,96,384]{2,1,0:T(8,128)(2,1)S(1)}, bf16[2,96,384]{2,1,0:T(8,128)(2,1)S(1)}, u32[]{:S(2)}, u32[]{:S(2)}) collective-permute-start(bf16[2,96,384]{2,1,0:T(8,128)(2,1)S(1)} %get-tuple-element.163), channel_id=1, source_target_pairs={{0,16},{4,20},{8,24},{12,28},{16,0},{20,4},{24,8},{28,12},{1,17},{... | collective-permute-start | bytes 442376 | tf_op jit(solution)/shard_map/ppermute | solution.py:475
  (103 other events, 1216.2 us)
Sparse Core Ops, SparseCore 0:
  243.6 131.4 all-reduce.2

commit v2 on v1

v2 whole, which is shorter than its diff:
```python
import functools

import jax
import jax.numpy as jnp
from jax import lax
from jax.experimental import pallas as pl
from jax.experimental.pallas import tpu as pltpu
from jax.sharding import PartitionSpec as P

D = 768
HEADS = 16
HEAD = D // HEADS
SIDE = 16
CELLS = 256
STEP = 5
CORES = 2

NORM_EPS = 1e-05
BETA_FIRST = 0.9
BETA_SECOND = 0.95
ADAM_EPS = 1e-08
RATE_MATRIX = 0.05
RATE_TABLE = 0.2
RATE_VECTOR = 0.5
DECAY_RATE = 0.1
CLIP_LIMIT = 0.01
MASK_FILL = -1e30
SCALE = HEAD ** (-0.5)
LOG2E = 1.4426950408889634
INV_SQRT_2PI = 0.3989422804014327

OWNERS = 8
HALF = D // (2 * OWNERS)
SMALL = 32

BF = jnp.bfloat16
F32 = jnp.float32
MIB = 1024 * 1024
NN = (((1,), (0,)), ((), ()))
NT = (((1,), (1,)), ((), ()))
TN = (((0,), (0,)), ((), ()))


def dot(a, b, dims=NN):
    return lax.dot_general(a, b, dims, preferred_element_type=F32)


def params(limit):
    return pltpu.CompilerParams(vmem_limit_bytes=limit)


def norm_stats(v):
    mean = jnp.mean(v, axis=-1, keepdims=True)
    centred = v - mean
    spread = jnp.mean(centred * centred, axis=-1, keepdims=True)
    rstd = lax.rsqrt(spread + NORM_EPS)
    return centred * rstd, rstd


def norm_back(c, gain, u, rstd):
    cg = c * gain
    mean_cg = jnp.mean(cg, axis=-1, keepdims=True)
    mean_cgu = jnp.mean(cg * u, axis=-1, keepdims=True)
    return rstd * (cg - mean_cg - u * mean_cgu)


def head_window(h):
    low = h * HEAD
    first = low // 128
    last = (low + HEAD - 1) // 128
    return first, last + 1 - first


def head_mask(h):
    first, tiles = head_window(h)
    lane = lax.broadcasted_iota(jnp.int32, (1, tiles * 128), 1) + first * 128
    return (lane >= h * HEAD) & (lane < (h + 1) * HEAD)


def crop_target(position, height, breadth, top, left):
    row = (position >> 4) - top
    col = (position & (SIDE - 1)) - left
    inside = (row >= 0) & (row < height) & (col >= 0) & (col < breadth)
    return jnp.where(inside, row * breadth + col, -1)


def attention_forward_kernel(
    scal, crop, x_ref, table_ref, w_ref, vec_ref,
    emb_ref, n1_ref, q_ref, k_ref, v_ref, p_ref, mixed_ref, after_ref, n2_ref,
):
    grid = scal[0] + pl.program_id(0)
    height, breadth, top, left = crop[grid, 0], crop[grid, 1], crop[grid, 2], crop[grid, 3]
    target = crop_target(
        lax.broadcasted_iota(jnp.int32, (1, CELLS), 1), height, breadth, top, left
    )
    cell = lax.broadcasted_iota(jnp.int32, (CELLS, CELLS), 0)
    onehot = jnp.where(cell == target, 1.0, 0.0).astype(BF)
    emb = x_ref[0].astype(F32) + dot(onehot, table_ref[...])
    emb_ref[...] = emb
    u, _ = norm_stats(emb)
    n1 = (u * vec_ref[0:1, :] + vec_ref[1:2, :]).astype(BF)
    n1_ref[...] = n1
    q_ref[...] = (dot(n1, w_ref[0]) + vec_ref[8:9, :]).astype(BF)
    k_ref[...] = dot(n1, w_ref[1]).astype(BF)
    v_ref[...] = (dot(n1, w_ref[2]) + vec_ref[9:10, :]).astype(BF)
    valid = lax.broadcasted_iota(jnp.int32, (1, CELLS), 1) < height * breadth
    tiles_out = [None] * (D // 128)
    for h in range(HEADS):
        first, tiles = head_window(h)
        lanes = slice(first * 128, (first + tiles) * 128)
        mask = head_mask(h)
        qh = jnp.where(mask, q_ref[:, lanes], 0).astype(BF)
        vh = jnp.where(mask, v_ref[:, lanes], 0).astype(BF)
        s = jnp.where(valid, dot(qh, k_ref[:, lanes], NT), MASK_FILL)
        top_score = jnp.max(s, axis=-1, keepdims=True)
        e = jnp.exp2((s - top_score) * (SCALE * LOG2E))
        p = (e * (1.0 / jnp.sum(e, axis=-1, keepdims=True))).astype(BF)
        p_ref[0, h] = p
        o = dot(p, vh)
        for t in range(tiles):
            part = o[:, t * 128 : (t + 1) * 128]
            at = first + t
            tiles_out[at] = part if tiles_out[at] is None else tiles_out[at] + part
    for t in range(D // 128):
        mixed_ref[:, t * 128 : (t + 1) * 128] = tiles_out[t].astype(BF)
    attention = dot(mixed_ref[...], w_ref[3], NT)
    after = emb_ref[...] + attention + vec_ref[2:3, :]
    after_ref[...] = after
    u2, _ = norm_stats(after)
    n2_ref[...] = (u2 * vec_ref[3:4, :] + vec_ref[4:5, :]).astype(BF)


def up_kernel(scal, n2_ref, w_ref, vec_ref, g_ref, hidden_ref, gp_ref, mine_ref, other_ref, gt_ref):
    j = pl.program_id(0)
    grids = g_ref.shape[0]

    @pl.when(j == 0)
    def _():
        for n in range(grids):
            gt_ref[:, n * CELLS : (n + 1) * CELLS] = g_ref[n].T

    bias = vec_ref[pl.ds(10 + j, 1), :]
    for n in range(grids):
        rows = slice(n * CELLS, (n + 1) * CELLS)
        pre = dot(n2_ref[rows, :], w_ref[0]) + bias
        phi = 0.5 + 0.5 * lax.erf(pre * (0.5**0.5))
        density = jnp.exp2(pre * pre * (-0.5 * LOG2E)) * INV_SQRT_2PI
        hidden_ref[0, rows, :] = (pre * phi).astype(BF)
        gp_ref[0, rows, :] = (phi + pre * density).astype(BF)
    grad = dot(gt_ref[...], hidden_ref[0]).astype(BF)
    keep(scal[1], 0, grad, mine_ref, other_ref)


def keep(core, at, grad, mine_ref, other_ref):
    parts = grad.reshape(OWNERS, 2, HALF, D)
    rows = slice(at * HALF, (at + 1) * HALF)

    @pl.when(core == 0)
    def _():
        mine_ref[:, rows, :] = parts[:, 0]
        other_ref[:, rows, :] = parts[:, 1]

    @pl.when(core != 0)
    def _():
        mine_ref[:, rows, :] = parts[:, 1]
        other_ref[:, rows, :] = parts[:, 0]


def down_kernel(hidden_ref, down_ref, after_ref, vec_ref, out_ref):
    total = dot(hidden_ref[0], down_ref[0], NT)
    for j in range(1, 4):
        total = total + dot(hidden_ref[j], down_ref[j], NT)
    out_ref[0] = (after_ref[...] + total + vec_ref[5:6, :]).astype(BF)


def mlp_kernel(
    scal, gp_ref, down_ref, up_ref, n2_ref, g_ref, after_any, vec_ref, mixed_any,
    ga_ref, galow_ref, mine_ref, other_ref, gb_ref, gn_ref,
    dn2_acc, n2t_ref, gpre_ref, after_ref, mixed_ref, sem,
):
    j = pl.program_id(0)
    grids = g_ref.shape[0]
    core = scal[1]
    late = (
        pltpu.make_async_copy(after_any, after_ref, sem.at[0]),
        pltpu.make_async_copy(mixed_any, mixed_ref, sem.at[1]),
    )

    @pl.when(j == 0)
    def _():
        for copy in late:
            copy.start()
        for n in range(grids):
            rows = slice(n * CELLS, (n + 1) * CELLS)
            n2t_ref[:, rows] = n2_ref[rows, :].T
        gb_ref[...] = jnp.zeros_like(gb_ref)
        gn_ref[...] = jnp.zeros_like(gn_ref)

    @pl.when(j < 4)
    def _():
        colsum = jnp.zeros((1, D), F32)
        for n in range(grids):
            rows = slice(n * CELLS, (n + 1) * CELLS)
            gh = dot(g_ref[n], down_ref[0])
            gpre = (gh * gp_ref[0, rows, :].astype(F32)).astype(BF)
            gpre_ref[rows, :] = gpre
            colsum = colsum + jnp.sum(gpre.astype(F32), axis=0, keepdims=True)
            part = dot(gpre, up_ref[0], NT)

            @pl.when(j == 0)
            def _():
                dn2_acc[rows, :] = part

            @pl.when(j > 0)
            def _():
                dn2_acc[rows, :] += part

        gb_ref[pl.ds(j, 1), :] = colsum
        keep(core, 0, dot(n2t_ref[...], gpre_ref[...]).astype(BF), mine_ref, other_ref)

    @pl.when(j == 4)
    def _():
        for copy in late:
            copy.wait()
        sums = [jnp.zeros((1, D), F32)] * 4
        for n in range(grids):
            rows = slice(n * CELLS, (n + 1) * CELLS)
            u, rstd = norm_stats(after_ref[rows, :])
            c = dn2_acc[rows, :]
            g = g_ref[n].astype(F32)
            ga = g + norm_back(c, vec_ref[3:4, :], u, rstd)
            ga_ref[rows, :] = ga
            galow = ga.astype(BF)
            galow_ref[rows, :] = galow
            n2t_ref[:, rows] = galow.T
            parts = (ga, c * u, c, g)
            sums = [s + jnp.sum(v, axis=0, keepdims=True) for s, v in zip(sums, parts)]
        for i in range(4):
            gn_ref[2 + i : 3 + i, :] = sums[i]
        keep(core, 0, dot(n2t_ref[...], mixed_ref[...]).astype(BF), mine_ref, other_ref)


def attention_backward_kernel(
    scal, crop, ga_ref, galow_ref, mixed_ref, p_ref, q_ref, k_ref, v_ref, emb_ref, n1_ref,
    w_ref, vec_ref, gn_ref, gb_ref,
    ig_ref, table_out, gs_out, mine_ref, other_ref,
    dm_ref, dq_all, dk_all, dv_all, n1t_ref, table_ref, gs_ref,
):
    i = pl.program_id(0)
    grids = pl.num_programs(0) - 1
    core = scal[1]

    @pl.when(i == 0)
    def _():
        table_ref[...] = jnp.zeros_like(table_ref)
        gs_ref[...] = jnp.zeros_like(gs_ref)

    @pl.when(i < grids)
    def _():
        grid = scal[0] + i
        height, breadth, top, left = crop[grid, 0], crop[grid, 1], crop[grid, 2], crop[grid, 3]
        here = pl.ds(pl.multiple_of(i * CELLS, CELLS), CELLS)
        n1t_ref[:, here] = n1_ref[...].T
        dm_ref[...] = dot(galow_ref[...], w_ref[3]).astype(BF)
        outs = [[None] * (D // 128) for _ in range(3)]
        for h in range(HEADS):
            first, tiles = head_window(h)
            lanes = slice(first * 128, (first + tiles) * 128)
            mask = head_mask(h)
            qh = jnp.where(mask, q_ref[:, lanes], 0).astype(BF)
            kh = jnp.where(mask, k_ref[:, lanes], 0).astype(BF)
            dmh = jnp.where(mask, dm_ref[:, lanes], 0).astype(BF)
            p = p_ref[0, h]
            dp = dot(dmh, v_ref[:, lanes], NT)
            delta = jnp.sum(
                dmh.astype(F32) * mixed_ref[:, lanes].astype(F32), axis=-1, keepdims=True
            )
            ds = (p.astype(F32) * (dp - delta)).astype(BF)
            got = (dot(ds, kh), dot(ds, qh, TN), dot(p, dmh, TN))
            for o in range(3):
                for t in range(tiles):
                    part = got[o][:, t * 128 : (t + 1) * 128]
                    at = first + t
                    outs[o][at] = part if outs[o][at] is None else outs[o][at] + part
        for t in range(D // 128):
            lanes = slice(t * 128, (t + 1) * 128)
            dq_all[here, lanes] = (outs[0][t] * SCALE).astype(BF)
            dk_all[here, lanes] = (outs[1][t] * SCALE).astype(BF)
            dv_all[here, lanes] = outs[2][t].astype(BF)
        dq, dk, dv = dq_all[here, :], dk_all[here, :], dv_all[here, :]
        c = dot(dq, w_ref[0], NT) + dot(dk, w_ref[1], NT) + dot(dv, w_ref[2], NT)
        u, rstd = norm_stats(emb_ref[...])
        ge = ga_ref[...] + norm_back(c, vec_ref[0:1, :], u, rstd)
        high = ge.astype(BF)
        ig_ref[0] = high
        low = (ge - high.astype(F32)).astype(BF)
        target = crop_target(
            lax.broadcasted_iota(jnp.int32, (CELLS, 1), 0), height, breadth, top, left
        )
        cell = lax.broadcasted_iota(jnp.int32, (CELLS, CELLS), 1)
        onehot = jnp.where(cell == target, 1.0, 0.0).astype(BF)
        table_ref[...] += dot(onehot, high) + dot(onehot, low)
        for row, v in enumerate((dq.astype(F32), dv.astype(F32), c * u, c)):
            gs_ref[row : row + 1, :] += jnp.sum(v, axis=0, keepdims=True)

    @pl.when(i == grids)
    def _():
        for b, ref in enumerate((dq_all, dk_all, dv_all)):
            keep(core, b, dot(n1t_ref[...], ref[...]).astype(BF), mine_ref, other_ref)
        table_out[...] = table_ref[...]
        gs_out[...] = gs_ref[...]
        start = 3 * HALF
        table = table_ref[...].astype(BF).reshape(OWNERS, 2, 16, D)
        norm = jnp.concatenate([gs_ref[2:4, :], gn_ref[2:6, :]], axis=0).astype(BF)
        split = jnp.concatenate([gs_ref[0:2, :], gb_ref[0:4, :]], axis=0).astype(BF)
        wide, thin = D // OWNERS, D // (4 * OWNERS)
        side = D // 2

        def small(ref, half):
            ref[:, start : start + 16, :] = table[:, half]
            ref[:, start + 16 : start + 32, :] = jnp.zeros((OWNERS, 16, D), BF)
            for dp in range(OWNERS):
                for x in range(2):
                    lane = x * side
                    ref[dp, start + 16 : start + 22, lane : lane + wide] = norm[
                        :, dp * wide : (dp + 1) * wide
                    ]
                    at = (2 * x + half) * (D // 4) + dp * thin
                    ref[dp, start + 24 : start + 30, lane : lane + thin] = split[:, at : at + thin]

        @pl.when(core == 0)
        def _():
            small(mine_ref, 0)
            small(other_ref, 1)

        @pl.when(core != 0)
        def _():
            small(mine_ref, 1)
            small(other_ref, 0)


def sds(shape, dtype):
    return jax.ShapeDtypeStruct(shape, dtype)


def half_shape(blocks, extra=0):
    return sds((OWNERS, blocks * HALF + extra, D), BF)


def whole_block(shape, buffers=None):
    zeros = (0,) * len(shape)
    mode = None if buffers is None else pl.Buffered(buffers)
    return pl.BlockSpec(shape, lambda i, *_: zeros, pipeline_mode=mode)


def attention_forward(scal, crop, x, table, w, vec, grids):
    tokens = grids * CELLS
    rows = pl.BlockSpec((CELLS, D), lambda i, *_: (i, 0))
    spec = pltpu.PrefetchScalarGridSpec(
        num_scalar_prefetch=2,
        grid=(grids,),
        in_specs=[
            pl.BlockSpec((1, CELLS, D), lambda i, s, c: (s[0] + i, 0, 0)),
            whole_block((CELLS, D)),
            whole_block((4, D, D), 1),
            whole_block((16, D)),
        ],
        out_specs=[
            rows, rows, rows, rows, rows,
            pl.BlockSpec((1, HEADS, CELLS, CELLS), lambda i, *_: (i, 0, 0, 0)),
            rows, rows, rows,
        ],
    )
    low, full = sds((tokens, D), BF), sds((tokens, D), F32)
    return pl.pallas_call(
        attention_forward_kernel,
        grid_spec=spec,
        out_shape=[
            full, low, low, low, low, sds((grids, HEADS, CELLS, CELLS), BF), low, full, low,
        ],
        compiler_params=params(32 * MIB),
        cost_estimate=pl.CostEstimate(
            flops=8 * tokens * D * D + 64 * tokens * CELLS * 256,
            bytes_accessed=24 * tokens * D,
            transcendentals=tokens * CELLS * HEADS,
        ),
        name="attention_forward",
    )(scal, crop, x, table, w, vec)


def up_forward(scal, n2, w, vec, cotangent, grids):
    tokens = grids * CELLS
    block = pl.BlockSpec((1, tokens, D), lambda j, *_: (j, 0, 0))
    half = pl.BlockSpec((OWNERS, HALF, D), lambda j, *_: (0, j, 0))
    spec = pltpu.PrefetchScalarGridSpec(
        num_scalar_prefetch=1,
        grid=(4,),
        in_specs=[
            whole_block((tokens, D), 1),
            pl.BlockSpec((1, D, D), lambda j, *_: (j, 0, 0)),
            whole_block((16, D)),
            pl.BlockSpec((grids, CELLS, D), lambda j, s: (s[2], 0, 0), pipeline_mode=pl.Buffered(1)),
        ],
        out_specs=[block, block, half, half],
        scratch_shapes=[pltpu.VMEM((D, tokens), BF)],
    )
    return pl.pallas_call(
        up_kernel,
        grid_spec=spec,
        out_shape=[
            sds((4, tokens, D), BF), sds((4, tokens, D), BF), half_shape(4), half_shape(4),
        ],
        compiler_params=params(32 * MIB),
        cost_estimate=pl.CostEstimate(
            flops=16 * tokens * D * D, bytes_accessed=40 * tokens * D, transcendentals=8 * tokens * D
        ),
        name="up_forward",
    )(scal, n2, w, vec, cotangent)


def down_forward(hidden, down, after, vec, grids):
    tokens = grids * CELLS
    return pl.pallas_call(
        down_kernel,
        grid=(grids,),
        in_specs=[
            pl.BlockSpec((4, CELLS, D), lambda i: (0, i, 0)),
            whole_block((4, D, D), 1),
            pl.BlockSpec((CELLS, D), lambda i: (i, 0)),
            whole_block((16, D)),
        ],
        out_specs=pl.BlockSpec((1, CELLS, D), lambda i: (i, 0, 0)),
        out_shape=sds((grids, CELLS, D), BF),
        compiler_params=params(24 * MIB),
        cost_estimate=pl.CostEstimate(
            flops=8 * tokens * D * D, bytes_accessed=20 * tokens * D, transcendentals=0
        ),
        name="down_forward",
    )(hidden, down, after, vec)


def mlp_backward(scal, gp, down, up, n2, cotangent, after, vec, mixed, grids):
    tokens = grids * CELLS
    last = lambda j: jnp.minimum(j, 3)
    block = pl.BlockSpec((1, tokens, D), lambda j, *_: (last(j), 0, 0))
    weight = pl.BlockSpec((1, D, D), lambda j, *_: (last(j), 0, 0))
    half = pl.BlockSpec((OWNERS, HALF, D), lambda j, *_: (0, j, 0))
    rows = whole_block((tokens, D))
    any_spec = pl.BlockSpec(memory_space=pl.ANY)
    spec = pltpu.PrefetchScalarGridSpec(
        num_scalar_prefetch=1,
        grid=(5,),
        in_specs=[
            block, weight, weight, whole_block((tokens, D), 1),
            pl.BlockSpec((grids, CELLS, D), lambda j, s: (s[2], 0, 0), pipeline_mode=pl.Buffered(1)),
            any_spec, whole_block((16, D)), any_spec,
        ],
        out_specs=[rows, rows, half, half, whole_block((8, D)), whole_block((8, D))],
        scratch_shapes=[
            pltpu.VMEM((tokens, D), F32), pltpu.VMEM((D, tokens), BF), pltpu.VMEM((tokens, D), BF),
            pltpu.VMEM((tokens, D), F32), pltpu.VMEM((tokens, D), BF),
            pltpu.SemaphoreType.DMA((2,)),
        ],
    )
    return pl.pallas_call(
        mlp_kernel,
        grid_spec=spec,
        out_shape=[
            sds((tokens, D), F32), sds((tokens, D), BF),
            half_shape(5), half_shape(5), sds((8, D), F32), sds((8, D), F32),
        ],
        compiler_params=params(40 * MIB * tokens // 768),
        cost_estimate=pl.CostEstimate(
            flops=26 * tokens * D * D, bytes_accessed=36 * tokens * D, transcendentals=0
        ),
        name="mlp_backward",
    )(scal, gp, down, up, n2, cotangent, after, vec, mixed)


def attention_backward(scal, crop, ga, galow, mixed, p, q, k, v, emb, n1, w, vec, gn, gb, grids):
    tokens = grids * CELLS
    last = lambda i: jnp.minimum(i, grids - 1)
    rows = pl.BlockSpec((CELLS, D), lambda i, *_: (last(i), 0))
    half = half_shape(3, SMALL)
    few = whole_block((8, D))
    spec = pltpu.PrefetchScalarGridSpec(
        num_scalar_prefetch=2,
        grid=(grids + 1,),
        in_specs=[
            rows, rows, rows,
            pl.BlockSpec((1, HEADS, CELLS, CELLS), lambda i, *_: (last(i), 0, 0, 0)),
            rows, rows, rows, rows, rows,
            whole_block((4, D, D), 1),
            whole_block((16, D)), few, few,
        ],
        out_specs=[
            pl.BlockSpec((1, CELLS, D), lambda i, *_: (last(i), 0, 0)),
            whole_block((CELLS, D)),
            few,
            whole_block(half.shape, 1), whole_block(half.shape, 1),
        ],
        scratch_shapes=[pltpu.VMEM((CELLS, D), BF)]
        + [pltpu.VMEM((tokens, D), BF)] * 3
        + [pltpu.VMEM((D, tokens), BF), pltpu.VMEM((CELLS, D), F32), pltpu.VMEM((8, D), F32)],
    )
    return pl.pallas_call(
        attention_backward_kernel,
        grid_spec=spec,
        out_shape=[sds((grids, CELLS, D), BF), sds((CELLS, D), F32), sds((8, D), F32), half, half],
        compiler_params=params(40 * MIB),
        cost_estimate=pl.CostEstimate(
            flops=14 * tokens * D * D + 128 * tokens * CELLS * 256,
            bytes_accessed=32 * tokens * D,
            transcendentals=0,
        ),
        name="attention_backward",
    )(scal, crop, ga, galow, mixed, p, q, k, v, emb, n1, w, vec, gn, gb)


class Place:
    def __init__(self, dp_size, mp_size):
        self.z_size = dp_size // 2
        dp, mp = lax.axis_index("dp"), lax.axis_index("mp")
        self.dp, self.mp = dp, mp
        self.z, self.y = dp // 2, dp % 2
        self.x, self.c = mp // 2, mp % 2
        self.core_pairs = [(i, i ^ 1) for i in range(mp_size)]
        self.x_pairs = [(i, i ^ 2) for i in range(mp_size)]
        self.y_pairs = [(i, i ^ 1) for i in range(dp_size)]
        self.z_shift = [
            [(i, ((i // 2 + s) % self.z_size) * 2 + i % 2) for i in range(dp_size)]
            for s in range(self.z_size)
        ]

        self.corner_pairs = [
            (d * mp_size + m, (d ^ 1) * mp_size + (m ^ 2))
            for d in range(dp_size)
            for m in range(mp_size)
        ]

    def core(self, v):
        return lax.ppermute(v, "mp", self.core_pairs)

    def over_corner(self, v):
        return lax.ppermute(v, ("dp", "mp"), self.corner_pairs)

    def over_x(self, v):
        return lax.ppermute(v, "mp", self.x_pairs)

    def over_y(self, v):
        return lax.ppermute(v, "dp", self.y_pairs)

    def over_z(self, v, shift):
        return lax.ppermute(v, "dp", self.z_shift[shift])


def after_op(value, *earlier):
    return lax.optimization_barrier((value,) + earlier)[0]


def together(*values):
    leaves, tree = jax.tree.flatten(values)
    return jax.tree.unflatten(tree, lax.optimization_barrier(leaves))


def assemble_kernel(rows, extra, where_ref, *refs):
    pieces, outs = refs[:10], refs[10:]
    z, y, x, c = where_ref[0], where_ref[1], where_ref[2], where_ref[3]
    depth = pieces[0].shape[1]
    for core_rel in range(2):
        own, by_x, by_y, diag0, diag1 = pieces[core_rel * 5 : core_rel * 5 + 5]
        core = c if core_rel == 0 else 1 - c
        for s in range(depth):
            zs = lax.rem(z - s + depth, depth)
            for xr in range(2):
                for yr in range(2):
                    xs = x if xr == 0 else 1 - x
                    ys = y if yr == 0 else 1 - y
                    dp = zs * 2 + ys
                    row = pl.ds(pl.multiple_of(dp * rows, rows), rows)
                    lane = pl.ds(pl.multiple_of(xs * (D // 2), D // 2), D // 2)
                    if xr and yr:
                        first, second = diag0[s], diag1[s]
                    else:
                        src = (own, by_x, by_y)[xr + 2 * yr]
                        first, second = src[0, s], src[1, s]
                    outs[0][core * 2, row, lane] = first[:rows]
                    outs[0][core * 2 + 1, row, lane] = second[:rows]
                    if extra:
                        share = pl.ds(pl.multiple_of((dp * 2 + core) * extra, extra), extra)
                        outs[1][share, lane] = first[rows:]
                        outs[2][dp, xs, core] = second[rows:]


def assemble(where, pieces, extra, dp_size):
    rows = D // dp_size
    outs = [sds((4, D, D), BF)]
    if extra:
        outs += [sds((dp_size * 2 * extra, D), BF), sds((dp_size, 2, 2, extra, D // 2), BF)]
    vmem = pl.BlockSpec(memory_space=pltpu.VMEM)
    return pl.pallas_call(
        functools.partial(assemble_kernel, rows, extra),
        in_specs=[pl.BlockSpec(memory_space=pltpu.SMEM)] + [vmem] * 10,
        out_specs=[vmem] * len(outs),
        out_shape=outs,
        compiler_params=params(16 * MIB),
        cost_estimate=pl.CostEstimate(flops=0, bytes_accessed=16 * D * D, transcendentals=0),
        name="assemble",
    )(where, *pieces)


def gather_z(place, u):
    return [u] + [place.over_z(u, s) for s in range(1, place.z_size)]


def gather_xy(place, parts):
    own = jnp.stack(parts, axis=1)
    return own, place.over_x(own), place.over_y(own)


def gather_diagonal(place, by_x, by_y):
    return place.over_y(by_x[0]), place.over_x(by_y[1])


def join(a, b):
    return (a.astype(F32) + b.astype(F32)).astype(BF)


class Reduction:
    def __init__(self, place):
        self.place = place

    def over_core(self, mine, other):
        zs = self.place.z_size
        got = self.place.core(other)
        h = join(mine, got)
        return h.reshape(zs, 2, h.shape[1], D)

    def pick_y(self, v, at):
        return lax.dynamic_index_in_dim(v, at, axis=v.ndim - 3, keepdims=False)

    def pick_x(self, v, at):
        return jnp.where(at == 0, v[..., : D // 2], v[..., D // 2 :])

    def send_y(self, v):
        y = self.place.y
        sent = self.pick_y(v, 1 - y)
        return self.pick_y(v, y), self.place.over_y(sent), sent

    def send_x(self, v):
        x = self.place.x
        sent = self.pick_x(v, 1 - x)
        return self.pick_x(v, x), self.place.over_x(sent), sent

    def send_z(self, v):
        zs, z = self.place.z_size, self.place.z
        parts = [lax.dynamic_index_in_dim(v, (z + s) % zs, axis=0, keepdims=False) for s in range(zs)]
        return parts[0], [self.place.over_z(parts[s], s) for s in range(1, zs)], parts

    def sum_z(self, kept, got):
        total = kept.astype(F32)
        for v in got:
            total = total + v.astype(F32)
        return total


def collect_kernel(where_ref, own, by_core, by_x, by_both, out, sem):
    x, c = where_ref[2], where_ref[3]
    grids = own.shape[0]
    copies = []
    for n, (piece, mp) in enumerate(
        ((own, 2 * x + c), (by_core, 2 * x + 1 - c), (by_x, 2 - 2 * x + c), (by_both, 3 - 2 * x - c))
    ):
        copies.append(pltpu.make_async_copy(piece, out.at[pl.ds(mp * grids, grids)], sem.at[n]))
    for copy in copies:
        copy.start()
    for copy in copies:
        copy.wait()


def start_grids(place, own):
    return own, place.core(own), place.over_x(own)


def finish_grids(place, where, pieces):
    own, by_core, by_x = pieces
    by_both = place.core(by_x)
    hbm = pl.BlockSpec(memory_space=pl.ANY)
    return pl.pallas_call(
        collect_kernel,
        in_specs=[pl.BlockSpec(memory_space=pltpu.SMEM)] + [hbm] * 4,
        out_specs=pl.BlockSpec(memory_space=pltpu.VMEM),
        out_shape=sds((4 * own.shape[0],) + own.shape[1:], own.dtype),
        scratch_shapes=[pltpu.SemaphoreType.DMA((4,))],
        compiler_params=params(12 * MIB),
        cost_estimate=pl.CostEstimate(flops=0, bytes_accessed=8 * own.size, transcendentals=0),
        name="collect",
    )(where, own, by_core, by_x, by_both)


def sum_plane(place, value):
    value = value + place.core(value)
    value = (value + place.over_x(value)) + (place.over_y(value) + place.over_corner(value))
    return [value] + [place.over_z(value, s) for s in range(1, place.z_size)]


ROWS1, ROWS2, ROWS3 = 4 * HALF, 5 * HALF, 3 * HALF
ROWS = ROWS1 + ROWS2 + ROWS3


def totals_kernel(where, *refs):
    keep1, got1, keep2, *got2 = refs[:6]
    keep3, *got3 = refs[6:10]
    kept_ref, sent_ref, tail_ref, square_ref = refs[10:]
    x, c = where[2], where[3]

    def total(first, others):
        value = first[...].astype(F32)
        for ref in others:
            value = value + ref[...].astype(F32)
        return value

    whole3 = total(keep3, got3)
    parts = (total(keep1, [got1]), total(keep2, got2), whole3[:ROWS3])
    wide = D // 4
    row = 0
    square = jnp.zeros((1, D // 2), F32)
    for value in parts:
        rows = slice(row, row + value.shape[0])
        left, right = value[:, :wide], value[:, wide:]

        @pl.when(c == 0)
        def _():
            kept_ref[rows, :] = left
            sent_ref[rows, :] = right

        @pl.when(c != 0)
        def _():
            kept_ref[rows, :] = right
            sent_ref[rows, :] = left

        square = square + jnp.sum(value * value, axis=0, keepdims=True)
        row += value.shape[0]
    tail = whole3[ROWS3:]
    tail_ref[...] = tail
    lane = lax.broadcasted_iota(jnp.int32, (16, D // 2), 1)
    line = lax.broadcasted_iota(jnp.int32, (16, D // 2), 0)
    owner = jnp.where((x == 0) & (c == 0), 1.0, 0.0)
    codes = tail[16:32]
    small = jnp.where(line < 8, jnp.where(lane < D // OWNERS, codes * owner, 0.0), 0.0)
    small = jnp.where((line >= 8) & (lane < D // (4 * OWNERS)), codes, small)
    square = square + jnp.sum(tail[:16] * tail[:16] + small * small, axis=0, keepdims=True)
    square_ref[...] = jnp.full((8, 128), jnp.sum(square), F32)


def totals(where, keep1, got1, keep2, got2, keep3, got3):
    vmem = pl.BlockSpec(memory_space=pltpu.VMEM)
    ins = [keep1, got1, keep2, *got2, keep3, *got3]
    return pl.pallas_call(
        totals_kernel,
        in_specs=[pl.BlockSpec(memory_space=pltpu.SMEM)] + [vmem] * len(ins),
        out_specs=[vmem] * 4,
        out_shape=[
            sds((ROWS, D // 4), F32), sds((ROWS, D // 4), F32), sds((SMALL, D // 2), F32),
            sds((8, 128), F32),
        ],
        compiler_params=params(16 * MIB),
        name="totals",
    )(where, *ins)


def update_kernel(where, *refs):
    kept, got, tail, t_core, t_x, t_both = refs[:6]
    squares = refs[6:10]
    state, outs = refs[10:25], refs[25:]
    x, c = where[2], where[3]
    square = (squares[0][0:1, 0:1] + squares[2][0:1, 0:1]) + (
        squares[1][0:1, 0:1] + squares[3][0:1, 0:1]
    )
    norm = jnp.sqrt(square)
    factor = jnp.minimum(1.0, CLIP_LIMIT / (norm + 1e-06))
    outs[0][...] = norm

    def step(at, index, gradient, rate, decay):
        weight, first, second = (state[at + 5 * i][index] for i in range(3))
        new = adam_step(weight, gradient, first, second, rate, decay)
        for i in range(3):
            outs[1 + at + 5 * i][index] = new[i]

    def block(row):
        rows = slice(row, row + HALF)
        own, other = kept[rows, :], got[rows, :]
        top = jnp.where(c == 0, own, other)
        bottom = jnp.where(c == 0, other, own)
        return jnp.concatenate([top, bottom], axis=0) * factor

    front = [ROWS1 + ROWS2 + HALF * b for b in range(3)] + [ROWS1 + HALF * b for b in range(4)]
    for b, row in enumerate(front):
        step(0, b, block(row), RATE_MATRIX, DECAY_RATE)
    back = [ROWS1 + 4 * HALF] + [HALF * b for b in range(4)]
    for b, row in enumerate(back):
        step(1, b, block(row).T, RATE_MATRIX, DECAY_RATE)
    norm_grad = tail[16:22, : D // OWNERS] * factor
    outs[16][...] = norm_grad
    step(3, Ellipsis, norm_grad, RATE_VECTOR, 0.0)
    step(2, Ellipsis, tail[24:30, : D // (4 * OWNERS)] * factor, RATE_VECTOR, 0.0)
    own, by_core, by_x, by_both = tail[0:16, :], t_core[...], t_x[...], t_both[...]
    here = jnp.concatenate(
        [jnp.where(c == 0, own, by_core), jnp.where(c == 0, by_core, own)], axis=0
    )
    there = jnp.concatenate(
        [jnp.where(c == 0, by_x, by_both), jnp.where(c == 0, by_both, by_x)], axis=0
    )
    side = D // 2
    for half in range(2):
        gradient = jnp.where(x == half, here, there) * factor
        lanes = (slice(None), slice(half * side, (half + 1) * side))
        step(4, lanes, gradient, RATE_TABLE, DECAY_RATE)


def update(where, kept, got, tail, t_core, t_x, t_both, squares, state):
    vmem = pl.BlockSpec(memory_space=pltpu.VMEM)
    ins = [kept, got, tail, t_core, t_x, t_both, *squares, *state]
    shapes = [sds((1, 1), F32)] + [sds(v.shape, F32) for v in state] + [sds(state[3].shape, F32)]
    return pl.pallas_call(
        update_kernel,
        in_specs=[pl.BlockSpec(memory_space=pltpu.SMEM)] + [vmem] * len(ins),
        out_specs=[vmem] * len(shapes),
        out_shape=shapes,
        compiler_params=params(24 * MIB),
        name="update",
    )(where, *ins)


def adam_step(weight, gradient, first, second, rate, decay):
    first_new = BETA_FIRST * first + (1.0 - BETA_FIRST) * gradient
    second_new = BETA_SECOND * second + (1.0 - BETA_SECOND) * gradient * gradient
    first_hat = first_new / (1.0 - BETA_FIRST**STEP)
    second_hat = second_new / (1.0 - BETA_SECOND**STEP)
    weight_new = weight - rate * (first_hat / (jnp.sqrt(second_hat) + ADAM_EPS) + decay * weight)
    return (weight_new, first_new, second_new)


def body(
    dp_size, mp_size,
    block_input, cotangent, crop_boxes, front_weights, back_weights, split_biases, norm_params,
    pos_table, front_first, back_weight_first_moment, split_first, norm_first, table_first,
    front_second, back_second, split_second, norm_second, table_second,
):
    place = Place(dp_size, mp_size)
    direct = dp_size == 8 and mp_size == 4
    x, y, z, c = place.x, place.y, place.z, place.c
    grids = block_input.shape[0] // mp_size
    scal = jnp.stack([place.mp * grids, c, place.mp, place.dp]).astype(jnp.int32)
    where = jnp.stack([z, y, x, c]).astype(jnp.int32)
    turned = jnp.swapaxes(back_weights, 1, 2).astype(BF)
    low_front = front_weights.astype(BF)
    rows, lanes = low_front.shape[1], low_front.shape[2]

    if direct:
        shards = jnp.concatenate([low_front[:3], turned[:1], low_front[3:], turned[1:]])
        shards = shards.reshape(3, 2, 2, rows, lanes)
        mine = lax.dynamic_index_in_dim(shards, c, axis=1, keepdims=False)
        sent = lax.dynamic_index_in_dim(shards, 1 - c, axis=1, keepdims=False)
        got = place.core(sent)
        units = jnp.where(
            c == 0, jnp.concatenate([mine, got], -1), jnp.concatenate([got, mine], -1)
        )
        extra = pos_table.shape[0] // 2
        half = jnp.where(c == 0, pos_table[:extra], pos_table[extra:]).astype(BF)
        half = jnp.where(x == 0, half[:, : D // 2], half[:, D // 2 :])
        packed = jnp.zeros((extra, D // 2), BF)
        packed = lax.dynamic_update_slice(packed, norm_params.astype(BF), (0, 0))
        packed = lax.dynamic_update_slice(packed, split_biases.astype(BF), (0, 128))
        first_unit = jnp.concatenate([units[0], jnp.stack([half, packed])], axis=1)
        parts1 = gather_z(place, first_unit)
        parts1, unit2 = together(parts1, units[1])
        own1 = gather_xy(place, parts1)
        parts2 = gather_z(place, unit2)
        own1 = list(together(*own1))
        diag1 = gather_diagonal(place, own1[1], own1[2])
        far1 = [place.core(v) for v in own1]
        diag1, far1, parts2, unit3 = together(diag1, far1, parts2, units[2])
        own2 = list(gather_xy(place, parts2))
        parts3 = gather_z(place, unit3)
        far1 += [place.core(v) for v in diag1]
        w_attn, table, codes = assemble(where, [*own1, *diag1, *far1], extra, dp_size)
        norms = jnp.swapaxes(codes[:, 0, 0, 0:6, : norm_params.shape[1]], 0, 1).reshape(6, D)
        splits = codes[:, :, :, 0:6, 128 : 128 + split_biases.shape[1]]
        splits = jnp.transpose(splits, (3, 1, 2, 0, 4)).reshape(6, D)
    else:

        def whole(v):
            v = lax.all_gather(v, "dp", axis=1, tiled=True)
            return lax.all_gather(v, "mp", axis=2, tiled=True)

        w_attn = whole(jnp.concatenate([low_front[:3], turned[:1]]))
        w_up, w_down = whole(low_front[3:]), whole(turned[1:])
        table = lax.all_gather(pos_table.astype(BF), "dp", axis=0, tiled=True)
        norms = lax.all_gather(norm_params.astype(BF), "dp", axis=1, tiled=True)
        splits = lax.all_gather(split_biases.astype(BF), ("mp", "dp"), axis=1, tiled=True)
    gap = jnp.zeros((2, D), F32)
    vec = jnp.concatenate([norms.astype(F32), gap, splits.astype(F32), gap])

    cells_here, norm_here = pos_table.shape[0], norm_params.shape[1]
    split_here = split_biases.shape[1]
    if direct:
        w_attn, own2[0], parts3[0] = together(w_attn, own2[0], parts3[0])
    fwd = attention_forward(scal, crop_boxes, block_input, table, w_attn, vec, grids)
    if direct:
        fwd, own2, parts3 = together(fwd, own2, parts3)
        diag2 = gather_diagonal(place, own2[1], own2[2])
        own3 = list(gather_xy(place, parts3))
        far2 = [place.core(v) for v in own2]
        diag2, far2, own3[0] = together(diag2, far2, own3[0])
        far2 += [place.core(v) for v in diag2]
        (w_up,) = assemble(where, [*own2, *diag2, *far2], 0, dp_size)
    emb, n1, q, k, v, p, mixed, after, n2 = fwd
    up = up_forward(scal, n2, w_up, vec, cotangent, grids)
    if direct:
        red = Reduction(place)
        up, own3 = together(up, own3)
        hidden, gp, down_mine, down_other = up
        diag3 = gather_diagonal(place, own3[1], own3[2])
        far3 = [place.core(v) for v in own3]
        h1 = red.over_core(down_mine, down_other)
        diag3, far3, h1 = together(diag3, far3, h1)
        far3 += [place.core(v) for v in diag3]
        keep1, got1, sent1 = red.send_y(h1)
        (w_down,) = assemble(where, [*own3, *diag3, *far3], 0, dp_size)
        w_down, sent1 = together(w_down, sent1)
        out = down_forward(hidden, w_down, after, vec, grids)
        gp, out = together(gp, out)
        out_pieces = start_grids(place, out)
        back = mlp_backward(scal, gp, w_down, w_up, n2, cotangent, after, vec, mixed, grids)
        back, got1, out_pieces = together(back, got1, out_pieces)
        ga, galow, up_mine, up_other, gb, gn = back
        keep1, got1, sent1 = red.send_z(join(keep1, got1))
        h2 = red.over_core(up_mine, up_other)
        cut = h2.shape[2] // 2
        keep2a, got2a, sent2a = red.send_y(h2[:, :, :cut])
        keep2b, got2b, sent2b = red.send_x(h2[:, :, cut:])
        galow, sent1, sent2a, sent2b = together(galow, sent1, sent2a, sent2b)
        back = attention_backward(
            scal, crop_boxes, ga, galow, mixed, p, q, k, v, emb, n1, w_attn, vec, gn, gb, grids
        )
        back, got1, got2a, got2b = together(back, got1, got2a, got2b)
        ig, dtable, gs, mine3, other3 = back
        h3 = red.over_core(mine3, other3)
        keep1, got1, _ = red.send_x(red.sum_z(keep1, got1).astype(BF))
        keep2a, got2a, _ = red.send_x(join(keep2a, got2a))
        keep2b, got2b, _ = red.send_y(join(keep2b, got2b))
        cut = h3.shape[2] // 2
        keep3a, got3a, _ = red.send_y(h3[:, :, :cut])
        keep3b, got3b, _ = red.send_x(h3[:, :, cut:])
        keep3a, keep3b, got1, got2a, got2b = together(keep3a, keep3b, got1, got2a, got2b)
        h2 = jnp.concatenate([join(keep2a, got2a), join(keep2b, got2b)], axis=1)
        keep2, got2, _ = red.send_z(h2)
        keep3a, got3a, got3b = together(keep3a, got3a, got3b)
        keep3a, got3a, _ = red.send_x(join(keep3a, got3a))
        keep3b, got3b, _ = red.send_y(join(keep3b, got3b))
        got3a, got3b, got2 = together(got3a, got3b, got2)
        h3 = jnp.concatenate([join(keep3a, got3a), join(keep3b, got3b)], axis=1)
        keep3, got3, _ = red.send_z(h3)
        ig, keep3 = together(ig, keep3)
        ig_pieces = start_grids(place, ig)
        block_output = finish_grids(place, where, out_pieces)
        got3, block_output = together(got3, block_output)
        kept, sent, tail, square = totals(where, keep1, got1, keep2, got2, keep3, got3)
        squares = sum_plane(place, square)
        got = place.core(sent)
        t_own = tail[:16]
        t_x = place.over_x(t_own)
        t_core, t_both = place.core(t_own), place.core(t_x)
        ig_pieces, t_x = together(ig_pieces, t_x)
        input_grad = finish_grids(place, where, ig_pieces)
        squares, input_grad = together(squares, input_grad)
        state = (
            front_weights, back_weights, split_biases, norm_params, pos_table,
            front_first, back_weight_first_moment, split_first, norm_first, table_first,
            front_second, back_second, split_second, norm_second, table_second,
        )
        new = update(where, kept, got, tail, t_core, t_x, t_both, squares, state)
        return (block_output, input_grad, new[0][0, 0], *new[1:])
    else:
        hidden, gp, down_mine, down_other = up
        out = down_forward(hidden, w_down, after, vec, grids)
        ga, galow, up_mine, up_other, gb, gn = mlp_backward(
            scal, gp, w_down, w_up, n2, cotangent, after, vec, mixed, grids
        )
        ig, dtable, gs, mine3, other3 = attention_backward(
            scal, crop_boxes, ga, galow, mixed, p, q, k, v, emb, n1, w_attn, vec, gn, gb, grids
        )

        def share(mine, other, blocks):
            low, high = jnp.where(c == 0, mine, other), jnp.where(c == 0, other, mine)
            full = jnp.stack([low, high], 1)[:, :, : blocks * HALF].astype(F32)
            full = full.reshape(OWNERS, 2, blocks, HALF, D)
            full = jnp.transpose(full, (2, 0, 1, 3, 4)).reshape(blocks, D, D)
            full = lax.psum_scatter(full, "dp", scatter_dimension=1, tiled=True)
            return lax.psum_scatter(full, "mp", scatter_dimension=2, tiled=True)

        down_share = share(down_mine, down_other, 4)
        up_share = share(up_mine, up_other, 5)
        out_share, up_share = up_share[4:], up_share[:4]
        qkv_share = share(mine3, other3, 3)
        block_output = lax.all_gather(out, "mp", axis=0, tiled=True)
        input_grad = lax.all_gather(ig, "mp", axis=0, tiled=True)
        norm_grad = jnp.concatenate([gs[2:4], gn[2:6]])
        split_grad = jnp.concatenate([gs[0:2], gb[0:4]])
        dtable = lax.psum(dtable, ("dp", "mp"))
        norm_grad = lax.psum(norm_grad, ("dp", "mp"))
        split_grad = lax.psum(split_grad, ("dp", "mp"))
        table_share = lax.dynamic_slice(dtable, (place.dp * cells_here, 0), (cells_here, D))
        norm_share = lax.dynamic_slice(norm_grad, (0, place.dp * norm_here), (6, norm_here))
        split_share = lax.dynamic_slice(
            split_grad, (0, (place.mp * dp_size + place.dp) * split_here), (6, split_here)
        )
        table_square = jnp.sum(table_share * table_share) / mp_size
    front_share = jnp.concatenate([qkv_share, up_share])
    back_share = jnp.concatenate([out_share, down_share])
    owner = (place.mp == 0).astype(F32)
    square = (
        jnp.sum(qkv_share * qkv_share)
        + jnp.sum(out_share * out_share)
        + jnp.sum(up_share * up_share)
        + jnp.sum(down_share * down_share)
        + jnp.sum(split_share * split_share)
        + owner * jnp.sum(norm_share * norm_share)
        + table_square
    )
    clip_norm = jnp.sqrt(lax.psum(square, ("dp", "mp")))
    factor = jnp.minimum(1.0, CLIP_LIMIT / (clip_norm + 1e-06))
    norm_clipped = norm_share * factor
    new_front, front_first_new, front_second_new = adam_step(
        front_weights, front_share * factor, front_first, front_second, RATE_MATRIX, DECAY_RATE
    )
    new_back, back_first_new, back_second_new = adam_step(
        back_weights,
        jnp.swapaxes(back_share, 1, 2) * factor,
        back_weight_first_moment,
        back_second,
        RATE_MATRIX,
        DECAY_RATE,
    )
    new_split, split_first_new, split_second_new = adam_step(
        split_biases, split_share * factor, split_first, split_second, RATE_VECTOR, 0.0
    )
    new_norm, norm_first_new, norm_second_new = adam_step(
        norm_params, norm_clipped, norm_first, norm_second, RATE_VECTOR, 0.0
    )
    new_table, table_first_new, table_second_new = adam_step(
        pos_table, table_share * factor, table_first, table_second, RATE_TABLE, DECAY_RATE
    )
    return (
        block_output, input_grad, clip_norm,
        new_front, new_back, new_split, new_norm, new_table,
        front_first_new, back_first_new, split_first_new, norm_first_new, table_first_new,
        front_second_new, back_second_new, split_second_new, norm_second_new, table_second_new,
        norm_clipped,
    )


def solution(mesh):
    front, back = P(None, "dp", "mp"), P(None, "mp", "dp")
    split, norm, table = P(None, ("mp", "dp")), P(None, "dp"), P("dp", None)
    state = (front, back, split, norm, table)
    rows = P("dp", None, None)
    return jax.shard_map(
        functools.partial(body, mesh.shape["dp"], mesh.shape["mp"]),
        mesh=mesh,
        in_specs=(rows, rows, P("dp", None)) + state * 3,
        out_specs=(rows, rows, P()) + state * 3 + (norm,),
        check_vma=False,
    )
```

time: 563 us -> 342 us (0.61)
  waiting for transfers between devices: 243 us -> 96.7 us
  Pallas kernels: 132 us -> 110 us
  between operations: 24.2 us -> 2.46 us
  other arithmetic: 33.4 us -> 12.5 us
    psum x1 -> x0, waiting for transfers between devices: 115 us -> none  [body(): lax.psum(jnp.concatenate([dtable, norm_grad, split_grad]), ('dp', 'mp'))]
    ppermute x13 -> x12, waiting for transfers between devices: 46.9 us -> 16 us  [over_y(): return lax.ppermute(v, 'dp', self.y_pairs)]
    ppermute x21, waiting for transfers between devices: 46.9 us -> 27 us  [over_z(): return lax.ppermute(v, 'dp', self.z_shift[shift])]
    pallas_call x3, Pallas kernels: 18.2 us -> 4.03 us  [assemble(): pl.pallas_call(functools.partial(assemble_kernel, rows, extra), in_specs=...]
    ppermute x15, waiting for transfers between devices: 33.5 us -> 46.8 us  [over_x(): return lax.ppermute(v, 'mp', self.x_pairs)]
    unnamed x127 -> x147, local copies, waits for them, and re-layouts: 9.3 us -> 20.9 us
    sub x5 -> x0, other arithmetic: 7.52 us -> none  [adam_step(): weight - rate * (first_hat / (jnp.sqrt(second_hat) + ADAM_EPS) + decay *...]
    convert_element_type x3 -> x1, other arithmetic: 6.65 us -> 0.15 us  [body(): keep1, got1, _ = red.send_x(red.sum_z(keep1, got1).astype(BF))]
  transfers between devices with their start and end apart: 77 -> 76, of which waited for: 30 -> 24; matrix products, arithmetic and copies ran while one was open for 10% -> 7% of each run, Pallas kernels for 24% -> 31%
where the time goes in v2:
time: 342 us; the launch traced here: 338 us
  Pallas kernels  110 us (32%)
  waiting for transfers between devices  96.7 us (28%)
  starting transfers between devices  80.4 us (24%)
  local copies, waits for them, and re-layouts  35.7 us (10%)
  other arithmetic  12.5 us (4%)
    ppermute x15, waiting for transfers between devices, over_x(): return lax.ppermute(v, 'mp', self.x_pairs)  46.8 us
    ppermute x21, starting transfers between devices, over_z(): return lax.ppermute(v, 'dp', self.z_shift[shift])  43.6 us
    pallas_call x1, Pallas kernels, attention_backward(): pl.pallas_call(attention_backward_kernel, grid_spec=spec, out_shape=[sds(...  31.7 us
    ppermute x21, waiting for transfers between devices, over_z(): return lax.ppermute(v, 'dp', self.z_shift[shift])  27 us
    pallas_call x1, Pallas kernels, mlp_backward(): pl.pallas_call(mlp_kernel, grid_spec=spec, out_shape=[sds((tokens, D), F3...  25 us
    unnamed x147, local copies, waits for them, and re-layouts  20.9 us
    pallas_call x1, Pallas kernels, attention_forward(): pl.pallas_call(attention_forward_kernel, grid_spec=spec, out_shape=[full,...  16.8 us
    ppermute x15, starting transfers between devices, over_x(): return lax.ppermute(v, 'mp', self.x_pairs)  16.1 us
  transfers between devices with their start and end apart: 76, of which 24 were waited for; matrix products, arithmetic and copies ran while one was open for 7% of the time, Pallas kernels for 31%

profile of v2, /device:TPU:0, one launch (start us, length us, event | category | flops | bytes accessed | tf_op | source)
XLA Modules:
  0.0 337.5 jit_solution(16912500938375388065)
XLA Ops:
  7.4 3.0 collective-permute-start.1
  10.4 2.6 collective-permute-start.2
  14.3 3.3 collective-permute-done.1
  17.7 6.9 %collective-permute-done.2 = bf16[2,112,384]{2,1,0:T(8,128)(2,1)S(1)} collective-permute-done((bf16[2,112,384]{2,1,0:T(8,128)(2,1)S(1)}, bf16[2,112,384]{2,1,0:T(8,128)(2,1)S(1)}, u32[]{:S(2)}, u32[]{:S(2)}) %collective-permute-start.2) | collective-permute-done | bytes 172064 | tf_op jit(solution)/shard_map/ppermute | solution.py:554
  27.8 4.2 %collective-permute-start.11 = (bf16[2,96,384]{2,1,0:T(8,128)(2,1)S(1)}, bf16[2,96,384]{2,1,0:T(8,128)(2,1)S(1)}, u32[]{:S(2)}, u32[]{:S(2)}) collective-permute-start(bf16[2,96,384]{2,1,0:T(8,128)(2,1)S(1)} %get-tuple-element.186), channel_id=1, source_target_pairs={{0,8},{4,12},{8,16},{12,20},{16,24},{20,28},{24,0},{28,4},{1,9},{5... | collective-permute-start | bytes 442376 | tf_op jit(solution)/shard_map/ppermute | solution.py:554
  33.5 8.5 %collective-permute-done.4 = bf16[2,4,112,384]{3,2,0,1:T(8,128)(2,1)S(1)} collective-permute-done((bf16[2,4,112,384]{3,2,0,1:T(8,128)(2,1)S(1)}, bf16[2,4,112,384]{3,2,0,1:T(8,128)(2,1)S(1)}, u32[]{:S(2)}, u32[]{:S(2)}) %collective-permute-start.4) | collective-permute-done | bytes 688160 | tf_op jit(solution)/shard_map/ppermute | solution.py:548
  44.5 4.6 %collective-permute-start.13 = (bf16[2,96,384]{2,1,0:T(8,128)(2,1)S(1)}, bf16[2,96,384]{2,1,0:T(8,128)(2,1)S(1)}, u32[]{:S(2)}, u32[]{:S(2)}) collective-permute-start(bf16[2,96,384]{2,1,0:T(8,128)(2,1)S(1)} %get-tuple-element.186), channel_id=1, source_target_pairs={{0,24},{4,28},{8,0},{12,4},{16,8},{20,12},{24,16},{28,20},{1,25},{... | collective-permute-start | bytes 442376 | tf_op jit(solution)/shard_map/ppermute | solution.py:554
  54.6 5.7 %collective-permute-done.6.refs_3_ = bf16[4,112,384]{2,1,0:T(8,128)(2,1)S(1)} collective-permute-done((bf16[4,112,384]{2,1,0:T(8,128)(2,1)}, bf16[4,112,384]{2,1,0:T(8,128)(2,1)S(1)}, u32[]{:S(2)}, u32[]{:S(2)}) %collective-permute-start.6) | collective-permute-done | bytes 344096 | tf_op jit(solution)/shard_map/ppermute | solution.py:551
  60.3 3.8 %collective-permute-done.7.refs_4_ = bf16[4,112,384]{2,1,0:T(8,128)(2,1)S(1)} collective-permute-done((bf16[4,112,384]{2,1,0:T(8,128)(2,1)}, bf16[4,112,384]{2,1,0:T(8,128)(2,1)S(1)}, u32[]{:S(2)}, u32[]{:S(2)}) %collective-permute-start.7) | collective-permute-done | bytes 344096 | tf_op jit(solution)/shard_map/ppermute | solution.py:548
  71.3 2.7 collective-permute-start.19
  77.9 2.3 copy-done.33
  82.5 16.8 %attention_forward.1 = (f32[768,768]{1,0:T(8,128)S(1)}, bf16[768,768]{1,0:T(8,128)(2,1)S(1)}, bf16[768,768]{1,0:T(8,128)(2,1)S(1)}, bf16[768,768]{1,0:T(8,128)(2...) custom-call(s32[4]{0:T(128)S(1)} %pad_add_fusion.scal, ...), custom_call_target="tpu_custom_call" | custom-call | flops 6845104128 | bytes 14155776 | tf_op jit(solution)/shard_map/attention_forward/pallas_call | solution.py:375
  109.7 5.9 %collective-permute-done.21.refs_3_ = bf16[4,96,384]{2,1,0:T(8,128)(2,1)S(1)} collective-permute-done((bf16[4,96,384]{2,1,0:T(8,128)(2,1)S(1)}, bf16[4,96,384]{2,1,0:T(8,128)(2,1)S(1)}, u32[]{:S(2)}, u32[]{:S(2)}) %collective-permute-start.21) | collective-permute-done | bytes 294944 | tf_op jit(solution)/shard_map/ppermute | solution.py:551
  122.0 13.6 %up_forward.1 = (bf16[4,768,768]{2,1,0:T(8,128)(2,1)S(1)}, bf16[4,768,768]{2,1,0:T(8,128)(2,1)S(1)}, bf16[8,192,768]{2,1,0:T(8,128)(2,1)S(1)}, bf16[8,192,768]{2,1,0:T(8,128)(2,1)S(1)}) custom-call(s32[4]{0:T(128)S(1)} %pad_add_fusion.scal, bf16[768,768]{1,0:T(8,128)(2,1)S(1)} %get-tuple-element.204.n2_ref, bf16[4,768,768]{2,1,0:T(8,128)(2,1)S(1)} %assemble.4.w_ref.up_ref, ...), custom_call_target="tpu_custom_call" | custom-call | flops 7247757312 | bytes 23592960 | tf_op jit(solution)/shard_map/up_forward/pallas_call | solution.py:407
  139.6 2.9 collective-permute-done.35
  145.0 2.6 collective-permute-done.30.refs_3_
  147.6 4.0 %collective-permute-done.31.refs_4_ = bf16[4,96,384]{2,1,0:T(8,128)(2,1)} collective-permute-done((bf16[4,96,384]{2,1,0:T(8,128)(2,1)S(1)}, bf16[4,96,384]{2,1,0:T(8,128)(2,1)}, u32[]{:S(2)}, u32[]{:S(2)}) %collective-permute-start.31) | collective-permute-done | bytes 294944 | tf_op jit(solution)/shard_map/ppermute | solution.py:548
  156.4 4.9 %down_forward.1.own = bf16[3,256,768]{2,1,0:T(8,128)(2,1)S(1)} custom-call(bf16[4,768,768]{2,1,0:T(8,128)(2,1)S(1)} %bitcast.120, bf16[4,768,768]{2,1,0:T(8,128)(2,1)S(1)} %assemble.5.down_ref, f32[768,768]{1,0:T(8,128)S(1)} %copy-done.38, f32[16,768]{1,0:T(8,128)S(1)} %copy-done.21), custom_call_target="tpu_custom_call" | custom-call | flops 3623878656 | bytes 11796480 | tf_op jit(solution)/shard_map/down_forward/pallas_call | solution.py:423
  162.0 25.0 %mlp_backward.1 = (f32[768,768]{1,0:T(8,128)S(1)}, bf16[768,768]{1,0:T(8,128)(2,1)S(1)}, bf16[8,240,768]{2,1,0:T(8,128)(2,1)S(1)}, bf16[8,240,768]{2,1,0:T(8,128...) custom-call(s32[4]{0:T(128)S(1)} %pad_add_fusion.scal, bf16[4,768,768]{2,1,0:T(8,128)(2,1)} %copy-done.39, ...), custom_call_target="tpu_custom_call" | custom-call | flops 11777605632 | bytes 21233664 | tf_op jit(solution)/shard_map/mlp_backward/pallas_call | solution.py:465
  198.3 2.8 add_convert_fusion
  204.4 31.7 %attention_backward.1 = (bf16[3,256,768]{2,1,0:T(8,128)(2,1)S(1)}, f32[256,768]{1,0:T(8,128)}, f32[8,768]{1,0:T(8,128)}, bf16[8,176,768]{2,1,0:T(8,128)(2,1)S(1)}, bf16[8,176,768]{2,1,0:T(8,128)(2,1)S(1)}) custom-call(s32[4]{0:T(128)S(1)} %pad_add_fusion.scal, s32[12,4]{1,0:T(8,128)S(1)} %copy-done.28, f32[768,768]{1,0:T(8,128)} %copy-done.41, ...), custom_call_target="tpu_custom_call" | custom-call | flops 12784238592 | bytes 18874368 | tf_op jit(solution)/shard_map/attention_backward/pallas_call | solution.py:506
  244.1 8.4 %collective-permute-done.48.refs_1_ = bf16[192,384]{1,0:T(8,128)(2,1)S(1)} collective-permute-done((bf16[192,384]{1,0:T(8,128)(2,1)S(1)}, bf16[192,384]{1,0:T(8,128)(2,1)S(1)}, u32[]{:S(2)}, u32[]{:S(2)}) %collective-permute-start.48) | collective-permute-done | bytes 147488 | tf_op jit(solution)/shard_map/ppermute | solution.py:548
  252.8 10.6 %collective-permute-done.52 = bf16[4,2,88,384]{3,2,0,1:T(8,128)(2,1)S(1)} collective-permute-done((bf16[4,2,88,384]{3,2,0,1:T(8,128)(2,1)S(1)}, bf16[4,2,88,384]{3,2,0,1:T(8,128)(2,1)S(1)}, u32[]{:S(2)}, u32[]{:S(2)}) %collective-permute-start.52) | collective-permute-done | bytes 540704 | tf_op jit(solution)/shard_map/ppermute | solution.py:548
  270.7 5.2 %collective-permute-done.55.refs_3_ = bf16[240,384]{1,0:T(8,128)(2,1)S(1)} collective-permute-done((bf16[240,384]{1,0:T(8,128)(2,1)S(1)}, bf16[240,384]{1,0:T(8,128)(2,1)S(1)}, u32[]{:S(2)}, u32[]{:S(2)}) %collective-permute-start.55) | collective-permute-done | bytes 184352 | tf_op jit(solution)/shard_map/ppermute | solution.py:554
  275.9 5.8 %collective-permute-done.56.refs_4_ = bf16[240,384]{1,0:T(8,128)(2,1)S(1)} collective-permute-done((bf16[240,384]{1,0:T(8,128)(2,1)S(1)}, bf16[240,384]{1,0:T(8,128)(2,1)S(1)}, u32[]{:S(2)}, u32[]{:S(2)}) %collective-permute-start.56) | collective-permute-done | bytes 184352 | tf_op jit(solution)/shard_map/ppermute | solution.py:554
  282.7 4.2 %collective-permute-start.58 = (bf16[176,384]{1,0:T(8,128)(2,1)S(1)}, bf16[176,384]{1,0:T(8,128)(2,1)S(1)}, u32[]{:S(2)}, u32[]{:S(2)}) collective-permute-start(bf16[176,384]{1,0:T(8,128)(2,1)S(1)} %get-tuple-element.342), channel_id=1, source_target_pairs={{0,8},{4,12},{8,16},{12,20},{16,24},{20,28},{24,0},{28,4},{1,9},{5... | collective-permute-start | bytes 405512 | tf_op jit(solution)/shard_map/ppermute | solution.py:554
  289.3 3.7 %collect.2 = bf16[12,256,768]{2,1,0:T(8,128)(2,1)} custom-call(s32[4]{0:T(128)S(1)} %pad_add_fusion.1.where_ref.where, bf16[3,256,768]{2,1,0:T(8,128)(2,1)S(1)} %copy-done.5, bf16[3,256,768]{2,1,0:T(8,128)(2,1)S(1)} %copy-done.7, bf16[3,256,768]{2,1,0:T(8,128)(2,1)S(1)} %copy-done.9, bf16[3,256,768]{2,1,0:T(8,128)(2,1)S(1)} %collective-permute-done.61.by_both), custom_call_target="tpu_custom_call" | custom-call | bytes 4718592 | tf_op jit(solution)/shard_map/collect/pallas_call | solution.py:689
  293.1 3.9 %collective-permute-done.59.refs_8_ = bf16[176,384]{1,0:T(8,128)(2,1)S(1)} collective-permute-done((bf16[176,384]{1,0:T(8,128)(2,1)S(1)}, bf16[176,384]{1,0:T(8,128)(2,1)S(1)}, u32[]{:S(2)}, u32[]{:S(2)}) %collective-permute-start.59) | collective-permute-done | bytes 135200 | tf_op jit(solution)/shard_map/ppermute | solution.py:554
  299.7 11.2 %collective-permute-done.71.refs_4_ = f32[16,384]{1,0:T(8,128)S(1)} collective-permute-done((f32[16,384]{1,0:T(8,128)S(1)}, f32[16,384]{1,0:T(8,128)S(1)}, u32[]{:S(2)}, u32[]{:S(2)}) %collective-permute-start.71) | collective-permute-done | bytes 24608 | tf_op jit(solution)/shard_map/ppermute | solution.py:548
  320.5 4.0 %collective-permute-start.66 = (f32[8,128]{1,0:T(8,128)S(1)}, f32[8,128]{1,0:T(8,128)}, u32[]{:S(2)}, u32[]{:S(2)}) collective-permute-start(f32[8,128]{1,0:T(8,128)S(1)} %add_add_fusion.refs_6_), channel_id=1, source_target_pairs={{0,8},{4,12},{8,16},{12,20},{16,24},{20,28},{24,0},{28,4},{1,9},{5... | collective-permute-start | bytes 12296 | tf_op jit(solution)/shard_map/ppermute | solution.py:554
  328.3 4.9 %collect.3 = bf16[12,256,768]{2,1,0:T(8,128)(2,1)} custom-call(s32[4]{0:T(128)S(1)} %pad_add_fusion.1.where_ref.where, bf16[3,256,768]{2,1,0:T(8,128)(2,1)S(1)} %get-tuple-element.295.own, bf16[3,256,768]{2,1,0:T(8,128)(2,1)S(1)} %collective-permute-done.69.by_core, bf16[3,256,768]{2,1,0:T(8,128)(2,1)} %collective-permute-done.70.by_x, ...), custom_call_target="tpu_custom_call" | custom-call | bytes 4718592 | tf_op jit(solution)/shard_map/collect/pallas_call | solution.py:689
  333.4 3.9 %update.1 = (f32[1,1]{1,0:T(1,128)}, f32[7,96,192]{2,1,0:T(8,128)}, f32[5,192,96]{2,1,0:T(8,128)}, f32[6,24]{1,0:T(8,128)}, f32[6,96]{1,0:T(8,128)}, /*index=5*/...) custom-call(s32[4]{0:T(128)S(1)} %pad_add_fusion.1.where_ref.where, ...), custom_call_target="tpu_custom_call" | custom-call | tf_op jit(solution)/shard_map/update/pallas_call | solution.py:825
  (361 shorter events, 111.7 us)
Async XLA Ops:
  24.7 17.3 %collective-permute-start.4 = (bf16[2,4,112,384]{3,2,0,1:T(8,128)(2,1)S(1)}, bf16[2,4,112,384]{3,2,0,1:T(8,128)(2,1)S(1)}, u32[]{:S(2)}, u32[]{:S(2)}) collective-permute-start(bf16[2,4,112,384]{3,2,0,1:T(8,128)(2,1)S(1)} %pad_maximum_fusion), channel_id=1, source_target_pairs={{0,2},{1,3},{2,0},{3,1},{4,6},{5,7},{6,4},{7,5},{8,10},{9,11},{10,... | collective-permute-start | bytes 2064392 | tf_op jit(solution)/shard_map/ppermute | solution.py:548
  26.2 17.0 %collective-permute-start.5 = (bf16[2,4,112,384]{3,2,0,1:T(8,128)(2,1)S(1)}, bf16[2,4,112,384]{3,2,0,1:T(8,128)(2,1)S(1)}, u32[]{:S(2)}, u32[]{:S(2)}) collective-permute-start(bf16[2,4,112,384]{3,2,0,1:T(8,128)(2,1)S(1)} %pad_maximum_fusion), channel_id=1, source_target_pairs={{0,4},{4,0},{8,12},{12,8},{16,20},{20,16},{24,28},{28,24},{1,5},{5... | collective-permute-start | bytes 2064392 | tf_op jit(solution)/shard_map/ppermute | solution.py:551
  27.8 16.7 %collective-permute-start.11 = (bf16[2,96,384]{2,1,0:T(8,128)(2,1)S(1)}, bf16[2,96,384]{2,1,0:T(8,128)(2,1)S(1)}, u32[]{:S(2)}, u32[]{:S(2)}) collective-permute-start(bf16[2,96,384]{2,1,0:T(8,128)(2,1)S(1)} %get-tuple-element.186), channel_id=1, source_target_pairs={{0,8},{4,12},{8,16},{12,20},{16,24},{20,28},{24,0},{28,4},{1,9},{5... | collective-permute-start | bytes 442376 | tf_op jit(solution)/shard_map/ppermute | solution.py:554
  31.9 18.0 %collective-permute-start.12 = (bf16[2,96,384]{2,1,0:T(8,128)(2,1)S(1)}, bf16[2,96,384]{2,1,0:T(8,128)(2,1)S(1)}, u32[]{:S(2)}, u32[]{:S(2)}) collective-permute-start(bf16[2,96,384]{2,1,0:T(8,128)(2,1)S(1)} %get-tuple-element.186), channel_id=1, source_target_pairs={{0,16},{4,20},{8,24},{12,28},{16,0},{20,4},{24,8},{28,12},{1,17},{... | collective-permute-start | bytes 442376 | tf_op jit(solution)/shard_map/ppermute | solution.py:554
  43.2 20.8 %collective-permute-start.10 = (bf16[2,4,112,384]{3,2,0,1:T(8,128)(2,1)S(1)}, bf16[2,4,112,384]{3,2,0,1:T(8,128)(2,1)S(1)}, u32[]{:S(2)}, u32[]{:S(2)}) collective-permute-start(bf16[2,4,112,384]{3,2,0,1:T(8,128)(2,1)S(1)} %collective-permute-done.5), channel_id=1, source_target_pairs={{0,1},{1,0},{2,3},{3,2},{4,5},{5,4},{6,7},{7,6},{8,9},{9,8},{10,11... | collective-permute-start | bytes 2064392 | tf_op jit(solution)/shard_map/ppermute | solution.py:542
  43.2 20.8 %collective-permute-start.8 = (bf16[2,4,112,384]{3,2,0,1:T(8,128)(2,1)S(1)}, bf16[2,4,112,384]{3,2,0,1:T(8,128)(2,1)}, u32[]{:S(2)}, u32[]{:S(2)}) collective-permute-start(bf16[2,4,112,384]{3,2,0,1:T(8,128)(2,1)S(1)} %pad_maximum_fusion), channel_id=1, source_target_pairs={{0,1},{1,0},{2,3},{3,2},{4,5},{5,4},{6,7},{7,6},{8,9},{9,8},{10,11... | collective-permute-start | bytes 2064392 | tf_op jit(solution)/shard_map/ppermute | solution.py:542
  43.7 20.3 %collective-permute-start.9 = (bf16[2,4,112,384]{3,2,0,1:T(8,128)(2,1)S(1)}, bf16[2,4,112,384]{3,2,0,1:T(8,128)(2,1)}, u32[]{:S(2)}, u32[]{:S(2)}) collective-permute-start(bf16[2,4,112,384]{3,2,0,1:T(8,128)(2,1)S(1)} %collective-permute-done.4), channel_id=1, source_target_pairs={{0,1},{1,0},{2,3},{3,2},{4,5},{5,4},{6,7},{7,6},{8,9},{9,8},{10,11... | collective-permute-start | bytes 2064392 | tf_op jit(solution)/shard_map/ppermute | solution.py:542
  65.2 39.3 %collective-permute-start.16 = (bf16[2,4,96,384]{3,2,0,1:T(8,128)(2,1)S(1)}, bf16[2,4,96,384]{3,2,0,1:T(8,128)(2,1)S(1)}, u32[]{:S(2)}, u32[]{:S(2)}) collective-permute-start(bf16[2,4,96,384]{3,2,0,1:T(8,128)(2,1)S(1)} %pad_maximum_fusion.2), channel_id=1, source_target_pairs={{0,2},{1,3},{2,0},{3,1},{4,6},{5,7},{6,4},{7,5},{8,10},{9,11},{10,... | collective-permute-start | bytes 1769480 | tf_op jit(solution)/shard_map/ppermute | solution.py:548
  65.8 38.7 %collective-permute-start.17 = (bf16[2,4,96,384]{3,2,0,1:T(8,128)(2,1)S(1)}, bf16[2,4,96,384]{3,2,0,1:T(8,128)(2,1)}, u32[]{:S(2)}, u32[]{:S(2)}) collective-permute-start(bf16[2,4,96,384]{3,2,0,1:T(8,128)(2,1)S(1)} %pad_maximum_fusion.2), channel_id=1, source_target_pairs={{0,4},{4,0},{8,12},{12,8},{16,20},{20,16},{24,28},{28,24},{1,5},{5... | collective-permute-start | bytes 1769480 | tf_op jit(solution)/shard_map/ppermute | solution.py:551
  69.7 34.7 %collective-permute-start.18 = (bf16[2,96,384]{2,1,0:T(8,128)(2,1)}, bf16[2,96,384]{2,1,0:T(8,128)(2,1)}, u32[]{:S(2)}, u32[]{:S(2)}) collective-permute-start(bf16[2,96,384]{2,1,0:T(8,128)(2,1)} %get-tuple-element.208), channel_id=1, source_target_pairs={{0,8},{4,12},{8,16},{12,20},{16,24},{20,28},{24,0},{28,4},{1,9},{5... | collective-permute-start | bytes 442376 | tf_op jit(solution)/shard_map/ppermute | solution.py:554
  71.3 33.1 %collective-permute-start.19 = (bf16[2,96,384]{2,1,0:T(8,128)(2,1)}, bf16[2,96,384]{2,1,0:T(8,128)(2,1)}, u32[]{:S(2)}, u32[]{:S(2)}) collective-permute-start(bf16[2,96,384]{2,1,0:T(8,128)(2,1)} %get-tuple-element.208), channel_id=1, source_target_pairs={{0,16},{4,20},{8,24},{12,28},{16,0},{20,4},{24,8},{28,12},{1,17},{... | collective-permute-start | bytes 442376 | tf_op jit(solution)/shard_map/ppermute | solution.py:554
  74.1 30.4 %collective-permute-start.20 = (bf16[2,96,384]{2,1,0:T(8,128)(2,1)}, bf16[2,96,384]{2,1,0:T(8,128)(2,1)}, u32[]{:S(2)}, u32[]{:S(2)}) collective-permute-start(bf16[2,96,384]{2,1,0:T(8,128)(2,1)} %get-tuple-element.208), channel_id=1, source_target_pairs={{0,24},{4,28},{8,0},{12,4},{16,8},{20,12},{24,16},{28,20},{1,25},{... | collective-permute-start | bytes 442376 | tf_op jit(solution)/shard_map/ppermute | solution.py:554
  117.7 20.1 %collective-permute-start.28 = (bf16[2,4,96,384]{3,2,1,0:T(8,128)(2,1)S(1)}, bf16[2,4,96,384]{3,2,1,0:T(8,128)(2,1)S(1)}, u32[]{:S(2)}, u32[]{:S(2)}) collective-permute-start(bf16[2,4,96,384]{3,2,1,0:T(8,128)(2,1)S(1)} %pad_maximum_fusion.3.refs_0_), channel_id=1, source_target_pairs={{0,2},{1,3},{2,0},{3,1},{4,6},{5,7},{6,4},{7,5},{8,10},{9,11},{10,... | collective-permute-start | bytes 1769480 | tf_op jit(solution)/shard_map/ppermute | solution.py:548
  119.3 18.6 %collective-permute-start.29 = (bf16[2,4,96,384]{3,2,1,0:T(8,128)(2,1)S(1)}, bf16[2,4,96,384]{3,2,1,0:T(8,128)(2,1)S(1)}, u32[]{:S(2)}, u32[]{:S(2)}) collective-permute-start(bf16[2,4,96,384]{3,2,1,0:T(8,128)(2,1)S(1)} %pad_maximum_fusion.3.refs_0_), channel_id=1, source_target_pairs={{0,4},{4,0},{8,12},{12,8},{16,20},{20,16},{24,28},{28,24},{1,5},{5... | collective-permute-start | bytes 1769480 | tf_op jit(solution)/shard_map/ppermute | solution.py:551
  153.7 35.8 %collective-permute-start.38 = (bf16[4,192,768]{2,1,0:T(8,128)(2,1)S(1)}, bf16[4,192,768]{2,1,0:T(8,128)(2,1)}, u32[]{:S(2)}, u32[]{:S(2)}) collective-permute-start(bf16[4,192,768]{2,1,0:T(8,128)(2,1)S(1)} %dynamic-slice_bitcast_fusion), channel_id=1, source_target_pairs={{0,4},{4,0},{8,12},{12,8},{16,20},{20,16},{24,28},{28,24},{1,5},{5... | collective-permute-start | bytes 3538952 | tf_op jit(solution)/shard_map/ppermute | solution.py:551
  161.3 28.2 %collective-permute-start.39 = (bf16[3,256,768]{2,1,0:T(8,128)(2,1)S(1)}, bf16[3,256,768]{2,1,0:T(8,128)(2,1)S(1)}, u32[]{:S(2)}, u32[]{:S(2)}) collective-permute-start(bf16[3,256,768]{2,1,0:T(8,128)(2,1)S(1)} %down_forward.1.own), channel_id=1, source_target_pairs={{0,1},{1,0},{2,3},{3,2},{4,5},{5,4},{6,7},{7,6},{8,9},{9,8},{10,11... | collective-permute-start | bytes 3538952 | tf_op jit(solution)/shard_map/ppermute | solution.py:542
  161.4 29.2 %collective-permute-start.40 = (bf16[3,256,768]{2,1,0:T(8,128)(2,1)S(1)}, bf16[3,256,768]{2,1,0:T(8,128)(2,1)S(1)}, u32[]{:S(2)}, u32[]{:S(2)}) collective-permute-start(bf16[3,256,768]{2,1,0:T(8,128)(2,1)S(1)} %down_forward.1.own), channel_id=1, source_target_pairs={{0,2},{1,3},{2,0},{3,1},{4,6},{5,7},{6,4},{7,5},{8,10},{9,11},{10,... | collective-permute-start | bytes 3538952 | tf_op jit(solution)/shard_map/ppermute | solution.py:548
  193.7 42.3 %collective-permute-start.42 = (bf16[192,768]{1,0:T(8,128)(2,1)S(1)}, bf16[192,768]{1,0:T(8,128)(2,1)S(1)}, u32[]{:S(2)}, u32[]{:S(2)}) collective-permute-start(bf16[192,768]{1,0:T(8,128)(2,1)S(1)} %get-tuple-element.329), channel_id=1, source_target_pairs={{0,8},{4,12},{8,16},{12,20},{16,24},{20,28},{24,0},{28,4},{1,9},{5... | collective-permute-start | bytes 884744 | tf_op jit(solution)/shard_map/ppermute | solution.py:554
  195.8 40.3 %collective-permute-start.43 = (bf16[192,768]{1,0:T(8,128)(2,1)S(1)}, bf16[192,768]{1,0:T(8,128)(2,1)S(1)}, u32[]{:S(2)}, u32[]{:S(2)}) collective-permute-start(bf16[192,768]{1,0:T(8,128)(2,1)S(1)} %get-tuple-element.328), channel_id=1, source_target_pairs={{0,16},{4,20},{8,24},{12,28},{16,0},{20,4},{24,8},{28,12},{1,17},{... | collective-permute-start | bytes 884744 | tf_op jit(solution)/shard_map/ppermute | solution.py:554
  196.0 40.1 %collective-permute-start.44 = (bf16[192,768]{1,0:T(8,128)(2,1)S(1)}, bf16[192,768]{1,0:T(8,128)(2,1)S(1)}, u32[]{:S(2)}, u32[]{:S(2)}) collective-permute-start(bf16[192,768]{1,0:T(8,128)(2,1)S(1)} %get-tuple-element.327), channel_id=1, source_target_pairs={{0,24},{4,28},{8,0},{12,4},{16,8},{20,12},{24,16},{28,20},{1,25},{... | collective-permute-start | bytes 884744 | tf_op jit(solution)/shard_map/ppermute | solution.py:554
  201.6 34.5 %collective-permute-start.46 = (bf16[4,2,120,384]{3,2,0,1:T(8,128)(2,1)S(1)}, bf16[4,2,120,384]{3,2,0,1:T(8,128)(2,1)S(1)}, u32[]{:S(2)}, u32[]{:S(2)}) collective-permute-start(bf16[4,2,120,384]{3,2,0,1:T(8,128)(2,1)S(1)} %broadcast_select_fusion), channel_id=1, source_target_pairs={{0,2},{1,3},{2,0},{3,1},{4,6},{5,7},{6,4},{7,5},{8,10},{9,11},{10,... | collective-permute-start | bytes 2211848 | tf_op jit(solution)/shard_map/ppermute | solution.py:548
  203.1 32.9 %collective-permute-start.45 = (bf16[4,120,768]{2,1,0:T(8,128)(2,1)S(1)}, bf16[4,120,768]{2,1,0:T(8,128)(2,1)S(1)}, u32[]{:S(2)}, u32[]{:S(2)}) collective-permute-start(bf16[4,120,768]{2,1,0:T(8,128)(2,1)S(1)} %dynamic-slice_bitcast_fusion.1), channel_id=1, source_target_pairs={{0,4},{4,0},{8,12},{12,8},{16,20},{20,16},{24,28},{28,24},{1,5},{5... | collective-permute-start | bytes 2211848 | tf_op jit(solution)/shard_map/ppermute | solution.py:551
  236.5 16.0 %collective-permute-start.50 = (bf16[4,120,384]{2,1,0:T(8,128)(2,1)S(1)}, bf16[4,120,384]{2,1,0:T(8,128)(2,1)S(1)}, u32[]{:S(2)}, u32[]{:S(2)}) collective-permute-start(bf16[4,120,384]{2,1,0:T(8,128)(2,1)S(1)} %dynamic-slice_bitcast_fusion.4), channel_id=1, source_target_pairs={{0,4},{4,0},{8,12},{12,8},{16,20},{20,16},{24,28},{28,24},{1,5},{5... | collective-permute-start | bytes 1105928 | tf_op jit(solution)/shard_map/ppermute | solution.py:551
  237.8 14.7 %collective-permute-start.49 = (bf16[4,120,384]{2,1,0:T(8,128)(2,1)S(1)}, bf16[4,120,384]{2,1,0:T(8,128)(2,1)S(1)}, u32[]{:S(2)}, u32[]{:S(2)}) collective-permute-start(bf16[4,120,384]{2,1,0:T(8,128)(2,1)S(1)} %broadcast_select_fusion.3), channel_id=1, source_target_pairs={{0,2},{1,3},{2,0},{3,1},{4,6},{5,7},{6,4},{7,5},{8,10},{9,11},{10,... | collective-permute-start | bytes 1105928 | tf_op jit(solution)/shard_map/ppermute | solution.py:548
  241.3 22.0 %collective-permute-start.52 = (bf16[4,2,88,384]{3,2,0,1:T(8,128)(2,1)S(1)}, bf16[4,2,88,384]{3,2,0,1:T(8,128)(2,1)S(1)}, u32[]{:S(2)}, u32[]{:S(2)}) collective-permute-start(bf16[4,2,88,384]{3,2,0,1:T(8,128)(2,1)S(1)} %get-tuple-element.331), channel_id=1, source_target_pairs={{0,2},{1,3},{2,0},{3,1},{4,6},{5,7},{6,4},{7,5},{8,10},{9,11},{10,... | collective-permute-start | bytes 1622024 | tf_op jit(solution)/shard_map/ppermute | solution.py:548
  242.8 20.5 %collective-permute-start.51 = (bf16[4,88,768]{2,1,0:T(8,128)(2,1)S(1)}, bf16[4,88,768]{2,1,0:T(8,128)(2,1)S(1)}, u32[]{:S(2)}, u32[]{:S(2)}) collective-permute-start(bf16[4,88,768]{2,1,0:T(8,128)(2,1)S(1)} %get-tuple-element.333), channel_id=1, source_target_pairs={{0,4},{4,0},{8,12},{12,8},{16,20},{20,16},{24,28},{28,24},{1,5},{5... | collective-permute-start | bytes 1622024 | tf_op jit(solution)/shard_map/ppermute | solution.py:551
  263.6 18.1 %collective-permute-start.54 = (bf16[4,88,384]{2,1,0:T(8,128)(2,1)S(1)}, bf16[4,88,384]{2,1,0:T(8,128)(2,1)S(1)}, u32[]{:S(2)}, u32[]{:S(2)}) collective-permute-start(bf16[4,88,384]{2,1,0:T(8,128)(2,1)S(1)} %dynamic-slice_bitcast_fusion.9), channel_id=1, source_target_pairs={{0,4},{4,0},{8,12},{12,8},{16,20},{20,16},{24,28},{28,24},{1,5},{5... | collective-permute-start | bytes 811016 | tf_op jit(solution)/shard_map/ppermute | solution.py:551
  264.8 16.8 %collective-permute-start.53 = (bf16[4,88,384]{2,1,0:T(8,128)(2,1)S(1)}, bf16[4,88,384]{2,1,0:T(8,128)(2,1)S(1)}, u32[]{:S(2)}, u32[]{:S(2)}) collective-permute-start(bf16[4,88,384]{2,1,0:T(8,128)(2,1)S(1)} %broadcast_select_fusion.4), channel_id=1, source_target_pairs={{0,2},{1,3},{2,0},{3,1},{4,6},{5,7},{6,4},{7,5},{8,10},{9,11},{10,... | collective-permute-start | bytes 811016 | tf_op jit(solution)/shard_map/ppermute | solution.py:548
  282.0 29.0 %collective-permute-start.69 = (bf16[3,256,768]{2,1,0:T(8,128)(2,1)S(1)}, bf16[3,256,768]{2,1,0:T(8,128)(2,1)S(1)}, u32[]{:S(2)}, u32[]{:S(2)}) collective-permute-start(bf16[3,256,768]{2,1,0:T(8,128)(2,1)S(1)} %get-tuple-element.295.own), channel_id=1, source_target_pairs={{0,1},{1,0},{2,3},{3,2},{4,5},{5,4},{6,7},{7,6},{8,9},{9,8},{10,11... | collective-permute-start | bytes 3538952 | tf_op jit(solution)/shard_map/ppermute | solution.py:542
  282.0 28.9 %collective-permute-start.70 = (bf16[3,256,768]{2,1,0:T(8,128)(2,1)S(1)}, bf16[3,256,768]{2,1,0:T(8,128)(2,1)}, u32[]{:S(2)}, u32[]{:S(2)}) collective-permute-start(bf16[3,256,768]{2,1,0:T(8,128)(2,1)S(1)} %get-tuple-element.295.own), channel_id=1, source_target_pairs={{0,2},{1,3},{2,0},{3,1},{4,6},{5,7},{6,4},{7,5},{8,10},{9,11},{10,... | collective-permute-start | bytes 3538952 | tf_op jit(solution)/shard_map/ppermute | solution.py:548
  317.9 15.4 %collective-permute-start.74 = (f32[16,384]{1,0:T(8,128)}, f32[16,384]{1,0:T(8,128)}, u32[]{:S(2)}, u32[]{:S(2)}) collective-permute-start(f32[16,384]{1,0:T(8,128)} %copy-done.67), channel_id=1, source_target_pairs={{0,1},{1,0},{2,3},{3,2},{4,5},{5,4},{6,7},{7,6},{8,9},{9,8},{10,11... | collective-permute-start | bytes 73736 | tf_op jit(solution)/shard_map/ppermute | solution.py:542
  318.5 14.8 %collective-permute-start.75 = (f32[16,384]{1,0:T(8,128)}, f32[16,384]{1,0:T(8,128)}, u32[]{:S(2)}, u32[]{:S(2)}) collective-permute-start(f32[16,384]{1,0:T(8,128)} %copy-done.23), channel_id=1, source_target_pairs={{0,1},{1,0},{2,3},{3,2},{4,5},{5,4},{6,7},{7,6},{8,9},{9,8},{10,11... | collective-permute-start | bytes 73736 | tf_op jit(solution)/shard_map/ppermute | solution.py:542
  (115 other events, 942.0 us)

commit v3 on v2

--- a/solution.py
+++ b/solution.py
@@ -41,6 +41,9 @@
 TN = (((0,), (0,)), ((), ()))
 
 
+NO_COST = pl.CostEstimate(flops=0, bytes_accessed=0, transcendentals=0)
+
+
 def dot(a, b, dims=NN):
     return lax.dot_general(a, b, dims, preferred_element_type=F32)
 
@@ -84,10 +87,72 @@
     return jnp.where(inside, row * breadth + col, -1)
 
 
+def load_weights(core, mine_ref, other_ref, w_ref, copy_ref, sem, token_ref):
+    copy = pltpu.make_async_copy(w_ref, copy_ref, sem)
+
+    @pl.when(pl.program_id(0) == 0)
+    def _():
+        token_ref[...] = jnp.zeros_like(token_ref)
+
+        def fill(low, high):
+            for b in range(2):
+                rows = slice(b * D, (b + 1) * D)
+                w_ref[b] = low[rows, :]
+                w_ref[2 + b] = high[rows, :]
+
+        @pl.when(core == 0)
+        def _():
+            fill(mine_ref, other_ref)
+
+        @pl.when(core != 0)
+        def _():
+            fill(other_ref, mine_ref)
+
+        copy.start()
+
+    @pl.when(pl.program_id(0) == pl.num_programs(0) - 1)
+    def _():
+        copy.wait()
+
+
 def attention_forward_kernel(
-    scal, crop, x_ref, table_ref, w_ref, vec_ref,
-    emb_ref, n1_ref, q_ref, k_ref, v_ref, p_ref, mixed_ref, after_ref, n2_ref,
+    scal, crop, x_ref, mine_ref, other_ref,
+    emb_ref, n1_ref, q_ref, k_ref, v_ref, p_ref, mixed_ref, after_ref, n2_ref, wcopy_ref, vec_ref, token_ref,
+    w_ref, table_ref, sem,
 ):
+    load_weights(scal[1], mine_ref, other_ref, w_ref, wcopy_ref, sem, token_ref)
+    part = CELLS // (2 * OWNERS)
+
+    @pl.when(pl.program_id(0) == 0)
+    def _():
+        for at, ref in ((scal[1], mine_ref), (1 - scal[1], other_ref)):
+            for dp in range(OWNERS):
+                row = pl.ds(pl.multiple_of((2 * dp + at) * part, part), part)
+                table_ref[row, :] = ref[2 * D + dp * part : 2 * D + (dp + 1) * part, :]
+        vec_ref[...] = jnp.zeros_like(vec_ref)
+        wide, thin = D // OWNERS, D // (4 * OWNERS)
+        first = 2 * D + CELLS // 2
+
+        def unpack(ref, core):
+            for dp in range(OWNERS):
+                rows = slice(first + dp * part, first + dp * part + 6)
+                if core == 0:
+                    vec_ref[0:6, dp * wide : (dp + 1) * wide] = ref[rows, 0:wide].astype(F32)
+                for x in range(2):
+                    lane = x * (D // 2) + 128
+                    at = (2 * x + core) * (D // 4) + dp * thin
+                    vec_ref[8:14, at : at + thin] = ref[rows, lane : lane + thin].astype(F32)
+
+        @pl.when(scal[1] == 0)
+        def _():
+            unpack(mine_ref, 0)
+            unpack(other_ref, 1)
+
+        @pl.when(scal[1] != 0)
+        def _():
+            unpack(other_ref, 0)
+            unpack(mine_ref, 1)
+
     grid = scal[0] + pl.program_id(0)
     height, breadth, top, left = crop[grid, 0], crop[grid, 1], crop[grid, 2], crop[grid, 3]
     target = crop_target(
@@ -130,8 +195,12 @@
     n2_ref[...] = (u2 * vec_ref[3:4, :] + vec_ref[4:5, :]).astype(BF)
 
 
-def up_kernel(scal, n2_ref, w_ref, vec_ref, g_ref, hidden_ref, gp_ref, mine_ref, other_ref, gt_ref):
+def up_kernel(
+    scal, n2_ref, low_ref, high_ref, vec_ref, g_ref,
+    hidden_ref, gp_ref, mine_ref, other_ref, wcopy_ref, token_ref, gt_ref, w_ref, sem,
+):
     j = pl.program_id(0)
+    load_weights(scal[1], low_ref, high_ref, w_ref, wcopy_ref, sem, token_ref)
     grids = g_ref.shape[0]
 
     @pl.when(j == 0)
@@ -142,7 +211,7 @@
     bias = vec_ref[pl.ds(10 + j, 1), :]
     for n in range(grids):
         rows = slice(n * CELLS, (n + 1) * CELLS)
-        pre = dot(n2_ref[rows, :], w_ref[0]) + bias
+        pre = dot(n2_ref[rows, :], w_ref[j]) + bias
         phi = 0.5 + 0.5 * lax.erf(pre * (0.5**0.5))
         density = jnp.exp2(pre * pre * (-0.5 * LOG2E)) * INV_SQRT_2PI
         hidden_ref[0, rows, :] = (pre * phi).astype(BF)
@@ -166,7 +235,10 @@
         other_ref[:, rows, :] = parts[:, 0]
 
 
-def down_kernel(hidden_ref, down_ref, after_ref, vec_ref, out_ref):
+def down_kernel(
+    scal, hidden_ref, low_ref, high_ref, after_ref, vec_ref, out_ref, wcopy_ref, token_ref, down_ref, sem
+):
+    load_weights(scal[1], low_ref, high_ref, down_ref, wcopy_ref, sem, token_ref)
     total = dot(hidden_ref[0], down_ref[0], NT)
     for j in range(1, 4):
         total = total + dot(hidden_ref[j], down_ref[j], NT)
@@ -175,7 +247,7 @@
 
 def mlp_kernel(
     scal, gp_ref, down_ref, up_ref, n2_ref, g_ref, after_any, vec_ref, mixed_any,
-    ga_ref, galow_ref, mine_ref, other_ref, gb_ref, gn_ref,
+    ga_ref, galow_ref, mine_ref, other_ref, gb_ref, gn_ref, token_ref,
     dn2_acc, n2t_ref, gpre_ref, after_ref, mixed_ref, sem,
 ):
     j = pl.program_id(0)
@@ -195,6 +267,7 @@
             n2t_ref[:, rows] = n2_ref[rows, :].T
         gb_ref[...] = jnp.zeros_like(gb_ref)
         gn_ref[...] = jnp.zeros_like(gn_ref)
+        token_ref[...] = jnp.zeros_like(token_ref)
 
     @pl.when(j < 4)
     def _():
@@ -243,7 +316,7 @@
 def attention_backward_kernel(
     scal, crop, ga_ref, galow_ref, mixed_ref, p_ref, q_ref, k_ref, v_ref, emb_ref, n1_ref,
     w_ref, vec_ref, gn_ref, gb_ref,
-    ig_ref, table_out, gs_out, mine_ref, other_ref,
+    ig_ref, table_out, gs_out, mine_ref, other_ref, token_ref,
     dm_ref, dq_all, dk_all, dv_all, n1t_ref, table_ref, gs_ref,
 ):
     i = pl.program_id(0)
@@ -254,6 +327,7 @@
     def _():
         table_ref[...] = jnp.zeros_like(table_ref)
         gs_ref[...] = jnp.zeros_like(gs_ref)
+        token_ref[...] = jnp.zeros_like(token_ref)
 
     @pl.when(i < grids)
     def _():
@@ -343,6 +417,20 @@
     return jax.ShapeDtypeStruct(shape, dtype)
 
 
+TOKEN = sds((8, 128), F32)
+
+
+def in_hbm(shape):
+    return pltpu.HBM(shape.shape, shape.dtype)
+
+
+def behind(value, token):
+    return lax.optimization_barrier((value, token))
+
+
+ANY = pl.BlockSpec(memory_space=pl.ANY)
+
+
 def half_shape(blocks, extra=0):
     return sds((OWNERS, blocks * HALF + extra, D), BF)
 
@@ -353,7 +441,7 @@
     return pl.BlockSpec(shape, lambda i, *_: zeros, pipeline_mode=mode)
 
 
-def attention_forward(scal, crop, x, table, w, vec, grids):
+def attention_forward(scal, crop, x, mine, other, grids, deps=()):
     tokens = grids * CELLS
     rows = pl.BlockSpec((CELLS, D), lambda i, *_: (i, 0))
     spec = pltpu.PrefetchScalarGridSpec(
@@ -361,34 +449,36 @@
         grid=(grids,),
         in_specs=[
             pl.BlockSpec((1, CELLS, D), lambda i, s, c: (s[0] + i, 0, 0)),
-            whole_block((CELLS, D)),
-            whole_block((4, D, D), 1),
-            whole_block((16, D)),
-        ],
+            whole_block(mine.shape, 1),
+            whole_block(mine.shape, 1),
+        ] + [ANY] * len(deps),
         out_specs=[
             rows, rows, rows, rows, rows,
             pl.BlockSpec((1, HEADS, CELLS, CELLS), lambda i, *_: (i, 0, 0, 0)),
             rows, rows, rows,
+            pl.BlockSpec(memory_space=pl.ANY),
+            whole_block((16, D)),
+            whole_block((8, 128)),
         ],
-    )
-    low, full = sds((tokens, D), BF), sds((tokens, D), F32)
+        scratch_shapes=[
+            pltpu.VMEM((4, D, D), BF), pltpu.VMEM((CELLS, D), BF), pltpu.SemaphoreType.DMA,
+        ],
+    )
+    low, full = pltpu.HBM((tokens, D), BF), pltpu.HBM((tokens, D), F32)
     return pl.pallas_call(
-        attention_forward_kernel,
+        ignoring(attention_forward_kernel, 5, len(deps)),
         grid_spec=spec,
         out_shape=[
-            full, low, low, low, low, sds((grids, HEADS, CELLS, CELLS), BF), low, full, low,
+            full, low, low, low, low, pltpu.HBM((grids, HEADS, CELLS, CELLS), BF), low, full,
+            sds((tokens, D), BF), pltpu.HBM((4, D, D), BF), sds((16, D), F32), TOKEN,
         ],
-        compiler_params=params(32 * MIB),
-        cost_estimate=pl.CostEstimate(
-            flops=8 * tokens * D * D + 64 * tokens * CELLS * 256,
-            bytes_accessed=24 * tokens * D,
-            transcendentals=tokens * CELLS * HEADS,
-        ),
+        compiler_params=params(40 * MIB),
+        cost_estimate=NO_COST,
         name="attention_forward",
-    )(scal, crop, x, table, w, vec)
-
-
-def up_forward(scal, n2, w, vec, cotangent, grids):
+    )(scal, crop, x, mine, other, *deps)
+
+
+def up_forward(scal, n2, mine, other, vec, cotangent, grids, deps=()):
     tokens = grids * CELLS
     block = pl.BlockSpec((1, tokens, D), lambda j, *_: (j, 0, 0))
     half = pl.BlockSpec((OWNERS, HALF, D), lambda j, *_: (0, j, 0))
@@ -397,49 +487,59 @@
         grid=(4,),
         in_specs=[
             whole_block((tokens, D), 1),
-            pl.BlockSpec((1, D, D), lambda j, *_: (j, 0, 0)),
+            whole_block((2 * D, D), 1),
+            whole_block((2 * D, D), 1),
             whole_block((16, D)),
             pl.BlockSpec((grids, CELLS, D), lambda j, s: (s[2], 0, 0), pipeline_mode=pl.Buffered(1)),
+        ] + [ANY] * len(deps),
+        out_specs=[block, block, half, half, pl.BlockSpec(memory_space=pl.ANY), whole_block((8, 128))],
+        scratch_shapes=[
+            pltpu.VMEM((D, tokens), BF), pltpu.VMEM((4, D, D), BF), pltpu.SemaphoreType.DMA,
         ],
-        out_specs=[block, block, half, half],
-        scratch_shapes=[pltpu.VMEM((D, tokens), BF)],
     )
     return pl.pallas_call(
-        up_kernel,
+        ignoring(up_kernel, 6, len(deps)),
         grid_spec=spec,
         out_shape=[
-            sds((4, tokens, D), BF), sds((4, tokens, D), BF), half_shape(4), half_shape(4),
+            sds((4, tokens, D), BF), pltpu.HBM((4, tokens, D), BF), half_shape(4), in_hbm(half_shape(4)),
+            pltpu.HBM((4, D, D), BF), TOKEN,
         ],
-        compiler_params=params(32 * MIB),
-        cost_estimate=pl.CostEstimate(
-            flops=16 * tokens * D * D, bytes_accessed=40 * tokens * D, transcendentals=8 * tokens * D
-        ),
+        compiler_params=params(40 * MIB * tokens // 768),
+        cost_estimate=NO_COST,
         name="up_forward",
-    )(scal, n2, w, vec, cotangent)
-
-
-def down_forward(hidden, down, after, vec, grids):
+    )(scal, n2, mine, other, vec, cotangent, *deps)
+
+
+def down_forward(scal, hidden, mine, other, after, vec, grids, deps=()):
     tokens = grids * CELLS
-    return pl.pallas_call(
-        down_kernel,
+    spec = pltpu.PrefetchScalarGridSpec(
+        num_scalar_prefetch=1,
         grid=(grids,),
         in_specs=[
-            pl.BlockSpec((4, CELLS, D), lambda i: (0, i, 0)),
-            whole_block((4, D, D), 1),
-            pl.BlockSpec((CELLS, D), lambda i: (i, 0)),
+            pl.BlockSpec((4, CELLS, D), lambda i, *_: (0, i, 0)),
+            whole_block((2 * D, D), 1),
+            whole_block((2 * D, D), 1),
+            pl.BlockSpec((CELLS, D), lambda i, *_: (i, 0)),
             whole_block((16, D)),
+        ] + [ANY] * len(deps),
+        out_specs=[
+            pl.BlockSpec((1, CELLS, D), lambda i, *_: (i, 0, 0)),
+            pl.BlockSpec(memory_space=pl.ANY),
+            whole_block((8, 128)),
         ],
-        out_specs=pl.BlockSpec((1, CELLS, D), lambda i: (i, 0, 0)),
-        out_shape=sds((grids, CELLS, D), BF),
+        scratch_shapes=[pltpu.VMEM((4, D, D), BF), pltpu.SemaphoreType.DMA],
+    )
+    return pl.pallas_call(
+        ignoring(down_kernel, 6, len(deps)),
+        grid_spec=spec,
+        out_shape=[pltpu.HBM((grids, CELLS, D), BF), pltpu.HBM((4, D, D), BF), TOKEN],
         compiler_params=params(24 * MIB),
-        cost_estimate=pl.CostEstimate(
-            flops=8 * tokens * D * D, bytes_accessed=20 * tokens * D, transcendentals=0
-        ),
+        cost_estimate=NO_COST,
         name="down_forward",
-    )(hidden, down, after, vec)
-
-
-def mlp_backward(scal, gp, down, up, n2, cotangent, after, vec, mixed, grids):
+    )(scal, hidden, mine, other, after, vec, *deps)
+
+
+def mlp_backward(scal, gp, down, up, n2, cotangent, after, vec, mixed, grids, deps=()):
     tokens = grids * CELLS
     last = lambda j: jnp.minimum(j, 3)
     block = pl.BlockSpec((1, tokens, D), lambda j, *_: (last(j), 0, 0))
@@ -454,8 +554,8 @@
             block, weight, weight, whole_block((tokens, D), 1),
             pl.BlockSpec((grids, CELLS, D), lambda j, s: (s[2], 0, 0), pipeline_mode=pl.Buffered(1)),
             any_spec, whole_block((16, D)), any_spec,
-        ],
-        out_specs=[rows, rows, half, half, whole_block((8, D)), whole_block((8, D))],
+        ] + [ANY] * len(deps),
+        out_specs=[rows, rows, half, half, whole_block((8, D)), whole_block((8, D)), whole_block((8, 128))],
         scratch_shapes=[
             pltpu.VMEM((tokens, D), F32), pltpu.VMEM((D, tokens), BF), pltpu.VMEM((tokens, D), BF),
             pltpu.VMEM((tokens, D), F32), pltpu.VMEM((tokens, D), BF),
@@ -463,21 +563,19 @@
         ],
     )
     return pl.pallas_call(
-        mlp_kernel,
+        ignoring(mlp_kernel, 9, len(deps)),
         grid_spec=spec,
         out_shape=[
             sds((tokens, D), F32), sds((tokens, D), BF),
-            half_shape(5), half_shape(5), sds((8, D), F32), sds((8, D), F32),
+            half_shape(5), in_hbm(half_shape(5)), sds((8, D), F32), sds((8, D), F32), TOKEN,
         ],
         compiler_params=params(40 * MIB * tokens // 768),
-        cost_estimate=pl.CostEstimate(
-            flops=26 * tokens * D * D, bytes_accessed=36 * tokens * D, transcendentals=0
-        ),
+        cost_estimate=NO_COST,
         name="mlp_backward",
-    )(scal, gp, down, up, n2, cotangent, after, vec, mixed)
-
-
-def attention_backward(scal, crop, ga, galow, mixed, p, q, k, v, emb, n1, w, vec, gn, gb, grids):
+    )(scal, gp, down, up, n2, cotangent, after, vec, mixed, *deps)
+
+
+def attention_backward(scal, crop, ga, galow, mixed, p, q, k, v, emb, n1, w, vec, gn, gb, grids, deps=()):
     tokens = grids * CELLS
     last = lambda i: jnp.minimum(i, grids - 1)
     rows = pl.BlockSpec((CELLS, D), lambda i, *_: (last(i), 0))
@@ -492,29 +590,28 @@
             rows, rows, rows, rows, rows,
             whole_block((4, D, D), 1),
             whole_block((16, D)), few, few,
-        ],
+        ] + [ANY] * len(deps),
         out_specs=[
             pl.BlockSpec((1, CELLS, D), lambda i, *_: (last(i), 0, 0)),
             whole_block((CELLS, D)),
             few,
             whole_block(half.shape, 1), whole_block(half.shape, 1),
+            whole_block((8, 128)),
         ],
         scratch_shapes=[pltpu.VMEM((CELLS, D), BF)]
         + [pltpu.VMEM((tokens, D), BF)] * 3
         + [pltpu.VMEM((D, tokens), BF), pltpu.VMEM((CELLS, D), F32), pltpu.VMEM((8, D), F32)],
     )
     return pl.pallas_call(
-        attention_backward_kernel,
+        ignoring(attention_backward_kernel, 15, len(deps)),
         grid_spec=spec,
-        out_shape=[sds((grids, CELLS, D), BF), sds((CELLS, D), F32), sds((8, D), F32), half, half],
+        out_shape=[
+            pltpu.HBM((grids, CELLS, D), BF), sds((CELLS, D), F32), sds((8, D), F32), half, in_hbm(half), TOKEN,
+        ],
         compiler_params=params(40 * MIB),
-        cost_estimate=pl.CostEstimate(
-            flops=14 * tokens * D * D + 128 * tokens * CELLS * 256,
-            bytes_accessed=32 * tokens * D,
-            transcendentals=0,
-        ),
+        cost_estimate=NO_COST,
         name="attention_backward",
-    )(scal, crop, ga, galow, mixed, p, q, k, v, emb, n1, w, vec, gn, gb)
+    )(scal, crop, ga, galow, mixed, p, q, k, v, emb, n1, w, vec, gn, gb, *deps)
 
 
 class Place:
@@ -554,154 +651,277 @@
         return lax.ppermute(v, "dp", self.z_shift[shift])
 
 
-def after_op(value, *earlier):
-    return lax.optimization_barrier((value,) + earlier)[0]
-
-
-def together(*values):
-    leaves, tree = jax.tree.flatten(values)
-    return jax.tree.unflatten(tree, lax.optimization_barrier(leaves))
-
-
-def assemble_kernel(rows, extra, where_ref, *refs):
-    pieces, outs = refs[:10], refs[10:]
-    z, y, x, c = where_ref[0], where_ref[1], where_ref[2], where_ref[3]
-    depth = pieces[0].shape[1]
-    for core_rel in range(2):
-        own, by_x, by_y, diag0, diag1 = pieces[core_rel * 5 : core_rel * 5 + 5]
-        core = c if core_rel == 0 else 1 - c
-        for s in range(depth):
-            zs = lax.rem(z - s + depth, depth)
-            for xr in range(2):
-                for yr in range(2):
-                    xs = x if xr == 0 else 1 - x
-                    ys = y if yr == 0 else 1 - y
-                    dp = zs * 2 + ys
-                    row = pl.ds(pl.multiple_of(dp * rows, rows), rows)
-                    lane = pl.ds(pl.multiple_of(xs * (D // 2), D // 2), D // 2)
+def ignoring(kernel, at, count):
+    return lambda *refs: kernel(*refs[:at], *refs[at + count :])
+
+
+def assemble_kernel(rows, extra, depth, views, where, *refs):
+    count = 1 + max(at for at, _ in views)
+    out, token = refs[count:]
+    token[...] = jnp.zeros_like(token)
+    z, y, x = where[0], where[1], where[2]
+    unit = rows + extra
+    held = [(refs[at], row) for at, row in views]
+    for s in range(depth):
+        zs = lax.rem(z - s + depth, depth)
+        for xr in range(2):
+            for yr in range(2):
+                xs = x if xr == 0 else 1 - x
+                ys = y if yr == 0 else 1 - y
+                dp = zs * 2 + ys
+                lane = pl.ds(pl.multiple_of(xs * (D // 2), D // 2), D // 2)
+                for b in range(2):
                     if xr and yr:
-                        first, second = diag0[s], diag1[s]
+                        ref, first = held[3 + b]
+                        first += s * unit
                     else:
-                        src = (own, by_x, by_y)[xr + 2 * yr]
-                        first, second = src[0, s], src[1, s]
-                    outs[0][core * 2, row, lane] = first[:rows]
-                    outs[0][core * 2 + 1, row, lane] = second[:rows]
+                        ref, first = held[xr + 2 * yr]
+                        first += (b * depth + s) * unit
+                    row = pl.ds(pl.multiple_of(b * D + dp * rows, rows), rows)
+                    out[row, lane] = ref[first : first + rows, :]
                     if extra:
-                        share = pl.ds(pl.multiple_of((dp * 2 + core) * extra, extra), extra)
-                        outs[1][share, lane] = first[rows:]
-                        outs[2][dp, xs, core] = second[rows:]
-
-
-def assemble(where, pieces, extra, dp_size):
-    rows = D // dp_size
-    outs = [sds((4, D, D), BF)]
-    if extra:
-        outs += [sds((dp_size * 2 * extra, D), BF), sds((dp_size, 2, 2, extra, D // 2), BF)]
+                        at = 2 * D + b * depth * 2 * extra + dp * extra
+                        row = pl.ds(pl.multiple_of(at, extra), extra)
+                        out[row, lane] = ref[first + rows : first + unit, :]
+
+
+def assemble(where, views, pieces, extra, dp_size, deps=()):
+    kernel = functools.partial(assemble_kernel, D // dp_size, extra, dp_size // 2, views)
+    shape = sds((2 * D + 2 * dp_size * extra, D), BF)
+    return call(kernel, "assemble", where, pieces, [shape], deps)
+
+
+def gather_z(place, u):
+    return [u] + [place.over_z(u, s) for s in range(1, place.z_size)]
+
+
+def call(kernel, name, where, ins, shapes, deps=(), limit=16):
     vmem = pl.BlockSpec(memory_space=pltpu.VMEM)
     return pl.pallas_call(
-        functools.partial(assemble_kernel, rows, extra),
-        in_specs=[pl.BlockSpec(memory_space=pltpu.SMEM)] + [vmem] * 10,
-        out_specs=[vmem] * len(outs),
-        out_shape=outs,
-        compiler_params=params(16 * MIB),
-        cost_estimate=pl.CostEstimate(flops=0, bytes_accessed=16 * D * D, transcendentals=0),
-        name="assemble",
-    )(where, *pieces)
-
-
-def gather_z(place, u):
-    return [u] + [place.over_z(u, s) for s in range(1, place.z_size)]
-
-
-def gather_xy(place, parts):
-    own = jnp.stack(parts, axis=1)
-    return own, place.over_x(own), place.over_y(own)
-
-
-def gather_diagonal(place, by_x, by_y):
-    return place.over_y(by_x[0]), place.over_x(by_y[1])
-
-
-def join(a, b):
-    return (a.astype(F32) + b.astype(F32)).astype(BF)
-
-
-class Reduction:
-    def __init__(self, place):
-        self.place = place
-
-    def over_core(self, mine, other):
-        zs = self.place.z_size
-        got = self.place.core(other)
-        h = join(mine, got)
-        return h.reshape(zs, 2, h.shape[1], D)
-
-    def pick_y(self, v, at):
-        return lax.dynamic_index_in_dim(v, at, axis=v.ndim - 3, keepdims=False)
-
-    def pick_x(self, v, at):
-        return jnp.where(at == 0, v[..., : D // 2], v[..., D // 2 :])
-
-    def send_y(self, v):
-        y = self.place.y
-        sent = self.pick_y(v, 1 - y)
-        return self.pick_y(v, y), self.place.over_y(sent), sent
-
-    def send_x(self, v):
-        x = self.place.x
-        sent = self.pick_x(v, 1 - x)
-        return self.pick_x(v, x), self.place.over_x(sent), sent
-
-    def send_z(self, v):
-        zs, z = self.place.z_size, self.place.z
-        parts = [lax.dynamic_index_in_dim(v, (z + s) % zs, axis=0, keepdims=False) for s in range(zs)]
-        return parts[0], [self.place.over_z(parts[s], s) for s in range(1, zs)], parts
-
-    def sum_z(self, kept, got):
-        total = kept.astype(F32)
-        for v in got:
-            total = total + v.astype(F32)
-        return total
-
-
-def collect_kernel(where_ref, own, by_core, by_x, by_both, out, sem):
-    x, c = where_ref[2], where_ref[3]
-    grids = own.shape[0]
-    copies = []
-    for n, (piece, mp) in enumerate(
-        ((own, 2 * x + c), (by_core, 2 * x + 1 - c), (by_x, 2 - 2 * x + c), (by_both, 3 - 2 * x - c))
-    ):
-        copies.append(pltpu.make_async_copy(piece, out.at[pl.ds(mp * grids, grids)], sem.at[n]))
-    for copy in copies:
-        copy.start()
-    for copy in copies:
-        copy.wait()
-
-
-def start_grids(place, own):
-    return own, place.core(own), place.over_x(own)
-
-
-def finish_grids(place, where, pieces):
-    own, by_core, by_x = pieces
-    by_both = place.core(by_x)
-    hbm = pl.BlockSpec(memory_space=pl.ANY)
-    return pl.pallas_call(
-        collect_kernel,
-        in_specs=[pl.BlockSpec(memory_space=pltpu.SMEM)] + [hbm] * 4,
-        out_specs=pl.BlockSpec(memory_space=pltpu.VMEM),
-        out_shape=sds((4 * own.shape[0],) + own.shape[1:], own.dtype),
-        scratch_shapes=[pltpu.SemaphoreType.DMA((4,))],
-        compiler_params=params(12 * MIB),
-        cost_estimate=pl.CostEstimate(flops=0, bytes_accessed=8 * own.size, transcendentals=0),
-        name="collect",
-    )(where, own, by_core, by_x, by_both)
-
-
-def sum_plane(place, value):
-    value = value + place.core(value)
-    value = (value + place.over_x(value)) + (place.over_y(value) + place.over_corner(value))
-    return [value] + [place.over_z(value, s) for s in range(1, place.z_size)]
+        ignoring(kernel, 1 + len(ins), len(deps)),
+        in_specs=[pl.BlockSpec(memory_space=pltpu.SMEM)] + [vmem] * len(ins) + [ANY] * len(deps),
+        out_specs=[vmem] * (len(shapes) + 1),
+        out_shape=[*shapes, TOKEN],
+        compiler_params=params(limit * MIB),
+        cost_estimate=NO_COST,
+        name=name,
+    )(where, *ins, *deps)
+
+
+def pack_kernel(count, has_next, unit_at, where, *refs):
+    parts, refs = refs[:count], refs[count:]
+    half, lows = 0, None
+    if has_next:
+        by_x, by_y, refs = refs[0], refs[1], refs[2:]
+        half = has_next
+    token = refs[-1]
+    token[...] = jnp.zeros_like(token)
+    outs = refs[:-1]
+    if unit_at:
+        units, outs = outs[0], outs[1:]
+        outs[-1][...] = units[unit_at]
+        outs = outs[:-1]
+    if half:
+        first_x, first_y = half[0], half[1]
+        size = half[2]
+        outs[-2][:size, :] = by_x[first_x : first_x + size, :]
+        outs[-1][:size, :] = by_y[first_y : first_y + size, :]
+    if count:
+        unit = parts[0].shape[1]
+        for b in range(2):
+            for s in range(count):
+                value = parts[s][b]
+                at = (b * count + s) * unit
+                outs[0][at : at + unit, :] = value
+                if half:
+                    outs[-2][size + at : size + at + unit, :] = value
+                    outs[-1][size + at : size + at + unit, :] = value
+
+
+def pack(where, parts, by_x, by_y, half, units=None, unit_at=0, deps=()):
+    count = len(parts)
+    shapes = []
+    rows = 2 * count * parts[0].shape[1] if count else 0
+    if count:
+        shapes.append(sds((rows, D // 2), BF))
+    ins = list(parts)
+    if half:
+        ins += [by_x, by_y]
+        shapes += [sds((half[2] + rows, D // 2), BF)] * 2
+    if unit_at:
+        ins.append(units)
+        shapes.append(sds(units.shape[1:], BF))
+    kernel = functools.partial(pack_kernel, count, half, unit_at)
+    return call(kernel, "pack", where, ins, shapes, deps)
+
+
+def add(a, b):
+    return a.astype(F32) + b.astype(F32)
+
+
+def dp_of(z, y):
+    return z * 2 + y
+
+
+def split_y(y, value_at, depth, send, keep):
+    for z in range(depth):
+        send[z] = value_at(dp_of(z, 1 - y)).astype(BF)
+        keep[z] = value_at(dp_of(z, y)).astype(BF)
+
+
+def split_x(x, value, send, keep):
+    side = D // 2
+    left, right = value[:, :side].astype(BF), value[:, side:].astype(BF)
+
+    @pl.when(x == 0)
+    def _():
+        send[...] = right
+        keep[...] = left
+
+    @pl.when(x != 0)
+    def _():
+        send[...] = left
+        keep[...] = right
+
+
+def first_y_kernel(where, mine, got, send, keep, token):
+    token[...] = jnp.zeros_like(token)
+    split_y(where[1], lambda dp: add(mine[dp], got[dp]), OWNERS // 2, send, keep)
+
+
+def first_y(where, mine, got, deps=()):
+    rows = mine.shape[1]
+    shape = sds((OWNERS // 2, rows, D), BF)
+    return call(first_y_kernel, "first_y", where, [mine, got], [shape, shape], deps)
+
+
+def first_both_kernel(cut, where, mine, got, send_y, keep_y, send_x, keep_x, token):
+    token[...] = jnp.zeros_like(token)
+    depth = OWNERS // 2
+    split_y(where[1], lambda dp: add(mine[dp, :cut], got[dp, :cut]), depth, send_y, keep_y)
+    for dp in range(OWNERS):
+        split_x(where[2], add(mine[dp, cut:], got[dp, cut:]), send_x.at[dp], keep_x.at[dp])
+
+
+def first_both(where, mine, got, deps=()):
+    rows = mine.shape[1]
+    cut = (2 * rows // 3) // 16 * 16
+    over_y = sds((OWNERS // 2, cut, D), BF)
+    over_x = sds((OWNERS, rows - cut, D // 2), BF)
+    kernel = functools.partial(first_both_kernel, cut)
+    return call(kernel, "first_both", where, [mine, got], [over_y, over_y, over_x, over_x], deps)
+
+
+def first_x_kernel(where, mine, got, send, keep, token):
+    token[...] = jnp.zeros_like(token)
+    for dp in range(OWNERS):
+        split_x(where[2], add(mine[dp], got[dp]), send.at[dp], keep.at[dp])
+
+
+def first_x(where, mine, got, deps=()):
+    shape = sds((OWNERS, mine.shape[1], D // 2), BF)
+    return call(first_x_kernel, "first_x", where, [mine, got], [shape, shape], deps)
+
+
+def second_y_kernel(where, mine, got, send, keep, token):
+    token[...] = jnp.zeros_like(token)
+    split_y(where[1], lambda dp: add(mine[dp], got[dp]), OWNERS // 2, send, keep)
+
+
+def second_y(where, mine, got, deps=()):
+    shape = sds((OWNERS // 2,) + mine.shape[1:], BF)
+    return call(second_y_kernel, "second_y", where, [mine, got], [shape, shape], deps)
+
+
+def second_both_kernel(where, keep_y, got_y, keep_x, got_x, send_a, left_a, send_b, left_b, token):
+    token[...] = jnp.zeros_like(token)
+    depth = OWNERS // 2
+    for z in range(depth):
+        split_x(where[2], add(keep_y[z], got_y[z]), send_a.at[z], left_a.at[z])
+    split_y(where[1], lambda dp: add(keep_x[dp], got_x[dp]), depth, send_b, left_b)
+
+
+def second_both(where, keep_y, got_y, keep_x, got_x, deps=()):
+    over_x = sds((OWNERS // 2, keep_y.shape[1], D // 2), BF)
+    over_y = sds((OWNERS // 2, keep_x.shape[1], D // 2), BF)
+    ins = [keep_y, got_y, keep_x, got_x]
+    return call(second_both_kernel, "second_both", where, ins, [over_x, over_x, over_y, over_y], deps)
+
+
+def split_z_kernel(pairs, where, *refs):
+    ins, outs = refs[: 2 * pairs], refs[2 * pairs : -1]
+    refs[-1][...] = jnp.zeros_like(refs[-1])
+    depth = ins[0].shape[0]
+    for s in range(depth):
+        z = lax.rem(where[0] + s, depth)
+        row = 0
+        for i in range(pairs):
+            value = add(ins[2 * i][z], ins[2 * i + 1][z]).astype(BF)
+            outs[s][row : row + value.shape[0], :] = value
+            row += value.shape[0]
+
+
+def split_z(where, *ins, deps=()):
+    depth, width = ins[0].shape[0], ins[0].shape[2]
+    rows = sum(v.shape[1] for v in ins[::2])
+    kernel = functools.partial(split_z_kernel, len(ins) // 2)
+    return call(kernel, "split_z", where, list(ins), [sds((rows, width), BF)] * depth, deps)
+
+
+def z_to_x_kernel(where, keep, *refs):
+    got, (send, left, token) = refs[:-3], refs[-3:]
+    token[...] = jnp.zeros_like(token)
+    total = keep[...].astype(F32)
+    for ref in got:
+        total = total + ref[...].astype(F32)
+    split_x(where[2], total, send, left)
+
+
+def z_to_x(where, keep, got, deps=()):
+    shape = sds((keep.shape[0], D // 2), BF)
+    return call(z_to_x_kernel, "z_to_x", where, [keep, *got], [shape, shape], deps)
+
+
+def pair_kernel(where, own, by_x, out, token):
+    token[...] = jnp.zeros_like(token)
+    out[0] = own[...]
+    out[1] = by_x[...]
+
+
+def collect_kernel(where, here, there, out, token):
+    token[...] = jnp.zeros_like(token)
+    x, c = where[2], where[3]
+    grids = here.shape[1]
+    for piece, core in ((here, c), (there, 1 - c)):
+        for half in range(2):
+            mp = 2 * (x if half == 0 else 1 - x) + core
+            for n in range(grids):
+                out[mp * grids + n] = piece[half, n]
+
+
+def pair_grids(where, own, by_x, deps=()):
+    return call(pair_kernel, "pair", where, [own, by_x], [sds((2,) + own.shape, own.dtype)], deps)
+
+
+def finish_grids(place, where, here):
+    shape = sds((here.shape[0] * 2 * here.shape[1],) + here.shape[2:], here.dtype)
+    return call(collect_kernel, "collect", where, [here, place.core(here)], [shape])
+
+
+def plane_kernel(where, own, by_x, by_y, by_corner, out, token):
+    token[...] = jnp.zeros_like(token)
+    out[0:16, :] = own[0:16, :]
+    out[16:32, :] = by_x[0:16, :]
+    here = own[16:24, :] + by_x[16:24, :]
+    out[32:40, :] = here + (by_y[...] + by_corner[...])
+
+
+def sum_plane(place, where, packed, square):
+    ins = [packed, place.over_x(packed), place.over_y(square), place.over_corner(square)]
+    here, _ = call(plane_kernel, "plane", where, ins, [sds((40, D // 2), F32)])
+    there = place.core(here)
+    value = here[32:40, :128] + there[32:40, :128]
+    return here, there, [value] + [place.over_z(value, s) for s in range(1, place.z_size)]
 
 
 ROWS1, ROWS2, ROWS3 = 4 * HALF, 5 * HALF, 3 * HALF
@@ -711,7 +931,8 @@
 def totals_kernel(where, *refs):
     keep1, got1, keep2, *got2 = refs[:6]
     keep3, *got3 = refs[6:10]
-    kept_ref, sent_ref, tail_ref, square_ref = refs[10:]
+    kept_ref, sent_ref, tail_ref, packed_ref, square_ref, token = refs[10:]
+    token[...] = jnp.zeros_like(token)
     x, c = where[2], where[3]
 
     def total(first, others):
@@ -750,29 +971,22 @@
     small = jnp.where(line < 8, jnp.where(lane < D // OWNERS, codes * owner, 0.0), 0.0)
     small = jnp.where((line >= 8) & (lane < D // (4 * OWNERS)), codes, small)
     square = square + jnp.sum(tail[:16] * tail[:16] + small * small, axis=0, keepdims=True)
-    square_ref[...] = jnp.full((8, 128), jnp.sum(square), F32)
-
-
-def totals(where, keep1, got1, keep2, got2, keep3, got3):
-    vmem = pl.BlockSpec(memory_space=pltpu.VMEM)
+    square_ref[...] = jnp.full((8, D // 2), jnp.sum(square), F32)
+    packed_ref[0:16, :] = tail[:16]
+    packed_ref[16:24, :] = square_ref[...]
+
+
+def totals(where, keep1, got1, keep2, got2, keep3, got3, deps=()):
     ins = [keep1, got1, keep2, *got2, keep3, *got3]
-    return pl.pallas_call(
-        totals_kernel,
-        in_specs=[pl.BlockSpec(memory_space=pltpu.SMEM)] + [vmem] * len(ins),
-        out_specs=[vmem] * 4,
-        out_shape=[
-            sds((ROWS, D // 4), F32), sds((ROWS, D // 4), F32), sds((SMALL, D // 2), F32),
-            sds((8, 128), F32),
-        ],
-        compiler_params=params(16 * MIB),
-        name="totals",
-    )(where, *ins)
+    half = sds((ROWS, D // 4), F32)
+    shapes = [half, half] + [sds((rows, D // 2), F32) for rows in (SMALL, 24, 8)]
+    return call(totals_kernel, "totals", where, ins, shapes, deps)
 
 
 def update_kernel(where, *refs):
-    kept, got, tail, t_core, t_x, t_both = refs[:6]
-    squares = refs[6:10]
-    state, outs = refs[10:25], refs[25:]
+    kept, got, tail, plane, other_plane = refs[:5]
+    squares = refs[5:9]
+    state, outs = refs[9:24], refs[24:]
     x, c = where[2], where[3]
     square = (squares[0][0:1, 0:1] + squares[2][0:1, 0:1]) + (
         squares[1][0:1, 0:1] + squares[3][0:1, 0:1]
@@ -804,7 +1018,8 @@
     outs[16][...] = norm_grad
     step(3, Ellipsis, norm_grad, RATE_VECTOR, 0.0)
     step(2, Ellipsis, tail[24:30, : D // (4 * OWNERS)] * factor, RATE_VECTOR, 0.0)
-    own, by_core, by_x, by_both = tail[0:16, :], t_core[...], t_x[...], t_both[...]
+    own, by_x = plane[0:16, :], plane[16:32, :]
+    by_core, by_both = other_plane[0:16, :], other_plane[16:32, :]
     here = jnp.concatenate(
         [jnp.where(c == 0, own, by_core), jnp.where(c == 0, by_core, own)], axis=0
     )
@@ -818,18 +1033,19 @@
         step(4, lanes, gradient, RATE_TABLE, DECAY_RATE)
 
 
-def update(where, kept, got, tail, t_core, t_x, t_both, squares, state):
+def update(where, kept, got, tail, here, there, squares, state, deps):
     vmem = pl.BlockSpec(memory_space=pltpu.VMEM)
-    ins = [kept, got, tail, t_core, t_x, t_both, *squares, *state]
+    ins = [kept, got, tail, here, there, *squares, *state]
     shapes = [sds((1, 1), F32)] + [sds(v.shape, F32) for v in state] + [sds(state[3].shape, F32)]
     return pl.pallas_call(
-        update_kernel,
-        in_specs=[pl.BlockSpec(memory_space=pltpu.SMEM)] + [vmem] * len(ins),
+        ignoring(update_kernel, 1 + len(ins), len(deps)),
+        in_specs=[pl.BlockSpec(memory_space=pltpu.SMEM)] + [vmem] * len(ins) + [ANY] * len(deps),
         out_specs=[vmem] * len(shapes),
         out_shape=shapes,
         compiler_params=params(24 * MIB),
+        cost_estimate=NO_COST,
         name="update",
-    )(where, *ins)
+    )(where, *ins, *deps)
 
 
 def adam_step(weight, gradient, first, second, rate, decay):
@@ -873,124 +1089,131 @@
         packed = lax.dynamic_update_slice(packed, norm_params.astype(BF), (0, 0))
         packed = lax.dynamic_update_slice(packed, split_biases.astype(BF), (0, 128))
         first_unit = jnp.concatenate([units[0], jnp.stack([half, packed])], axis=1)
-        parts1 = gather_z(place, first_unit)
-        parts1, unit2 = together(parts1, units[1])
-        own1 = gather_xy(place, parts1)
-        parts2 = gather_z(place, unit2)
-        own1 = list(together(*own1))
-        diag1 = gather_diagonal(place, own1[1], own1[2])
-        far1 = [place.core(v) for v in own1]
-        diag1, far1, parts2, unit3 = together(diag1, far1, parts2, units[2])
-        own2 = list(gather_xy(place, parts2))
-        parts3 = gather_z(place, unit3)
-        far1 += [place.core(v) for v in diag1]
-        w_attn, table, codes = assemble(where, [*own1, *diag1, *far1], extra, dp_size)
-        norms = jnp.swapaxes(codes[:, 0, 0, 0:6, : norm_params.shape[1]], 0, 1).reshape(6, D)
-        splits = codes[:, :, :, 0:6, 128 : 128 + split_biases.shape[1]]
-        splits = jnp.transpose(splits, (3, 1, 2, 0, 4)).reshape(6, D)
+        own1, unit2, _ = pack(where, gather_z(place, first_unit), None, None, None, units, 1)
+        x1, y1 = place.over_x(own1), place.over_y(own1)
+        size1, size2 = own1.shape[0] // 2, units.shape[1] * units.shape[2] * place.z_size // 2
+        own2, sent_y, sent_x, unit3, _ = pack(
+            where, gather_z(place, unit2), x1, y1, (0, size1, size1), units, 2
+        )
+        y2, x2 = place.over_y(sent_y), place.over_x(sent_x)
+        own3, sent_y, sent_x, token3 = pack(
+            where, gather_z(place, unit3), x2, y2, (size1, size1 + size2, size2)
+        )
+        y3, x3 = place.over_y(sent_y), place.over_x(sent_x)
+        attn_mine, _ = assemble(
+            where, ((0, 0), (1, 0), (2, 0), (4, 0), (3, 0)), (own1, x1, y1, x2, y2), extra, dp_size,
+            (token3,),
+        )
+        attn_other = place.core(attn_mine)
+        first_deps = (token3,)
     else:
 
-        def whole(v):
+        def halves(v):
             v = lax.all_gather(v, "dp", axis=1, tiled=True)
-            return lax.all_gather(v, "mp", axis=2, tiled=True)
-
-        w_attn = whole(jnp.concatenate([low_front[:3], turned[:1]]))
-        w_up, w_down = whole(low_front[3:]), whole(turned[1:])
+            v = lax.all_gather(v, "mp", axis=2, tiled=True).reshape(2, 2 * D, D)
+            return jnp.where(c == 0, v[0], v[1]), jnp.where(c == 0, v[1], v[0])
+
+        attn_mine, attn_other = halves(jnp.concatenate([low_front[:3], turned[:1]]))
+        up_pair, down_pair = halves(low_front[3:]), halves(turned[1:])
         table = lax.all_gather(pos_table.astype(BF), "dp", axis=0, tiled=True)
+        table = table.reshape(OWNERS, 2, CELLS // (2 * OWNERS), D)
+        table = jnp.swapaxes(table, 0, 1).reshape(2, CELLS // 2, D)
         norms = lax.all_gather(norm_params.astype(BF), "dp", axis=1, tiled=True)
         splits = lax.all_gather(split_biases.astype(BF), ("mp", "dp"), axis=1, tiled=True)
-    gap = jnp.zeros((2, D), F32)
-    vec = jnp.concatenate([norms.astype(F32), gap, splits.astype(F32), gap])
-
+        norms = jnp.swapaxes(norms.reshape(6, OWNERS, D // OWNERS), 0, 1)
+        splits = jnp.transpose(splits.reshape(6, 2, 2, OWNERS, -1), (2, 3, 0, 1, 4))
+        codes = jnp.zeros((2, OWNERS, CELLS // (2 * OWNERS), D), BF)
+        codes = codes.at[:, :, 0:6, : norms.shape[2]].set(norms)
+        for side in range(2):
+            lane = side * (D // 2) + 128
+            codes = codes.at[:, :, 0:6, lane : lane + splits.shape[4]].set(splits[:, :, :, side])
+        table = jnp.concatenate([table, codes.reshape(2, -1, D)], axis=1)
+        attn_mine = jnp.concatenate([attn_mine, jnp.where(c == 0, table[0], table[1])])
+        attn_other = jnp.concatenate([attn_other, jnp.where(c == 0, table[1], table[0])])
+        first_deps = ()
+
+    emb, normed1, q, k, v, p, mixed, after, normed2, w_attn, vec, token = attention_forward(
+        scal, crop_boxes, block_input, attn_mine, attn_other, grids, first_deps
+    )
+    deps = ()
+    if direct:
+        sent_y, sent_x, token4 = pack(where, [], x3, y3, (size2, 2 * size2, size2), deps=(token,))
+        y4, x4 = place.over_y(sent_y), place.over_x(sent_x)
+        half, _ = assemble(
+            where, ((0, 0), (1, size1), (2, size1), (4, 0), (3, 0)), (own2, x2, y2, x3, y3), 0, dp_size,
+            (token4,),
+        )
+        up_pair = half, place.core(half)
+        deps = (token4,)
+    hidden, gp, down_mine, down_other, w_up, token = up_forward(
+        scal, normed2, *up_pair, vec, cotangent, grids, deps
+    )
+    if direct:
+        half, token = assemble(
+            where, ((0, 0), (1, size2), (2, size2), (4, 0), (3, 0)), (own3, x3, y3, x4, y4), 0, dp_size,
+            (token,),
+        )
+        down_pair = half, place.core(half)
+        down_other, token = behind(down_other, token)
+        sent, keep1, token = first_y(where, down_mine, place.core(down_other))
+        got1 = place.over_y(sent)
+        deps = (token,)
+    out, w_down, token = down_forward(scal, hidden, *down_pair, after, vec, grids, deps)
+    if direct:
+        out_x = place.over_x(out)
+        deps = (token,)
+    ga, galow, up_mine, up_other, gb, gn, token = mlp_backward(
+        scal, gp, w_down, w_up, normed2, cotangent, after, vec, mixed, grids, deps
+    )
+    if direct:
+        out_pair, token = pair_grids(where, out, out_x, (token,))
+        keep1, *sent, token1 = split_z(where, keep1, got1, deps=(token,))
+        got1 = [place.over_z(sent[s - 1], s) for s in range(1, place.z_size)]
+        up_other, token1 = behind(up_other, token1)
+        sent_x, keep2, token2 = first_x(where, up_mine, place.core(up_other), (token1,))
+        got2 = place.over_x(sent_x)
+        block_output, token3 = finish_grids(place, where, out_pair)
+        deps = (token1, token2, token3)
+    ig, dtable, gs, mine3, other3, token = attention_backward(
+        scal, crop_boxes, ga, galow, mixed, p, q, k, v, emb, normed1, w_attn, vec, gn, gb, grids, deps
+    )
     cells_here, norm_here = pos_table.shape[0], norm_params.shape[1]
     split_here = split_biases.shape[1]
     if direct:
-        w_attn, own2[0], parts3[0] = together(w_attn, own2[0], parts3[0])
-    fwd = attention_forward(scal, crop_boxes, block_input, table, w_attn, vec, grids)
-    if direct:
-        fwd, own2, parts3 = together(fwd, own2, parts3)
-        diag2 = gather_diagonal(place, own2[1], own2[2])
-        own3 = list(gather_xy(place, parts3))
-        far2 = [place.core(v) for v in own2]
-        diag2, far2, own3[0] = together(diag2, far2, own3[0])
-        far2 += [place.core(v) for v in diag2]
-        (w_up,) = assemble(where, [*own2, *diag2, *far2], 0, dp_size)
-    emb, n1, q, k, v, p, mixed, after, n2 = fwd
-    up = up_forward(scal, n2, w_up, vec, cotangent, grids)
-    if direct:
-        red = Reduction(place)
-        up, own3 = together(up, own3)
-        hidden, gp, down_mine, down_other = up
-        diag3 = gather_diagonal(place, own3[1], own3[2])
-        far3 = [place.core(v) for v in own3]
-        h1 = red.over_core(down_mine, down_other)
-        diag3, far3, h1 = together(diag3, far3, h1)
-        far3 += [place.core(v) for v in diag3]
-        keep1, got1, sent1 = red.send_y(h1)
-        (w_down,) = assemble(where, [*own3, *diag3, *far3], 0, dp_size)
-        w_down, sent1 = together(w_down, sent1)
-        out = down_forward(hidden, w_down, after, vec, grids)
-        gp, out = together(gp, out)
-        out_pieces = start_grids(place, out)
-        back = mlp_backward(scal, gp, w_down, w_up, n2, cotangent, after, vec, mixed, grids)
-        back, got1, out_pieces = together(back, got1, out_pieces)
-        ga, galow, up_mine, up_other, gb, gn = back
-        keep1, got1, sent1 = red.send_z(join(keep1, got1))
-        h2 = red.over_core(up_mine, up_other)
-        cut = h2.shape[2] // 2
-        keep2a, got2a, sent2a = red.send_y(h2[:, :, :cut])
-        keep2b, got2b, sent2b = red.send_x(h2[:, :, cut:])
-        galow, sent1, sent2a, sent2b = together(galow, sent1, sent2a, sent2b)
-        back = attention_backward(
-            scal, crop_boxes, ga, galow, mixed, p, q, k, v, emb, n1, w_attn, vec, gn, gb, grids
+        sent1, keep1, token1 = z_to_x(where, keep1, got1, (token,))
+        got1 = place.over_x(sent1)
+        sent_y, keep2, token2 = second_y(where, keep2, got2, (token1,))
+        got2 = place.over_y(sent_y)
+        ig_x = place.over_x(ig)
+        other3, token2 = behind(other3, token2)
+        sent_y, keep3a, sent_x, keep3b, token3 = first_both(
+            where, mine3, place.core(other3), (token1, token2)
         )
-        back, got1, got2a, got2b = together(back, got1, got2a, got2b)
-        ig, dtable, gs, mine3, other3 = back
-        h3 = red.over_core(mine3, other3)
-        keep1, got1, _ = red.send_x(red.sum_z(keep1, got1).astype(BF))
-        keep2a, got2a, _ = red.send_x(join(keep2a, got2a))
-        keep2b, got2b, _ = red.send_y(join(keep2b, got2b))
-        cut = h3.shape[2] // 2
-        keep3a, got3a, _ = red.send_y(h3[:, :, :cut])
-        keep3b, got3b, _ = red.send_x(h3[:, :, cut:])
-        keep3a, keep3b, got1, got2a, got2b = together(keep3a, keep3b, got1, got2a, got2b)
-        h2 = jnp.concatenate([join(keep2a, got2a), join(keep2b, got2b)], axis=1)
-        keep2, got2, _ = red.send_z(h2)
-        keep3a, got3a, got3b = together(keep3a, got3a, got3b)
-        keep3a, got3a, _ = red.send_x(join(keep3a, got3a))
-        keep3b, got3b, _ = red.send_y(join(keep3b, got3b))
-        got3a, got3b, got2 = together(got3a, got3b, got2)
-        h3 = jnp.concatenate([join(keep3a, got3a), join(keep3b, got3b)], axis=1)
-        keep3, got3, _ = red.send_z(h3)
-        ig, keep3 = together(ig, keep3)
-        ig_pieces = start_grids(place, ig)
-        block_output = finish_grids(place, where, out_pieces)
-        got3, block_output = together(got3, block_output)
-        kept, sent, tail, square = totals(where, keep1, got1, keep2, got2, keep3, got3)
-        squares = sum_plane(place, square)
+        got3a, got3b = place.over_y(sent_y), place.over_x(sent_x)
+        keep2, *sent, token = split_z(where, keep2, got2, deps=(token3,))
+        got2 = [place.over_z(sent[s - 1], s) for s in range(1, place.z_size)]
+        sent_x, keep3a, sent_y, keep3b, token = second_both(
+            where, keep3a, got3a, keep3b, got3b, (token,)
+        )
+        got3a, got3b = place.over_x(sent_x), place.over_y(sent_y)
+        keep3, *sent, token = split_z(where, keep3a, got3a, keep3b, got3b, deps=(token, *got2))
+        got3 = [place.over_z(sent[s - 1], s) for s in range(1, place.z_size)]
+        ig_pair, token = pair_grids(where, ig, ig_x, (token,))
+        input_grad, token = finish_grids(place, where, ig_pair)
+        kept, sent, tail, packed, square, _ = totals(
+            where, keep1, got1, keep2, got2, keep3, got3, (token,)
+        )
         got = place.core(sent)
-        t_own = tail[:16]
-        t_x = place.over_x(t_own)
-        t_core, t_both = place.core(t_own), place.core(t_x)
-        ig_pieces, t_x = together(ig_pieces, t_x)
-        input_grad = finish_grids(place, where, ig_pieces)
-        squares, input_grad = together(squares, input_grad)
+        here, there, squares = sum_plane(place, where, packed, square)
         state = (
             front_weights, back_weights, split_biases, norm_params, pos_table,
             front_first, back_weight_first_moment, split_first, norm_first, table_first,
             front_second, back_second, split_second, norm_second, table_second,
         )
-        new = update(where, kept, got, tail, t_core, t_x, t_both, squares, state)
+        state = [pltpu.with_memory_space_constraint(v, pltpu.HBM) for v in state]
+        new = update(where, kept, got, tail, here, there, squares, state, ())
         return (block_output, input_grad, new[0][0, 0], *new[1:])
     else:
-        hidden, gp, down_mine, down_other = up
-        out = down_forward(hidden, w_down, after, vec, grids)
-        ga, galow, up_mine, up_other, gb, gn = mlp_backward(
-            scal, gp, w_down, w_up, n2, cotangent, after, vec, mixed, grids
-        )
-        ig, dtable, gs, mine3, other3 = attention_backward(
-            scal, crop_boxes, ga, galow, mixed, p, q, k, v, emb, n1, w_attn, vec, gn, gb, grids
-        )
 
         def share(mine, other, blocks):
             low, high = jnp.where(c == 0, mine, other), jnp.where(c == 0, other, mine)

time: 342 us -> 315 us (0.921)
  local copies, waits for them, and re-layouts: 35.7 us -> 6.36 us
  starting transfers between devices: 80.4 us -> 54.6 us
  Pallas kernels: 110 us -> 134 us
  waiting for transfers between devices: 96.7 us -> 113 us
  other arithmetic: 12.5 us -> 1.79 us
    pallas_call x12 -> x28, Pallas kernels: 110 us -> 134 us  [the longest x22 31.9 us: call(): pl.pallas_call(ignoring(kernel, 1 + len(ins), len(deps)), in_specs=[pl.Bl...]
    ppermute x21, waiting for transfers between devices: 27 us -> 51.3 us  [over_z(): return lax.ppermute(v, 'dp', self.z_shift[shift])]
    ppermute x15 -> x11, waiting for transfers between devices: 46.8 us -> 23.2 us  [over_x(): return lax.ppermute(v, 'mp', self.x_pairs)]
    unnamed x147 -> x39, local copies, waits for them, and re-layouts: 20.9 us -> 3.51 us
    ppermute x27 -> x11, waiting for transfers between devices: 4.9 us -> 20.8 us  [core(): return lax.ppermute(v, 'mp', self.core_pairs)]
    ppermute x21, starting transfers between devices: 43.6 us -> 34.2 us  [over_z(): return lax.ppermute(v, 'dp', self.z_shift[shift])]
    convert_element_type x14 -> x0, other arithmetic: 8.74 us -> none  [the longest x11 8.57 us: join(): return (a.astype(F32) + b.astype(F32)).astype(BF)]
    ppermute x12 -> x9, starting transfers between devices: 13.5 us -> 5.98 us  [over_y(): return lax.ppermute(v, 'dp', self.y_pairs)]
  transfers between devices with their start and end apart: 76 -> 53, of which waited for: 24 -> 28; matrix products, arithmetic and copies ran while one was open for 7% -> 0% of each run, Pallas kernels for 31% -> 35%
where the time goes in v3:
time: 315 us; the launch traced here: 311 us
  Pallas kernels  134 us (43%)
  waiting for transfers between devices  113 us (36%)
  starting transfers between devices  54.6 us (17%)
  local copies, waits for them, and re-layouts  6.36 us (2%)
    ppermute x21, waiting for transfers between devices, over_z(): return lax.ppermute(v, 'dp', self.z_shift[shift])  51.3 us
    ppermute x21, starting transfers between devices, over_z(): return lax.ppermute(v, 'dp', self.z_shift[shift])  34.2 us
    pallas_call x22, Pallas kernels, call(): pl.pallas_call(ignoring(kernel, 1 + len(ins), len(deps)), in_specs=[pl.Bl...  31.9 us
    pallas_call x1, Pallas kernels, attention_backward(): pl.pallas_call(ignoring(attention_backward_kernel, 15, len(deps)), grid_s...  31.5 us
    pallas_call x1, Pallas kernels, mlp_backward(): pl.pallas_call(ignoring(mlp_kernel, 9, len(deps)), grid_spec=spec, out_sh...  25.2 us
    ppermute x11, waiting for transfers between devices, over_x(): return lax.ppermute(v, 'mp', self.x_pairs)  23.2 us
    ppermute x11, waiting for transfers between devices, core(): return lax.ppermute(v, 'mp', self.core_pairs)  20.8 us
    pallas_call x1, Pallas kernels, attention_forward(): pl.pallas_call(ignoring(attention_forward_kernel, 5, len(deps)), grid_spe...  20.1 us
  transfers between devices with their start and end apart: 53, of which 28 were waited for; matrix products, arithmetic and copies ran while one was open for 0% of the time, Pallas kernels for 35%

profile of v3, /device:TPU:0, one launch (start us, length us, event | category | flops | bytes accessed | tf_op | source)
XLA Modules:
  0.0 311.3 jit_solution(12800905188726968916)
XLA Ops:
  6.7 5.0 %collective-permute-start.3 = (bf16[2,112,384]{2,1,0:T(8,128)(2,1)S(1)}, bf16[2,112,384]{2,1,0:T(8,128)(2,1)S(1)}, u32[]{:S(2)}, u32[]{:S(2)}) collective-permute-start(bf16[2,112,384]{2,1,0:T(8,128)(2,1)S(1)} %maximum_maximum_fusion.refs_1_), channel_id=1, source_target_pairs={{0,24},{4,28},{8,0},{12,4},{16,8},{20,12},{24,16},{28,20},{1,25},{... | collective-permute-start | bytes 516104 | tf_op jit(solution)/shard_map/ppermute | solution.py:651
  12.8 3.7 %collective-permute-done.3.refs_4_ = bf16[2,112,384]{2,1,0:T(8,128)(2,1)S(1)} collective-permute-done((bf16[2,112,384]{2,1,0:T(8,128)(2,1)S(1)}, bf16[2,112,384]{2,1,0:T(8,128)(2,1)S(1)}, u32[]{:S(2)}, u32[]{:S(2)}) %collective-permute-start.3) | collective-permute-done | bytes 172064 | tf_op jit(solution)/shard_map/ppermute | solution.py:651
  16.6 10.1 %collective-permute-done.2.refs_3_ = bf16[2,112,384]{2,1,0:T(8,128)(2,1)S(1)} collective-permute-done((bf16[2,112,384]{2,1,0:T(8,128)(2,1)S(1)}, bf16[2,112,384]{2,1,0:T(8,128)(2,1)S(1)}, u32[]{:S(2)}, u32[]{:S(2)}) %collective-permute-start.2) | collective-permute-done | bytes 172064 | tf_op jit(solution)/shard_map/ppermute | solution.py:651
  33.6 2.0 collective-permute-start.6
  36.8 9.0 %collective-permute-done.7.refs_3_ = bf16[2,96,384]{2,1,0:T(8,128)(2,1)S(1)} collective-permute-done((bf16[2,96,384]{2,1,0:T(8,128)(2,1)S(1)}, bf16[2,96,384]{2,1,0:T(8,128)(2,1)S(1)}, u32[]{:S(2)}, u32[]{:S(2)}) %collective-permute-start.7) | collective-permute-done | bytes 147488 | tf_op jit(solution)/shard_map/ppermute | solution.py:651
  49.2 2.4 collective-permute-start.12
  54.4 8.2 %collective-permute-done.12.refs_3_ = bf16[2,96,384]{2,1,0:T(8,128)(2,1)S(1)} collective-permute-done((bf16[2,96,384]{2,1,0:T(8,128)(2,1)S(1)}, bf16[2,96,384]{2,1,0:T(8,128)(2,1)S(1)}, u32[]{:S(2)}, u32[]{:S(2)}) %collective-permute-start.12) | collective-permute-done | bytes 147488 | tf_op jit(solution)/shard_map/ppermute | solution.py:651
  62.6 5.6 %collective-permute-done.9.refs_5_.refs_4_.refs_2_ = bf16[1216,384]{1,0:T(8,128)(2,1)S(1)} collective-permute-done((bf16[1216,384]{1,0:T(8,128)(2,1)S(1)}, bf16[1216,384]{1,0:T(8,128)(2,1)S(1)}, u32[]{:S(2)}, u32[]{:S(2)}) %collective-permute-start.9) | collective-permute-done | bytes 933920 | tf_op jit(solution)/shard_map/ppermute | solution.py:645
  71.5 2.3 assemble.3
  75.2 4.1 %collective-permute-done.14.refs_4_ = bf16[1792,768]{1,0:T(8,128)(2,1)} collective-permute-done((bf16[1792,768]{1,0:T(8,128)(2,1)}, bf16[1792,768]{1,0:T(8,128)(2,1)}, u32[]{:S(2)}, u32[]{:S(2)}) %collective-permute-start.14) | collective-permute-done | bytes 2752544 | tf_op jit(solution)/shard_map/ppermute | solution.py:639
  79.2 2.3 copy-done.2
  81.6 20.1 %attention_forward.1 = (f32[768,768]{1,0:T(8,128)}, bf16[768,768]{1,0:T(8,128)(2,1)}, bf16[768,768]{1,0:T(8,128)(2,1)}, bf16[768,768]{1,0:T(8,128)(2,1)}, bf16[7...) custom-call(s32[4]{0:T(128)S(1)} %pad_add_fusion.1.refs_0_, ...), custom_call_target="tpu_custom_call" | custom-call | tf_op jit(solution)/shard_map/attention_forward/pallas_call | solution.py:468
  106.1 3.3 %collective-permute-done.17.refs_3_ = bf16[1536,768]{1,0:T(8,128)(2,1)S(1)} collective-permute-done((bf16[1536,768]{1,0:T(8,128)(2,1)S(1)}, bf16[1536,768]{1,0:T(8,128)(2,1)S(1)}, u32[]{:S(2)}, u32[]{:S(2)}) %collective-permute-start.17) | collective-permute-done | bytes 2359328 | tf_op jit(solution)/shard_map/ppermute | solution.py:639
  109.3 14.1 %up_forward.1 = (bf16[4,768,768]{2,1,0:T(8,128)(2,1)S(1)}, bf16[4,768,768]{2,1,0:T(8,128)(2,1)}, bf16[8,192,768]{2,1,0:T(8,128)(2,1)S(1)}, bf16[8,192,768]{2,1,0...) custom-call(s32[4]{0:T(128)S(1)} %pad_add_fusion.1.refs_0_, ...), custom_call_target="tpu_custom_call" | custom-call | tf_op jit(solution)/shard_map/up_forward/pallas_call | solution.py:500
  125.9 2.3 collective-permute-done.21.refs_2_
  131.4 6.3 %down_forward.1 = (bf16[3,256,768]{2,1,0:T(8,128)(2,1)}, bf16[4,768,768]{2,1,0:T(8,128)(2,1)}, f32[8,128]{1,0:T(8,128)S(1)}) custom-call(s32[4]{0:T(128)S(1)} %pad_add_fusion.1.refs_0_, bf16[4,768,768]{2,1,0:T(8,128)(2,1)S(1)} %get-tuple-element.153.refs_1_, bf16[1536,768]{1,0:T(8,128)(2,1)S(1)} %get-tuple-element.158.refs_2_, ...), custom_call_target="tpu_custom_call" | custom-call | tf_op jit(solution)/shard_map/down_forward/pallas_call | solution.py:532
  138.9 25.2 %mlp_backward.1 = (f32[768,768]{1,0:T(8,128)S(1)}, bf16[768,768]{1,0:T(8,128)(2,1)S(1)}, bf16[8,240,768]{2,1,0:T(8,128)(2,1)S(1)}, bf16[8,240,768]{2,1,0:T(8,128...) custom-call(s32[4]{0:T(128)S(1)} %pad_add_fusion.1.refs_0_, ...), custom_call_target="tpu_custom_call" | custom-call | tf_op jit(solution)/shard_map/mlp_backward/pallas_call | solution.py:565
  168.4 4.9 %collective-permute-done.25.refs_2_ = bf16[8,240,768]{2,1,0:T(8,128)(2,1)S(1)} collective-permute-done((bf16[8,240,768]{2,1,0:T(8,128)(2,1)S(1)}, bf16[8,240,768]{2,1,0:T(8,128)(2,1)S(1)}, u32[]{:S(2)}, u32[]{:S(2)}) %collective-permute-start.25) | collective-permute-done | bytes 2949152 | tf_op jit(solution)/shard_map/ppermute | solution.py:639
  178.2 3.0 collective-permute-start.30
  181.1 3.0 collect.2
  184.2 31.5 %attention_backward.1 = (bf16[3,256,768]{2,1,0:T(8,128)(2,1)}, f32[256,768]{1,0:T(8,128)}, f32[8,768]{1,0:T(8,128)}, bf16[8,176,768]{2,1,0:T(8,128)(2,1)S(1)}, b...) custom-call(s32[4]{0:T(128)S(1)} %pad_add_fusion.1.refs_0_, s32[12,4]{1,0:T(8,128)S(1)} %copy.45.refs_1_, ...), custom_call_target="tpu_custom_call" | custom-call | tf_op jit(solution)/shard_map/attention_backward/pallas_call | solution.py:605
  219.3 2.5 collective-permute-done.31.refs_2_
  224.7 13.3 %collective-permute-done.34.refs_2_ = bf16[4,240,384]{2,1,0:T(8,128)(2,1)S(1)} collective-permute-done((bf16[4,240,384]{2,1,0:T(8,128)(2,1)S(1)}, bf16[4,240,384]{2,1,0:T(8,128)(2,1)S(1)}, u32[]{:S(2)}, u32[]{:S(2)}) %collective-permute-start.34) | collective-permute-done | bytes 737312 | tf_op jit(solution)/shard_map/ppermute | solution.py:648
  238.9 15.5 %collective-permute-done.33.refs_4_ = bf16[8,64,384]{2,1,0:T(8,128)(2,1)S(1)} collective-permute-done((bf16[8,64,384]{2,1,0:T(8,128)(2,1)S(1)}, bf16[8,64,384]{2,1,0:T(8,128)(2,1)S(1)}, u32[]{:S(2)}, u32[]{:S(2)}) %collective-permute-start.33) | collective-permute-done | bytes 393248 | tf_op jit(solution)/shard_map/ppermute | solution.py:645
  259.5 7.9 %collective-permute-done.38.refs_7_.refs_5_ = bf16[240,384]{1,0:T(8,128)(2,1)S(1)} collective-permute-done((bf16[240,384]{1,0:T(8,128)(2,1)S(1)}, bf16[240,384]{1,0:T(8,128)(2,1)S(1)}, u32[]{:S(2)}, u32[]{:S(2)}) %collective-permute-start.38) | collective-permute-done | bytes 184352 | tf_op jit(solution)/shard_map/ppermute | solution.py:651
  269.9 4.1 %collective-permute-start.42 = (bf16[176,384]{1,0:T(8,128)(2,1)S(1)}, bf16[176,384]{1,0:T(8,128)(2,1)S(1)}, u32[]{:S(2)}, u32[]{:S(2)}) collective-permute-start(bf16[176,384]{1,0:T(8,128)(2,1)S(1)} %get-tuple-element.230), channel_id=1, source_target_pairs={{0,8},{4,12},{8,16},{12,20},{16,24},{20,28},{24,0},{28,4},{1,9},{5... | collective-permute-start | bytes 405512 | tf_op jit(solution)/shard_map/ppermute | solution.py:651
  276.4 3.0 collect.3
  279.4 5.2 %collective-permute-done.43.refs_9_ = bf16[176,384]{1,0:T(8,128)(2,1)S(1)} collective-permute-done((bf16[176,384]{1,0:T(8,128)(2,1)S(1)}, bf16[176,384]{1,0:T(8,128)(2,1)S(1)}, u32[]{:S(2)}, u32[]{:S(2)}) %collective-permute-start.43) | collective-permute-done | bytes 135200 | tf_op jit(solution)/shard_map/ppermute | solution.py:651
  290.2 2.3 collective-permute-done.48.refs_4_
  295.8 4.4 %collective-permute-start.52 = (f32[8,128]{1,0:T(8,128)S(1)}, f32[8,128]{1,0:T(8,128)S(1)}, u32[]{:S(2)}, u32[]{:S(2)}) collective-permute-start(f32[8,128]{1,0:T(8,128)S(1)} %slice_add_fusion.refs_6_), channel_id=1, source_target_pairs={{0,24},{4,28},{8,0},{12,4},{16,8},{20,12},{24,16},{28,20},{1,25},{... | collective-permute-start | bytes 12296 | tf_op jit(solution)/shard_map/ppermute | solution.py:651
  301.5 3.2 %collective-permute-done.51.refs_8_ = f32[8,128]{1,0:T(8,128)S(1)} collective-permute-done((f32[8,128]{1,0:T(8,128)S(1)}, f32[8,128]{1,0:T(8,128)S(1)}, u32[]{:S(2)}, u32[]{:S(2)}) %collective-permute-start.51) | collective-permute-done | bytes 4128 | tf_op jit(solution)/shard_map/ppermute | solution.py:651
  306.0 5.1 %update.1 = (f32[1,1]{1,0:T(1,128)}, f32[7,96,192]{2,1,0:T(8,128)}, f32[5,192,96]{2,1,0:T(8,128)}, f32[6,24]{1,0:T(8,128)}, f32[6,96]{1,0:T(8,128)}, /*index=5*/...) custom-call(s32[4]{0:T(128)S(1)} %pad_add_fusion.refs_0_, ...), custom_call_target="tpu_custom_call" | custom-call | tf_op jit(solution)/shard_map/update/pallas_call | solution.py:1040
  (162 shorter events, 75.2 us)
Async XLA Ops:
  11.7 14.9 %collective-permute-start.2 = (bf16[2,112,384]{2,1,0:T(8,128)(2,1)S(1)}, bf16[2,112,384]{2,1,0:T(8,128)(2,1)S(1)}, u32[]{:S(2)}, u32[]{:S(2)}) collective-permute-start(bf16[2,112,384]{2,1,0:T(8,128)(2,1)S(1)} %maximum_maximum_fusion.refs_1_), channel_id=1, source_target_pairs={{0,16},{4,20},{8,24},{12,28},{16,0},{20,4},{24,8},{28,12},{1,17},{... | collective-permute-start | bytes 516104 | tf_op jit(solution)/shard_map/ppermute | solution.py:651
  11.7 14.9 %collective-permute-start.1 = (bf16[2,112,384]{2,1,0:T(8,128)(2,1)S(1)}, bf16[2,112,384]{2,1,0:T(8,128)(2,1)S(1)}, u32[]{:S(2)}, u32[]{:S(2)}) collective-permute-start(bf16[2,112,384]{2,1,0:T(8,128)(2,1)S(1)} %maximum_maximum_fusion.refs_1_), channel_id=1, source_target_pairs={{0,8},{4,12},{8,16},{12,20},{16,24},{20,28},{24,0},{28,4},{1,9},{5... | collective-permute-start | bytes 516104 | tf_op jit(solution)/shard_map/ppermute | solution.py:651
  27.8 18.0 %collective-permute-start.5 = (bf16[896,384]{1,0:T(8,128)(2,1)S(1)}, bf16[896,384]{1,0:T(8,128)(2,1)S(1)}, u32[]{:S(2)}, u32[]{:S(2)}) collective-permute-start(bf16[896,384]{1,0:T(8,128)(2,1)S(1)} %get-tuple-element.138.refs_1_), channel_id=1, source_target_pairs={{0,4},{4,0},{8,12},{12,8},{16,20},{20,16},{24,28},{28,24},{1,5},{5... | collective-permute-start | bytes 2064392 | tf_op jit(solution)/shard_map/ppermute | solution.py:648
  29.3 16.7 %collective-permute-start.4 = (bf16[896,384]{1,0:T(8,128)(2,1)S(1)}, bf16[896,384]{1,0:T(8,128)(2,1)S(1)}, u32[]{:S(2)}, u32[]{:S(2)}) collective-permute-start(bf16[896,384]{1,0:T(8,128)(2,1)S(1)} %get-tuple-element.138.refs_1_), channel_id=1, source_target_pairs={{0,2},{1,3},{2,0},{3,1},{4,6},{5,7},{6,4},{7,5},{8,10},{9,11},{10,... | collective-permute-start | bytes 2064392 | tf_op jit(solution)/shard_map/ppermute | solution.py:645
  31.6 14.2 %collective-permute-start.7 = (bf16[2,96,384]{2,1,0:T(8,128)(2,1)S(1)}, bf16[2,96,384]{2,1,0:T(8,128)(2,1)S(1)}, u32[]{:S(2)}, u32[]{:S(2)}) collective-permute-start(bf16[2,96,384]{2,1,0:T(8,128)(2,1)S(1)} %get-tuple-element.139.refs_1_), channel_id=1, source_target_pairs={{0,16},{4,20},{8,24},{12,28},{16,0},{20,4},{24,8},{28,12},{1,17},{... | collective-permute-start | bytes 442376 | tf_op jit(solution)/shard_map/ppermute | solution.py:651
  33.6 12.2 %collective-permute-start.6 = (bf16[2,96,384]{2,1,0:T(8,128)(2,1)S(1)}, bf16[2,96,384]{2,1,0:T(8,128)(2,1)S(1)}, u32[]{:S(2)}, u32[]{:S(2)}) collective-permute-start(bf16[2,96,384]{2,1,0:T(8,128)(2,1)S(1)} %get-tuple-element.139.refs_1_), channel_id=1, source_target_pairs={{0,8},{4,12},{8,16},{12,20},{16,24},{20,28},{24,0},{28,4},{1,9},{5... | collective-permute-start | bytes 442376 | tf_op jit(solution)/shard_map/ppermute | solution.py:651
  47.2 21.1 %collective-permute-start.9 = (bf16[1216,384]{1,0:T(8,128)(2,1)S(1)}, bf16[1216,384]{1,0:T(8,128)(2,1)S(1)}, u32[]{:S(2)}, u32[]{:S(2)}) collective-permute-start(bf16[1216,384]{1,0:T(8,128)(2,1)S(1)} %get-tuple-element.140), channel_id=1, source_target_pairs={{0,2},{1,3},{2,0},{3,1},{4,6},{5,7},{6,4},{7,5},{8,10},{9,11},{10,... | collective-permute-start | bytes 2801672 | tf_op jit(solution)/shard_map/ppermute | solution.py:645
  48.7 20.8 %collective-permute-start.10 = (bf16[1216,384]{1,0:T(8,128)(2,1)S(1)}, bf16[1216,384]{1,0:T(8,128)(2,1)S(1)}, u32[]{:S(2)}, u32[]{:S(2)}) collective-permute-start(bf16[1216,384]{1,0:T(8,128)(2,1)S(1)} %get-tuple-element.141), channel_id=1, source_target_pairs={{0,4},{4,0},{8,12},{12,8},{16,20},{20,16},{24,28},{28,24},{1,5},{5... | collective-permute-start | bytes 2801672 | tf_op jit(solution)/shard_map/ppermute | solution.py:648
  49.2 13.5 %collective-permute-start.12 = (bf16[2,96,384]{2,1,0:T(8,128)(2,1)S(1)}, bf16[2,96,384]{2,1,0:T(8,128)(2,1)S(1)}, u32[]{:S(2)}, u32[]{:S(2)}) collective-permute-start(bf16[2,96,384]{2,1,0:T(8,128)(2,1)S(1)} %get-tuple-element.142.refs_1_), channel_id=1, source_target_pairs={{0,16},{4,20},{8,24},{12,28},{16,0},{20,4},{24,8},{28,12},{1,17},{... | collective-permute-start | bytes 442376 | tf_op jit(solution)/shard_map/ppermute | solution.py:651
  51.6 11.1 %collective-permute-start.11 = (bf16[2,96,384]{2,1,0:T(8,128)(2,1)S(1)}, bf16[2,96,384]{2,1,0:T(8,128)(2,1)S(1)}, u32[]{:S(2)}, u32[]{:S(2)}) collective-permute-start(bf16[2,96,384]{2,1,0:T(8,128)(2,1)S(1)} %get-tuple-element.142.refs_1_), channel_id=1, source_target_pairs={{0,8},{4,12},{8,16},{12,20},{16,24},{20,28},{24,0},{28,4},{1,9},{5... | collective-permute-start | bytes 442376 | tf_op jit(solution)/shard_map/ppermute | solution.py:651
  73.8 27.8 %collective-permute-start.15 = (bf16[1152,384]{1,0:T(8,128)(2,1)}, bf16[1152,384]{1,0:T(8,128)(2,1)S(1)}, u32[]{:S(2)}, u32[]{:S(2)}) collective-permute-start(bf16[1152,384]{1,0:T(8,128)(2,1)} %get-tuple-element.147), channel_id=1, source_target_pairs={{0,2},{1,3},{2,0},{3,1},{4,6},{5,7},{6,4},{7,5},{8,10},{9,11},{10,... | collective-permute-start | bytes 2654216 | tf_op jit(solution)/shard_map/ppermute | solution.py:645
  74.4 27.3 %collective-permute-start.16 = (bf16[1152,384]{1,0:T(8,128)(2,1)}, bf16[1152,384]{1,0:T(8,128)(2,1)}, u32[]{:S(2)}, u32[]{:S(2)}) collective-permute-start(bf16[1152,384]{1,0:T(8,128)(2,1)} %get-tuple-element.148), channel_id=1, source_target_pairs={{0,4},{4,0},{8,12},{12,8},{16,20},{20,16},{24,28},{28,24},{1,5},{5... | collective-permute-start | bytes 2654216 | tf_op jit(solution)/shard_map/ppermute | solution.py:648
  104.9 18.7 %collective-permute-start.18 = (bf16[384,384]{1,0:T(8,128)(2,1)S(1)}, bf16[384,384]{1,0:T(8,128)(2,1)S(1)}, u32[]{:S(2)}, u32[]{:S(2)}) collective-permute-start(bf16[384,384]{1,0:T(8,128)(2,1)S(1)} %get-tuple-element.155), channel_id=1, source_target_pairs={{0,2},{1,3},{2,0},{3,1},{4,6},{5,7},{6,4},{7,5},{8,10},{9,11},{10,... | collective-permute-start | bytes 884744 | tf_op jit(solution)/shard_map/ppermute | solution.py:645
  105.5 18.2 %collective-permute-start.19 = (bf16[384,384]{1,0:T(8,128)(2,1)S(1)}, bf16[384,384]{1,0:T(8,128)(2,1)S(1)}, u32[]{:S(2)}, u32[]{:S(2)}) collective-permute-start(bf16[384,384]{1,0:T(8,128)(2,1)S(1)} %get-tuple-element.156), channel_id=1, source_target_pairs={{0,4},{4,0},{8,12},{12,8},{16,20},{20,16},{24,28},{28,24},{1,5},{5... | collective-permute-start | bytes 884744 | tf_op jit(solution)/shard_map/ppermute | solution.py:648
  137.7 28.3 %collective-permute-start.22 = (bf16[3,256,768]{2,1,0:T(8,128)(2,1)}, bf16[3,256,768]{2,1,0:T(8,128)(2,1)S(1)}, u32[]{:S(2)}, u32[]{:S(2)}) collective-permute-start(bf16[3,256,768]{2,1,0:T(8,128)(2,1)} %get-tuple-element.163.refs_1_), channel_id=1, source_target_pairs={{0,2},{1,3},{2,0},{3,1},{4,6},{5,7},{6,4},{7,5},{8,10},{9,11},{10,... | collective-permute-start | bytes 3538952 | tf_op jit(solution)/shard_map/ppermute | solution.py:645
  138.3 28.4 %collective-permute-start.24 = (bf16[4,192,768]{2,1,0:T(8,128)(2,1)S(1)}, bf16[4,192,768]{2,1,0:T(8,128)(2,1)S(1)}, u32[]{:S(2)}, u32[]{:S(2)}) collective-permute-start(bf16[4,192,768]{2,1,0:T(8,128)(2,1)S(1)} %get-tuple-element.185), channel_id=1, source_target_pairs={{0,4},{4,0},{8,12},{12,8},{16,20},{20,16},{24,28},{28,24},{1,5},{5... | collective-permute-start | bytes 3538952 | tf_op jit(solution)/shard_map/ppermute | solution.py:648
  167.9 13.3 %collective-permute-start.23 = (bf16[2,3,256,768]{3,2,1,0:T(8,128)(2,1)S(1)}, bf16[2,3,256,768]{3,2,1,0:T(8,128)(2,1)S(1)}, u32[]{:S(2)}, u32[]{:S(2)}) collective-permute-start(bf16[2,3,256,768]{3,2,1,0:T(8,128)(2,1)S(1)} %get-tuple-element.170.refs_1_), channel_id=1, source_target_pairs={{0,1},{1,0},{2,3},{3,2},{4,5},{5,4},{6,7},{7,6},{8,9},{9,8},{10,11... | collective-permute-start | bytes 7077896 | tf_op jit(solution)/shard_map/ppermute | solution.py:639
  175.2 41.3 %collective-permute-start.27 = (bf16[8,240,384]{2,1,0:T(8,128)(2,1)S(1)}, bf16[8,240,384]{2,1,0:T(8,128)(2,1)S(1)}, u32[]{:S(2)}, u32[]{:S(2)}) collective-permute-start(bf16[8,240,384]{2,1,0:T(8,128)(2,1)S(1)} %get-tuple-element.197), channel_id=1, source_target_pairs={{0,2},{1,3},{2,0},{3,1},{4,6},{5,7},{6,4},{7,5},{8,10},{9,11},{10,... | collective-permute-start | bytes 4423688 | tf_op jit(solution)/shard_map/ppermute | solution.py:645
  175.9 39.8 %collective-permute-start.28 = (bf16[192,768]{1,0:T(8,128)(2,1)S(1)}, bf16[192,768]{1,0:T(8,128)(2,1)S(1)}, u32[]{:S(2)}, u32[]{:S(2)}) collective-permute-start(bf16[192,768]{1,0:T(8,128)(2,1)S(1)} %get-tuple-element.199), channel_id=1, source_target_pairs={{0,8},{4,12},{8,16},{12,20},{16,24},{20,28},{24,0},{28,4},{1,9},{5... | collective-permute-start | bytes 884744 | tf_op jit(solution)/shard_map/ppermute | solution.py:651
  176.2 39.4 %collective-permute-start.29 = (bf16[192,768]{1,0:T(8,128)(2,1)S(1)}, bf16[192,768]{1,0:T(8,128)(2,1)S(1)}, u32[]{:S(2)}, u32[]{:S(2)}) collective-permute-start(bf16[192,768]{1,0:T(8,128)(2,1)S(1)} %get-tuple-element.200), channel_id=1, source_target_pairs={{0,16},{4,20},{8,24},{12,28},{16,0},{20,4},{24,8},{28,12},{1,17},{... | collective-permute-start | bytes 884744 | tf_op jit(solution)/shard_map/ppermute | solution.py:651
  178.2 37.5 %collective-permute-start.30 = (bf16[192,768]{1,0:T(8,128)(2,1)S(1)}, bf16[192,768]{1,0:T(8,128)(2,1)S(1)}, u32[]{:S(2)}, u32[]{:S(2)}) collective-permute-start(bf16[192,768]{1,0:T(8,128)(2,1)S(1)} %get-tuple-element.201), channel_id=1, source_target_pairs={{0,24},{4,28},{8,0},{12,4},{16,8},{20,12},{24,16},{28,20},{1,25},{... | collective-permute-start | bytes 884744 | tf_op jit(solution)/shard_map/ppermute | solution.py:651
  217.6 50.6 %collective-permute-start.26 = (bf16[3,256,768]{2,1,0:T(8,128)(2,1)S(1)}, bf16[3,256,768]{2,1,0:T(8,128)(2,1)S(1)}, u32[]{:S(2)}, u32[]{:S(2)}) collective-permute-start(bf16[3,256,768]{2,1,0:T(8,128)(2,1)S(1)} %copy-done.7), channel_id=1, source_target_pairs={{0,2},{1,3},{2,0},{3,1},{4,6},{5,7},{6,4},{7,5},{8,10},{9,11},{10,... | collective-permute-start | bytes 3538952 | tf_op jit(solution)/shard_map/ppermute | solution.py:645
  218.7 19.3 %collective-permute-start.34 = (bf16[4,240,384]{2,1,0:T(8,128)(2,1)S(1)}, bf16[4,240,384]{2,1,0:T(8,128)(2,1)S(1)}, u32[]{:S(2)}, u32[]{:S(2)}) collective-permute-start(bf16[4,240,384]{2,1,0:T(8,128)(2,1)S(1)} %get-tuple-element.212), channel_id=1, source_target_pairs={{0,4},{4,0},{8,12},{12,8},{16,20},{20,16},{24,28},{28,24},{1,5},{5... | collective-permute-start | bytes 2211848 | tf_op jit(solution)/shard_map/ppermute | solution.py:648
  223.0 31.3 %collective-permute-start.32 = (bf16[4,112,768]{2,1,0:T(8,128)(2,1)S(1)}, bf16[4,112,768]{2,1,0:T(8,128)(2,1)S(1)}, u32[]{:S(2)}, u32[]{:S(2)}) collective-permute-start(bf16[4,112,768]{2,1,0:T(8,128)(2,1)S(1)} %get-tuple-element.208), channel_id=1, source_target_pairs={{0,4},{4,0},{8,12},{12,8},{16,20},{20,16},{24,28},{28,24},{1,5},{5... | collective-permute-start | bytes 2064392 | tf_op jit(solution)/shard_map/ppermute | solution.py:648
  223.6 30.8 %collective-permute-start.33 = (bf16[8,64,384]{2,1,0:T(8,128)(2,1)S(1)}, bf16[8,64,384]{2,1,0:T(8,128)(2,1)S(1)}, u32[]{:S(2)}, u32[]{:S(2)}) collective-permute-start(bf16[8,64,384]{2,1,0:T(8,128)(2,1)S(1)} %get-tuple-element.210), channel_id=1, source_target_pairs={{0,2},{1,3},{2,0},{3,1},{4,6},{5,7},{6,4},{7,5},{8,10},{9,11},{10,... | collective-permute-start | bytes 1179656 | tf_op jit(solution)/shard_map/ppermute | solution.py:645
  238.8 19.4 %collective-permute-start.37 = (bf16[240,384]{1,0:T(8,128)(2,1)S(1)}, bf16[240,384]{1,0:T(8,128)(2,1)S(1)}, u32[]{:S(2)}, u32[]{:S(2)}) collective-permute-start(bf16[240,384]{1,0:T(8,128)(2,1)S(1)} %get-tuple-element.220), channel_id=1, source_target_pairs={{0,8},{4,12},{8,16},{12,20},{16,24},{20,28},{24,0},{28,4},{1,9},{5... | collective-permute-start | bytes 552968 | tf_op jit(solution)/shard_map/ppermute | solution.py:651
  255.5 12.0 %collective-permute-start.35 = (bf16[4,112,384]{2,1,0:T(8,128)(2,1)S(1)}, bf16[4,112,384]{2,1,0:T(8,128)(2,1)S(1)}, u32[]{:S(2)}, u32[]{:S(2)}) collective-permute-start(bf16[4,112,384]{2,1,0:T(8,128)(2,1)S(1)} %get-tuple-element.216), channel_id=1, source_target_pairs={{0,2},{1,3},{2,0},{3,1},{4,6},{5,7},{6,4},{7,5},{8,10},{9,11},{10,... | collective-permute-start | bytes 1032200 | tf_op jit(solution)/shard_map/ppermute | solution.py:645
  256.7 10.8 %collective-permute-start.36 = (bf16[4,64,384]{2,1,0:T(8,128)(2,1)S(1)}, bf16[4,64,384]{2,1,0:T(8,128)(2,1)S(1)}, u32[]{:S(2)}, u32[]{:S(2)}) collective-permute-start(bf16[4,64,384]{2,1,0:T(8,128)(2,1)S(1)} %get-tuple-element.218), channel_id=1, source_target_pairs={{0,4},{4,0},{8,12},{12,8},{16,20},{20,16},{24,28},{28,24},{1,5},{5... | collective-permute-start | bytes 589832 | tf_op jit(solution)/shard_map/ppermute | solution.py:648
  257.2 10.1 %collective-permute-start.38 = (bf16[240,384]{1,0:T(8,128)(2,1)S(1)}, bf16[240,384]{1,0:T(8,128)(2,1)S(1)}, u32[]{:S(2)}, u32[]{:S(2)}) collective-permute-start(bf16[240,384]{1,0:T(8,128)(2,1)S(1)} %get-tuple-element.221), channel_id=1, source_target_pairs={{0,16},{4,20},{8,24},{12,28},{16,0},{20,4},{24,8},{28,12},{1,17},{... | collective-permute-start | bytes 552968 | tf_op jit(solution)/shard_map/ppermute | solution.py:651
  269.3 10.1 %collective-permute-start.41 = (bf16[192,384]{1,0:T(8,128)(2,1)S(1)}, bf16[192,384]{1,0:T(8,128)(2,1)S(1)}, u32[]{:S(2)}, u32[]{:S(2)}) collective-permute-start(bf16[192,384]{1,0:T(8,128)(2,1)S(1)} %get-tuple-element.227), channel_id=1, source_target_pairs={{0,2},{1,3},{2,0},{3,1},{4,6},{5,7},{6,4},{7,5},{8,10},{9,11},{10,... | collective-permute-start | bytes 442376 | tf_op jit(solution)/shard_map/ppermute | solution.py:645
  274.0 10.6 %collective-permute-start.43 = (bf16[176,384]{1,0:T(8,128)(2,1)S(1)}, bf16[176,384]{1,0:T(8,128)(2,1)S(1)}, u32[]{:S(2)}, u32[]{:S(2)}) collective-permute-start(bf16[176,384]{1,0:T(8,128)(2,1)S(1)} %get-tuple-element.231), channel_id=1, source_target_pairs={{0,16},{4,20},{8,24},{12,28},{16,0},{20,4},{24,8},{28,12},{1,17},{... | collective-permute-start | bytes 405512 | tf_op jit(solution)/shard_map/ppermute | solution.py:651
  286.6 14.2 %collective-permute-start.45 = (f32[576,192]{0,1:T(8,128)S(1)}, f32[576,192]{0,1:T(8,128)S(1)}, u32[]{:S(2)}, u32[]{:S(2)}) collective-permute-start(f32[576,192]{0,1:T(8,128)S(1)} %copy.47), channel_id=1, source_target_pairs={{0,1},{1,0},{2,3},{3,2},{4,5},{5,4},{6,7},{7,6},{8,9},{9,8},{10,11... | collective-permute-start | bytes 1327112 | tf_op jit(solution)/shard_map/ppermute | solution.py:639
  (38 other events, 216.5 us)

commit v4 on v3

--- a/solution.py
+++ b/solution.py
@@ -175,13 +175,16 @@
         lanes = slice(first * 128, (first + tiles) * 128)
         mask = head_mask(h)
         qh = jnp.where(mask, q_ref[:, lanes], 0).astype(BF)
-        vh = jnp.where(mask, v_ref[:, lanes], 0).astype(BF)
         s = jnp.where(valid, dot(qh, k_ref[:, lanes], NT), MASK_FILL)
         top_score = jnp.max(s, axis=-1, keepdims=True)
         e = jnp.exp2((s - top_score) * (SCALE * LOG2E))
-        p = (e * (1.0 / jnp.sum(e, axis=-1, keepdims=True))).astype(BF)
-        p_ref[0, h] = p
-        o = dot(p, vh)
+        p_ref[0, h] = (e * (1.0 / jnp.sum(e, axis=-1, keepdims=True))).astype(BF)
+    for h in range(HEADS):
+        first, tiles = head_window(h)
+        lanes = slice(first * 128, (first + tiles) * 128)
+        mask = head_mask(h)
+        vh = jnp.where(mask, v_ref[:, lanes], 0).astype(BF)
+        o = dot(p_ref[0, h], vh)
         for t in range(tiles):
             part = o[:, t * 128 : (t + 1) * 128]
             at = first + t
@@ -265,6 +268,7 @@
         for n in range(grids):
             rows = slice(n * CELLS, (n + 1) * CELLS)
             n2t_ref[:, rows] = n2_ref[rows, :].T
+        dn2_acc[...] = jnp.zeros_like(dn2_acc)
         gb_ref[...] = jnp.zeros_like(gb_ref)
         gn_ref[...] = jnp.zeros_like(gn_ref)
         token_ref[...] = jnp.zeros_like(token_ref)
@@ -278,16 +282,9 @@
             gpre = (gh * gp_ref[0, rows, :].astype(F32)).astype(BF)
             gpre_ref[rows, :] = gpre
             colsum = colsum + jnp.sum(gpre.astype(F32), axis=0, keepdims=True)
-            part = dot(gpre, up_ref[0], NT)
-
-            @pl.when(j == 0)
-            def _():
-                dn2_acc[rows, :] = part
-
-            @pl.when(j > 0)
-            def _():
-                dn2_acc[rows, :] += part
-
+        for n in range(grids):
+            rows = slice(n * CELLS, (n + 1) * CELLS)
+            dn2_acc[rows, :] += dot(gpre_ref[rows, :], up_ref[0], NT)
         gb_ref[pl.ds(j, 1), :] = colsum
         keep(core, 0, dot(n2t_ref[...], gpre_ref[...]).astype(BF), mine_ref, other_ref)
 
@@ -317,7 +314,7 @@
     scal, crop, ga_ref, galow_ref, mixed_ref, p_ref, q_ref, k_ref, v_ref, emb_ref, n1_ref,
     w_ref, vec_ref, gn_ref, gb_ref,
     ig_ref, table_out, gs_out, mine_ref, other_ref, token_ref,
-    dm_ref, dq_all, dk_all, dv_all, n1t_ref, table_ref, gs_ref,
+    dm_ref, ds_ref, dq_all, dk_all, dv_all, n1t_ref, table_ref, gs_ref,
 ):
     i = pl.program_id(0)
     grids = pl.num_programs(0) - 1
@@ -341,16 +338,21 @@
             first, tiles = head_window(h)
             lanes = slice(first * 128, (first + tiles) * 128)
             mask = head_mask(h)
-            qh = jnp.where(mask, q_ref[:, lanes], 0).astype(BF)
-            kh = jnp.where(mask, k_ref[:, lanes], 0).astype(BF)
             dmh = jnp.where(mask, dm_ref[:, lanes], 0).astype(BF)
-            p = p_ref[0, h]
             dp = dot(dmh, v_ref[:, lanes], NT)
             delta = jnp.sum(
                 dmh.astype(F32) * mixed_ref[:, lanes].astype(F32), axis=-1, keepdims=True
             )
-            ds = (p.astype(F32) * (dp - delta)).astype(BF)
-            got = (dot(ds, kh), dot(ds, qh, TN), dot(p, dmh, TN))
+            ds_ref[h] = (p_ref[0, h].astype(F32) * (dp - delta)).astype(BF)
+        for h in range(HEADS):
+            first, tiles = head_window(h)
+            lanes = slice(first * 128, (first + tiles) * 128)
+            mask = head_mask(h)
+            qh = jnp.where(mask, q_ref[:, lanes], 0).astype(BF)
+            kh = jnp.where(mask, k_ref[:, lanes], 0).astype(BF)
+            dmh = jnp.where(mask, dm_ref[:, lanes], 0).astype(BF)
+            ds = ds_ref[h]
+            got = (dot(ds, kh), dot(ds, qh, TN), dot(p_ref[0, h], dmh, TN))
             for o in range(3):
                 for t in range(tiles):
                     part = got[o][:, t * 128 : (t + 1) * 128]
@@ -598,7 +600,7 @@
             whole_block(half.shape, 1), whole_block(half.shape, 1),
             whole_block((8, 128)),
         ],
-        scratch_shapes=[pltpu.VMEM((CELLS, D), BF)]
+        scratch_shapes=[pltpu.VMEM((CELLS, D), BF), pltpu.VMEM((HEADS, CELLS, CELLS), BF)]
         + [pltpu.VMEM((tokens, D), BF)] * 3
         + [pltpu.VMEM((D, tokens), BF), pltpu.VMEM((CELLS, D), F32), pltpu.VMEM((8, D), F32)],
     )
@@ -903,9 +905,9 @@
     return call(pair_kernel, "pair", where, [own, by_x], [sds((2,) + own.shape, own.dtype)], deps)
 
 
-def finish_grids(place, where, here):
+def finish_grids(where, here, there, deps=()):
     shape = sds((here.shape[0] * 2 * here.shape[1],) + here.shape[2:], here.dtype)
-    return call(collect_kernel, "collect", where, [here, place.core(here)], [shape])
+    return call(collect_kernel, "collect", where, [here, there], [shape], deps)
 
 
 def plane_kernel(where, own, by_x, by_y, by_corner, out, token):
@@ -1172,8 +1174,8 @@
         up_other, token1 = behind(up_other, token1)
         sent_x, keep2, token2 = first_x(where, up_mine, place.core(up_other), (token1,))
         got2 = place.over_x(sent_x)
-        block_output, token3 = finish_grids(place, where, out_pair)
-        deps = (token1, token2, token3)
+        out_far = place.core(out_pair)
+        deps = (token1, token2)
     ig, dtable, gs, mine3, other3, token = attention_backward(
         scal, crop_boxes, ga, galow, mixed, p, q, k, v, emb, normed1, w_attn, vec, gn, gb, grids, deps
     )
@@ -1190,6 +1192,7 @@
             where, mine3, place.core(other3), (token1, token2)
         )
         got3a, got3b = place.over_y(sent_y), place.over_x(sent_x)
+        block_output, token3 = finish_grids(where, out_pair, out_far, (token3,))
         keep2, *sent, token = split_z(where, keep2, got2, deps=(token3,))
         got2 = [place.over_z(sent[s - 1], s) for s in range(1, place.z_size)]
         sent_x, keep3a, sent_y, keep3b, token = second_both(
@@ -1199,7 +1202,7 @@
         keep3, *sent, token = split_z(where, keep3a, got3a, keep3b, got3b, deps=(token, *got2))
         got3 = [place.over_z(sent[s - 1], s) for s in range(1, place.z_size)]
         ig_pair, token = pair_grids(where, ig, ig_x, (token,))
-        input_grad, token = finish_grids(place, where, ig_pair)
+        input_grad, token = finish_grids(where, ig_pair, place.core(ig_pair))
         kept, sent, tail, packed, square, _ = totals(
             where, keep1, got1, keep2, got2, keep3, got3, (token,)
         )

time: 315 us -> 304 us (0.965)
  Pallas kernels: 134 us -> 122 us
    ppermute x11, waiting for transfers between devices: 23.2 us -> 28.2 us  [over_x(): return lax.ppermute(v, 'mp', self.x_pairs)]
    pallas_call x1, Pallas kernels: 31.5 us -> 26.7 us  [attention_backward(): pl.pallas_call(ignoring(attention_backward_kernel, 15, len(deps)), grid_s...]
    pallas_call x1, Pallas kernels: 25.2 us -> 21 us  [mlp_backward(): pl.pallas_call(ignoring(mlp_kernel, 9, len(deps)), grid_spec=spec, out_sh...]
    pallas_call x1, Pallas kernels: 20.1 us -> 16.7 us  [attention_forward(): pl.pallas_call(ignoring(attention_forward_kernel, 5, len(deps)), grid_spe...]
    ppermute x9, waiting for transfers between devices: 15.5 us -> 12.2 us  [over_y(): return lax.ppermute(v, 'dp', self.y_pairs)]
  transfers between devices with their start and end apart: 53 -> 53, of which waited for: 28 -> 30; matrix products, arithmetic and copies ran while one was open for 0% -> 0% of each run, Pallas kernels for 35% -> 31%
where the time goes in v4:
time: 304 us; the launch traced here: 301 us
  Pallas kernels  122 us (40%)
  waiting for transfers between devices  116 us (38%)
  starting transfers between devices  54.2 us (18%)
  local copies, waits for them, and re-layouts  6.3 us (2%)
    ppermute x21, waiting for transfers between devices, over_z(): return lax.ppermute(v, 'dp', self.z_shift[shift])  50.7 us
    ppermute x21, starting transfers between devices, over_z(): return lax.ppermute(v, 'dp', self.z_shift[shift])  34.8 us
    pallas_call x22, Pallas kernels, call(): pl.pallas_call(ignoring(kernel, 1 + len(ins), len(deps)), in_specs=[pl.Bl...  31.7 us
    ppermute x11, waiting for transfers between devices, over_x(): return lax.ppermute(v, 'mp', self.x_pairs)  28.2 us
    pallas_call x1, Pallas kernels, attention_backward(): pl.pallas_call(ignoring(attention_backward_kernel, 15, len(deps)), grid_s...  26.7 us
    ppermute x11, waiting for transfers between devices, core(): return lax.ppermute(v, 'mp', self.core_pairs)  22.4 us
    pallas_call x1, Pallas kernels, mlp_backward(): pl.pallas_call(ignoring(mlp_kernel, 9, len(deps)), grid_spec=spec, out_sh...  21 us
    pallas_call x1, Pallas kernels, attention_forward(): pl.pallas_call(ignoring(attention_forward_kernel, 5, len(deps)), grid_spe...  16.7 us
  transfers between devices with their start and end apart: 53, of which 30 were waited for; matrix products, arithmetic and copies ran while one was open for 0% of the time, Pallas kernels for 31%

profile of v4, /device:TPU:0, one launch (start us, length us, event | category | flops | bytes accessed | tf_op | source)
XLA Modules:
  0.0 300.7 jit_solution(6587791619525048125)
XLA Ops:
  6.7 5.0 %collective-permute-start.3 = (bf16[2,112,384]{2,1,0:T(8,128)(2,1)S(1)}, bf16[2,112,384]{2,1,0:T(8,128)(2,1)S(1)}, u32[]{:S(2)}, u32[]{:S(2)}) collective-permute-start(bf16[2,112,384]{2,1,0:T(8,128)(2,1)S(1)} %maximum_maximum_fusion.refs_1_), channel_id=1, source_target_pairs={{0,24},{4,28},{8,0},{12,4},{16,8},{20,12},{24,16},{28,20},{1,25},{... | collective-permute-start | bytes 516104 | tf_op jit(solution)/shard_map/ppermute | solution.py:653
  12.8 3.7 %collective-permute-done.3.refs_4_ = bf16[2,112,384]{2,1,0:T(8,128)(2,1)S(1)} collective-permute-done((bf16[2,112,384]{2,1,0:T(8,128)(2,1)S(1)}, bf16[2,112,384]{2,1,0:T(8,128)(2,1)S(1)}, u32[]{:S(2)}, u32[]{:S(2)}) %collective-permute-start.3) | collective-permute-done | bytes 172064 | tf_op jit(solution)/shard_map/ppermute | solution.py:653
  16.6 10.1 %collective-permute-done.2.refs_3_ = bf16[2,112,384]{2,1,0:T(8,128)(2,1)S(1)} collective-permute-done((bf16[2,112,384]{2,1,0:T(8,128)(2,1)S(1)}, bf16[2,112,384]{2,1,0:T(8,128)(2,1)S(1)}, u32[]{:S(2)}, u32[]{:S(2)}) %collective-permute-start.2) | collective-permute-done | bytes 172064 | tf_op jit(solution)/shard_map/ppermute | solution.py:653
  36.8 9.0 %collective-permute-done.7.refs_3_ = bf16[2,96,384]{2,1,0:T(8,128)(2,1)S(1)} collective-permute-done((bf16[2,96,384]{2,1,0:T(8,128)(2,1)S(1)}, bf16[2,96,384]{2,1,0:T(8,128)(2,1)S(1)}, u32[]{:S(2)}, u32[]{:S(2)}) %collective-permute-start.7) | collective-permute-done | bytes 147488 | tf_op jit(solution)/shard_map/ppermute | solution.py:653
  49.2 2.4 collective-permute-start.12
  54.4 8.2 %collective-permute-done.12.refs_3_ = bf16[2,96,384]{2,1,0:T(8,128)(2,1)S(1)} collective-permute-done((bf16[2,96,384]{2,1,0:T(8,128)(2,1)S(1)}, bf16[2,96,384]{2,1,0:T(8,128)(2,1)S(1)}, u32[]{:S(2)}, u32[]{:S(2)}) %collective-permute-start.12) | collective-permute-done | bytes 147488 | tf_op jit(solution)/shard_map/ppermute | solution.py:653
  62.6 5.6 %collective-permute-done.9.refs_5_.refs_4_.refs_2_ = bf16[1216,384]{1,0:T(8,128)(2,1)S(1)} collective-permute-done((bf16[1216,384]{1,0:T(8,128)(2,1)S(1)}, bf16[1216,384]{1,0:T(8,128)(2,1)S(1)}, u32[]{:S(2)}, u32[]{:S(2)}) %collective-permute-start.9) | collective-permute-done | bytes 933920 | tf_op jit(solution)/shard_map/ppermute | solution.py:647
  71.5 2.3 assemble.3
  75.2 4.1 %collective-permute-done.14.refs_4_ = bf16[1792,768]{1,0:T(8,128)(2,1)} collective-permute-done((bf16[1792,768]{1,0:T(8,128)(2,1)}, bf16[1792,768]{1,0:T(8,128)(2,1)}, u32[]{:S(2)}, u32[]{:S(2)}) %collective-permute-start.14) | collective-permute-done | bytes 2752544 | tf_op jit(solution)/shard_map/ppermute | solution.py:641
  79.2 2.3 copy-done.2
  81.6 16.7 %attention_forward.1 = (f32[768,768]{1,0:T(8,128)}, bf16[768,768]{1,0:T(8,128)(2,1)}, bf16[768,768]{1,0:T(8,128)(2,1)}, bf16[768,768]{1,0:T(8,128)(2,1)}, bf16[7...) custom-call(s32[4]{0:T(128)S(1)} %pad_add_fusion.1.refs_0_, ...), custom_call_target="tpu_custom_call" | custom-call | tf_op jit(solution)/shard_map/attention_forward/pallas_call | solution.py:470
  102.7 3.3 %collective-permute-done.17.refs_3_ = bf16[1536,768]{1,0:T(8,128)(2,1)S(1)} collective-permute-done((bf16[1536,768]{1,0:T(8,128)(2,1)S(1)}, bf16[1536,768]{1,0:T(8,128)(2,1)S(1)}, u32[]{:S(2)}, u32[]{:S(2)}) %collective-permute-start.17) | collective-permute-done | bytes 2359328 | tf_op jit(solution)/shard_map/ppermute | solution.py:641
  106.0 14.1 %up_forward.1 = (bf16[4,768,768]{2,1,0:T(8,128)(2,1)S(1)}, bf16[4,768,768]{2,1,0:T(8,128)(2,1)}, bf16[8,192,768]{2,1,0:T(8,128)(2,1)S(1)}, bf16[8,192,768]{2,1,0...) custom-call(s32[4]{0:T(128)S(1)} %pad_add_fusion.1.refs_0_, ...), custom_call_target="tpu_custom_call" | custom-call | tf_op jit(solution)/shard_map/up_forward/pallas_call | solution.py:502
  122.6 2.3 collective-permute-done.21.refs_2_
  128.1 6.3 %down_forward.1 = (bf16[3,256,768]{2,1,0:T(8,128)(2,1)}, bf16[4,768,768]{2,1,0:T(8,128)(2,1)}, f32[8,128]{1,0:T(8,128)S(1)}) custom-call(s32[4]{0:T(128)S(1)} %pad_add_fusion.1.refs_0_, bf16[4,768,768]{2,1,0:T(8,128)(2,1)S(1)} %get-tuple-element.153.refs_1_, bf16[1536,768]{1,0:T(8,128)(2,1)S(1)} %get-tuple-element.158.refs_2_, ...), custom_call_target="tpu_custom_call" | custom-call | tf_op jit(solution)/shard_map/down_forward/pallas_call | solution.py:534
  135.6 21.0 %mlp_backward.1 = (f32[768,768]{1,0:T(8,128)S(1)}, bf16[768,768]{1,0:T(8,128)(2,1)S(1)}, bf16[8,240,768]{2,1,0:T(8,128)(2,1)S(1)}, bf16[8,240,768]{2,1,0:T(8,128...) custom-call(s32[4]{0:T(128)S(1)} %pad_add_fusion.1.refs_0_, ...), custom_call_target="tpu_custom_call" | custom-call | tf_op jit(solution)/shard_map/mlp_backward/pallas_call | solution.py:567
  156.5 6.1 %collective-permute-done.22.refs_2_ = bf16[3,256,768]{2,1,0:T(8,128)(2,1)S(1)} collective-permute-done((bf16[3,256,768]{2,1,0:T(8,128)(2,1)}, bf16[3,256,768]{2,1,0:T(8,128)(2,1)S(1)}, u32[]{:S(2)}, u32[]{:S(2)}) %collective-permute-start.22) | collective-permute-done | bytes 1179680 | tf_op jit(solution)/shard_map/ppermute | solution.py:647
  164.5 5.4 %collective-permute-done.25.refs_2_ = bf16[8,240,768]{2,1,0:T(8,128)(2,1)S(1)} collective-permute-done((bf16[8,240,768]{2,1,0:T(8,128)(2,1)S(1)}, bf16[8,240,768]{2,1,0:T(8,128)(2,1)S(1)}, u32[]{:S(2)}, u32[]{:S(2)}) %collective-permute-start.25) | collective-permute-done | bytes 2949152 | tf_op jit(solution)/shard_map/ppermute | solution.py:641
  174.9 2.9 collective-permute-start.29
  177.8 26.7 %attention_backward.1 = (bf16[3,256,768]{2,1,0:T(8,128)(2,1)}, f32[256,768]{1,0:T(8,128)}, f32[8,768]{1,0:T(8,128)}, bf16[8,176,768]{2,1,0:T(8,128)(2,1)S(1)}, b...) custom-call(s32[4]{0:T(128)S(1)} %pad_add_fusion.1.refs_0_, s32[12,4]{1,0:T(8,128)S(1)} %copy.45.refs_1_, ...), custom_call_target="tpu_custom_call" | custom-call | tf_op jit(solution)/shard_map/attention_backward/pallas_call | solution.py:607
  209.0 2.6 collective-permute-done.30.refs_2_
  214.9 3.0 %collect.2 = (bf16[12,256,768]{2,1,0:T(8,128)(2,1)}, f32[8,128]{1,0:T(8,128)S(1)}) custom-call(s32[4]{0:T(128)S(1)} %pad_add_fusion.refs_0_, bf16[2,3,256,768]{3,2,1,0:T(8,128)(2,1)S(1)} %get-tuple-element.170.refs_1_, bf16[2,3,256,768]{3,2,1,0:T(8,128)(2,1)S(1)} %collective-permute-done.23.refs_2_, f32[8,128]{1,0:T(8,128)S(1)} %get-tuple-element.204.refs_3_), custom_call_target="tpu_custom_call" | custom-call | tf_op jit(solution)/shard_map/collect/pallas_call | solution.py:702
  217.9 9.8 %collective-permute-done.34.refs_2_ = bf16[4,240,384]{2,1,0:T(8,128)(2,1)S(1)} collective-permute-done((bf16[4,240,384]{2,1,0:T(8,128)(2,1)S(1)}, bf16[4,240,384]{2,1,0:T(8,128)(2,1)S(1)}, u32[]{:S(2)}, u32[]{:S(2)}) %collective-permute-start.34) | collective-permute-done | bytes 737312 | tf_op jit(solution)/shard_map/ppermute | solution.py:650
  228.9 15.2 %collective-permute-done.33.refs_4_ = bf16[8,64,384]{2,1,0:T(8,128)(2,1)S(1)} collective-permute-done((bf16[8,64,384]{2,1,0:T(8,128)(2,1)S(1)}, bf16[8,64,384]{2,1,0:T(8,128)(2,1)S(1)}, u32[]{:S(2)}, u32[]{:S(2)}) %collective-permute-start.33) | collective-permute-done | bytes 393248 | tf_op jit(solution)/shard_map/ppermute | solution.py:647
  246.3 2.2 collective-permute-start.38
  249.2 7.5 %collective-permute-done.38.refs_7_.refs_5_ = bf16[240,384]{1,0:T(8,128)(2,1)S(1)} collective-permute-done((bf16[240,384]{1,0:T(8,128)(2,1)S(1)}, bf16[240,384]{1,0:T(8,128)(2,1)S(1)}, u32[]{:S(2)}, u32[]{:S(2)}) %collective-permute-start.38) | collective-permute-done | bytes 184352 | tf_op jit(solution)/shard_map/ppermute | solution.py:653
  260.6 3.1 %collective-permute-start.42 = (bf16[176,384]{1,0:T(8,128)(2,1)S(1)}, bf16[176,384]{1,0:T(8,128)(2,1)S(1)}, u32[]{:S(2)}, u32[]{:S(2)}) collective-permute-start(bf16[176,384]{1,0:T(8,128)(2,1)S(1)} %get-tuple-element.230), channel_id=1, source_target_pairs={{0,8},{4,12},{8,16},{12,20},{16,24},{20,28},{24,0},{28,4},{1,9},{5... | collective-permute-start | bytes 405512 | tf_op jit(solution)/shard_map/ppermute | solution.py:653
  266.1 3.0 %collect.3 = (bf16[12,256,768]{2,1,0:T(8,128)(2,1)}, f32[8,128]{1,0:T(8,128)S(1)}) custom-call(s32[4]{0:T(128)S(1)} %pad_add_fusion.refs_0_, bf16[2,3,256,768]{3,2,1,0:T(8,128)(2,1)S(1)} %get-tuple-element.224.refs_1_, bf16[2,3,256,768]{3,2,1,0:T(8,128)(2,1)S(1)} %collective-permute-done.40.refs_2_), custom_call_target="tpu_custom_call" | custom-call | tf_op jit(solution)/shard_map/collect/pallas_call | solution.py:702
  269.1 4.8 %collective-permute-done.43.refs_9_ = bf16[176,384]{1,0:T(8,128)(2,1)S(1)} collective-permute-done((bf16[176,384]{1,0:T(8,128)(2,1)S(1)}, bf16[176,384]{1,0:T(8,128)(2,1)S(1)}, u32[]{:S(2)}, u32[]{:S(2)}) %collective-permute-start.43) | collective-permute-done | bytes 135200 | tf_op jit(solution)/shard_map/ppermute | solution.py:653
  285.1 4.8 %collective-permute-start.52 = (f32[8,128]{1,0:T(8,128)S(1)}, f32[8,128]{1,0:T(8,128)S(1)}, u32[]{:S(2)}, u32[]{:S(2)}) collective-permute-start(f32[8,128]{1,0:T(8,128)S(1)} %slice_add_fusion.refs_6_), channel_id=1, source_target_pairs={{0,24},{4,28},{8,0},{12,4},{16,8},{20,12},{24,16},{28,20},{1,25},{... | collective-permute-start | bytes 12296 | tf_op jit(solution)/shard_map/ppermute | solution.py:653
  291.2 3.2 %collective-permute-done.51.refs_8_ = f32[8,128]{1,0:T(8,128)S(1)} collective-permute-done((f32[8,128]{1,0:T(8,128)S(1)}, f32[8,128]{1,0:T(8,128)S(1)}, u32[]{:S(2)}, u32[]{:S(2)}) %collective-permute-start.51) | collective-permute-done | bytes 4128 | tf_op jit(solution)/shard_map/ppermute | solution.py:653
  295.4 5.1 %update.1 = (f32[1,1]{1,0:T(1,128)}, f32[7,96,192]{2,1,0:T(8,128)}, f32[5,192,96]{2,1,0:T(8,128)}, f32[6,24]{1,0:T(8,128)}, f32[6,96]{1,0:T(8,128)}, /*index=5*/...) custom-call(s32[4]{0:T(128)S(1)} %pad_add_fusion.refs_0_, ...), custom_call_target="tpu_custom_call" | custom-call | tf_op jit(solution)/shard_map/update/pallas_call | solution.py:1042
  (162 shorter events, 77.3 us)
Async XLA Ops:
  6.7 9.8 %collective-permute-start.3 = (bf16[2,112,384]{2,1,0:T(8,128)(2,1)S(1)}, bf16[2,112,384]{2,1,0:T(8,128)(2,1)S(1)}, u32[]{:S(2)}, u32[]{:S(2)}) collective-permute-start(bf16[2,112,384]{2,1,0:T(8,128)(2,1)S(1)} %maximum_maximum_fusion.refs_1_), channel_id=1, source_target_pairs={{0,24},{4,28},{8,0},{12,4},{16,8},{20,12},{24,16},{28,20},{1,25},{... | collective-permute-start | bytes 516104 | tf_op jit(solution)/shard_map/ppermute | solution.py:653
  11.7 14.9 %collective-permute-start.2 = (bf16[2,112,384]{2,1,0:T(8,128)(2,1)S(1)}, bf16[2,112,384]{2,1,0:T(8,128)(2,1)S(1)}, u32[]{:S(2)}, u32[]{:S(2)}) collective-permute-start(bf16[2,112,384]{2,1,0:T(8,128)(2,1)S(1)} %maximum_maximum_fusion.refs_1_), channel_id=1, source_target_pairs={{0,16},{4,20},{8,24},{12,28},{16,0},{20,4},{24,8},{28,12},{1,17},{... | collective-permute-start | bytes 516104 | tf_op jit(solution)/shard_map/ppermute | solution.py:653
  11.7 14.9 %collective-permute-start.1 = (bf16[2,112,384]{2,1,0:T(8,128)(2,1)S(1)}, bf16[2,112,384]{2,1,0:T(8,128)(2,1)S(1)}, u32[]{:S(2)}, u32[]{:S(2)}) collective-permute-start(bf16[2,112,384]{2,1,0:T(8,128)(2,1)S(1)} %maximum_maximum_fusion.refs_1_), channel_id=1, source_target_pairs={{0,8},{4,12},{8,16},{12,20},{16,24},{20,28},{24,0},{28,4},{1,9},{5... | collective-permute-start | bytes 516104 | tf_op jit(solution)/shard_map/ppermute | solution.py:653
  27.8 18.0 %collective-permute-start.5 = (bf16[896,384]{1,0:T(8,128)(2,1)S(1)}, bf16[896,384]{1,0:T(8,128)(2,1)S(1)}, u32[]{:S(2)}, u32[]{:S(2)}) collective-permute-start(bf16[896,384]{1,0:T(8,128)(2,1)S(1)} %get-tuple-element.138.refs_1_), channel_id=1, source_target_pairs={{0,4},{4,0},{8,12},{12,8},{16,20},{20,16},{24,28},{28,24},{1,5},{5... | collective-permute-start | bytes 2064392 | tf_op jit(solution)/shard_map/ppermute | solution.py:650
  29.3 16.7 %collective-permute-start.4 = (bf16[896,384]{1,0:T(8,128)(2,1)S(1)}, bf16[896,384]{1,0:T(8,128)(2,1)S(1)}, u32[]{:S(2)}, u32[]{:S(2)}) collective-permute-start(bf16[896,384]{1,0:T(8,128)(2,1)S(1)} %get-tuple-element.138.refs_1_), channel_id=1, source_target_pairs={{0,2},{1,3},{2,0},{3,1},{4,6},{5,7},{6,4},{7,5},{8,10},{9,11},{10,... | collective-permute-start | bytes 2064392 | tf_op jit(solution)/shard_map/ppermute | solution.py:647
  31.6 14.2 %collective-permute-start.7 = (bf16[2,96,384]{2,1,0:T(8,128)(2,1)S(1)}, bf16[2,96,384]{2,1,0:T(8,128)(2,1)S(1)}, u32[]{:S(2)}, u32[]{:S(2)}) collective-permute-start(bf16[2,96,384]{2,1,0:T(8,128)(2,1)S(1)} %get-tuple-element.139.refs_1_), channel_id=1, source_target_pairs={{0,16},{4,20},{8,24},{12,28},{16,0},{20,4},{24,8},{28,12},{1,17},{... | collective-permute-start | bytes 442376 | tf_op jit(solution)/shard_map/ppermute | solution.py:653
  33.6 12.2 %collective-permute-start.6 = (bf16[2,96,384]{2,1,0:T(8,128)(2,1)S(1)}, bf16[2,96,384]{2,1,0:T(8,128)(2,1)S(1)}, u32[]{:S(2)}, u32[]{:S(2)}) collective-permute-start(bf16[2,96,384]{2,1,0:T(8,128)(2,1)S(1)} %get-tuple-element.139.refs_1_), channel_id=1, source_target_pairs={{0,8},{4,12},{8,16},{12,20},{16,24},{20,28},{24,0},{28,4},{1,9},{5... | collective-permute-start | bytes 442376 | tf_op jit(solution)/shard_map/ppermute | solution.py:653
  47.2 21.1 %collective-permute-start.9 = (bf16[1216,384]{1,0:T(8,128)(2,1)S(1)}, bf16[1216,384]{1,0:T(8,128)(2,1)S(1)}, u32[]{:S(2)}, u32[]{:S(2)}) collective-permute-start(bf16[1216,384]{1,0:T(8,128)(2,1)S(1)} %get-tuple-element.140), channel_id=1, source_target_pairs={{0,2},{1,3},{2,0},{3,1},{4,6},{5,7},{6,4},{7,5},{8,10},{9,11},{10,... | collective-permute-start | bytes 2801672 | tf_op jit(solution)/shard_map/ppermute | solution.py:647
  48.7 20.8 %collective-permute-start.10 = (bf16[1216,384]{1,0:T(8,128)(2,1)S(1)}, bf16[1216,384]{1,0:T(8,128)(2,1)S(1)}, u32[]{:S(2)}, u32[]{:S(2)}) collective-permute-start(bf16[1216,384]{1,0:T(8,128)(2,1)S(1)} %get-tuple-element.141), channel_id=1, source_target_pairs={{0,4},{4,0},{8,12},{12,8},{16,20},{20,16},{24,28},{28,24},{1,5},{5... | collective-permute-start | bytes 2801672 | tf_op jit(solution)/shard_map/ppermute | solution.py:650
  49.2 13.5 %collective-permute-start.12 = (bf16[2,96,384]{2,1,0:T(8,128)(2,1)S(1)}, bf16[2,96,384]{2,1,0:T(8,128)(2,1)S(1)}, u32[]{:S(2)}, u32[]{:S(2)}) collective-permute-start(bf16[2,96,384]{2,1,0:T(8,128)(2,1)S(1)} %get-tuple-element.142.refs_1_), channel_id=1, source_target_pairs={{0,16},{4,20},{8,24},{12,28},{16,0},{20,4},{24,8},{28,12},{1,17},{... | collective-permute-start | bytes 442376 | tf_op jit(solution)/shard_map/ppermute | solution.py:653
  51.6 11.1 %collective-permute-start.11 = (bf16[2,96,384]{2,1,0:T(8,128)(2,1)S(1)}, bf16[2,96,384]{2,1,0:T(8,128)(2,1)S(1)}, u32[]{:S(2)}, u32[]{:S(2)}) collective-permute-start(bf16[2,96,384]{2,1,0:T(8,128)(2,1)S(1)} %get-tuple-element.142.refs_1_), channel_id=1, source_target_pairs={{0,8},{4,12},{8,16},{12,20},{16,24},{20,28},{24,0},{28,4},{1,9},{5... | collective-permute-start | bytes 442376 | tf_op jit(solution)/shard_map/ppermute | solution.py:653
  73.8 24.5 %collective-permute-start.15 = (bf16[1152,384]{1,0:T(8,128)(2,1)}, bf16[1152,384]{1,0:T(8,128)(2,1)S(1)}, u32[]{:S(2)}, u32[]{:S(2)}) collective-permute-start(bf16[1152,384]{1,0:T(8,128)(2,1)} %get-tuple-element.147), channel_id=1, source_target_pairs={{0,2},{1,3},{2,0},{3,1},{4,6},{5,7},{6,4},{7,5},{8,10},{9,11},{10,... | collective-permute-start | bytes 2654216 | tf_op jit(solution)/shard_map/ppermute | solution.py:647
  74.4 23.9 %collective-permute-start.16 = (bf16[1152,384]{1,0:T(8,128)(2,1)}, bf16[1152,384]{1,0:T(8,128)(2,1)}, u32[]{:S(2)}, u32[]{:S(2)}) collective-permute-start(bf16[1152,384]{1,0:T(8,128)(2,1)} %get-tuple-element.148), channel_id=1, source_target_pairs={{0,4},{4,0},{8,12},{12,8},{16,20},{20,16},{24,28},{28,24},{1,5},{5... | collective-permute-start | bytes 2654216 | tf_op jit(solution)/shard_map/ppermute | solution.py:650
  101.6 18.7 %collective-permute-start.18 = (bf16[384,384]{1,0:T(8,128)(2,1)S(1)}, bf16[384,384]{1,0:T(8,128)(2,1)S(1)}, u32[]{:S(2)}, u32[]{:S(2)}) collective-permute-start(bf16[384,384]{1,0:T(8,128)(2,1)S(1)} %get-tuple-element.155), channel_id=1, source_target_pairs={{0,2},{1,3},{2,0},{3,1},{4,6},{5,7},{6,4},{7,5},{8,10},{9,11},{10,... | collective-permute-start | bytes 884744 | tf_op jit(solution)/shard_map/ppermute | solution.py:647
  102.2 18.2 %collective-permute-start.19 = (bf16[384,384]{1,0:T(8,128)(2,1)S(1)}, bf16[384,384]{1,0:T(8,128)(2,1)S(1)}, u32[]{:S(2)}, u32[]{:S(2)}) collective-permute-start(bf16[384,384]{1,0:T(8,128)(2,1)S(1)} %get-tuple-element.156), channel_id=1, source_target_pairs={{0,4},{4,0},{8,12},{12,8},{16,20},{20,16},{24,28},{28,24},{1,5},{5... | collective-permute-start | bytes 884744 | tf_op jit(solution)/shard_map/ppermute | solution.py:650
  134.4 28.3 %collective-permute-start.22 = (bf16[3,256,768]{2,1,0:T(8,128)(2,1)}, bf16[3,256,768]{2,1,0:T(8,128)(2,1)S(1)}, u32[]{:S(2)}, u32[]{:S(2)}) collective-permute-start(bf16[3,256,768]{2,1,0:T(8,128)(2,1)} %get-tuple-element.163.refs_1_), channel_id=1, source_target_pairs={{0,2},{1,3},{2,0},{3,1},{4,6},{5,7},{6,4},{7,5},{8,10},{9,11},{10,... | collective-permute-start | bytes 3538952 | tf_op jit(solution)/shard_map/ppermute | solution.py:647
  135.0 28.4 %collective-permute-start.24 = (bf16[4,192,768]{2,1,0:T(8,128)(2,1)S(1)}, bf16[4,192,768]{2,1,0:T(8,128)(2,1)S(1)}, u32[]{:S(2)}, u32[]{:S(2)}) collective-permute-start(bf16[4,192,768]{2,1,0:T(8,128)(2,1)S(1)} %get-tuple-element.184), channel_id=1, source_target_pairs={{0,4},{4,0},{8,12},{12,8},{16,20},{20,16},{24,28},{28,24},{1,5},{5... | collective-permute-start | bytes 3538952 | tf_op jit(solution)/shard_map/ppermute | solution.py:650
  171.9 34.4 %collective-permute-start.26 = (bf16[8,240,384]{2,1,0:T(8,128)(2,1)S(1)}, bf16[8,240,384]{2,1,0:T(8,128)(2,1)S(1)}, u32[]{:S(2)}, u32[]{:S(2)}) collective-permute-start(bf16[8,240,384]{2,1,0:T(8,128)(2,1)S(1)} %get-tuple-element.194), channel_id=1, source_target_pairs={{0,2},{1,3},{2,0},{3,1},{4,6},{5,7},{6,4},{7,5},{8,10},{9,11},{10,... | collective-permute-start | bytes 4423688 | tf_op jit(solution)/shard_map/ppermute | solution.py:647
  172.5 31.9 %collective-permute-start.27 = (bf16[192,768]{1,0:T(8,128)(2,1)S(1)}, bf16[192,768]{1,0:T(8,128)(2,1)S(1)}, u32[]{:S(2)}, u32[]{:S(2)}) collective-permute-start(bf16[192,768]{1,0:T(8,128)(2,1)S(1)} %get-tuple-element.196), channel_id=1, source_target_pairs={{0,8},{4,12},{8,16},{12,20},{16,24},{20,28},{24,0},{28,4},{1,9},{5... | collective-permute-start | bytes 884744 | tf_op jit(solution)/shard_map/ppermute | solution.py:653
  172.9 31.6 %collective-permute-start.28 = (bf16[192,768]{1,0:T(8,128)(2,1)S(1)}, bf16[192,768]{1,0:T(8,128)(2,1)S(1)}, u32[]{:S(2)}, u32[]{:S(2)}) collective-permute-start(bf16[192,768]{1,0:T(8,128)(2,1)S(1)} %get-tuple-element.197), channel_id=1, source_target_pairs={{0,16},{4,20},{8,24},{12,28},{16,0},{20,4},{24,8},{28,12},{1,17},{... | collective-permute-start | bytes 884744 | tf_op jit(solution)/shard_map/ppermute | solution.py:653
  174.9 29.6 %collective-permute-start.29 = (bf16[192,768]{1,0:T(8,128)(2,1)S(1)}, bf16[192,768]{1,0:T(8,128)(2,1)S(1)}, u32[]{:S(2)}, u32[]{:S(2)}) collective-permute-start(bf16[192,768]{1,0:T(8,128)(2,1)S(1)} %get-tuple-element.198), channel_id=1, source_target_pairs={{0,24},{4,28},{8,0},{12,4},{16,8},{20,12},{24,16},{28,20},{1,25},{... | collective-permute-start | bytes 884744 | tf_op jit(solution)/shard_map/ppermute | solution.py:653
  207.8 50.4 %collective-permute-start.31 = (bf16[3,256,768]{2,1,0:T(8,128)(2,1)S(1)}, bf16[3,256,768]{2,1,0:T(8,128)(2,1)S(1)}, u32[]{:S(2)}, u32[]{:S(2)}) collective-permute-start(bf16[3,256,768]{2,1,0:T(8,128)(2,1)S(1)} %copy-done.7), channel_id=1, source_target_pairs={{0,2},{1,3},{2,0},{3,1},{4,6},{5,7},{6,4},{7,5},{8,10},{9,11},{10,... | collective-permute-start | bytes 3538952 | tf_op jit(solution)/shard_map/ppermute | solution.py:647
  208.4 19.4 %collective-permute-start.34 = (bf16[4,240,384]{2,1,0:T(8,128)(2,1)S(1)}, bf16[4,240,384]{2,1,0:T(8,128)(2,1)S(1)}, u32[]{:S(2)}, u32[]{:S(2)}) collective-permute-start(bf16[4,240,384]{2,1,0:T(8,128)(2,1)S(1)} %get-tuple-element.212), channel_id=1, source_target_pairs={{0,4},{4,0},{8,12},{12,8},{16,20},{20,16},{24,28},{28,24},{1,5},{5... | collective-permute-start | bytes 2211848 | tf_op jit(solution)/shard_map/ppermute | solution.py:650
  212.7 31.5 %collective-permute-start.32 = (bf16[4,112,768]{2,1,0:T(8,128)(2,1)S(1)}, bf16[4,112,768]{2,1,0:T(8,128)(2,1)S(1)}, u32[]{:S(2)}, u32[]{:S(2)}) collective-permute-start(bf16[4,112,768]{2,1,0:T(8,128)(2,1)S(1)} %get-tuple-element.208), channel_id=1, source_target_pairs={{0,4},{4,0},{8,12},{12,8},{16,20},{20,16},{24,28},{28,24},{1,5},{5... | collective-permute-start | bytes 2064392 | tf_op jit(solution)/shard_map/ppermute | solution.py:650
  213.3 30.8 %collective-permute-start.33 = (bf16[8,64,384]{2,1,0:T(8,128)(2,1)S(1)}, bf16[8,64,384]{2,1,0:T(8,128)(2,1)S(1)}, u32[]{:S(2)}, u32[]{:S(2)}) collective-permute-start(bf16[8,64,384]{2,1,0:T(8,128)(2,1)S(1)} %get-tuple-element.210), channel_id=1, source_target_pairs={{0,2},{1,3},{2,0},{3,1},{4,6},{5,7},{6,4},{7,5},{8,10},{9,11},{10,... | collective-permute-start | bytes 1179656 | tf_op jit(solution)/shard_map/ppermute | solution.py:647
  228.5 20.1 %collective-permute-start.37 = (bf16[240,384]{1,0:T(8,128)(2,1)S(1)}, bf16[240,384]{1,0:T(8,128)(2,1)S(1)}, u32[]{:S(2)}, u32[]{:S(2)}) collective-permute-start(bf16[240,384]{1,0:T(8,128)(2,1)S(1)} %get-tuple-element.220), channel_id=1, source_target_pairs={{0,8},{4,12},{8,16},{12,20},{16,24},{20,28},{24,0},{28,4},{1,9},{5... | collective-permute-start | bytes 552968 | tf_op jit(solution)/shard_map/ppermute | solution.py:653
  245.1 12.4 %collective-permute-start.35 = (bf16[4,112,384]{2,1,0:T(8,128)(2,1)S(1)}, bf16[4,112,384]{2,1,0:T(8,128)(2,1)S(1)}, u32[]{:S(2)}, u32[]{:S(2)}) collective-permute-start(bf16[4,112,384]{2,1,0:T(8,128)(2,1)S(1)} %get-tuple-element.216), channel_id=1, source_target_pairs={{0,2},{1,3},{2,0},{3,1},{4,6},{5,7},{6,4},{7,5},{8,10},{9,11},{10,... | collective-permute-start | bytes 1032200 | tf_op jit(solution)/shard_map/ppermute | solution.py:647
  245.8 11.8 %collective-permute-start.36 = (bf16[4,64,384]{2,1,0:T(8,128)(2,1)S(1)}, bf16[4,64,384]{2,1,0:T(8,128)(2,1)S(1)}, u32[]{:S(2)}, u32[]{:S(2)}) collective-permute-start(bf16[4,64,384]{2,1,0:T(8,128)(2,1)S(1)} %get-tuple-element.218), channel_id=1, source_target_pairs={{0,4},{4,0},{8,12},{12,8},{16,20},{20,16},{24,28},{28,24},{1,5},{5... | collective-permute-start | bytes 589832 | tf_op jit(solution)/shard_map/ppermute | solution.py:650
  246.3 10.4 %collective-permute-start.38 = (bf16[240,384]{1,0:T(8,128)(2,1)S(1)}, bf16[240,384]{1,0:T(8,128)(2,1)S(1)}, u32[]{:S(2)}, u32[]{:S(2)}) collective-permute-start(bf16[240,384]{1,0:T(8,128)(2,1)S(1)} %get-tuple-element.221), channel_id=1, source_target_pairs={{0,16},{4,20},{8,24},{12,28},{16,0},{20,4},{24,8},{28,12},{1,17},{... | collective-permute-start | bytes 552968 | tf_op jit(solution)/shard_map/ppermute | solution.py:653
  263.7 10.3 %collective-permute-start.43 = (bf16[176,384]{1,0:T(8,128)(2,1)S(1)}, bf16[176,384]{1,0:T(8,128)(2,1)S(1)}, u32[]{:S(2)}, u32[]{:S(2)}) collective-permute-start(bf16[176,384]{1,0:T(8,128)(2,1)S(1)} %get-tuple-element.231), channel_id=1, source_target_pairs={{0,16},{4,20},{8,24},{12,28},{16,0},{20,4},{24,8},{28,12},{1,17},{... | collective-permute-start | bytes 405512 | tf_op jit(solution)/shard_map/ppermute | solution.py:653
  264.0 9.9 %collective-permute-start.44 = (bf16[176,384]{1,0:T(8,128)(2,1)S(1)}, bf16[176,384]{1,0:T(8,128)(2,1)S(1)}, u32[]{:S(2)}, u32[]{:S(2)}) collective-permute-start(bf16[176,384]{1,0:T(8,128)(2,1)S(1)} %get-tuple-element.232), channel_id=1, source_target_pairs={{0,24},{4,28},{8,0},{12,4},{16,8},{20,12},{24,16},{28,20},{1,25},{... | collective-permute-start | bytes 405512 | tf_op jit(solution)/shard_map/ppermute | solution.py:653
  276.0 14.5 %collective-permute-start.45 = (f32[576,192]{0,1:T(8,128)S(1)}, f32[576,192]{0,1:T(8,128)S(1)}, u32[]{:S(2)}, u32[]{:S(2)}) collective-permute-start(f32[576,192]{0,1:T(8,128)S(1)} %copy.47), channel_id=1, source_target_pairs={{0,1},{1,0},{2,3},{3,2},{4,5},{5,4},{6,7},{7,6},{8,9},{9,8},{10,11... | collective-permute-start | bytes 1327112 | tf_op jit(solution)/shard_map/ppermute | solution.py:641
  (38 other events, 223.2 us)

commit v5 on v4

--- a/solution.py
+++ b/solution.py
@@ -930,21 +930,28 @@
 ROWS = ROWS1 + ROWS2 + ROWS3
 
 
+def sums_kernel(where, keep, *refs):
+    got, (total, token) = refs[:-2], refs[-2:]
+    token[...] = jnp.zeros_like(token)
+    value = keep[...].astype(F32)
+    for ref in got:
+        value = value + ref[...].astype(F32)
+    total[...] = value
+
+
+def sums(where, keep, got, deps=()):
+    return call(sums_kernel, "sums", where, [keep, *got], [sds(keep.shape, F32)], deps)
+
+
 def totals_kernel(where, *refs):
-    keep1, got1, keep2, *got2 = refs[:6]
-    keep3, *got3 = refs[6:10]
-    kept_ref, sent_ref, tail_ref, packed_ref, square_ref, token = refs[10:]
+    keep1, got1, total2, keep3, *got3 = refs[:-6]
+    kept_ref, sent_ref, tail_ref, packed_ref, square_ref, token = refs[-6:]
     token[...] = jnp.zeros_like(token)
     x, c = where[2], where[3]
-
-    def total(first, others):
-        value = first[...].astype(F32)
-        for ref in others:
-            value = value + ref[...].astype(F32)
-        return value
-
-    whole3 = total(keep3, got3)
-    parts = (total(keep1, [got1]), total(keep2, got2), whole3[:ROWS3])
+    whole3 = keep3[...].astype(F32)
+    for ref in got3:
+        whole3 = whole3 + ref[...].astype(F32)
+    parts = (add(keep1[...], got1[...]), total2[...], whole3[:ROWS3])
     wide = D // 4
     row = 0
     square = jnp.zeros((1, D // 2), F32)
@@ -978,8 +985,8 @@
     packed_ref[16:24, :] = square_ref[...]
 
 
-def totals(where, keep1, got1, keep2, got2, keep3, got3, deps=()):
-    ins = [keep1, got1, keep2, *got2, keep3, *got3]
+def totals(where, keep1, got1, total2, keep3, got3, deps=()):
+    ins = [keep1, got1, total2, keep3, *got3]
     half = sds((ROWS, D // 4), F32)
     shapes = [half, half] + [sds((rows, D // 2), F32) for rows in (SMALL, 24, 8)]
     return call(totals_kernel, "totals", where, ins, shapes, deps)
@@ -1066,6 +1073,7 @@
     front_second, back_second, split_second, norm_second, table_second,
 ):
     place = Place(dp_size, mp_size)
+    block_input = pltpu.with_memory_space_constraint(block_input, pltpu.HBM)
     direct = dp_size == 8 and mp_size == 4
     x, y, z, c = place.x, place.y, place.z, place.c
     grids = block_input.shape[0] // mp_size
@@ -1195,16 +1203,17 @@
         block_output, token3 = finish_grids(where, out_pair, out_far, (token3,))
         keep2, *sent, token = split_z(where, keep2, got2, deps=(token3,))
         got2 = [place.over_z(sent[s - 1], s) for s in range(1, place.z_size)]
+        total2, token = sums(where, keep2, got2, (token,))
         sent_x, keep3a, sent_y, keep3b, token = second_both(
             where, keep3a, got3a, keep3b, got3b, (token,)
         )
         got3a, got3b = place.over_x(sent_x), place.over_y(sent_y)
-        keep3, *sent, token = split_z(where, keep3a, got3a, keep3b, got3b, deps=(token, *got2))
+        ig_pair, token = pair_grids(where, ig, ig_x, (token,))
+        keep3, *sent, token = split_z(where, keep3a, got3a, keep3b, got3b, deps=(token,))
         got3 = [place.over_z(sent[s - 1], s) for s in range(1, place.z_size)]
-        ig_pair, token = pair_grids(where, ig, ig_x, (token,))
-        input_grad, token = finish_grids(where, ig_pair, place.core(ig_pair))
+        input_grad, token = finish_grids(where, ig_pair, place.core(ig_pair), (token,))
         kept, sent, tail, packed, square, _ = totals(
-            where, keep1, got1, keep2, got2, keep3, got3, (token,)
+            where, keep1, got1, total2, keep3, got3, (token,)
         )
         got = place.core(sent)
         here, there, squares = sum_plane(place, where, packed, square)

time: 304 us -> 302 us (level)
  waiting for transfers between devices: 116 us -> 110 us
  starting transfers between devices: 54.2 us -> 60 us
    ppermute x11, waiting for transfers between devices: 28.2 us -> 14.9 us  [over_x(): return lax.ppermute(v, 'mp', self.x_pairs)]
    ppermute x9, waiting for transfers between devices: 12.2 us -> 18 us  [over_y(): return lax.ppermute(v, 'dp', self.y_pairs)]
    ppermute x11, starting transfers between devices: 9.26 us -> 13.9 us  [over_x(): return lax.ppermute(v, 'mp', self.x_pairs)]
    ppermute x21, waiting for transfers between devices: 50.7 us -> 55.3 us  [over_z(): return lax.ppermute(v, 'dp', self.z_shift[shift])]
    pallas_call x22 -> x23, Pallas kernels: 31.7 us -> 32 us  [call(): pl.pallas_call(ignoring(kernel, 1 + len(ins), len(deps)), in_specs=[pl.Bl...]
  transfers between devices with their start and end apart: 53 -> 53, of which waited for: 30 -> 34; matrix products, arithmetic and copies ran while one was open for 0% -> 0% of each run, Pallas kernels for 31% -> 32%
where the time goes in v5:
time: 302 us; the launch traced here: 299 us
  Pallas kernels  122 us (40%)
  waiting for transfers between devices  110 us (36%)
  starting transfers between devices  60 us (20%)
  local copies, waits for them, and re-layouts  3.7 us (1%)
    ppermute x21, waiting for transfers between devices, over_z(): return lax.ppermute(v, 'dp', self.z_shift[shift])  55.3 us
    ppermute x21, starting transfers between devices, over_z(): return lax.ppermute(v, 'dp', self.z_shift[shift])  35.9 us
    pallas_call x23, Pallas kernels, call(): pl.pallas_call(ignoring(kernel, 1 + len(ins), len(deps)), in_specs=[pl.Bl...  32 us
    pallas_call x1, Pallas kernels, attention_backward(): pl.pallas_call(ignoring(attention_backward_kernel, 15, len(deps)), grid_s...  26.5 us
    pallas_call x1, Pallas kernels, mlp_backward(): pl.pallas_call(ignoring(mlp_kernel, 9, len(deps)), grid_spec=spec, out_sh...  20.9 us
    ppermute x11, waiting for transfers between devices, core(): return lax.ppermute(v, 'mp', self.core_pairs)  19.9 us
    ppermute x9, waiting for transfers between devices, over_y(): return lax.ppermute(v, 'dp', self.y_pairs)  18 us
    pallas_call x1, Pallas kernels, attention_forward(): pl.pallas_call(ignoring(attention_forward_kernel, 5, len(deps)), grid_spe...  16.9 us
  transfers between devices with their start and end apart: 53, of which 34 were waited for; matrix products, arithmetic and copies ran while one was open for 0% of the time, Pallas kernels for 32%

profile of v5, /device:TPU:0, one launch (start us, length us, event | category | flops | bytes accessed | tf_op | source)
XLA Modules:
  0.0 298.6 jit_solution(7125028591602924934)
XLA Ops:
  6.7 5.0 %collective-permute-start.3 = (bf16[2,112,384]{2,1,0:T(8,128)(2,1)S(1)}, bf16[2,112,384]{2,1,0:T(8,128)(2,1)S(1)}, u32[]{:S(2)}, u32[]{:S(2)}) collective-permute-start(bf16[2,112,384]{2,1,0:T(8,128)(2,1)S(1)} %maximum_maximum_fusion.refs_1_), channel_id=1, source_target_pairs={{0,24},{4,28},{8,0},{12,4},{16,8},{20,12},{24,16},{28,20},{1,25},{... | collective-permute-start | bytes 516104 | tf_op jit(solution)/shard_map/ppermute | solution.py:653
  12.8 3.7 %collective-permute-done.3.refs_4_ = bf16[2,112,384]{2,1,0:T(8,128)(2,1)S(1)} collective-permute-done((bf16[2,112,384]{2,1,0:T(8,128)(2,1)S(1)}, bf16[2,112,384]{2,1,0:T(8,128)(2,1)S(1)}, u32[]{:S(2)}, u32[]{:S(2)}) %collective-permute-start.3) | collective-permute-done | bytes 172064 | tf_op jit(solution)/shard_map/ppermute | solution.py:653
  16.6 10.1 %collective-permute-done.2.refs_3_ = bf16[2,112,384]{2,1,0:T(8,128)(2,1)S(1)} collective-permute-done((bf16[2,112,384]{2,1,0:T(8,128)(2,1)S(1)}, bf16[2,112,384]{2,1,0:T(8,128)(2,1)S(1)}, u32[]{:S(2)}, u32[]{:S(2)}) %collective-permute-start.2) | collective-permute-done | bytes 172064 | tf_op jit(solution)/shard_map/ppermute | solution.py:653
  36.8 9.0 %collective-permute-done.7.refs_3_ = bf16[2,96,384]{2,1,0:T(8,128)(2,1)S(1)} collective-permute-done((bf16[2,96,384]{2,1,0:T(8,128)(2,1)S(1)}, bf16[2,96,384]{2,1,0:T(8,128)(2,1)S(1)}, u32[]{:S(2)}, u32[]{:S(2)}) %collective-permute-start.7) | collective-permute-done | bytes 147488 | tf_op jit(solution)/shard_map/ppermute | solution.py:653
  49.2 2.4 collective-permute-start.12
  51.6 2.5 collective-permute-start.11
  54.4 8.2 %collective-permute-done.12.refs_3_ = bf16[2,96,384]{2,1,0:T(8,128)(2,1)S(1)} collective-permute-done((bf16[2,96,384]{2,1,0:T(8,128)(2,1)S(1)}, bf16[2,96,384]{2,1,0:T(8,128)(2,1)S(1)}, u32[]{:S(2)}, u32[]{:S(2)}) %collective-permute-start.12) | collective-permute-done | bytes 147488 | tf_op jit(solution)/shard_map/ppermute | solution.py:653
  62.6 5.6 %collective-permute-done.9.refs_5_.refs_4_.refs_2_ = bf16[1216,384]{1,0:T(8,128)(2,1)S(1)} collective-permute-done((bf16[1216,384]{1,0:T(8,128)(2,1)S(1)}, bf16[1216,384]{1,0:T(8,128)(2,1)S(1)}, u32[]{:S(2)}, u32[]{:S(2)}) %collective-permute-start.9) | collective-permute-done | bytes 933920 | tf_op jit(solution)/shard_map/ppermute | solution.py:647
  75.2 4.1 %collective-permute-done.14.refs_4_ = bf16[1792,768]{1,0:T(8,128)(2,1)} collective-permute-done((bf16[1792,768]{1,0:T(8,128)(2,1)}, bf16[1792,768]{1,0:T(8,128)(2,1)}, u32[]{:S(2)}, u32[]{:S(2)}) %collective-permute-start.14) | collective-permute-done | bytes 2752544 | tf_op jit(solution)/shard_map/ppermute | solution.py:641
  79.2 16.9 %attention_forward.1 = (f32[768,768]{1,0:T(8,128)}, bf16[768,768]{1,0:T(8,128)(2,1)}, bf16[768,768]{1,0:T(8,128)(2,1)}, bf16[768,768]{1,0:T(8,128)(2,1)}, bf16[7...) custom-call(s32[4]{0:T(128)S(1)} %pad_add_fusion.1.refs_0_, ...), custom_call_target="tpu_custom_call" | custom-call | tf_op jit(solution)/shard_map/attention_forward/pallas_call | solution.py:470
  101.6 2.4 collective-permute-done.17.refs_3_
  104.1 14.1 %up_forward.1 = (bf16[4,768,768]{2,1,0:T(8,128)(2,1)S(1)}, bf16[4,768,768]{2,1,0:T(8,128)(2,1)}, bf16[8,192,768]{2,1,0:T(8,128)(2,1)S(1)}, bf16[8,192,768]{2,1,0...) custom-call(s32[4]{0:T(128)S(1)} %pad_add_fusion.1.refs_0_, ...), custom_call_target="tpu_custom_call" | custom-call | tf_op jit(solution)/shard_map/up_forward/pallas_call | solution.py:502
  126.2 6.3 %down_forward.1 = (bf16[3,256,768]{2,1,0:T(8,128)(2,1)}, bf16[4,768,768]{2,1,0:T(8,128)(2,1)}, f32[8,128]{1,0:T(8,128)S(1)}) custom-call(s32[4]{0:T(128)S(1)} %pad_add_fusion.1.refs_0_, bf16[4,768,768]{2,1,0:T(8,128)(2,1)S(1)} %get-tuple-element.156.refs_1_, bf16[1536,768]{1,0:T(8,128)(2,1)S(1)} %get-tuple-element.161.refs_2_, ...), custom_call_target="tpu_custom_call" | custom-call | tf_op jit(solution)/shard_map/down_forward/pallas_call | solution.py:534
  134.6 20.9 %mlp_backward.1 = (f32[768,768]{1,0:T(8,128)S(1)}, bf16[768,768]{1,0:T(8,128)(2,1)S(1)}, bf16[8,240,768]{2,1,0:T(8,128)(2,1)S(1)}, bf16[8,240,768]{2,1,0:T(8,128...) custom-call(s32[4]{0:T(128)S(1)} %pad_add_fusion.1.refs_0_, ...), custom_call_target="tpu_custom_call" | custom-call | tf_op jit(solution)/shard_map/mlp_backward/pallas_call | solution.py:567
  155.5 5.2 %collective-permute-done.22.refs_2_ = bf16[3,256,768]{2,1,0:T(8,128)(2,1)S(1)} collective-permute-done((bf16[3,256,768]{2,1,0:T(8,128)(2,1)}, bf16[3,256,768]{2,1,0:T(8,128)(2,1)S(1)}, u32[]{:S(2)}, u32[]{:S(2)}) %collective-permute-start.22) | collective-permute-done | bytes 1179680 | tf_op jit(solution)/shard_map/ppermute | solution.py:647
  162.7 5.4 %collective-permute-done.25.refs_2_ = bf16[8,240,768]{2,1,0:T(8,128)(2,1)S(1)} collective-permute-done((bf16[8,240,768]{2,1,0:T(8,128)(2,1)S(1)}, bf16[8,240,768]{2,1,0:T(8,128)(2,1)S(1)}, u32[]{:S(2)}, u32[]{:S(2)}) %collective-permute-start.25) | collective-permute-done | bytes 2949152 | tf_op jit(solution)/shard_map/ppermute | solution.py:641
  173.5 2.9 collective-permute-start.29
  176.4 26.5 %attention_backward.1 = (bf16[3,256,768]{2,1,0:T(8,128)(2,1)}, f32[256,768]{1,0:T(8,128)}, f32[8,768]{1,0:T(8,128)}, bf16[8,176,768]{2,1,0:T(8,128)(2,1)S(1)}, b...) custom-call(s32[4]{0:T(128)S(1)} %pad_add_fusion.1.refs_0_, s32[12,4]{1,0:T(8,128)S(1)} %copy.45.refs_1_, ...), custom_call_target="tpu_custom_call" | custom-call | tf_op jit(solution)/shard_map/attention_backward/pallas_call | solution.py:607
  213.0 3.0 %collect.2 = (bf16[12,256,768]{2,1,0:T(8,128)(2,1)}, f32[8,128]{1,0:T(8,128)S(1)}) custom-call(s32[4]{0:T(128)S(1)} %pad_add_fusion.refs_0_, bf16[2,3,256,768]{3,2,1,0:T(8,128)(2,1)S(1)} %get-tuple-element.173.refs_1_, bf16[2,3,256,768]{3,2,1,0:T(8,128)(2,1)S(1)} %collective-permute-done.23.refs_2_, f32[8,128]{1,0:T(8,128)S(1)} %get-tuple-element.207.refs_3_), custom_call_target="tpu_custom_call" | custom-call | tf_op jit(solution)/shard_map/collect/pallas_call | solution.py:702
  216.1 10.7 %collective-permute-done.34.refs_2_ = bf16[4,240,384]{2,1,0:T(8,128)(2,1)S(1)} collective-permute-done((bf16[4,240,384]{2,1,0:T(8,128)(2,1)S(1)}, bf16[4,240,384]{2,1,0:T(8,128)(2,1)S(1)}, u32[]{:S(2)}, u32[]{:S(2)}) %collective-permute-start.34) | collective-permute-done | bytes 737312 | tf_op jit(solution)/shard_map/ppermute | solution.py:650
  229.6 6.2 %collective-permute-done.35.refs_2_ = bf16[240,384]{1,0:T(8,128)(2,1)S(1)} collective-permute-done((bf16[240,384]{1,0:T(8,128)(2,1)S(1)}, bf16[240,384]{1,0:T(8,128)(2,1)S(1)}, u32[]{:S(2)}, u32[]{:S(2)}) %collective-permute-start.35) | collective-permute-done | bytes 184352 | tf_op jit(solution)/shard_map/ppermute | solution.py:653
  235.8 5.9 %collective-permute-done.36.refs_3_ = bf16[240,384]{1,0:T(8,128)(2,1)S(1)} collective-permute-done((bf16[240,384]{1,0:T(8,128)(2,1)S(1)}, bf16[240,384]{1,0:T(8,128)(2,1)S(1)}, u32[]{:S(2)}, u32[]{:S(2)}) %collective-permute-start.36) | collective-permute-done | bytes 184352 | tf_op jit(solution)/shard_map/ppermute | solution.py:653
  241.7 3.3 %collective-permute-done.37.refs_4_ = bf16[240,384]{1,0:T(8,128)(2,1)S(1)} collective-permute-done((bf16[240,384]{1,0:T(8,128)(2,1)S(1)}, bf16[240,384]{1,0:T(8,128)(2,1)S(1)}, u32[]{:S(2)}, u32[]{:S(2)}) %collective-permute-start.37) | collective-permute-done | bytes 184352 | tf_op jit(solution)/shard_map/ppermute | solution.py:653
  250.4 5.1 %collective-permute-done.40.refs_4_ = bf16[4,64,384]{2,1,0:T(8,128)(2,1)S(1)} collective-permute-done((bf16[4,64,384]{2,1,0:T(8,128)(2,1)S(1)}, bf16[4,64,384]{2,1,0:T(8,128)(2,1)S(1)}, u32[]{:S(2)}, u32[]{:S(2)}) %collective-permute-start.40) | collective-permute-done | bytes 196640 | tf_op jit(solution)/shard_map/ppermute | solution.py:650
  255.5 3.1 %collective-permute-done.39.refs_2_ = bf16[4,112,384]{2,1,0:T(8,128)(2,1)S(1)} collective-permute-done((bf16[4,112,384]{2,1,0:T(8,128)(2,1)S(1)}, bf16[4,112,384]{2,1,0:T(8,128)(2,1)S(1)}, u32[]{:S(2)}, u32[]{:S(2)}) %collective-permute-start.39) | collective-permute-done | bytes 344096 | tf_op jit(solution)/shard_map/ppermute | solution.py:647
  259.3 2.5 collective-permute-start.42
  263.4 2.8 collective-permute-start.44
  266.2 3.0 %collect.3 = (bf16[12,256,768]{2,1,0:T(8,128)(2,1)}, f32[8,128]{1,0:T(8,128)S(1)}) custom-call(s32[4]{0:T(128)S(1)} %pad_add_fusion.refs_0_, bf16[2,3,256,768]{3,2,1,0:T(8,128)(2,1)S(1)} %get-tuple-element.224.refs_1_, bf16[2,3,256,768]{3,2,1,0:T(8,128)(2,1)S(1)} %collective-permute-done.38.refs_2_, f32[8,128]{1,0:T(8,128)S(1)} %get-tuple-element.230.refs_3_), custom_call_target="tpu_custom_call" | custom-call | tf_op jit(solution)/shard_map/collect/pallas_call | solution.py:702
  269.3 2.7 collective-permute-done.43.refs_6_
  282.1 5.6 %collective-permute-start.52 = (f32[8,128]{1,0:T(8,128)S(1)}, f32[8,128]{1,0:T(8,128)S(1)}, u32[]{:S(2)}, u32[]{:S(2)}) collective-permute-start(f32[8,128]{1,0:T(8,128)S(1)} %slice_add_fusion.refs_6_), channel_id=1, source_target_pairs={{0,24},{4,28},{8,0},{12,4},{16,8},{20,12},{24,16},{28,20},{1,25},{... | collective-permute-start | bytes 12296 | tf_op jit(solution)/shard_map/ppermute | solution.py:653
  289.1 3.2 %collective-permute-done.51.refs_8_ = f32[8,128]{1,0:T(8,128)S(1)} collective-permute-done((f32[8,128]{1,0:T(8,128)S(1)}, f32[8,128]{1,0:T(8,128)S(1)}, u32[]{:S(2)}, u32[]{:S(2)}) %collective-permute-start.51) | collective-permute-done | bytes 4128 | tf_op jit(solution)/shard_map/ppermute | solution.py:653
  293.2 5.1 %update.1 = (f32[1,1]{1,0:T(1,128)}, f32[7,96,192]{2,1,0:T(8,128)}, f32[5,192,96]{2,1,0:T(8,128)}, f32[6,24]{1,0:T(8,128)}, f32[6,96]{1,0:T(8,128)}, /*index=5*/...) custom-call(s32[4]{0:T(128)S(1)} %pad_add_fusion.refs_0_, ...), custom_call_target="tpu_custom_call" | custom-call | tf_op jit(solution)/shard_map/update/pallas_call | solution.py:1049
  (161 shorter events, 83.5 us)
Async XLA Ops:
  6.7 9.8 %collective-permute-start.3 = (bf16[2,112,384]{2,1,0:T(8,128)(2,1)S(1)}, bf16[2,112,384]{2,1,0:T(8,128)(2,1)S(1)}, u32[]{:S(2)}, u32[]{:S(2)}) collective-permute-start(bf16[2,112,384]{2,1,0:T(8,128)(2,1)S(1)} %maximum_maximum_fusion.refs_1_), channel_id=1, source_target_pairs={{0,24},{4,28},{8,0},{12,4},{16,8},{20,12},{24,16},{28,20},{1,25},{... | collective-permute-start | bytes 516104 | tf_op jit(solution)/shard_map/ppermute | solution.py:653
  11.7 14.9 %collective-permute-start.2 = (bf16[2,112,384]{2,1,0:T(8,128)(2,1)S(1)}, bf16[2,112,384]{2,1,0:T(8,128)(2,1)S(1)}, u32[]{:S(2)}, u32[]{:S(2)}) collective-permute-start(bf16[2,112,384]{2,1,0:T(8,128)(2,1)S(1)} %maximum_maximum_fusion.refs_1_), channel_id=1, source_target_pairs={{0,16},{4,20},{8,24},{12,28},{16,0},{20,4},{24,8},{28,12},{1,17},{... | collective-permute-start | bytes 516104 | tf_op jit(solution)/shard_map/ppermute | solution.py:653
  11.7 14.9 %collective-permute-start.1 = (bf16[2,112,384]{2,1,0:T(8,128)(2,1)S(1)}, bf16[2,112,384]{2,1,0:T(8,128)(2,1)S(1)}, u32[]{:S(2)}, u32[]{:S(2)}) collective-permute-start(bf16[2,112,384]{2,1,0:T(8,128)(2,1)S(1)} %maximum_maximum_fusion.refs_1_), channel_id=1, source_target_pairs={{0,8},{4,12},{8,16},{12,20},{16,24},{20,28},{24,0},{28,4},{1,9},{5... | collective-permute-start | bytes 516104 | tf_op jit(solution)/shard_map/ppermute | solution.py:653
  27.8 18.0 %collective-permute-start.5 = (bf16[896,384]{1,0:T(8,128)(2,1)S(1)}, bf16[896,384]{1,0:T(8,128)(2,1)S(1)}, u32[]{:S(2)}, u32[]{:S(2)}) collective-permute-start(bf16[896,384]{1,0:T(8,128)(2,1)S(1)} %get-tuple-element.141.refs_1_), channel_id=1, source_target_pairs={{0,4},{4,0},{8,12},{12,8},{16,20},{20,16},{24,28},{28,24},{1,5},{5... | collective-permute-start | bytes 2064392 | tf_op jit(solution)/shard_map/ppermute | solution.py:650
  29.3 16.7 %collective-permute-start.4 = (bf16[896,384]{1,0:T(8,128)(2,1)S(1)}, bf16[896,384]{1,0:T(8,128)(2,1)S(1)}, u32[]{:S(2)}, u32[]{:S(2)}) collective-permute-start(bf16[896,384]{1,0:T(8,128)(2,1)S(1)} %get-tuple-element.141.refs_1_), channel_id=1, source_target_pairs={{0,2},{1,3},{2,0},{3,1},{4,6},{5,7},{6,4},{7,5},{8,10},{9,11},{10,... | collective-permute-start | bytes 2064392 | tf_op jit(solution)/shard_map/ppermute | solution.py:647
  31.6 14.2 %collective-permute-start.7 = (bf16[2,96,384]{2,1,0:T(8,128)(2,1)S(1)}, bf16[2,96,384]{2,1,0:T(8,128)(2,1)S(1)}, u32[]{:S(2)}, u32[]{:S(2)}) collective-permute-start(bf16[2,96,384]{2,1,0:T(8,128)(2,1)S(1)} %get-tuple-element.142.refs_1_), channel_id=1, source_target_pairs={{0,16},{4,20},{8,24},{12,28},{16,0},{20,4},{24,8},{28,12},{1,17},{... | collective-permute-start | bytes 442376 | tf_op jit(solution)/shard_map/ppermute | solution.py:653
  33.6 12.2 %collective-permute-start.6 = (bf16[2,96,384]{2,1,0:T(8,128)(2,1)S(1)}, bf16[2,96,384]{2,1,0:T(8,128)(2,1)S(1)}, u32[]{:S(2)}, u32[]{:S(2)}) collective-permute-start(bf16[2,96,384]{2,1,0:T(8,128)(2,1)S(1)} %get-tuple-element.142.refs_1_), channel_id=1, source_target_pairs={{0,8},{4,12},{8,16},{12,20},{16,24},{20,28},{24,0},{28,4},{1,9},{5... | collective-permute-start | bytes 442376 | tf_op jit(solution)/shard_map/ppermute | solution.py:653
  47.2 21.1 %collective-permute-start.9 = (bf16[1216,384]{1,0:T(8,128)(2,1)S(1)}, bf16[1216,384]{1,0:T(8,128)(2,1)S(1)}, u32[]{:S(2)}, u32[]{:S(2)}) collective-permute-start(bf16[1216,384]{1,0:T(8,128)(2,1)S(1)} %get-tuple-element.143), channel_id=1, source_target_pairs={{0,2},{1,3},{2,0},{3,1},{4,6},{5,7},{6,4},{7,5},{8,10},{9,11},{10,... | collective-permute-start | bytes 2801672 | tf_op jit(solution)/shard_map/ppermute | solution.py:647
  48.7 20.8 %collective-permute-start.10 = (bf16[1216,384]{1,0:T(8,128)(2,1)S(1)}, bf16[1216,384]{1,0:T(8,128)(2,1)S(1)}, u32[]{:S(2)}, u32[]{:S(2)}) collective-permute-start(bf16[1216,384]{1,0:T(8,128)(2,1)S(1)} %get-tuple-element.144), channel_id=1, source_target_pairs={{0,4},{4,0},{8,12},{12,8},{16,20},{20,16},{24,28},{28,24},{1,5},{5... | collective-permute-start | bytes 2801672 | tf_op jit(solution)/shard_map/ppermute | solution.py:650
  49.2 13.5 %collective-permute-start.12 = (bf16[2,96,384]{2,1,0:T(8,128)(2,1)S(1)}, bf16[2,96,384]{2,1,0:T(8,128)(2,1)S(1)}, u32[]{:S(2)}, u32[]{:S(2)}) collective-permute-start(bf16[2,96,384]{2,1,0:T(8,128)(2,1)S(1)} %get-tuple-element.145.refs_1_), channel_id=1, source_target_pairs={{0,16},{4,20},{8,24},{12,28},{16,0},{20,4},{24,8},{28,12},{1,17},{... | collective-permute-start | bytes 442376 | tf_op jit(solution)/shard_map/ppermute | solution.py:653
  51.6 11.1 %collective-permute-start.11 = (bf16[2,96,384]{2,1,0:T(8,128)(2,1)S(1)}, bf16[2,96,384]{2,1,0:T(8,128)(2,1)S(1)}, u32[]{:S(2)}, u32[]{:S(2)}) collective-permute-start(bf16[2,96,384]{2,1,0:T(8,128)(2,1)S(1)} %get-tuple-element.145.refs_1_), channel_id=1, source_target_pairs={{0,8},{4,12},{8,16},{12,20},{16,24},{20,28},{24,0},{28,4},{1,9},{5... | collective-permute-start | bytes 442376 | tf_op jit(solution)/shard_map/ppermute | solution.py:653
  73.8 22.3 %collective-permute-start.15 = (bf16[1152,384]{1,0:T(8,128)(2,1)}, bf16[1152,384]{1,0:T(8,128)(2,1)S(1)}, u32[]{:S(2)}, u32[]{:S(2)}) collective-permute-start(bf16[1152,384]{1,0:T(8,128)(2,1)} %get-tuple-element.150), channel_id=1, source_target_pairs={{0,2},{1,3},{2,0},{3,1},{4,6},{5,7},{6,4},{7,5},{8,10},{9,11},{10,... | collective-permute-start | bytes 2654216 | tf_op jit(solution)/shard_map/ppermute | solution.py:647
  74.4 22.0 %collective-permute-start.16 = (bf16[1152,384]{1,0:T(8,128)(2,1)}, bf16[1152,384]{1,0:T(8,128)(2,1)}, u32[]{:S(2)}, u32[]{:S(2)}) collective-permute-start(bf16[1152,384]{1,0:T(8,128)(2,1)} %get-tuple-element.151), channel_id=1, source_target_pairs={{0,4},{4,0},{8,12},{12,8},{16,20},{20,16},{24,28},{28,24},{1,5},{5... | collective-permute-start | bytes 2654216 | tf_op jit(solution)/shard_map/ppermute | solution.py:650
  99.6 18.9 %collective-permute-start.18 = (bf16[384,384]{1,0:T(8,128)(2,1)S(1)}, bf16[384,384]{1,0:T(8,128)(2,1)S(1)}, u32[]{:S(2)}, u32[]{:S(2)}) collective-permute-start(bf16[384,384]{1,0:T(8,128)(2,1)S(1)} %get-tuple-element.158), channel_id=1, source_target_pairs={{0,2},{1,3},{2,0},{3,1},{4,6},{5,7},{6,4},{7,5},{8,10},{9,11},{10,... | collective-permute-start | bytes 884744 | tf_op jit(solution)/shard_map/ppermute | solution.py:647
  101.0 17.4 %collective-permute-start.19 = (bf16[384,384]{1,0:T(8,128)(2,1)S(1)}, bf16[384,384]{1,0:T(8,128)(2,1)S(1)}, u32[]{:S(2)}, u32[]{:S(2)}) collective-permute-start(bf16[384,384]{1,0:T(8,128)(2,1)S(1)} %get-tuple-element.159), channel_id=1, source_target_pairs={{0,4},{4,0},{8,12},{12,8},{16,20},{20,16},{24,28},{28,24},{1,5},{5... | collective-permute-start | bytes 884744 | tf_op jit(solution)/shard_map/ppermute | solution.py:650
  132.5 28.3 %collective-permute-start.22 = (bf16[3,256,768]{2,1,0:T(8,128)(2,1)}, bf16[3,256,768]{2,1,0:T(8,128)(2,1)S(1)}, u32[]{:S(2)}, u32[]{:S(2)}) collective-permute-start(bf16[3,256,768]{2,1,0:T(8,128)(2,1)} %get-tuple-element.166.refs_1_), channel_id=1, source_target_pairs={{0,2},{1,3},{2,0},{3,1},{4,6},{5,7},{6,4},{7,5},{8,10},{9,11},{10,... | collective-permute-start | bytes 3538952 | tf_op jit(solution)/shard_map/ppermute | solution.py:647
  134.0 27.7 %collective-permute-start.24 = (bf16[4,192,768]{2,1,0:T(8,128)(2,1)S(1)}, bf16[4,192,768]{2,1,0:T(8,128)(2,1)S(1)}, u32[]{:S(2)}, u32[]{:S(2)}) collective-permute-start(bf16[4,192,768]{2,1,0:T(8,128)(2,1)S(1)} %get-tuple-element.187), channel_id=1, source_target_pairs={{0,4},{4,0},{8,12},{12,8},{16,20},{20,16},{24,28},{28,24},{1,5},{5... | collective-permute-start | bytes 3538952 | tf_op jit(solution)/shard_map/ppermute | solution.py:650
  170.0 34.4 %collective-permute-start.26 = (bf16[8,240,384]{2,1,0:T(8,128)(2,1)S(1)}, bf16[8,240,384]{2,1,0:T(8,128)(2,1)S(1)}, u32[]{:S(2)}, u32[]{:S(2)}) collective-permute-start(bf16[8,240,384]{2,1,0:T(8,128)(2,1)S(1)} %get-tuple-element.197), channel_id=1, source_target_pairs={{0,2},{1,3},{2,0},{3,1},{4,6},{5,7},{6,4},{7,5},{8,10},{9,11},{10,... | collective-permute-start | bytes 4423688 | tf_op jit(solution)/shard_map/ppermute | solution.py:647
  171.5 31.4 %collective-permute-start.27 = (bf16[192,768]{1,0:T(8,128)(2,1)S(1)}, bf16[192,768]{1,0:T(8,128)(2,1)S(1)}, u32[]{:S(2)}, u32[]{:S(2)}) collective-permute-start(bf16[192,768]{1,0:T(8,128)(2,1)S(1)} %get-tuple-element.199), channel_id=1, source_target_pairs={{0,8},{4,12},{8,16},{12,20},{16,24},{20,28},{24,0},{28,4},{1,9},{5... | collective-permute-start | bytes 884744 | tf_op jit(solution)/shard_map/ppermute | solution.py:653
  171.6 31.4 %collective-permute-start.28 = (bf16[192,768]{1,0:T(8,128)(2,1)S(1)}, bf16[192,768]{1,0:T(8,128)(2,1)S(1)}, u32[]{:S(2)}, u32[]{:S(2)}) collective-permute-start(bf16[192,768]{1,0:T(8,128)(2,1)S(1)} %get-tuple-element.200), channel_id=1, source_target_pairs={{0,16},{4,20},{8,24},{12,28},{16,0},{20,4},{24,8},{28,12},{1,17},{... | collective-permute-start | bytes 884744 | tf_op jit(solution)/shard_map/ppermute | solution.py:653
  173.5 29.5 %collective-permute-start.29 = (bf16[192,768]{1,0:T(8,128)(2,1)S(1)}, bf16[192,768]{1,0:T(8,128)(2,1)S(1)}, u32[]{:S(2)}, u32[]{:S(2)}) collective-permute-start(bf16[192,768]{1,0:T(8,128)(2,1)S(1)} %get-tuple-element.201), channel_id=1, source_target_pairs={{0,24},{4,28},{8,0},{12,4},{16,8},{20,12},{24,16},{28,20},{1,25},{... | collective-permute-start | bytes 884744 | tf_op jit(solution)/shard_map/ppermute | solution.py:653
  205.9 41.0 %collective-permute-start.31 = (bf16[3,256,768]{2,1,0:T(8,128)(2,1)S(1)}, bf16[3,256,768]{2,1,0:T(8,128)(2,1)S(1)}, u32[]{:S(2)}, u32[]{:S(2)}) collective-permute-start(bf16[3,256,768]{2,1,0:T(8,128)(2,1)S(1)} %copy-done.6), channel_id=1, source_target_pairs={{0,2},{1,3},{2,0},{3,1},{4,6},{5,7},{6,4},{7,5},{8,10},{9,11},{10,... | collective-permute-start | bytes 3538952 | tf_op jit(solution)/shard_map/ppermute | solution.py:647
  207.3 19.4 %collective-permute-start.34 = (bf16[4,240,384]{2,1,0:T(8,128)(2,1)S(1)}, bf16[4,240,384]{2,1,0:T(8,128)(2,1)S(1)}, u32[]{:S(2)}, u32[]{:S(2)}) collective-permute-start(bf16[4,240,384]{2,1,0:T(8,128)(2,1)S(1)} %get-tuple-element.215), channel_id=1, source_target_pairs={{0,4},{4,0},{8,12},{12,8},{16,20},{20,16},{24,28},{28,24},{1,5},{5... | collective-permute-start | bytes 2211848 | tf_op jit(solution)/shard_map/ppermute | solution.py:650
  210.8 34.9 %collective-permute-start.32 = (bf16[4,112,768]{2,1,0:T(8,128)(2,1)S(1)}, bf16[4,112,768]{2,1,0:T(8,128)(2,1)S(1)}, u32[]{:S(2)}, u32[]{:S(2)}) collective-permute-start(bf16[4,112,768]{2,1,0:T(8,128)(2,1)S(1)} %get-tuple-element.211), channel_id=1, source_target_pairs={{0,4},{4,0},{8,12},{12,8},{16,20},{20,16},{24,28},{28,24},{1,5},{5... | collective-permute-start | bytes 2064392 | tf_op jit(solution)/shard_map/ppermute | solution.py:650
  211.5 34.2 %collective-permute-start.33 = (bf16[8,64,384]{2,1,0:T(8,128)(2,1)S(1)}, bf16[8,64,384]{2,1,0:T(8,128)(2,1)S(1)}, u32[]{:S(2)}, u32[]{:S(2)}) collective-permute-start(bf16[8,64,384]{2,1,0:T(8,128)(2,1)S(1)} %get-tuple-element.213), channel_id=1, source_target_pairs={{0,2},{1,3},{2,0},{3,1},{4,6},{5,7},{6,4},{7,5},{8,10},{9,11},{10,... | collective-permute-start | bytes 1179656 | tf_op jit(solution)/shard_map/ppermute | solution.py:647
  227.6 14.1 %collective-permute-start.36 = (bf16[240,384]{1,0:T(8,128)(2,1)S(1)}, bf16[240,384]{1,0:T(8,128)(2,1)S(1)}, u32[]{:S(2)}, u32[]{:S(2)}) collective-permute-start(bf16[240,384]{1,0:T(8,128)(2,1)S(1)} %get-tuple-element.219), channel_id=1, source_target_pairs={{0,16},{4,20},{8,24},{12,28},{16,0},{20,4},{24,8},{28,12},{1,17},{... | collective-permute-start | bytes 552968 | tf_op jit(solution)/shard_map/ppermute | solution.py:653
  247.6 18.6 %collective-permute-start.38 = (bf16[2,3,256,768]{3,2,1,0:T(8,128)(2,1)S(1)}, bf16[2,3,256,768]{3,2,1,0:T(8,128)(2,1)S(1)}, u32[]{:S(2)}, u32[]{:S(2)}) collective-permute-start(bf16[2,3,256,768]{3,2,1,0:T(8,128)(2,1)S(1)} %get-tuple-element.224.refs_1_), channel_id=1, source_target_pairs={{0,1},{1,0},{2,3},{3,2},{4,5},{5,4},{6,7},{7,6},{8,9},{9,8},{10,11... | collective-permute-start | bytes 7077896 | tf_op jit(solution)/shard_map/ppermute | solution.py:641
  247.7 10.9 %collective-permute-start.39 = (bf16[4,112,384]{2,1,0:T(8,128)(2,1)S(1)}, bf16[4,112,384]{2,1,0:T(8,128)(2,1)S(1)}, u32[]{:S(2)}, u32[]{:S(2)}) collective-permute-start(bf16[4,112,384]{2,1,0:T(8,128)(2,1)S(1)} %get-tuple-element.226), channel_id=1, source_target_pairs={{0,2},{1,3},{2,0},{3,1},{4,6},{5,7},{6,4},{7,5},{8,10},{9,11},{10,... | collective-permute-start | bytes 1032200 | tf_op jit(solution)/shard_map/ppermute | solution.py:647
  249.0 20.3 %collective-permute-start.41 = (bf16[192,384]{1,0:T(8,128)(2,1)S(1)}, bf16[192,384]{1,0:T(8,128)(2,1)S(1)}, u32[]{:S(2)}, u32[]{:S(2)}) collective-permute-start(bf16[192,384]{1,0:T(8,128)(2,1)S(1)} %get-tuple-element.233), channel_id=1, source_target_pairs={{0,2},{1,3},{2,0},{3,1},{4,6},{5,7},{6,4},{7,5},{8,10},{9,11},{10,... | collective-permute-start | bytes 442376 | tf_op jit(solution)/shard_map/ppermute | solution.py:647
  259.3 10.0 %collective-permute-start.42 = (bf16[176,384]{1,0:T(8,128)(2,1)S(1)}, bf16[176,384]{1,0:T(8,128)(2,1)S(1)}, u32[]{:S(2)}, u32[]{:S(2)}) collective-permute-start(bf16[176,384]{1,0:T(8,128)(2,1)S(1)} %get-tuple-element.236), channel_id=1, source_target_pairs={{0,8},{4,12},{8,16},{12,20},{16,24},{20,28},{24,0},{28,4},{1,9},{5... | collective-permute-start | bytes 405512 | tf_op jit(solution)/shard_map/ppermute | solution.py:653
  261.8 10.1 %collective-permute-start.43 = (bf16[176,384]{1,0:T(8,128)(2,1)S(1)}, bf16[176,384]{1,0:T(8,128)(2,1)S(1)}, u32[]{:S(2)}, u32[]{:S(2)}) collective-permute-start(bf16[176,384]{1,0:T(8,128)(2,1)S(1)} %get-tuple-element.237), channel_id=1, source_target_pairs={{0,16},{4,20},{8,24},{12,28},{16,0},{20,4},{24,8},{28,12},{1,17},{... | collective-permute-start | bytes 405512 | tf_op jit(solution)/shard_map/ppermute | solution.py:653
  273.9 14.5 %collective-permute-start.45 = (f32[576,192]{0,1:T(8,128)S(1)}, f32[576,192]{0,1:T(8,128)S(1)}, u32[]{:S(2)}, u32[]{:S(2)}) collective-permute-start(f32[576,192]{0,1:T(8,128)S(1)} %copy.47), channel_id=1, source_target_pairs={{0,1},{1,0},{2,3},{3,2},{4,5},{5,4},{6,7},{7,6},{8,9},{9,8},{10,11... | collective-permute-start | bytes 1327112 | tf_op jit(solution)/shard_map/ppermute | solution.py:641
  (37 other events, 221.4 us)

commit v6 on v5

--- a/solution.py
+++ b/solution.py
@@ -1106,15 +1106,16 @@
             where, gather_z(place, unit2), x1, y1, (0, size1, size1), units, 2
         )
         y2, x2 = place.over_y(sent_y), place.over_x(sent_x)
+        parts3 = gather_z(place, unit3)
+        attn_mine, token = assemble(
+            where, ((0, 0), (1, 0), (2, 0), (4, 0), (3, 0)), (own1, x1, y1, x2, y2), extra, dp_size,
+            tuple(parts3[1:]),
+        )
+        attn_other = place.core(attn_mine)
         own3, sent_y, sent_x, token3 = pack(
-            where, gather_z(place, unit3), x2, y2, (size1, size1 + size2, size2)
+            where, parts3, x2, y2, (size1, size1 + size2, size2), deps=(token,)
         )
         y3, x3 = place.over_y(sent_y), place.over_x(sent_x)
-        attn_mine, _ = assemble(
-            where, ((0, 0), (1, 0), (2, 0), (4, 0), (3, 0)), (own1, x1, y1, x2, y2), extra, dp_size,
-            (token3,),
-        )
-        attn_other = place.core(attn_mine)
         first_deps = (token3,)
     else:
 
@@ -1147,13 +1148,13 @@
     )
     deps = ()
     if direct:
+        half, token = assemble(
+            where, ((0, 0), (1, size1), (2, size1), (4, 0), (3, 0)), (own2, x2, y2, x3, y3), 0, dp_size,
+            (token,),
+        )
+        up_pair = half, place.core(half)
         sent_y, sent_x, token4 = pack(where, [], x3, y3, (size2, 2 * size2, size2), deps=(token,))
         y4, x4 = place.over_y(sent_y), place.over_x(sent_x)
-        half, _ = assemble(
-            where, ((0, 0), (1, size1), (2, size1), (4, 0), (3, 0)), (own2, x2, y2, x3, y3), 0, dp_size,
-            (token4,),
-        )
-        up_pair = half, place.core(half)
         deps = (token4,)
     hidden, gp, down_mine, down_other, w_up, token = up_forward(
         scal, normed2, *up_pair, vec, cotangent, grids, deps

time: 302 us -> 301 us (level)
    ppermute x11, waiting for transfers between devices: 19.9 us -> 15.9 us  [core(): return lax.ppermute(v, 'mp', self.core_pairs)]
  transfers between devices with their start and end apart: 53 -> 53, of which waited for: 34 -> 35; matrix products, arithmetic and copies ran while one was open for 0% -> 0% of each run, Pallas kernels for 32% -> 33%
where the time goes in v6:
time: 301 us; the launch traced here: 298 us
  Pallas kernels  121 us (40%)
  waiting for transfers between devices  109 us (36%)
  starting transfers between devices  60.1 us (20%)
  local copies, waits for them, and re-layouts  4.49 us (1%)
    ppermute x21, waiting for transfers between devices, over_z(): return lax.ppermute(v, 'dp', self.z_shift[shift])  55.3 us
    ppermute x21, starting transfers between devices, over_z(): return lax.ppermute(v, 'dp', self.z_shift[shift])  35.9 us
    pallas_call x23, Pallas kernels, call(): pl.pallas_call(ignoring(kernel, 1 + len(ins), len(deps)), in_specs=[pl.Bl...  31.5 us
    pallas_call x1, Pallas kernels, attention_backward(): pl.pallas_call(ignoring(attention_backward_kernel, 15, len(deps)), grid_s...  26.5 us
    pallas_call x1, Pallas kernels, mlp_backward(): pl.pallas_call(ignoring(mlp_kernel, 9, len(deps)), grid_spec=spec, out_sh...  20.9 us
    ppermute x9, waiting for transfers between devices, over_y(): return lax.ppermute(v, 'dp', self.y_pairs)  18 us
    ppermute x11, waiting for transfers between devices, over_x(): return lax.ppermute(v, 'mp', self.x_pairs)  17.6 us
    pallas_call x1, Pallas kernels, attention_forward(): pl.pallas_call(ignoring(attention_forward_kernel, 5, len(deps)), grid_spe...  16.9 us
  transfers between devices with their start and end apart: 53, of which 35 were waited for; matrix products, arithmetic and copies ran while one was open for 0% of the time, Pallas kernels for 33%

profile of v6, /device:TPU:0, one launch (start us, length us, event | category | flops | bytes accessed | tf_op | source)
XLA Modules:
  0.0 297.7 jit_solution(9116287698228988699)
XLA Ops:
  6.7 5.0 %collective-permute-start.3 = (bf16[2,112,384]{2,1,0:T(8,128)(2,1)S(1)}, bf16[2,112,384]{2,1,0:T(8,128)(2,1)S(1)}, u32[]{:S(2)}, u32[]{:S(2)}) collective-permute-start(bf16[2,112,384]{2,1,0:T(8,128)(2,1)S(1)} %maximum_maximum_fusion.refs_1_), channel_id=1, source_target_pairs={{0,24},{4,28},{8,0},{12,4},{16,8},{20,12},{24,16},{28,20},{1,25},{... | collective-permute-start | bytes 516104 | tf_op jit(solution)/shard_map/ppermute | solution.py:653
  12.8 3.7 %collective-permute-done.3.refs_4_ = bf16[2,112,384]{2,1,0:T(8,128)(2,1)S(1)} collective-permute-done((bf16[2,112,384]{2,1,0:T(8,128)(2,1)S(1)}, bf16[2,112,384]{2,1,0:T(8,128)(2,1)S(1)}, u32[]{:S(2)}, u32[]{:S(2)}) %collective-permute-start.3) | collective-permute-done | bytes 172064 | tf_op jit(solution)/shard_map/ppermute | solution.py:653
  16.6 10.1 %collective-permute-done.2.refs_3_ = bf16[2,112,384]{2,1,0:T(8,128)(2,1)S(1)} collective-permute-done((bf16[2,112,384]{2,1,0:T(8,128)(2,1)S(1)}, bf16[2,112,384]{2,1,0:T(8,128)(2,1)S(1)}, u32[]{:S(2)}, u32[]{:S(2)}) %collective-permute-start.2) | collective-permute-done | bytes 172064 | tf_op jit(solution)/shard_map/ppermute | solution.py:653
  36.8 9.0 %collective-permute-done.7.refs_3_ = bf16[2,96,384]{2,1,0:T(8,128)(2,1)S(1)} collective-permute-done((bf16[2,96,384]{2,1,0:T(8,128)(2,1)S(1)}, bf16[2,96,384]{2,1,0:T(8,128)(2,1)S(1)}, u32[]{:S(2)}, u32[]{:S(2)}) %collective-permute-start.7) | collective-permute-done | bytes 147488 | tf_op jit(solution)/shard_map/ppermute | solution.py:653
  49.2 2.4 collective-permute-start.12
  51.6 2.5 collective-permute-start.11
  54.4 8.2 %collective-permute-done.12.refs_7_.refs_3_ = bf16[2,96,384]{2,1,0:T(8,128)(2,1)S(1)} collective-permute-done((bf16[2,96,384]{2,1,0:T(8,128)(2,1)S(1)}, bf16[2,96,384]{2,1,0:T(8,128)(2,1)S(1)}, u32[]{:S(2)}, u32[]{:S(2)}) %collective-permute-start.12) | collective-permute-done | bytes 147488 | tf_op jit(solution)/shard_map/ppermute | solution.py:653
  62.6 5.6 %collective-permute-done.9.refs_4_.refs_5_.refs_2_ = bf16[1216,384]{1,0:T(8,128)(2,1)S(1)} collective-permute-done((bf16[1216,384]{1,0:T(8,128)(2,1)S(1)}, bf16[1216,384]{1,0:T(8,128)(2,1)S(1)}, u32[]{:S(2)}, u32[]{:S(2)}) %collective-permute-start.9) | collective-permute-done | bytes 933920 | tf_op jit(solution)/shard_map/ppermute | solution.py:647
  77.3 16.9 %attention_forward.1 = (f32[768,768]{1,0:T(8,128)}, bf16[768,768]{1,0:T(8,128)(2,1)}, bf16[768,768]{1,0:T(8,128)(2,1)}, bf16[768,768]{1,0:T(8,128)(2,1)}, bf16[7...) custom-call(s32[4]{0:T(128)S(1)} %pad_add_fusion.1.refs_0_, ...), custom_call_target="tpu_custom_call" | custom-call | tf_op jit(solution)/shard_map/attention_forward/pallas_call | solution.py:470
  94.1 2.7 collective-permute-done.15.refs_4_.refs_1_.refs_2_
  103.2 14.1 %up_forward.1 = (bf16[4,768,768]{2,1,0:T(8,128)(2,1)S(1)}, bf16[4,768,768]{2,1,0:T(8,128)(2,1)}, bf16[8,192,768]{2,1,0:T(8,128)(2,1)S(1)}, bf16[8,192,768]{2,1,0...) custom-call(s32[4]{0:T(128)S(1)} %pad_add_fusion.1.refs_0_, ...), custom_call_target="tpu_custom_call" | custom-call | tf_op jit(solution)/shard_map/up_forward/pallas_call | solution.py:502
  119.8 2.3 collective-permute-done.21.refs_2_
  125.3 6.3 %down_forward.1 = (bf16[3,256,768]{2,1,0:T(8,128)(2,1)}, bf16[4,768,768]{2,1,0:T(8,128)(2,1)}, f32[8,128]{1,0:T(8,128)S(1)}) custom-call(s32[4]{0:T(128)S(1)} %pad_add_fusion.1.refs_0_, bf16[4,768,768]{2,1,0:T(8,128)(2,1)S(1)} %get-tuple-element.160.refs_1_, bf16[1536,768]{1,0:T(8,128)(2,1)S(1)} %get-tuple-element.165.refs_2_, ...), custom_call_target="tpu_custom_call" | custom-call | tf_op jit(solution)/shard_map/down_forward/pallas_call | solution.py:534
  133.8 20.9 %mlp_backward.1 = (f32[768,768]{1,0:T(8,128)S(1)}, bf16[768,768]{1,0:T(8,128)(2,1)S(1)}, bf16[8,240,768]{2,1,0:T(8,128)(2,1)S(1)}, bf16[8,240,768]{2,1,0:T(8,128...) custom-call(s32[4]{0:T(128)S(1)} %pad_add_fusion.1.refs_0_, ...), custom_call_target="tpu_custom_call" | custom-call | tf_op jit(solution)/shard_map/mlp_backward/pallas_call | solution.py:567
  154.7 5.2 %collective-permute-done.22.refs_2_ = bf16[3,256,768]{2,1,0:T(8,128)(2,1)S(1)} collective-permute-done((bf16[3,256,768]{2,1,0:T(8,128)(2,1)}, bf16[3,256,768]{2,1,0:T(8,128)(2,1)S(1)}, u32[]{:S(2)}, u32[]{:S(2)}) %collective-permute-start.22) | collective-permute-done | bytes 1179680 | tf_op jit(solution)/shard_map/ppermute | solution.py:647
  161.8 5.4 %collective-permute-done.25.refs_2_ = bf16[8,240,768]{2,1,0:T(8,128)(2,1)S(1)} collective-permute-done((bf16[8,240,768]{2,1,0:T(8,128)(2,1)S(1)}, bf16[8,240,768]{2,1,0:T(8,128)(2,1)S(1)}, u32[]{:S(2)}, u32[]{:S(2)}) %collective-permute-start.25) | collective-permute-done | bytes 2949152 | tf_op jit(solution)/shard_map/ppermute | solution.py:641
  172.7 2.9 collective-permute-start.29
  175.6 26.5 %attention_backward.1 = (bf16[3,256,768]{2,1,0:T(8,128)(2,1)}, f32[256,768]{1,0:T(8,128)}, f32[8,768]{1,0:T(8,128)}, bf16[8,176,768]{2,1,0:T(8,128)(2,1)S(1)}, b...) custom-call(s32[4]{0:T(128)S(1)} %pad_add_fusion.1.refs_0_, s32[12,4]{1,0:T(8,128)S(1)} %copy.45.refs_1_, ...), custom_call_target="tpu_custom_call" | custom-call | tf_op jit(solution)/shard_map/attention_backward/pallas_call | solution.py:607
  212.2 3.0 %collect.2 = (bf16[12,256,768]{2,1,0:T(8,128)(2,1)}, f32[8,128]{1,0:T(8,128)S(1)}) custom-call(s32[4]{0:T(128)S(1)} %pad_add_fusion.refs_0_, bf16[2,3,256,768]{3,2,1,0:T(8,128)(2,1)S(1)} %get-tuple-element.177.refs_1_, bf16[2,3,256,768]{3,2,1,0:T(8,128)(2,1)S(1)} %collective-permute-done.23.refs_2_, f32[8,128]{1,0:T(8,128)S(1)} %get-tuple-element.211.refs_3_), custom_call_target="tpu_custom_call" | custom-call | tf_op jit(solution)/shard_map/collect/pallas_call | solution.py:702
  215.2 10.7 %collective-permute-done.34.refs_2_ = bf16[4,240,384]{2,1,0:T(8,128)(2,1)S(1)} collective-permute-done((bf16[4,240,384]{2,1,0:T(8,128)(2,1)S(1)}, bf16[4,240,384]{2,1,0:T(8,128)(2,1)S(1)}, u32[]{:S(2)}, u32[]{:S(2)}) %collective-permute-start.34) | collective-permute-done | bytes 737312 | tf_op jit(solution)/shard_map/ppermute | solution.py:650
  228.7 6.2 %collective-permute-done.35.refs_2_ = bf16[240,384]{1,0:T(8,128)(2,1)S(1)} collective-permute-done((bf16[240,384]{1,0:T(8,128)(2,1)S(1)}, bf16[240,384]{1,0:T(8,128)(2,1)S(1)}, u32[]{:S(2)}, u32[]{:S(2)}) %collective-permute-start.35) | collective-permute-done | bytes 184352 | tf_op jit(solution)/shard_map/ppermute | solution.py:653
  234.9 5.9 %collective-permute-done.36.refs_3_ = bf16[240,384]{1,0:T(8,128)(2,1)S(1)} collective-permute-done((bf16[240,384]{1,0:T(8,128)(2,1)S(1)}, bf16[240,384]{1,0:T(8,128)(2,1)S(1)}, u32[]{:S(2)}, u32[]{:S(2)}) %collective-permute-start.36) | collective-permute-done | bytes 184352 | tf_op jit(solution)/shard_map/ppermute | solution.py:653
  240.8 3.3 %collective-permute-done.37.refs_4_ = bf16[240,384]{1,0:T(8,128)(2,1)S(1)} collective-permute-done((bf16[240,384]{1,0:T(8,128)(2,1)S(1)}, bf16[240,384]{1,0:T(8,128)(2,1)S(1)}, u32[]{:S(2)}, u32[]{:S(2)}) %collective-permute-start.37) | collective-permute-done | bytes 184352 | tf_op jit(solution)/shard_map/ppermute | solution.py:653
  249.5 5.1 %collective-permute-done.40.refs_4_ = bf16[4,64,384]{2,1,0:T(8,128)(2,1)S(1)} collective-permute-done((bf16[4,64,384]{2,1,0:T(8,128)(2,1)S(1)}, bf16[4,64,384]{2,1,0:T(8,128)(2,1)S(1)}, u32[]{:S(2)}, u32[]{:S(2)}) %collective-permute-start.40) | collective-permute-done | bytes 196640 | tf_op jit(solution)/shard_map/ppermute | solution.py:650
  254.6 3.2 %collective-permute-done.39.refs_2_ = bf16[4,112,384]{2,1,0:T(8,128)(2,1)S(1)} collective-permute-done((bf16[4,112,384]{2,1,0:T(8,128)(2,1)S(1)}, bf16[4,112,384]{2,1,0:T(8,128)(2,1)S(1)}, u32[]{:S(2)}, u32[]{:S(2)}) %collective-permute-start.39) | collective-permute-done | bytes 344096 | tf_op jit(solution)/shard_map/ppermute | solution.py:647
  258.5 2.5 collective-permute-start.42
  262.5 2.8 collective-permute-start.44
  265.4 3.0 %collect.3 = (bf16[12,256,768]{2,1,0:T(8,128)(2,1)}, f32[8,128]{1,0:T(8,128)S(1)}) custom-call(s32[4]{0:T(128)S(1)} %pad_add_fusion.refs_0_, bf16[2,3,256,768]{3,2,1,0:T(8,128)(2,1)S(1)} %get-tuple-element.228.refs_1_, bf16[2,3,256,768]{3,2,1,0:T(8,128)(2,1)S(1)} %collective-permute-done.38.refs_2_, f32[8,128]{1,0:T(8,128)S(1)} %get-tuple-element.234.refs_3_), custom_call_target="tpu_custom_call" | custom-call | tf_op jit(solution)/shard_map/collect/pallas_call | solution.py:702
  268.4 2.7 collective-permute-done.43.refs_6_
  281.3 5.6 %collective-permute-start.52 = (f32[8,128]{1,0:T(8,128)S(1)}, f32[8,128]{1,0:T(8,128)S(1)}, u32[]{:S(2)}, u32[]{:S(2)}) collective-permute-start(f32[8,128]{1,0:T(8,128)S(1)} %slice_add_fusion.refs_6_), channel_id=1, source_target_pairs={{0,24},{4,28},{8,0},{12,4},{16,8},{20,12},{24,16},{28,20},{1,25},{... | collective-permute-start | bytes 12296 | tf_op jit(solution)/shard_map/ppermute | solution.py:653
  288.2 3.2 %collective-permute-done.51.refs_8_ = f32[8,128]{1,0:T(8,128)S(1)} collective-permute-done((f32[8,128]{1,0:T(8,128)S(1)}, f32[8,128]{1,0:T(8,128)S(1)}, u32[]{:S(2)}, u32[]{:S(2)}) %collective-permute-start.51) | collective-permute-done | bytes 4128 | tf_op jit(solution)/shard_map/ppermute | solution.py:653
  292.3 5.1 %update.1 = (f32[1,1]{1,0:T(1,128)}, f32[7,96,192]{2,1,0:T(8,128)}, f32[5,192,96]{2,1,0:T(8,128)}, f32[6,24]{1,0:T(8,128)}, f32[6,96]{1,0:T(8,128)}, /*index=5*/...) custom-call(s32[4]{0:T(128)S(1)} %pad_add_fusion.refs_0_, ...), custom_call_target="tpu_custom_call" | custom-call | tf_op jit(solution)/shard_map/update/pallas_call | solution.py:1049
  (161 shorter events, 84.1 us)
Async XLA Ops:
  6.7 9.8 %collective-permute-start.3 = (bf16[2,112,384]{2,1,0:T(8,128)(2,1)S(1)}, bf16[2,112,384]{2,1,0:T(8,128)(2,1)S(1)}, u32[]{:S(2)}, u32[]{:S(2)}) collective-permute-start(bf16[2,112,384]{2,1,0:T(8,128)(2,1)S(1)} %maximum_maximum_fusion.refs_1_), channel_id=1, source_target_pairs={{0,24},{4,28},{8,0},{12,4},{16,8},{20,12},{24,16},{28,20},{1,25},{... | collective-permute-start | bytes 516104 | tf_op jit(solution)/shard_map/ppermute | solution.py:653
  11.7 14.9 %collective-permute-start.2 = (bf16[2,112,384]{2,1,0:T(8,128)(2,1)S(1)}, bf16[2,112,384]{2,1,0:T(8,128)(2,1)S(1)}, u32[]{:S(2)}, u32[]{:S(2)}) collective-permute-start(bf16[2,112,384]{2,1,0:T(8,128)(2,1)S(1)} %maximum_maximum_fusion.refs_1_), channel_id=1, source_target_pairs={{0,16},{4,20},{8,24},{12,28},{16,0},{20,4},{24,8},{28,12},{1,17},{... | collective-permute-start | bytes 516104 | tf_op jit(solution)/shard_map/ppermute | solution.py:653
  11.7 14.9 %collective-permute-start.1 = (bf16[2,112,384]{2,1,0:T(8,128)(2,1)S(1)}, bf16[2,112,384]{2,1,0:T(8,128)(2,1)S(1)}, u32[]{:S(2)}, u32[]{:S(2)}) collective-permute-start(bf16[2,112,384]{2,1,0:T(8,128)(2,1)S(1)} %maximum_maximum_fusion.refs_1_), channel_id=1, source_target_pairs={{0,8},{4,12},{8,16},{12,20},{16,24},{20,28},{24,0},{28,4},{1,9},{5... | collective-permute-start | bytes 516104 | tf_op jit(solution)/shard_map/ppermute | solution.py:653
  27.8 18.0 %collective-permute-start.5 = (bf16[896,384]{1,0:T(8,128)(2,1)S(1)}, bf16[896,384]{1,0:T(8,128)(2,1)S(1)}, u32[]{:S(2)}, u32[]{:S(2)}) collective-permute-start(bf16[896,384]{1,0:T(8,128)(2,1)S(1)} %get-tuple-element.143.refs_1_), channel_id=1, source_target_pairs={{0,4},{4,0},{8,12},{12,8},{16,20},{20,16},{24,28},{28,24},{1,5},{5... | collective-permute-start | bytes 2064392 | tf_op jit(solution)/shard_map/ppermute | solution.py:650
  29.3 16.7 %collective-permute-start.4 = (bf16[896,384]{1,0:T(8,128)(2,1)S(1)}, bf16[896,384]{1,0:T(8,128)(2,1)S(1)}, u32[]{:S(2)}, u32[]{:S(2)}) collective-permute-start(bf16[896,384]{1,0:T(8,128)(2,1)S(1)} %get-tuple-element.143.refs_1_), channel_id=1, source_target_pairs={{0,2},{1,3},{2,0},{3,1},{4,6},{5,7},{6,4},{7,5},{8,10},{9,11},{10,... | collective-permute-start | bytes 2064392 | tf_op jit(solution)/shard_map/ppermute | solution.py:647
  31.6 14.2 %collective-permute-start.7 = (bf16[2,96,384]{2,1,0:T(8,128)(2,1)S(1)}, bf16[2,96,384]{2,1,0:T(8,128)(2,1)S(1)}, u32[]{:S(2)}, u32[]{:S(2)}) collective-permute-start(bf16[2,96,384]{2,1,0:T(8,128)(2,1)S(1)} %get-tuple-element.144.refs_1_), channel_id=1, source_target_pairs={{0,16},{4,20},{8,24},{12,28},{16,0},{20,4},{24,8},{28,12},{1,17},{... | collective-permute-start | bytes 442376 | tf_op jit(solution)/shard_map/ppermute | solution.py:653
  33.6 12.2 %collective-permute-start.6 = (bf16[2,96,384]{2,1,0:T(8,128)(2,1)S(1)}, bf16[2,96,384]{2,1,0:T(8,128)(2,1)S(1)}, u32[]{:S(2)}, u32[]{:S(2)}) collective-permute-start(bf16[2,96,384]{2,1,0:T(8,128)(2,1)S(1)} %get-tuple-element.144.refs_1_), channel_id=1, source_target_pairs={{0,8},{4,12},{8,16},{12,20},{16,24},{20,28},{24,0},{28,4},{1,9},{5... | collective-permute-start | bytes 442376 | tf_op jit(solution)/shard_map/ppermute | solution.py:653
  47.2 21.1 %collective-permute-start.9 = (bf16[1216,384]{1,0:T(8,128)(2,1)S(1)}, bf16[1216,384]{1,0:T(8,128)(2,1)S(1)}, u32[]{:S(2)}, u32[]{:S(2)}) collective-permute-start(bf16[1216,384]{1,0:T(8,128)(2,1)S(1)} %get-tuple-element.145), channel_id=1, source_target_pairs={{0,2},{1,3},{2,0},{3,1},{4,6},{5,7},{6,4},{7,5},{8,10},{9,11},{10,... | collective-permute-start | bytes 2801672 | tf_op jit(solution)/shard_map/ppermute | solution.py:647
  48.7 20.8 %collective-permute-start.10 = (bf16[1216,384]{1,0:T(8,128)(2,1)S(1)}, bf16[1216,384]{1,0:T(8,128)(2,1)S(1)}, u32[]{:S(2)}, u32[]{:S(2)}) collective-permute-start(bf16[1216,384]{1,0:T(8,128)(2,1)S(1)} %get-tuple-element.146), channel_id=1, source_target_pairs={{0,4},{4,0},{8,12},{12,8},{16,20},{20,16},{24,28},{28,24},{1,5},{5... | collective-permute-start | bytes 2801672 | tf_op jit(solution)/shard_map/ppermute | solution.py:650
  49.2 13.5 %collective-permute-start.12 = (bf16[2,96,384]{2,1,0:T(8,128)(2,1)S(1)}, bf16[2,96,384]{2,1,0:T(8,128)(2,1)S(1)}, u32[]{:S(2)}, u32[]{:S(2)}) collective-permute-start(bf16[2,96,384]{2,1,0:T(8,128)(2,1)S(1)} %get-tuple-element.147.refs_1_), channel_id=1, source_target_pairs={{0,16},{4,20},{8,24},{12,28},{16,0},{20,4},{24,8},{28,12},{1,17},{... | collective-permute-start | bytes 442376 | tf_op jit(solution)/shard_map/ppermute | solution.py:653
  51.6 11.1 %collective-permute-start.11 = (bf16[2,96,384]{2,1,0:T(8,128)(2,1)S(1)}, bf16[2,96,384]{2,1,0:T(8,128)(2,1)S(1)}, u32[]{:S(2)}, u32[]{:S(2)}) collective-permute-start(bf16[2,96,384]{2,1,0:T(8,128)(2,1)S(1)} %get-tuple-element.147.refs_1_), channel_id=1, source_target_pairs={{0,8},{4,12},{8,16},{12,20},{16,24},{20,28},{24,0},{28,4},{1,9},{5... | collective-permute-start | bytes 442376 | tf_op jit(solution)/shard_map/ppermute | solution.py:653
  74.6 22.3 %collective-permute-start.15 = (bf16[1152,384]{1,0:T(8,128)(2,1)}, bf16[1152,384]{1,0:T(8,128)(2,1)S(1)}, u32[]{:S(2)}, u32[]{:S(2)}) collective-permute-start(bf16[1152,384]{1,0:T(8,128)(2,1)} %get-tuple-element.153), channel_id=1, source_target_pairs={{0,2},{1,3},{2,0},{3,1},{4,6},{5,7},{6,4},{7,5},{8,10},{9,11},{10,... | collective-permute-start | bytes 2654216 | tf_op jit(solution)/shard_map/ppermute | solution.py:647
  75.1 22.1 %collective-permute-start.16 = (bf16[1152,384]{1,0:T(8,128)(2,1)}, bf16[1152,384]{1,0:T(8,128)(2,1)}, u32[]{:S(2)}, u32[]{:S(2)}) collective-permute-start(bf16[1152,384]{1,0:T(8,128)(2,1)} %get-tuple-element.154), channel_id=1, source_target_pairs={{0,4},{4,0},{8,12},{12,8},{16,20},{20,16},{24,28},{28,24},{1,5},{5... | collective-permute-start | bytes 2654216 | tf_op jit(solution)/shard_map/ppermute | solution.py:650
  100.0 17.6 %collective-permute-start.18 = (bf16[384,384]{1,0:T(8,128)(2,1)S(1)}, bf16[384,384]{1,0:T(8,128)(2,1)S(1)}, u32[]{:S(2)}, u32[]{:S(2)}) collective-permute-start(bf16[384,384]{1,0:T(8,128)(2,1)S(1)} %get-tuple-element.162), channel_id=1, source_target_pairs={{0,2},{1,3},{2,0},{3,1},{4,6},{5,7},{6,4},{7,5},{8,10},{9,11},{10,... | collective-permute-start | bytes 884744 | tf_op jit(solution)/shard_map/ppermute | solution.py:647
  101.5 16.0 %collective-permute-start.19 = (bf16[384,384]{1,0:T(8,128)(2,1)S(1)}, bf16[384,384]{1,0:T(8,128)(2,1)S(1)}, u32[]{:S(2)}, u32[]{:S(2)}) collective-permute-start(bf16[384,384]{1,0:T(8,128)(2,1)S(1)} %get-tuple-element.163), channel_id=1, source_target_pairs={{0,4},{4,0},{8,12},{12,8},{16,20},{20,16},{24,28},{28,24},{1,5},{5... | collective-permute-start | bytes 884744 | tf_op jit(solution)/shard_map/ppermute | solution.py:650
  131.6 28.3 %collective-permute-start.22 = (bf16[3,256,768]{2,1,0:T(8,128)(2,1)}, bf16[3,256,768]{2,1,0:T(8,128)(2,1)S(1)}, u32[]{:S(2)}, u32[]{:S(2)}) collective-permute-start(bf16[3,256,768]{2,1,0:T(8,128)(2,1)} %get-tuple-element.170.refs_1_), channel_id=1, source_target_pairs={{0,2},{1,3},{2,0},{3,1},{4,6},{5,7},{6,4},{7,5},{8,10},{9,11},{10,... | collective-permute-start | bytes 3538952 | tf_op jit(solution)/shard_map/ppermute | solution.py:647
  133.2 27.7 %collective-permute-start.24 = (bf16[4,192,768]{2,1,0:T(8,128)(2,1)S(1)}, bf16[4,192,768]{2,1,0:T(8,128)(2,1)S(1)}, u32[]{:S(2)}, u32[]{:S(2)}) collective-permute-start(bf16[4,192,768]{2,1,0:T(8,128)(2,1)S(1)} %get-tuple-element.191), channel_id=1, source_target_pairs={{0,4},{4,0},{8,12},{12,8},{16,20},{20,16},{24,28},{28,24},{1,5},{5... | collective-permute-start | bytes 3538952 | tf_op jit(solution)/shard_map/ppermute | solution.py:650
  169.2 34.4 %collective-permute-start.26 = (bf16[8,240,384]{2,1,0:T(8,128)(2,1)S(1)}, bf16[8,240,384]{2,1,0:T(8,128)(2,1)S(1)}, u32[]{:S(2)}, u32[]{:S(2)}) collective-permute-start(bf16[8,240,384]{2,1,0:T(8,128)(2,1)S(1)} %get-tuple-element.201), channel_id=1, source_target_pairs={{0,2},{1,3},{2,0},{3,1},{4,6},{5,7},{6,4},{7,5},{8,10},{9,11},{10,... | collective-permute-start | bytes 4423688 | tf_op jit(solution)/shard_map/ppermute | solution.py:647
  170.7 31.4 %collective-permute-start.27 = (bf16[192,768]{1,0:T(8,128)(2,1)S(1)}, bf16[192,768]{1,0:T(8,128)(2,1)S(1)}, u32[]{:S(2)}, u32[]{:S(2)}) collective-permute-start(bf16[192,768]{1,0:T(8,128)(2,1)S(1)} %get-tuple-element.203), channel_id=1, source_target_pairs={{0,8},{4,12},{8,16},{12,20},{16,24},{20,28},{24,0},{28,4},{1,9},{5... | collective-permute-start | bytes 884744 | tf_op jit(solution)/shard_map/ppermute | solution.py:653
  170.8 31.4 %collective-permute-start.28 = (bf16[192,768]{1,0:T(8,128)(2,1)S(1)}, bf16[192,768]{1,0:T(8,128)(2,1)S(1)}, u32[]{:S(2)}, u32[]{:S(2)}) collective-permute-start(bf16[192,768]{1,0:T(8,128)(2,1)S(1)} %get-tuple-element.204), channel_id=1, source_target_pairs={{0,16},{4,20},{8,24},{12,28},{16,0},{20,4},{24,8},{28,12},{1,17},{... | collective-permute-start | bytes 884744 | tf_op jit(solution)/shard_map/ppermute | solution.py:653
  172.7 29.5 %collective-permute-start.29 = (bf16[192,768]{1,0:T(8,128)(2,1)S(1)}, bf16[192,768]{1,0:T(8,128)(2,1)S(1)}, u32[]{:S(2)}, u32[]{:S(2)}) collective-permute-start(bf16[192,768]{1,0:T(8,128)(2,1)S(1)} %get-tuple-element.205), channel_id=1, source_target_pairs={{0,24},{4,28},{8,0},{12,4},{16,8},{20,12},{24,16},{28,20},{1,25},{... | collective-permute-start | bytes 884744 | tf_op jit(solution)/shard_map/ppermute | solution.py:653
  205.1 41.0 %collective-permute-start.31 = (bf16[3,256,768]{2,1,0:T(8,128)(2,1)S(1)}, bf16[3,256,768]{2,1,0:T(8,128)(2,1)S(1)}, u32[]{:S(2)}, u32[]{:S(2)}) collective-permute-start(bf16[3,256,768]{2,1,0:T(8,128)(2,1)S(1)} %copy-done.6), channel_id=1, source_target_pairs={{0,2},{1,3},{2,0},{3,1},{4,6},{5,7},{6,4},{7,5},{8,10},{9,11},{10,... | collective-permute-start | bytes 3538952 | tf_op jit(solution)/shard_map/ppermute | solution.py:647
  206.5 19.4 %collective-permute-start.34 = (bf16[4,240,384]{2,1,0:T(8,128)(2,1)S(1)}, bf16[4,240,384]{2,1,0:T(8,128)(2,1)S(1)}, u32[]{:S(2)}, u32[]{:S(2)}) collective-permute-start(bf16[4,240,384]{2,1,0:T(8,128)(2,1)S(1)} %get-tuple-element.219), channel_id=1, source_target_pairs={{0,4},{4,0},{8,12},{12,8},{16,20},{20,16},{24,28},{28,24},{1,5},{5... | collective-permute-start | bytes 2211848 | tf_op jit(solution)/shard_map/ppermute | solution.py:650
  210.0 34.9 %collective-permute-start.32 = (bf16[4,112,768]{2,1,0:T(8,128)(2,1)S(1)}, bf16[4,112,768]{2,1,0:T(8,128)(2,1)S(1)}, u32[]{:S(2)}, u32[]{:S(2)}) collective-permute-start(bf16[4,112,768]{2,1,0:T(8,128)(2,1)S(1)} %get-tuple-element.215), channel_id=1, source_target_pairs={{0,4},{4,0},{8,12},{12,8},{16,20},{20,16},{24,28},{28,24},{1,5},{5... | collective-permute-start | bytes 2064392 | tf_op jit(solution)/shard_map/ppermute | solution.py:650
  210.6 34.2 %collective-permute-start.33 = (bf16[8,64,384]{2,1,0:T(8,128)(2,1)S(1)}, bf16[8,64,384]{2,1,0:T(8,128)(2,1)S(1)}, u32[]{:S(2)}, u32[]{:S(2)}) collective-permute-start(bf16[8,64,384]{2,1,0:T(8,128)(2,1)S(1)} %get-tuple-element.217), channel_id=1, source_target_pairs={{0,2},{1,3},{2,0},{3,1},{4,6},{5,7},{6,4},{7,5},{8,10},{9,11},{10,... | collective-permute-start | bytes 1179656 | tf_op jit(solution)/shard_map/ppermute | solution.py:647
  226.7 14.1 %collective-permute-start.36 = (bf16[240,384]{1,0:T(8,128)(2,1)S(1)}, bf16[240,384]{1,0:T(8,128)(2,1)S(1)}, u32[]{:S(2)}, u32[]{:S(2)}) collective-permute-start(bf16[240,384]{1,0:T(8,128)(2,1)S(1)} %get-tuple-element.223), channel_id=1, source_target_pairs={{0,16},{4,20},{8,24},{12,28},{16,0},{20,4},{24,8},{28,12},{1,17},{... | collective-permute-start | bytes 552968 | tf_op jit(solution)/shard_map/ppermute | solution.py:653
  246.8 18.6 %collective-permute-start.38 = (bf16[2,3,256,768]{3,2,1,0:T(8,128)(2,1)S(1)}, bf16[2,3,256,768]{3,2,1,0:T(8,128)(2,1)S(1)}, u32[]{:S(2)}, u32[]{:S(2)}) collective-permute-start(bf16[2,3,256,768]{3,2,1,0:T(8,128)(2,1)S(1)} %get-tuple-element.228.refs_1_), channel_id=1, source_target_pairs={{0,1},{1,0},{2,3},{3,2},{4,5},{5,4},{6,7},{7,6},{8,9},{9,8},{10,11... | collective-permute-start | bytes 7077896 | tf_op jit(solution)/shard_map/ppermute | solution.py:641
  246.8 10.9 %collective-permute-start.39 = (bf16[4,112,384]{2,1,0:T(8,128)(2,1)S(1)}, bf16[4,112,384]{2,1,0:T(8,128)(2,1)S(1)}, u32[]{:S(2)}, u32[]{:S(2)}) collective-permute-start(bf16[4,112,384]{2,1,0:T(8,128)(2,1)S(1)} %get-tuple-element.230), channel_id=1, source_target_pairs={{0,2},{1,3},{2,0},{3,1},{4,6},{5,7},{6,4},{7,5},{8,10},{9,11},{10,... | collective-permute-start | bytes 1032200 | tf_op jit(solution)/shard_map/ppermute | solution.py:647
  248.2 20.3 %collective-permute-start.41 = (bf16[192,384]{1,0:T(8,128)(2,1)S(1)}, bf16[192,384]{1,0:T(8,128)(2,1)S(1)}, u32[]{:S(2)}, u32[]{:S(2)}) collective-permute-start(bf16[192,384]{1,0:T(8,128)(2,1)S(1)} %get-tuple-element.237), channel_id=1, source_target_pairs={{0,2},{1,3},{2,0},{3,1},{4,6},{5,7},{6,4},{7,5},{8,10},{9,11},{10,... | collective-permute-start | bytes 442376 | tf_op jit(solution)/shard_map/ppermute | solution.py:647
  258.5 10.0 %collective-permute-start.42 = (bf16[176,384]{1,0:T(8,128)(2,1)S(1)}, bf16[176,384]{1,0:T(8,128)(2,1)S(1)}, u32[]{:S(2)}, u32[]{:S(2)}) collective-permute-start(bf16[176,384]{1,0:T(8,128)(2,1)S(1)} %get-tuple-element.240), channel_id=1, source_target_pairs={{0,8},{4,12},{8,16},{12,20},{16,24},{20,28},{24,0},{28,4},{1,9},{5... | collective-permute-start | bytes 405512 | tf_op jit(solution)/shard_map/ppermute | solution.py:653
  261.0 10.1 %collective-permute-start.43 = (bf16[176,384]{1,0:T(8,128)(2,1)S(1)}, bf16[176,384]{1,0:T(8,128)(2,1)S(1)}, u32[]{:S(2)}, u32[]{:S(2)}) collective-permute-start(bf16[176,384]{1,0:T(8,128)(2,1)S(1)} %get-tuple-element.241), channel_id=1, source_target_pairs={{0,16},{4,20},{8,24},{12,28},{16,0},{20,4},{24,8},{28,12},{1,17},{... | collective-permute-start | bytes 405512 | tf_op jit(solution)/shard_map/ppermute | solution.py:653
  273.0 14.5 %collective-permute-start.45 = (f32[576,192]{0,1:T(8,128)S(1)}, f32[576,192]{0,1:T(8,128)S(1)}, u32[]{:S(2)}, u32[]{:S(2)}) collective-permute-start(f32[576,192]{0,1:T(8,128)S(1)} %copy.47), channel_id=1, source_target_pairs={{0,1},{1,0},{2,3},{3,2},{4,5},{5,4},{6,7},{7,6},{8,9},{9,8},{10,11... | collective-permute-start | bytes 1327112 | tf_op jit(solution)/shard_map/ppermute | solution.py:641
  (37 other events, 243.0 us)

commit v7 on v6

--- a/solution.py
+++ b/solution.py
@@ -710,6 +710,25 @@
     )(where, *ins, *deps)
 
 
+def shards_kernel(where, front, back, mine, sent, token):
+    token[...] = jnp.zeros_like(token)
+    chunks = ((0, 1, 2, 7), (3, 4, 5, 6), (8, 9, 10, 11))
+
+    def fill(low, high):
+        for k, blocks in enumerate(chunks):
+            for j, at in enumerate(blocks):
+                value = front[at] if at < 7 else back[at - 7].T
+                (low if j < 2 else high)[k, j % 2] = value.astype(BF)
+
+    @pl.when(where[3] == 0)
+    def _():
+        fill(mine, sent)
+
+    @pl.when(where[3] != 0)
+    def _():
+        fill(sent, mine)
+
+
 def pack_kernel(count, has_next, unit_at, where, *refs):
     parts, refs = refs[:count], refs[count:]
     half, lows = 0, None
@@ -1084,10 +1103,9 @@
     rows, lanes = low_front.shape[1], low_front.shape[2]
 
     if direct:
-        shards = jnp.concatenate([low_front[:3], turned[:1], low_front[3:], turned[1:]])
-        shards = shards.reshape(3, 2, 2, rows, lanes)
-        mine = lax.dynamic_index_in_dim(shards, c, axis=1, keepdims=False)
-        sent = lax.dynamic_index_in_dim(shards, 1 - c, axis=1, keepdims=False)
+        shape = sds((3, 2, front_weights.shape[1], front_weights.shape[2]), BF)
+        held = [pltpu.with_memory_space_constraint(v, pltpu.HBM) for v in (front_weights, back_weights)]
+        mine, sent, _ = call(shards_kernel, "shards", where, held, [shape, shape])
         got = place.core(sent)
         units = jnp.where(
             c == 0, jnp.concatenate([mine, got], -1), jnp.concatenate([got, mine], -1)

time: 301 us -> 300 us (level)
    pallas_call x23 -> x24, Pallas kernels: 31.5 us -> 33.5 us  [call(): pl.pallas_call(ignoring(kernel, 1 + len(ins), len(deps)), in_specs=[pl.Bl...]
  transfers between devices with their start and end apart: 53 -> 53, of which waited for: 35 -> 34; matrix products, arithmetic and copies ran while one was open for 0% -> 1% of each run, Pallas kernels for 33% -> 33%
where the time goes in v7:
time: 300 us; the launch traced here: 297 us
  Pallas kernels  123 us (41%)
  waiting for transfers between devices  108 us (36%)
  starting transfers between devices  60.2 us (20%)
    ppermute x21, waiting for transfers between devices, over_z(): return lax.ppermute(v, 'dp', self.z_shift[shift])  55.8 us
    ppermute x21, starting transfers between devices, over_z(): return lax.ppermute(v, 'dp', self.z_shift[shift])  36.1 us
    pallas_call x24, Pallas kernels, call(): pl.pallas_call(ignoring(kernel, 1 + len(ins), len(deps)), in_specs=[pl.Bl...  33.5 us
    pallas_call x1, Pallas kernels, attention_backward(): pl.pallas_call(ignoring(attention_backward_kernel, 15, len(deps)), grid_s...  26.5 us
    pallas_call x1, Pallas kernels, mlp_backward(): pl.pallas_call(ignoring(mlp_kernel, 9, len(deps)), grid_spec=spec, out_sh...  20.9 us
    ppermute x9, waiting for transfers between devices, over_y(): return lax.ppermute(v, 'dp', self.y_pairs)  18 us
    ppermute x11, waiting for transfers between devices, over_x(): return lax.ppermute(v, 'mp', self.x_pairs)  17.1 us
    pallas_call x1, Pallas kernels, attention_forward(): pl.pallas_call(ignoring(attention_forward_kernel, 5, len(deps)), grid_spe...  16.9 us
  transfers between devices with their start and end apart: 53, of which 34 were waited for; matrix products, arithmetic and copies ran while one was open for 1% of the time, Pallas kernels for 33%

profile of v7, /device:TPU:0, one launch (start us, length us, event | category | flops | bytes accessed | tf_op | source)
XLA Modules:
  0.0 297.3 jit_solution(15644675175959419124)
XLA Ops:
  6.2 4.6 %collective-permute-start.3 = (bf16[2,112,384]{2,1,0:T(8,128)(2,1)S(1)}, bf16[2,112,384]{2,1,0:T(8,128)(2,1)S(1)}, u32[]{:S(2)}, u32[]{:S(2)}) collective-permute-start(bf16[2,112,384]{2,1,0:T(8,128)(2,1)S(1)} %maximum_maximum_fusion.refs_1_), channel_id=1, source_target_pairs={{0,24},{4,28},{8,0},{12,4},{16,8},{20,12},{24,16},{28,20},{1,25},{... | collective-permute-start | bytes 516104 | tf_op jit(solution)/shard_map/ppermute | solution.py:653
  11.9 3.8 %collective-permute-done.3.refs_4_ = bf16[2,112,384]{2,1,0:T(8,128)(2,1)S(1)} collective-permute-done((bf16[2,112,384]{2,1,0:T(8,128)(2,1)S(1)}, bf16[2,112,384]{2,1,0:T(8,128)(2,1)S(1)}, u32[]{:S(2)}, u32[]{:S(2)}) %collective-permute-start.3) | collective-permute-done | bytes 172064 | tf_op jit(solution)/shard_map/ppermute | solution.py:653
  15.6 10.5 %collective-permute-done.2.refs_3_ = bf16[2,112,384]{2,1,0:T(8,128)(2,1)S(1)} collective-permute-done((bf16[2,112,384]{2,1,0:T(8,128)(2,1)S(1)}, bf16[2,112,384]{2,1,0:T(8,128)(2,1)S(1)}, u32[]{:S(2)}, u32[]{:S(2)}) %collective-permute-start.2) | collective-permute-done | bytes 172064 | tf_op jit(solution)/shard_map/ppermute | solution.py:653
  36.2 9.2 %collective-permute-done.7.refs_3_ = bf16[2,96,384]{2,1,0:T(8,128)(2,1)S(1)} collective-permute-done((bf16[2,96,384]{2,1,0:T(8,128)(2,1)S(1)}, bf16[2,96,384]{2,1,0:T(8,128)(2,1)S(1)}, u32[]{:S(2)}, u32[]{:S(2)}) %collective-permute-start.7) | collective-permute-done | bytes 147488 | tf_op jit(solution)/shard_map/ppermute | solution.py:653
  48.7 2.5 collective-permute-start.12
  51.2 2.5 collective-permute-start.11
  54.2 8.2 %collective-permute-done.12.refs_7_.refs_3_ = bf16[2,96,384]{2,1,0:T(8,128)(2,1)S(1)} collective-permute-done((bf16[2,96,384]{2,1,0:T(8,128)(2,1)S(1)}, bf16[2,96,384]{2,1,0:T(8,128)(2,1)S(1)}, u32[]{:S(2)}, u32[]{:S(2)}) %collective-permute-start.12) | collective-permute-done | bytes 147488 | tf_op jit(solution)/shard_map/ppermute | solution.py:653
  62.4 5.4 %collective-permute-done.9.refs_4_.refs_5_.refs_2_ = bf16[1216,384]{1,0:T(8,128)(2,1)S(1)} collective-permute-done((bf16[1216,384]{1,0:T(8,128)(2,1)S(1)}, bf16[1216,384]{1,0:T(8,128)(2,1)S(1)}, u32[]{:S(2)}, u32[]{:S(2)}) %collective-permute-start.9) | collective-permute-done | bytes 933920 | tf_op jit(solution)/shard_map/ppermute | solution.py:647
  76.8 16.9 %attention_forward.1 = (f32[768,768]{1,0:T(8,128)}, bf16[768,768]{1,0:T(8,128)(2,1)}, bf16[768,768]{1,0:T(8,128)(2,1)}, bf16[768,768]{1,0:T(8,128)(2,1)}, bf16[7...) custom-call(s32[4]{0:T(128)S(1)} %pad_add_fusion.1.refs_0_, ...), custom_call_target="tpu_custom_call" | custom-call | tf_op jit(solution)/shard_map/attention_forward/pallas_call | solution.py:470
  93.7 2.8 collective-permute-done.15.refs_4_.refs_1_.refs_2_
  102.8 14.1 %up_forward.1 = (bf16[4,768,768]{2,1,0:T(8,128)(2,1)S(1)}, bf16[4,768,768]{2,1,0:T(8,128)(2,1)}, bf16[8,192,768]{2,1,0:T(8,128)(2,1)S(1)}, bf16[8,192,768]{2,1,0...) custom-call(s32[4]{0:T(128)S(1)} %pad_add_fusion.1.refs_0_, ...), custom_call_target="tpu_custom_call" | custom-call | tf_op jit(solution)/shard_map/up_forward/pallas_call | solution.py:502
  119.4 2.3 collective-permute-done.21.refs_2_
  124.9 6.3 %down_forward.1 = (bf16[3,256,768]{2,1,0:T(8,128)(2,1)}, bf16[4,768,768]{2,1,0:T(8,128)(2,1)}, f32[8,128]{1,0:T(8,128)S(1)}) custom-call(s32[4]{0:T(128)S(1)} %pad_add_fusion.1.refs_0_, bf16[4,768,768]{2,1,0:T(8,128)(2,1)S(1)} %get-tuple-element.164.refs_1_, bf16[1536,768]{1,0:T(8,128)(2,1)S(1)} %get-tuple-element.169.refs_2_, ...), custom_call_target="tpu_custom_call" | custom-call | tf_op jit(solution)/shard_map/down_forward/pallas_call | solution.py:534
  133.4 20.9 %mlp_backward.1 = (f32[768,768]{1,0:T(8,128)S(1)}, bf16[768,768]{1,0:T(8,128)(2,1)S(1)}, bf16[8,240,768]{2,1,0:T(8,128)(2,1)S(1)}, bf16[8,240,768]{2,1,0:T(8,128...) custom-call(s32[4]{0:T(128)S(1)} %pad_add_fusion.1.refs_0_, ...), custom_call_target="tpu_custom_call" | custom-call | tf_op jit(solution)/shard_map/mlp_backward/pallas_call | solution.py:567
  154.3 5.2 %collective-permute-done.22.refs_2_ = bf16[3,256,768]{2,1,0:T(8,128)(2,1)S(1)} collective-permute-done((bf16[3,256,768]{2,1,0:T(8,128)(2,1)}, bf16[3,256,768]{2,1,0:T(8,128)(2,1)S(1)}, u32[]{:S(2)}, u32[]{:S(2)}) %collective-permute-start.22) | collective-permute-done | bytes 1179680 | tf_op jit(solution)/shard_map/ppermute | solution.py:647
  161.4 5.4 %collective-permute-done.25.refs_2_ = bf16[8,240,768]{2,1,0:T(8,128)(2,1)S(1)} collective-permute-done((bf16[8,240,768]{2,1,0:T(8,128)(2,1)S(1)}, bf16[8,240,768]{2,1,0:T(8,128)(2,1)S(1)}, u32[]{:S(2)}, u32[]{:S(2)}) %collective-permute-start.25) | collective-permute-done | bytes 2949152 | tf_op jit(solution)/shard_map/ppermute | solution.py:641
  172.5 2.9 collective-permute-start.29
  175.4 26.5 %attention_backward.1 = (bf16[3,256,768]{2,1,0:T(8,128)(2,1)}, f32[256,768]{1,0:T(8,128)}, f32[8,768]{1,0:T(8,128)}, bf16[8,176,768]{2,1,0:T(8,128)(2,1)S(1)}, b...) custom-call(s32[4]{0:T(128)S(1)} %pad_add_fusion.1.refs_0_, s32[12,4]{1,0:T(8,128)S(1)} %copy.39.refs_1_, ...), custom_call_target="tpu_custom_call" | custom-call | tf_op jit(solution)/shard_map/attention_backward/pallas_call | solution.py:607
  211.8 3.0 %collect.2 = (bf16[12,256,768]{2,1,0:T(8,128)(2,1)}, f32[8,128]{1,0:T(8,128)S(1)}) custom-call(s32[4]{0:T(128)S(1)} %pad_add_fusion.refs_0_, bf16[2,3,256,768]{3,2,1,0:T(8,128)(2,1)S(1)} %get-tuple-element.181.refs_1_, bf16[2,3,256,768]{3,2,1,0:T(8,128)(2,1)S(1)} %collective-permute-done.23.refs_2_, f32[8,128]{1,0:T(8,128)S(1)} %get-tuple-element.215.refs_3_), custom_call_target="tpu_custom_call" | custom-call | tf_op jit(solution)/shard_map/collect/pallas_call | solution.py:702
  214.8 10.7 %collective-permute-done.34.refs_2_ = bf16[4,240,384]{2,1,0:T(8,128)(2,1)S(1)} collective-permute-done((bf16[4,240,384]{2,1,0:T(8,128)(2,1)S(1)}, bf16[4,240,384]{2,1,0:T(8,128)(2,1)S(1)}, u32[]{:S(2)}, u32[]{:S(2)}) %collective-permute-start.34) | collective-permute-done | bytes 737312 | tf_op jit(solution)/shard_map/ppermute | solution.py:650
  228.5 6.0 %collective-permute-done.35.refs_2_ = bf16[240,384]{1,0:T(8,128)(2,1)S(1)} collective-permute-done((bf16[240,384]{1,0:T(8,128)(2,1)S(1)}, bf16[240,384]{1,0:T(8,128)(2,1)S(1)}, u32[]{:S(2)}, u32[]{:S(2)}) %collective-permute-start.35) | collective-permute-done | bytes 184352 | tf_op jit(solution)/shard_map/ppermute | solution.py:653
  234.5 5.9 %collective-permute-done.36.refs_3_ = bf16[240,384]{1,0:T(8,128)(2,1)S(1)} collective-permute-done((bf16[240,384]{1,0:T(8,128)(2,1)S(1)}, bf16[240,384]{1,0:T(8,128)(2,1)S(1)}, u32[]{:S(2)}, u32[]{:S(2)}) %collective-permute-start.36) | collective-permute-done | bytes 184352 | tf_op jit(solution)/shard_map/ppermute | solution.py:653
  240.4 3.4 %collective-permute-done.37.refs_4_ = bf16[240,384]{1,0:T(8,128)(2,1)S(1)} collective-permute-done((bf16[240,384]{1,0:T(8,128)(2,1)S(1)}, bf16[240,384]{1,0:T(8,128)(2,1)S(1)}, u32[]{:S(2)}, u32[]{:S(2)}) %collective-permute-start.37) | collective-permute-done | bytes 184352 | tf_op jit(solution)/shard_map/ppermute | solution.py:653
  249.1 5.1 %collective-permute-done.40.refs_4_ = bf16[4,64,384]{2,1,0:T(8,128)(2,1)S(1)} collective-permute-done((bf16[4,64,384]{2,1,0:T(8,128)(2,1)S(1)}, bf16[4,64,384]{2,1,0:T(8,128)(2,1)S(1)}, u32[]{:S(2)}, u32[]{:S(2)}) %collective-permute-start.40) | collective-permute-done | bytes 196640 | tf_op jit(solution)/shard_map/ppermute | solution.py:650
  254.3 3.1 %collective-permute-done.39.refs_2_ = bf16[4,112,384]{2,1,0:T(8,128)(2,1)S(1)} collective-permute-done((bf16[4,112,384]{2,1,0:T(8,128)(2,1)S(1)}, bf16[4,112,384]{2,1,0:T(8,128)(2,1)S(1)}, u32[]{:S(2)}, u32[]{:S(2)}) %collective-permute-start.39) | collective-permute-done | bytes 344096 | tf_op jit(solution)/shard_map/ppermute | solution.py:647
  258.1 2.5 collective-permute-start.42
  262.1 2.8 collective-permute-start.44
  265.0 3.0 %collect.3 = (bf16[12,256,768]{2,1,0:T(8,128)(2,1)}, f32[8,128]{1,0:T(8,128)S(1)}) custom-call(s32[4]{0:T(128)S(1)} %pad_add_fusion.refs_0_, bf16[2,3,256,768]{3,2,1,0:T(8,128)(2,1)S(1)} %get-tuple-element.232.refs_1_, bf16[2,3,256,768]{3,2,1,0:T(8,128)(2,1)S(1)} %collective-permute-done.38.refs_2_, f32[8,128]{1,0:T(8,128)S(1)} %get-tuple-element.238.refs_3_), custom_call_target="tpu_custom_call" | custom-call | tf_op jit(solution)/shard_map/collect/pallas_call | solution.py:702
  268.0 2.7 collective-permute-done.43.refs_6_
  280.9 5.6 %collective-permute-start.52 = (f32[8,128]{1,0:T(8,128)S(1)}, f32[8,128]{1,0:T(8,128)S(1)}, u32[]{:S(2)}, u32[]{:S(2)}) collective-permute-start(f32[8,128]{1,0:T(8,128)S(1)} %slice_add_fusion.refs_6_), channel_id=1, source_target_pairs={{0,24},{4,28},{8,0},{12,4},{16,8},{20,12},{24,16},{28,20},{1,25},{... | collective-permute-start | bytes 12296 | tf_op jit(solution)/shard_map/ppermute | solution.py:653
  287.9 3.2 %collective-permute-done.51.refs_8_ = f32[8,128]{1,0:T(8,128)S(1)} collective-permute-done((f32[8,128]{1,0:T(8,128)S(1)}, f32[8,128]{1,0:T(8,128)S(1)}, u32[]{:S(2)}, u32[]{:S(2)}) %collective-permute-start.51) | collective-permute-done | bytes 4128 | tf_op jit(solution)/shard_map/ppermute | solution.py:653
  291.9 5.1 %update.1 = (f32[1,1]{1,0:T(1,128)}, f32[7,96,192]{2,1,0:T(8,128)}, f32[5,192,96]{2,1,0:T(8,128)}, f32[6,24]{1,0:T(8,128)}, f32[6,96]{1,0:T(8,128)}, /*index=5*/...) custom-call(s32[4]{0:T(128)S(1)} %pad_add_fusion.refs_0_, ...), custom_call_target="tpu_custom_call" | custom-call | tf_op jit(solution)/shard_map/update/pallas_call | solution.py:1068
  (145 shorter events, 83.7 us)
Async XLA Ops:
  6.2 9.4 %collective-permute-start.3 = (bf16[2,112,384]{2,1,0:T(8,128)(2,1)S(1)}, bf16[2,112,384]{2,1,0:T(8,128)(2,1)S(1)}, u32[]{:S(2)}, u32[]{:S(2)}) collective-permute-start(bf16[2,112,384]{2,1,0:T(8,128)(2,1)S(1)} %maximum_maximum_fusion.refs_1_), channel_id=1, source_target_pairs={{0,24},{4,28},{8,0},{12,4},{16,8},{20,12},{24,16},{28,20},{1,25},{... | collective-permute-start | bytes 516104 | tf_op jit(solution)/shard_map/ppermute | solution.py:653
  10.9 15.3 %collective-permute-start.2 = (bf16[2,112,384]{2,1,0:T(8,128)(2,1)S(1)}, bf16[2,112,384]{2,1,0:T(8,128)(2,1)S(1)}, u32[]{:S(2)}, u32[]{:S(2)}) collective-permute-start(bf16[2,112,384]{2,1,0:T(8,128)(2,1)S(1)} %maximum_maximum_fusion.refs_1_), channel_id=1, source_target_pairs={{0,16},{4,20},{8,24},{12,28},{16,0},{20,4},{24,8},{28,12},{1,17},{... | collective-permute-start | bytes 516104 | tf_op jit(solution)/shard_map/ppermute | solution.py:653
  10.9 15.3 %collective-permute-start.1 = (bf16[2,112,384]{2,1,0:T(8,128)(2,1)S(1)}, bf16[2,112,384]{2,1,0:T(8,128)(2,1)S(1)}, u32[]{:S(2)}, u32[]{:S(2)}) collective-permute-start(bf16[2,112,384]{2,1,0:T(8,128)(2,1)S(1)} %maximum_maximum_fusion.refs_1_), channel_id=1, source_target_pairs={{0,8},{4,12},{8,16},{12,20},{16,24},{20,28},{24,0},{28,4},{1,9},{5... | collective-permute-start | bytes 516104 | tf_op jit(solution)/shard_map/ppermute | solution.py:653
  27.3 18.2 %collective-permute-start.5 = (bf16[896,384]{1,0:T(8,128)(2,1)S(1)}, bf16[896,384]{1,0:T(8,128)(2,1)S(1)}, u32[]{:S(2)}, u32[]{:S(2)}) collective-permute-start(bf16[896,384]{1,0:T(8,128)(2,1)S(1)} %get-tuple-element.147.refs_1_), channel_id=1, source_target_pairs={{0,4},{4,0},{8,12},{12,8},{16,20},{20,16},{24,28},{28,24},{1,5},{5... | collective-permute-start | bytes 2064392 | tf_op jit(solution)/shard_map/ppermute | solution.py:650
  28.8 16.8 %collective-permute-start.4 = (bf16[896,384]{1,0:T(8,128)(2,1)S(1)}, bf16[896,384]{1,0:T(8,128)(2,1)S(1)}, u32[]{:S(2)}, u32[]{:S(2)}) collective-permute-start(bf16[896,384]{1,0:T(8,128)(2,1)S(1)} %get-tuple-element.147.refs_1_), channel_id=1, source_target_pairs={{0,2},{1,3},{2,0},{3,1},{4,6},{5,7},{6,4},{7,5},{8,10},{9,11},{10,... | collective-permute-start | bytes 2064392 | tf_op jit(solution)/shard_map/ppermute | solution.py:647
  31.0 14.4 %collective-permute-start.7 = (bf16[2,96,384]{2,1,0:T(8,128)(2,1)S(1)}, bf16[2,96,384]{2,1,0:T(8,128)(2,1)S(1)}, u32[]{:S(2)}, u32[]{:S(2)}) collective-permute-start(bf16[2,96,384]{2,1,0:T(8,128)(2,1)S(1)} %get-tuple-element.148.refs_1_), channel_id=1, source_target_pairs={{0,16},{4,20},{8,24},{12,28},{16,0},{20,4},{24,8},{28,12},{1,17},{... | collective-permute-start | bytes 442376 | tf_op jit(solution)/shard_map/ppermute | solution.py:653
  33.1 12.3 %collective-permute-start.6 = (bf16[2,96,384]{2,1,0:T(8,128)(2,1)S(1)}, bf16[2,96,384]{2,1,0:T(8,128)(2,1)S(1)}, u32[]{:S(2)}, u32[]{:S(2)}) collective-permute-start(bf16[2,96,384]{2,1,0:T(8,128)(2,1)S(1)} %get-tuple-element.148.refs_1_), channel_id=1, source_target_pairs={{0,8},{4,12},{8,16},{12,20},{16,24},{20,28},{24,0},{28,4},{1,9},{5... | collective-permute-start | bytes 442376 | tf_op jit(solution)/shard_map/ppermute | solution.py:653
  46.7 21.1 %collective-permute-start.9 = (bf16[1216,384]{1,0:T(8,128)(2,1)S(1)}, bf16[1216,384]{1,0:T(8,128)(2,1)S(1)}, u32[]{:S(2)}, u32[]{:S(2)}) collective-permute-start(bf16[1216,384]{1,0:T(8,128)(2,1)S(1)} %get-tuple-element.149), channel_id=1, source_target_pairs={{0,2},{1,3},{2,0},{3,1},{4,6},{5,7},{6,4},{7,5},{8,10},{9,11},{10,... | collective-permute-start | bytes 2801672 | tf_op jit(solution)/shard_map/ppermute | solution.py:647
  48.2 20.9 %collective-permute-start.10 = (bf16[1216,384]{1,0:T(8,128)(2,1)S(1)}, bf16[1216,384]{1,0:T(8,128)(2,1)S(1)}, u32[]{:S(2)}, u32[]{:S(2)}) collective-permute-start(bf16[1216,384]{1,0:T(8,128)(2,1)S(1)} %get-tuple-element.150), channel_id=1, source_target_pairs={{0,4},{4,0},{8,12},{12,8},{16,20},{20,16},{24,28},{28,24},{1,5},{5... | collective-permute-start | bytes 2801672 | tf_op jit(solution)/shard_map/ppermute | solution.py:650
  48.7 13.7 %collective-permute-start.12 = (bf16[2,96,384]{2,1,0:T(8,128)(2,1)S(1)}, bf16[2,96,384]{2,1,0:T(8,128)(2,1)S(1)}, u32[]{:S(2)}, u32[]{:S(2)}) collective-permute-start(bf16[2,96,384]{2,1,0:T(8,128)(2,1)S(1)} %get-tuple-element.151.refs_1_), channel_id=1, source_target_pairs={{0,16},{4,20},{8,24},{12,28},{16,0},{20,4},{24,8},{28,12},{1,17},{... | collective-permute-start | bytes 442376 | tf_op jit(solution)/shard_map/ppermute | solution.py:653
  51.2 11.2 %collective-permute-start.11 = (bf16[2,96,384]{2,1,0:T(8,128)(2,1)S(1)}, bf16[2,96,384]{2,1,0:T(8,128)(2,1)S(1)}, u32[]{:S(2)}, u32[]{:S(2)}) collective-permute-start(bf16[2,96,384]{2,1,0:T(8,128)(2,1)S(1)} %get-tuple-element.151.refs_1_), channel_id=1, source_target_pairs={{0,8},{4,12},{8,16},{12,20},{16,24},{20,28},{24,0},{28,4},{1,9},{5... | collective-permute-start | bytes 442376 | tf_op jit(solution)/shard_map/ppermute | solution.py:653
  74.2 22.3 %collective-permute-start.15 = (bf16[1152,384]{1,0:T(8,128)(2,1)}, bf16[1152,384]{1,0:T(8,128)(2,1)S(1)}, u32[]{:S(2)}, u32[]{:S(2)}) collective-permute-start(bf16[1152,384]{1,0:T(8,128)(2,1)} %get-tuple-element.157), channel_id=1, source_target_pairs={{0,2},{1,3},{2,0},{3,1},{4,6},{5,7},{6,4},{7,5},{8,10},{9,11},{10,... | collective-permute-start | bytes 2654216 | tf_op jit(solution)/shard_map/ppermute | solution.py:647
  74.7 22.1 %collective-permute-start.16 = (bf16[1152,384]{1,0:T(8,128)(2,1)}, bf16[1152,384]{1,0:T(8,128)(2,1)}, u32[]{:S(2)}, u32[]{:S(2)}) collective-permute-start(bf16[1152,384]{1,0:T(8,128)(2,1)} %get-tuple-element.158), channel_id=1, source_target_pairs={{0,4},{4,0},{8,12},{12,8},{16,20},{20,16},{24,28},{28,24},{1,5},{5... | collective-permute-start | bytes 2654216 | tf_op jit(solution)/shard_map/ppermute | solution.py:650
  99.5 17.6 %collective-permute-start.18 = (bf16[384,384]{1,0:T(8,128)(2,1)S(1)}, bf16[384,384]{1,0:T(8,128)(2,1)S(1)}, u32[]{:S(2)}, u32[]{:S(2)}) collective-permute-start(bf16[384,384]{1,0:T(8,128)(2,1)S(1)} %get-tuple-element.166), channel_id=1, source_target_pairs={{0,2},{1,3},{2,0},{3,1},{4,6},{5,7},{6,4},{7,5},{8,10},{9,11},{10,... | collective-permute-start | bytes 884744 | tf_op jit(solution)/shard_map/ppermute | solution.py:647
  101.1 16.1 %collective-permute-start.19 = (bf16[384,384]{1,0:T(8,128)(2,1)S(1)}, bf16[384,384]{1,0:T(8,128)(2,1)S(1)}, u32[]{:S(2)}, u32[]{:S(2)}) collective-permute-start(bf16[384,384]{1,0:T(8,128)(2,1)S(1)} %get-tuple-element.167), channel_id=1, source_target_pairs={{0,4},{4,0},{8,12},{12,8},{16,20},{20,16},{24,28},{28,24},{1,5},{5... | collective-permute-start | bytes 884744 | tf_op jit(solution)/shard_map/ppermute | solution.py:650
  131.2 28.3 %collective-permute-start.22 = (bf16[3,256,768]{2,1,0:T(8,128)(2,1)}, bf16[3,256,768]{2,1,0:T(8,128)(2,1)S(1)}, u32[]{:S(2)}, u32[]{:S(2)}) collective-permute-start(bf16[3,256,768]{2,1,0:T(8,128)(2,1)} %get-tuple-element.174.refs_1_), channel_id=1, source_target_pairs={{0,2},{1,3},{2,0},{3,1},{4,6},{5,7},{6,4},{7,5},{8,10},{9,11},{10,... | collective-permute-start | bytes 3538952 | tf_op jit(solution)/shard_map/ppermute | solution.py:647
  132.8 27.7 %collective-permute-start.24 = (bf16[4,192,768]{2,1,0:T(8,128)(2,1)S(1)}, bf16[4,192,768]{2,1,0:T(8,128)(2,1)S(1)}, u32[]{:S(2)}, u32[]{:S(2)}) collective-permute-start(bf16[4,192,768]{2,1,0:T(8,128)(2,1)S(1)} %get-tuple-element.195), channel_id=1, source_target_pairs={{0,4},{4,0},{8,12},{12,8},{16,20},{20,16},{24,28},{28,24},{1,5},{5... | collective-permute-start | bytes 3538952 | tf_op jit(solution)/shard_map/ppermute | solution.py:650
  168.8 34.4 %collective-permute-start.26 = (bf16[8,240,384]{2,1,0:T(8,128)(2,1)S(1)}, bf16[8,240,384]{2,1,0:T(8,128)(2,1)S(1)}, u32[]{:S(2)}, u32[]{:S(2)}) collective-permute-start(bf16[8,240,384]{2,1,0:T(8,128)(2,1)S(1)} %get-tuple-element.205), channel_id=1, source_target_pairs={{0,2},{1,3},{2,0},{3,1},{4,6},{5,7},{6,4},{7,5},{8,10},{9,11},{10,... | collective-permute-start | bytes 4423688 | tf_op jit(solution)/shard_map/ppermute | solution.py:647
  170.3 31.6 %collective-permute-start.27 = (bf16[192,768]{1,0:T(8,128)(2,1)S(1)}, bf16[192,768]{1,0:T(8,128)(2,1)S(1)}, u32[]{:S(2)}, u32[]{:S(2)}) collective-permute-start(bf16[192,768]{1,0:T(8,128)(2,1)S(1)} %get-tuple-element.207), channel_id=1, source_target_pairs={{0,8},{4,12},{8,16},{12,20},{16,24},{20,28},{24,0},{28,4},{1,9},{5... | collective-permute-start | bytes 884744 | tf_op jit(solution)/shard_map/ppermute | solution.py:653
  170.5 31.4 %collective-permute-start.28 = (bf16[192,768]{1,0:T(8,128)(2,1)S(1)}, bf16[192,768]{1,0:T(8,128)(2,1)S(1)}, u32[]{:S(2)}, u32[]{:S(2)}) collective-permute-start(bf16[192,768]{1,0:T(8,128)(2,1)S(1)} %get-tuple-element.208), channel_id=1, source_target_pairs={{0,16},{4,20},{8,24},{12,28},{16,0},{20,4},{24,8},{28,12},{1,17},{... | collective-permute-start | bytes 884744 | tf_op jit(solution)/shard_map/ppermute | solution.py:653
  172.5 29.5 %collective-permute-start.29 = (bf16[192,768]{1,0:T(8,128)(2,1)S(1)}, bf16[192,768]{1,0:T(8,128)(2,1)S(1)}, u32[]{:S(2)}, u32[]{:S(2)}) collective-permute-start(bf16[192,768]{1,0:T(8,128)(2,1)S(1)} %get-tuple-element.209), channel_id=1, source_target_pairs={{0,24},{4,28},{8,0},{12,4},{16,8},{20,12},{24,16},{28,20},{1,25},{... | collective-permute-start | bytes 884744 | tf_op jit(solution)/shard_map/ppermute | solution.py:653
  204.7 41.0 %collective-permute-start.31 = (bf16[3,256,768]{2,1,0:T(8,128)(2,1)S(1)}, bf16[3,256,768]{2,1,0:T(8,128)(2,1)S(1)}, u32[]{:S(2)}, u32[]{:S(2)}) collective-permute-start(bf16[3,256,768]{2,1,0:T(8,128)(2,1)S(1)} %copy-done.6), channel_id=1, source_target_pairs={{0,2},{1,3},{2,0},{3,1},{4,6},{5,7},{6,4},{7,5},{8,10},{9,11},{10,... | collective-permute-start | bytes 3538952 | tf_op jit(solution)/shard_map/ppermute | solution.py:647
  206.1 19.4 %collective-permute-start.34 = (bf16[4,240,384]{2,1,0:T(8,128)(2,1)S(1)}, bf16[4,240,384]{2,1,0:T(8,128)(2,1)S(1)}, u32[]{:S(2)}, u32[]{:S(2)}) collective-permute-start(bf16[4,240,384]{2,1,0:T(8,128)(2,1)S(1)} %get-tuple-element.223), channel_id=1, source_target_pairs={{0,4},{4,0},{8,12},{12,8},{16,20},{20,16},{24,28},{28,24},{1,5},{5... | collective-permute-start | bytes 2211848 | tf_op jit(solution)/shard_map/ppermute | solution.py:650
  209.6 34.9 %collective-permute-start.32 = (bf16[4,112,768]{2,1,0:T(8,128)(2,1)S(1)}, bf16[4,112,768]{2,1,0:T(8,128)(2,1)S(1)}, u32[]{:S(2)}, u32[]{:S(2)}) collective-permute-start(bf16[4,112,768]{2,1,0:T(8,128)(2,1)S(1)} %get-tuple-element.219), channel_id=1, source_target_pairs={{0,4},{4,0},{8,12},{12,8},{16,20},{20,16},{24,28},{28,24},{1,5},{5... | collective-permute-start | bytes 2064392 | tf_op jit(solution)/shard_map/ppermute | solution.py:650
  210.2 34.2 %collective-permute-start.33 = (bf16[8,64,384]{2,1,0:T(8,128)(2,1)S(1)}, bf16[8,64,384]{2,1,0:T(8,128)(2,1)S(1)}, u32[]{:S(2)}, u32[]{:S(2)}) collective-permute-start(bf16[8,64,384]{2,1,0:T(8,128)(2,1)S(1)} %get-tuple-element.221), channel_id=1, source_target_pairs={{0,2},{1,3},{2,0},{3,1},{4,6},{5,7},{6,4},{7,5},{8,10},{9,11},{10,... | collective-permute-start | bytes 1179656 | tf_op jit(solution)/shard_map/ppermute | solution.py:647
  226.5 13.9 %collective-permute-start.36 = (bf16[240,384]{1,0:T(8,128)(2,1)S(1)}, bf16[240,384]{1,0:T(8,128)(2,1)S(1)}, u32[]{:S(2)}, u32[]{:S(2)}) collective-permute-start(bf16[240,384]{1,0:T(8,128)(2,1)S(1)} %get-tuple-element.227), channel_id=1, source_target_pairs={{0,16},{4,20},{8,24},{12,28},{16,0},{20,4},{24,8},{28,12},{1,17},{... | collective-permute-start | bytes 552968 | tf_op jit(solution)/shard_map/ppermute | solution.py:653
  246.4 18.6 %collective-permute-start.38 = (bf16[2,3,256,768]{3,2,1,0:T(8,128)(2,1)S(1)}, bf16[2,3,256,768]{3,2,1,0:T(8,128)(2,1)S(1)}, u32[]{:S(2)}, u32[]{:S(2)}) collective-permute-start(bf16[2,3,256,768]{3,2,1,0:T(8,128)(2,1)S(1)} %get-tuple-element.232.refs_1_), channel_id=1, source_target_pairs={{0,1},{1,0},{2,3},{3,2},{4,5},{5,4},{6,7},{7,6},{8,9},{9,8},{10,11... | collective-permute-start | bytes 7077896 | tf_op jit(solution)/shard_map/ppermute | solution.py:641
  246.5 10.9 %collective-permute-start.39 = (bf16[4,112,384]{2,1,0:T(8,128)(2,1)S(1)}, bf16[4,112,384]{2,1,0:T(8,128)(2,1)S(1)}, u32[]{:S(2)}, u32[]{:S(2)}) collective-permute-start(bf16[4,112,384]{2,1,0:T(8,128)(2,1)S(1)} %get-tuple-element.234), channel_id=1, source_target_pairs={{0,2},{1,3},{2,0},{3,1},{4,6},{5,7},{6,4},{7,5},{8,10},{9,11},{10,... | collective-permute-start | bytes 1032200 | tf_op jit(solution)/shard_map/ppermute | solution.py:647
  247.8 20.2 %collective-permute-start.41 = (bf16[192,384]{1,0:T(8,128)(2,1)S(1)}, bf16[192,384]{1,0:T(8,128)(2,1)S(1)}, u32[]{:S(2)}, u32[]{:S(2)}) collective-permute-start(bf16[192,384]{1,0:T(8,128)(2,1)S(1)} %get-tuple-element.241), channel_id=1, source_target_pairs={{0,2},{1,3},{2,0},{3,1},{4,6},{5,7},{6,4},{7,5},{8,10},{9,11},{10,... | collective-permute-start | bytes 442376 | tf_op jit(solution)/shard_map/ppermute | solution.py:647
  258.1 10.0 %collective-permute-start.42 = (bf16[176,384]{1,0:T(8,128)(2,1)S(1)}, bf16[176,384]{1,0:T(8,128)(2,1)S(1)}, u32[]{:S(2)}, u32[]{:S(2)}) collective-permute-start(bf16[176,384]{1,0:T(8,128)(2,1)S(1)} %get-tuple-element.244), channel_id=1, source_target_pairs={{0,8},{4,12},{8,16},{12,20},{16,24},{20,28},{24,0},{28,4},{1,9},{5... | collective-permute-start | bytes 405512 | tf_op jit(solution)/shard_map/ppermute | solution.py:653
  260.6 10.1 %collective-permute-start.43 = (bf16[176,384]{1,0:T(8,128)(2,1)S(1)}, bf16[176,384]{1,0:T(8,128)(2,1)S(1)}, u32[]{:S(2)}, u32[]{:S(2)}) collective-permute-start(bf16[176,384]{1,0:T(8,128)(2,1)S(1)} %get-tuple-element.245), channel_id=1, source_target_pairs={{0,16},{4,20},{8,24},{12,28},{16,0},{20,4},{24,8},{28,12},{1,17},{... | collective-permute-start | bytes 405512 | tf_op jit(solution)/shard_map/ppermute | solution.py:653
  272.6 14.5 %collective-permute-start.45 = (f32[576,192]{0,1:T(8,128)S(1)}, f32[576,192]{0,1:T(8,128)S(1)}, u32[]{:S(2)}, u32[]{:S(2)}) collective-permute-start(f32[576,192]{0,1:T(8,128)S(1)} %copy.41), channel_id=1, source_target_pairs={{0,1},{1,0},{2,3},{3,2},{4,5},{5,4},{6,7},{7,6},{8,9},{9,8},{10,11... | collective-permute-start | bytes 1327112 | tf_op jit(solution)/shard_map/ppermute | solution.py:641
  (34 other events, 238.6 us)
